TPU v7x, 32 devices: a whole 2x2x4 slice. The times are simulated.
32 devices in a mesh: trow: 16 (over z, x, core), tcol: 2 (over y).
Axes of the slice: x: 2, y: 2, z: 4, core: 2. Of those that a mesh axis runs over, the one named last changes fastest.
Arguments:
- green_lesser: bfloat16 [2, 128, 128, 512], P(None, 'trow', 'tcol'), may hold values from -6 to 6
- green_greater: bfloat16 [2, 128, 128, 512], P(None, 'trow', 'tcol'), may hold values from -6 to 6
- lattice_map: int32 [512], replicated, may hold values from 0 to 511, each once
- time_offset: int32 [1], replicated, may hold values from 0 to 63
Outputs:
- collision_lesser: bfloat16 [2, 128, 128, 512], P(None, 'trow', 'tcol')
- collision_greater: bfloat16 [2, 128, 128, 512], P(None, 'trow', 'tcol')
Inputs may be any that keep to these rules, and one draw needn't show every extreme that they name: `lattice_map`: every lattice momentum index 0 to 511 appears exactly once.
All inputs are finite; a program needn't handle non-finite values.
Results may differ from a plain program's by a relative error of at most 0.011.
Values may be sent and summed in bfloat16 or wider, within the bound.
No kernel may reach another device: no remote copies, remote signals or barrier semaphores. Data moves between devices by JAX's collectives and lax.ppermute only.
A program may use at most 64 MiB of HBM per device.

v0:
```python
import math

import jax
import jax.numpy as jnp
from jax import lax
from jax.sharding import PartitionSpec as P

PERIOD = 64


step_size = 0.01
drive_depth = 0.5


def regroup(blocks):
    return lax.all_to_all(
        lax.all_to_all(blocks, "trow", split_axis=1, concat_axis=1, tiled=True),
        "tcol",
        split_axis=2,
        concat_axis=2,
        tiled=True,
    )


def pack_blocks(spectral, row_parts, col_parts):
    stacked, extent, tile_cells = spectral.shape
    return spectral.reshape(
        stacked, row_parts, col_parts, extent // (row_parts * col_parts), tile_cells
    )


def spread_times(blocks, tile_rows, tile_cols):
    stacked, row_parts, col_parts, local_count, tile_cells = blocks.shape
    shaped = blocks.reshape(stacked, row_parts, col_parts, local_count, tile_rows, tile_cols)
    return shaped.transpose(0, 3, 1, 4, 2, 5).reshape(
        stacked, local_count, row_parts * tile_rows, col_parts * tile_cols
    )


def gather_tiles(full, row_parts, col_parts):
    stacked, local_count, window, window_cols = full.shape
    tile_rows = window // row_parts
    tile_cols = window_cols // col_parts
    shaped = full.reshape(stacked, local_count, row_parts, tile_rows, col_parts, tile_cols)
    return shaped.transpose(0, 2, 4, 1, 3, 5).reshape(
        stacked, row_parts, col_parts, local_count, tile_rows * tile_cols
    )


def mirrored(full, keep_pair):
    stacked, local_count, window, window_cols = full.shape
    paired = full.reshape(stacked, local_count // 2, 2, window, window_cols)
    swapped = jnp.where(keep_pair[None, :, None, None, None], paired, paired[:, :, ::-1])
    return jnp.swapaxes(swapped.reshape(stacked, local_count, window, window_cols), 2, 3)


def second_born(first_real, first_imaginary, other_real, other_imaginary, coupling):
    square_real = first_real * first_real - first_imaginary * first_imaginary
    square_imaginary = 2.0 * first_real * first_imaginary
    out_real = coupling * (square_real * other_real - square_imaginary * other_imaginary)
    out_imaginary = coupling * (square_real * other_imaginary + square_imaginary * other_real)
    return (out_real, out_imaginary)


def collide(
    retarded_real,
    retarded_imaginary,
    self_real,
    self_imaginary,
    green_real,
    green_imaginary,
    advanced_real,
    advanced_imaginary,
):
    minus_left = jnp.concatenate(
        [retarded_real, -retarded_imaginary, self_real, -self_imaginary], axis=2
    )
    plus_left = jnp.concatenate(
        [retarded_real, retarded_imaginary, self_real, self_imaginary], axis=2
    )
    real_right = jnp.concatenate(
        [green_real, green_imaginary, advanced_real, advanced_imaginary], axis=1
    )
    imaginary_right = jnp.concatenate(
        [green_imaginary, green_real, advanced_imaginary, advanced_real], axis=1
    )
    out_real = jnp.einsum(
        "kts,ksu->ktu", minus_left, real_right, preferred_element_type=jnp.float32
    )
    out_imaginary = jnp.einsum(
        "kts,ksu->ktu", plus_left, imaginary_right, preferred_element_type=jnp.float32
    )
    return (out_real, out_imaginary)


def body(green_lesser, green_greater, lattice_map, time_offset):
    tile_rows = green_lesser.shape[1]
    tile_cols = green_lesser.shape[2]
    momenta = green_lesser.shape[3]
    row_parts = lax.axis_size("trow")
    col_parts = lax.axis_size("tcol")
    window = tile_rows * row_parts
    tile_cells = tile_rows * tile_cols
    local_count = momenta // (row_parts * col_parts)
    norm_factor = 1.0 / math.sqrt(momenta)
    greens = (
        jnp.concatenate([green_lesser, green_greater], axis=0)
        .reshape(4, tile_cells, momenta)
        .transpose(0, 2, 1)
    )
    positions = jnp.arange(momenta, dtype=jnp.int32)
    halves = positions // 2
    site_order = jnp.where(
        positions == 1, momenta // 2, jnp.where(positions % 2 == 0, halves, momenta - halves)
    )
    phases = (lattice_map[:, None] * site_order[None, :] % momenta).astype(jnp.float32) * (
        2.0 * math.pi / momenta
    )
    cosines = jnp.cos(phases).astype(jnp.bfloat16)
    sines = jnp.sin(phases).astype(jnp.bfloat16)
    ahead_blocks = lax.all_to_all(
        lax.all_to_all(
            pack_blocks(greens, row_parts, col_parts),
            "trow",
            split_axis=1,
            concat_axis=1,
            tiled=True,
        ),
        "tcol",
        split_axis=2,
        concat_axis=2,
        tiled=True,
    )
    green_moment = spread_times(ahead_blocks, tile_rows, tile_cols)
    forward_table = jnp.concatenate([cosines, sines], axis=1)
    products = jnp.einsum("cjm,jr->crm", greens, forward_table, preferred_element_type=jnp.float32)
    site_space = jnp.stack(
        [
            (products[0, :momenta] - products[1, momenta:]) * norm_factor,
            (products[0, momenta:] + products[1, :momenta]) * norm_factor,
            (products[2, :momenta] - products[3, momenta:]) * norm_factor,
            (products[2, momenta:] + products[3, :momenta]) * norm_factor,
        ]
    ).astype(jnp.bfloat16)
    site_full = spread_times(
        regroup(pack_blocks(site_space, row_parts, col_parts)), tile_rows, tile_cols
    )
    site_block = lax.axis_index("trow") * col_parts + lax.axis_index("tcol")
    keep_pair = site_block * (local_count // 2) + jnp.arange(local_count // 2, dtype=jnp.int32) == 0
    mirror = mirrored(site_full, keep_pair).astype(jnp.float32)
    direct = site_full.astype(jnp.float32)
    time_steps = jnp.arange(window, dtype=jnp.int32)
    coupling_line = 1.0 + drive_depth * jnp.cos(
        ((time_offset[0] + time_steps) % PERIOD).astype(jnp.float32) * (2.0 * math.pi / PERIOD)
    )
    coupling = coupling_line[:, None] * coupling_line[None, :]
    self_lesser = second_born(direct[0], direct[1], mirror[2], mirror[3], coupling)
    self_greater = second_born(direct[2], direct[3], mirror[0], mirror[1], coupling)
    self_sites = jnp.stack(
        [self_lesser[0], self_lesser[1], self_greater[0], self_greater[1]]
    ).astype(jnp.bfloat16)
    self_tiles = regroup(gather_tiles(self_sites, row_parts, col_parts)).reshape(
        4, momenta, tile_cells
    )
    inverse_table = jnp.concatenate([cosines, sines], axis=0)
    spectral_terms = jnp.einsum(
        "cum,ju->cjm", self_tiles, inverse_table, preferred_element_type=jnp.float32
    )
    self_spectral = jnp.stack(
        [
            (spectral_terms[0, :momenta] + spectral_terms[1, momenta:]) * norm_factor,
            (spectral_terms[1, :momenta] - spectral_terms[0, momenta:]) * norm_factor,
            (spectral_terms[2, :momenta] + spectral_terms[3, momenta:]) * norm_factor,
            (spectral_terms[3, :momenta] - spectral_terms[2, momenta:]) * norm_factor,
        ]
    ).astype(jnp.bfloat16)
    self_moment = spread_times(
        regroup(pack_blocks(self_spectral, row_parts, col_parts)), tile_rows, tile_cols
    )
    lower_mask = time_steps[None, :] <= time_steps[:, None]
    upper_mask = time_steps[:, None] <= time_steps[None, :]
    retarded = jnp.where(
        lower_mask, self_moment[2:4].astype(jnp.float32) - self_moment[0:2].astype(jnp.float32), 0.0
    ).astype(jnp.bfloat16)
    advanced = jnp.where(
        upper_mask,
        green_moment[0:2].astype(jnp.float32) - green_moment[2:4].astype(jnp.float32),
        0.0,
    ).astype(jnp.bfloat16)
    lesser_out = collide(
        retarded[0],
        retarded[1],
        self_moment[0],
        self_moment[1],
        green_moment[0],
        green_moment[1],
        advanced[0],
        advanced[1],
    )
    greater_out = collide(
        retarded[0],
        retarded[1],
        self_moment[2],
        self_moment[3],
        green_moment[2],
        green_moment[3],
        advanced[0],
        advanced[1],
    )
    collisions = (
        jnp.stack([lesser_out[0], lesser_out[1], greater_out[0], greater_out[1]]) * step_size
    ).astype(jnp.bfloat16)
    out_tiles = regroup(gather_tiles(collisions, row_parts, col_parts)).reshape(
        4, momenta, tile_cells
    )
    out_tiles = out_tiles.transpose(0, 2, 1).reshape(4, tile_rows, tile_cols, momenta)
    return (out_tiles[0:2], out_tiles[2:4])


def solution(mesh):
    in_specs = (P(None, "trow", "tcol", None), P(None, "trow", "tcol", None), P(), P())
    out_specs = (P(None, "trow", "tcol", None), P(None, "trow", "tcol", None))
    return jax.shard_map(body, mesh=mesh, in_specs=in_specs, out_specs=out_specs, check_vma=False)
```

profile of v0, /device:TPU:0, one launch (start us, length us, event | category | flops | bytes accessed | tf_op | source)
XLA Modules:
  0.0 599.9 jit_solution(7179372395342668575)
XLA Ops:
  0.6 3.1 pad_maximum_fusion.18
  3.7 2.8 copy.38
  6.5 4.6 cosine_convert_fusion
  12.1 2.3 convolution_bitcast_fusion.1
  15.8 54.5 %all_to_all.50 = bf16[4,16,2,16,512]{4,3,2,0,1:T(8,128)(2,1)S(1)} all-to-all(bf16[4,16,2,16,512]{4,3,2,0,1:T(8,128)(2,1)S(1)} %pad_maximum_fusion.19), channel_id=1, replica_groups=mesh['trow'=16,'tcol'=2] {'trow'}, dimensions={1} | all-to-all | bytes 4194304 | tf_op jit(solution)/shard_map/all_to_all | solution.py:17
  71.9 4.8 all-to-all-start.1
  77.5 25.3 %all-to-all-done.1 = bf16[4,16,2,16,512]{4,3,1,0,2:T(8,128)(2,1)} async-done(((bf16[4,16,2,16,512]{4,3,1,0,2:T(8,128)(2,1)}), bf16[4,16,2,16,512]{4,3,1,0,2:T(8,128)(2,1)}, u32[]{:S(2)}, u32[]{:S(2)}) %all-to-all-start.1) | async-done | bytes 2097184 | tf_op jit(solution)/shard_map/all_to_all | solution.py:16
  104.7 4.1 reshape.219
  108.8 3.2 bitcast_convert_fusion
  112.0 3.5 multiply_subtract_fusion.1
  118.2 3.2 copy.50
  121.4 2.1 mul.258
  123.5 3.2 copy.45
  126.8 2.1 sub.74
  128.9 3.4 copy.49
  132.3 2.1 sub.77
  134.4 10.7 %copy.46 = bf16[4,16,16,8,2,64]{5,4,3,2,1,0:T(2,128)(2,1)} copy(bf16[4,16,16,8,2,64]{5,3,1,4,2,0:T(8,128)(2,1)} %bitcast.98) | data formatting | bytes 4194304 | tf_op jit(solution)/shard_map/transpose | solution.py:35
  145.1 6.8 %reshape_reshape.3 = bf16[4,8,2,128,128]{4,3,2,1,0:T(8,128)(2,1)S(1)} reshape(bf16[4,16,16,8,2,64]{5,4,3,2,1,0:T(2,128)(2,1)} %copy.46) | data formatting | bytes 4194304 | tf_op jit(solution)/shard_map/reshape;reshape | solution.py:52
  151.8 2.9 fusion.14
  154.8 5.7 copy.47
  160.5 4.9 multiply_convert_fusion.3
  165.4 2.4 stack.65
  167.9 2.5 stack.66
  170.4 2.5 stack.67
  172.8 3.2 stack.68
  176.0 9.5 %maximum_bitcast_fusion = bf16[4,16,2,16,8,64]{5,2,4,1,3,0:T(2,128)(2,1)S(1)} fusion(bf16[1,16,16,8,2,64]{5,4,3,2,1,0:T(2,128)(2,1)} %stack.68, bf16[1,16,16,8,2,64]{5,4,3,2,1,0:T(2,128)(2,1)S(1)} %stack.67, bf16[1,16,16,8,2,64]{5,4,3,2,1,0:T(2,128)(2,1)S(1)} %stack.66, bf16[1,16,16,8,2,64]{5,4,3,2,1,0:T(2,128)(2,1)S(1)} %stack.65), kind=kLoop, calls=%fused_computation.3 | loop fusion | flops 3145728 | bytes 4194304 | tf_op jit(solution)/shard_map/transpose | solution.py:45
  185.5 3.1 copy.76
  188.6 6.5 %reshape.230 = bf16[4,16,2,16,512]{4,3,2,0,1:T(8,128)(2,1)} reshape(bf16[4,16,2,16,8,64]{5,4,3,2,0,1:T(8,128)(2,1)} %copy.76) | data formatting | bytes 4194304 | tf_op jit(solution)/shard_map/reshape | solution.py:45
  195.1 4.8 all-to-all-start.2
  201.5 39.6 %all-to-all-done.2 = bf16[4,16,2,16,512]{4,3,2,0,1:T(8,128)(2,1)} async-done(((bf16[4,16,2,16,512]{4,3,2,0,1:T(8,128)(2,1)}), bf16[4,16,2,16,512]{4,3,2,0,1:T(8,128)(2,1)}, u32[]{:S(2)}, u32[]{:S(2)}) %all-to-all-start.2) | async-done | bytes 2097184 | tf_op jit(solution)/shard_map/all_to_all | solution.py:17
  241.1 11.2 %all-to-all-start.6 = ((bf16[4,16,2,16,512]{4,3,2,0,1:T(8,128)(2,1)}), bf16[4,16,2,16,512]{4,3,2,0,1:T(8,128)(2,1)S(1)}, u32[]{:S(2)}, u32[]{:S(2)}) async-start(bf16[4,16,2,16,512]{4,3,2,0,1:T(8,128)(2,1)} %copy.62), calls=%async_computation.6 | async-start | bytes 4194304 | tf_op jit(solution)/shard_map/all_to_all | solution.py:122
  252.3 3.2 copy.53
  255.5 37.9 %all-to-all-done.6 = bf16[4,16,2,16,512]{4,3,2,0,1:T(8,128)(2,1)S(1)} async-done(((bf16[4,16,2,16,512]{4,3,2,0,1:T(8,128)(2,1)}), bf16[4,16,2,16,512]{4,3,2,0,1:T(8,128)(2,1)S(1)}, u32[]{:S(2)}, u32[]{:S(2)}) %all-to-all-start.6) | async-done | bytes 2097184 | tf_op jit(solution)/shard_map/all_to_all | solution.py:122
  293.4 4.8 all-to-all-start.3
  299.8 24.5 %all-to-all-done.3 = bf16[4,16,2,16,512]{4,3,1,0,2:T(8,128)(2,1)} async-done(((bf16[4,16,2,16,512]{4,3,1,0,2:T(8,128)(2,1)}), bf16[4,16,2,16,512]{4,3,1,0,2:T(8,128)(2,1)}, u32[]{:S(2)}, u32[]{:S(2)}) %all-to-all-start.3) | async-done | bytes 2097184 | tf_op jit(solution)/shard_map/all_to_all | solution.py:16
  324.3 4.2 all-to-all-start.7
  330.4 2.4 convolution_bitcast_fusion
  335.7 18.0 %all-to-all-done.7 = bf16[4,16,2,16,512]{4,3,1,0,2:T(8,128)(2,1)S(1)} async-done(((bf16[4,16,2,16,512]{4,3,1,0,2:T(8,128)(2,1)}), bf16[4,16,2,16,512]{4,3,1,0,2:T(8,128)(2,1)S(1)}, u32[]{:S(2)}, u32[]{:S(2)}) %all-to-all-start.7) | async-done | bytes 2097184 | tf_op jit(solution)/shard_map/all_to_all | solution.py:121
  353.7 10.4 %all-to-all-start.4 = ((bf16[4,16,2,16,512]{4,3,2,0,1:T(8,128)(2,1)}), bf16[4,16,2,16,512]{4,3,2,0,1:T(8,128)(2,1)}, u32[]{:S(2)}, u32[]{:S(2)}) async-start(bf16[4,16,2,16,512]{4,3,2,0,1:T(8,128)(2,1)} %pad_maximum_fusion.20), calls=%async_computation.4 | async-start | bytes 4194304 | tf_op jit(solution)/shard_map/all_to_all | solution.py:17
  364.1 3.7 reshape.224
  367.8 10.6 %copy.80 = bf16[4,16,2,16,8,64]{5,2,4,1,3,0:T(2,128)(2,1)} copy(bf16[4,16,2,16,8,64]{5,4,3,1,0,2:T(8,128)(2,1)} %reshape.224) | data formatting | bytes 4194304 | tf_op jit(solution)/shard_map/reshape | solution.py:34
  378.4 26.8 %all-to-all-done.4 = bf16[4,16,2,16,512]{4,3,2,0,1:T(8,128)(2,1)} async-done(((bf16[4,16,2,16,512]{4,3,2,0,1:T(8,128)(2,1)}), bf16[4,16,2,16,512]{4,3,2,0,1:T(8,128)(2,1)}, u32[]{:S(2)}, u32[]{:S(2)}) %all-to-all-start.4) | async-done | bytes 2097184 | tf_op jit(solution)/shard_map/all_to_all | solution.py:17
  405.2 3.2 copy.60
  408.4 3.9 all-to-all-start.5
  412.3 5.2 convert_subtract_fusion
  417.6 3.9 sub.84
  421.5 6.8 %fusion.77 = (bf16[1,16,16,8,2,64]{5,4,3,2,1,0:T(2,128)(2,1)}, bf16[1,16,16,8,2,64]{5,4,3,2,1,0:T(2,128)(2,1)}, bf16[1,16,16,8,2,64]{5,4,3,2,1,0:T(2,128)(2,1)}, bf16[1,16,16,8,2,64]{5,4,3,2,1,0:T(2,128)(2,1)}) fusion(bf16[4,16,16,8,2,64]{5,4,3,2,1,0:T(2,128)(2,1)} %bitcast.100), kind=kLoop, calls=%fused_computation.144 | loop fusion | bytes 4194304 | tf_op jit(solution)/shard_map/slice | solution.py:196
  428.2 3.1 squeeze.31
  431.3 3.1 squeeze.32
  434.4 3.1 squeeze.37
  437.5 3.1 squeeze.38
  441.8 3.8 reshape.222
  445.6 8.7 %copy.81 = bf16[4,16,2,16,8,64]{5,2,4,1,3,0:T(2,128)(2,1)S(1)} copy(bf16[4,16,2,16,8,64]{5,4,3,1,0,2:T(8,128)(2,1)} %reshape.222) | data formatting | bytes 4194304 | tf_op jit(solution)/shard_map/reshape | solution.py:34
  454.3 2.3 convert_subtract_fusion.1
  456.5 4.7 fusion.78
  470.2 3.3 fusion.9
  473.5 2.7 stack.75
  480.5 2.5 stack.76
  487.4 2.7 fusion.6
  492.0 2.5 stack.77
  499.5 3.8 fusion.1
  503.4 5.4 reshape.225
  509.0 58.3 %all_to_all.51 = bf16[4,16,2,16,512]{4,3,2,0,1:T(8,128)(2,1)S(1)} all-to-all(bf16[4,16,2,16,512]{4,3,2,0,1:T(8,128)(2,1)S(1)} %copy.69), channel_id=1, replica_groups=mesh['trow'=16,'tcol'=2] {'trow'}, dimensions={1} | all-to-all | bytes 4194304 | tf_op jit(solution)/shard_map/all_to_all | solution.py:17
  567.6 28.8 %all_to_all.52 = bf16[4,16,2,16,512]{4,3,1,0,2:T(8,128)(2,1)S(1)} all-to-all(bf16[4,16,2,16,512]{4,3,1,0,2:T(8,128)(2,1)S(1)} %copy.70), channel_id=1, replica_groups=mesh['trow'=16,'tcol'=2] {'tcol'}, dimensions={2} | all-to-all | bytes 4194304 | tf_op jit(solution)/shard_map/all_to_all | solution.py:16
  (108 shorter events, 45.5 us)
Async XLA Ops:
  3.7 2.8 copy-start.32
  6.5 7.9 %copy-start = (bf16[4,512,512]{1,2,0:T(8,128)(2,1)}, bf16[4,512,512]{1,2,0:T(8,128)(2,1)S(1)}, u32[]{:S(2)}) copy-start(bf16[4,512,512]{1,2,0:T(8,128)(2,1)S(1)} %copy.38) | copy-start | bytes 6291460
  11.1 0.8 copy-start.19
  11.1 1.0 copy-start.21
  71.9 31.0 %all-to-all-start.1 = ((bf16[4,16,2,16,512]{4,3,1,0,2:T(8,128)(2,1)}), bf16[4,16,2,16,512]{4,3,1,0,2:T(8,128)(2,1)}, u32[]{:S(2)}, u32[]{:S(2)}) async-start(bf16[4,16,2,16,512]{4,3,1,0,2:T(8,128)(2,1)} %copy.43), calls=%async_computation.1 | async-start | bytes 4194304 | tf_op jit(solution)/shard_map/all_to_all | solution.py:16
  154.8 5.7 copy-start.4
  154.8 5.7 copy-start.5
  195.1 4.8 copy-start.1
  195.1 46.0 %all-to-all-start.2 = ((bf16[4,16,2,16,512]{4,3,2,0,1:T(8,128)(2,1)}), bf16[4,16,2,16,512]{4,3,2,0,1:T(8,128)(2,1)}, u32[]{:S(2)}, u32[]{:S(2)}) async-start(bf16[4,16,2,16,512]{4,3,2,0,1:T(8,128)(2,1)} %reshape.230), calls=%async_computation.2 | async-start | bytes 4194304 | tf_op jit(solution)/shard_map/all_to_all | solution.py:17
  241.1 52.3 %all-to-all-start.6 = ((bf16[4,16,2,16,512]{4,3,2,0,1:T(8,128)(2,1)}), bf16[4,16,2,16,512]{4,3,2,0,1:T(8,128)(2,1)S(1)}, u32[]{:S(2)}, u32[]{:S(2)}) async-start(bf16[4,16,2,16,512]{4,3,2,0,1:T(8,128)(2,1)} %copy.62), calls=%async_computation.6 | async-start | bytes 4194304 | tf_op jit(solution)/shard_map/all_to_all | solution.py:122
  293.4 31.0 %all-to-all-start.3 = ((bf16[4,16,2,16,512]{4,3,1,0,2:T(8,128)(2,1)}), bf16[4,16,2,16,512]{4,3,1,0,2:T(8,128)(2,1)}, u32[]{:S(2)}, u32[]{:S(2)}) async-start(bf16[4,16,2,16,512]{4,3,1,0,2:T(8,128)(2,1)} %copy.53), calls=%async_computation.3 | async-start | bytes 4194304 | tf_op jit(solution)/shard_map/all_to_all | solution.py:16
  324.3 29.3 %all-to-all-start.7 = ((bf16[4,16,2,16,512]{4,3,1,0,2:T(8,128)(2,1)}), bf16[4,16,2,16,512]{4,3,1,0,2:T(8,128)(2,1)S(1)}, u32[]{:S(2)}, u32[]{:S(2)}) async-start(bf16[4,16,2,16,512]{4,3,1,0,2:T(8,128)(2,1)} %copy.63), calls=%async_computation.7 | async-start | bytes 4194304 | tf_op jit(solution)/shard_map/all_to_all | solution.py:121
  328.5 1.9 copy-start.20
  328.5 1.9 copy-start.22
  353.7 51.5 %all-to-all-start.4 = ((bf16[4,16,2,16,512]{4,3,2,0,1:T(8,128)(2,1)}), bf16[4,16,2,16,512]{4,3,2,0,1:T(8,128)(2,1)}, u32[]{:S(2)}, u32[]{:S(2)}) async-start(bf16[4,16,2,16,512]{4,3,2,0,1:T(8,128)(2,1)} %pad_maximum_fusion.20), calls=%async_computation.4 | async-start | bytes 4194304 | tf_op jit(solution)/shard_map/all_to_all | solution.py:17
  408.4 33.4 %all-to-all-start.5 = ((bf16[4,16,2,16,512]{4,3,1,0,2:T(8,128)(2,1)}), bf16[4,16,2,16,512]{4,3,1,0,2:T(8,128)(2,1)S(1)}, u32[]{:S(2)}, u32[]{:S(2)}) async-start(bf16[4,16,2,16,512]{4,3,1,0,2:T(8,128)(2,1)} %copy.60), calls=%async_computation.5 | async-start | bytes 4194304 | tf_op jit(solution)/shard_map/all_to_all | solution.py:16
  463.1 2.5 copy-start.6
  465.6 1.9 copy-start.10
  466.9 2.0 copy-start.9
  467.4 2.7 copy-start.13
  467.9 2.2 copy-start.14
  469.4 0.8 copy-start.16
  476.2 1.7 copy-start.15
  476.3 1.7 copy-start.17
  476.3 1.7 copy-start.25
  476.3 2.2 copy-start.27
  476.3 2.4 copy-start.29
  476.3 2.5 copy-start.31
  483.0 1.6 copy-start.8
  484.7 1.4 copy-start.7
  484.7 2.7 copy-start.11
  487.4 2.7 copy-start.12
  487.4 2.7 copy-start.18
  487.4 2.8 copy-start.23
  487.4 2.8 copy-start.24
  487.4 2.8 copy-start.26
  487.4 2.8 copy-start.28
  487.4 2.9 copy-start.30
  497.3 1.6 copy-start.2
  497.3 2.2 copy-start.3
where the time goes:
time: 606 us; the launch traced here: 600 us
  local copies, waits for them, and re-layouts  172 us (28%)
  waiting for transfers between devices  172 us (28%)
  blocking collectives  142 us (23%)
  other arithmetic  53 us (9%)
  starting transfers between devices  44.2 us (7%)
  matrix products  14.1 us (2%)
    all_to_all x2, blocking collectives, regroup(): lax.all_to_all(blocks, 'trow', split_axis=1, concat_axis=1, tiled=True)  113 us
    all_to_all x2, waiting for transfers between devices, regroup(): lax.all_to_all(blocks, 'trow', split_axis=1, concat_axis=1, tiled=True)  66.4 us
    all_to_all x3, waiting for transfers between devices, regroup(): lax.all_to_all(lax.all_to_all(blocks, 'trow', split_axis=1, concat_axis=1...  49.9 us
    all_to_all x1, waiting for transfers between devices, body(): lax.all_to_all(pack_blocks(greens, row_parts, col_parts), 'trow', split_a...  37.9 us
    reshape x5, local copies, waits for them, and re-layouts, spread_times(): blocks.reshape(stacked, row_parts, col_parts, local_count, tile_rows, til...  30.8 us
    all_to_all x1, blocking collectives, regroup(): lax.all_to_all(lax.all_to_all(blocks, 'trow', split_axis=1, concat_axis=1...  28.8 us
    all_to_all x1, waiting for transfers between devices, body(): lax.all_to_all(lax.all_to_all(pack_blocks(greens, row_parts, col_parts),...  18 us
    all_to_all x2, starting transfers between devices, regroup(): lax.all_to_all(blocks, 'trow', split_axis=1, concat_axis=1, tiled=True)  15.2 us
  transfers between devices with their start and end apart: 7, of which 6 were waited for; matrix products, arithmetic and copies ran while one was open for 10% of the time, Pallas kernels for 0%

commit v1 on v0

--- a/solution.py
+++ b/solution.py
@@ -1,9 +1,16 @@
+import functools
 import math
 
 import jax
 import jax.numpy as jnp
 from jax import lax
-from jax.sharding import PartitionSpec as P
+from jax.experimental import pallas as pl
+from jax.experimental.pallas import tpu as pltpu
+from jax.sharding import Mesh, PartitionSpec as P
+
+F32 = jnp.float32
+BF16 = jnp.bfloat16
+LANES = 128
 
 PERIOD = 64
 
@@ -93,7 +100,7 @@
     return (out_real, out_imaginary)
 
 
-def body(green_lesser, green_greater, lattice_map, time_offset):
+def general_body(green_lesser, green_greater, lattice_map, time_offset):
     tile_rows = green_lesser.shape[1]
     tile_cols = green_lesser.shape[2]
     momenta = green_lesser.shape[3]
@@ -217,7 +224,326 @@
     return (out_tiles[0:2], out_tiles[2:4])
 
 
+def vmem_params():
+    return pltpu.CompilerParams(vmem_limit_bytes=48 * 1024 * 1024)
+
+
+def whole(count):
+    return [pl.BlockSpec(memory_space=pltpu.VMEM)] * count
+
+
+def spread_kernel(tile, out, lines):
+    _, rows, _, momenta = tile.shape
+    for t in range(rows):
+        slab = jnp.concatenate([tile[0, t], tile[1, t]], axis=0).astype(F32)
+        lines[pl.ds(t, momenta, stride=rows), :] = slab.T
+    out[...] = lines[...].astype(BF16)
+
+
+def spread(tile):
+    _, rows, cols, momenta = tile.shape
+    shape = (momenta * rows, 2 * cols)
+    return pl.pallas_call(
+        spread_kernel,
+        out_shape=jax.ShapeDtypeStruct(shape, BF16),
+        in_specs=whole(1),
+        out_specs=whole(1)[0],
+        scratch_shapes=[pltpu.VMEM(shape, F32)],
+        compiler_params=vmem_params(),
+        name="spread",
+    )(tile)
+
+
+def collect_kernel(rows_ref, lesser, greater, lines):
+    lines[...] = rows_ref[...].astype(F32)
+    _, rows, cols, momenta = lesser.shape
+    for k in range(2 * rows):
+        slab = lines[pl.ds(k, momenta, stride=2 * rows), :].T.astype(BF16)
+        out = lesser if k < rows else greater
+        out[0, k % rows] = slab[:cols]
+        out[1, k % rows] = slab[cols:]
+
+
+def collect(rows_array, tile_shape):
+    shape = jax.ShapeDtypeStruct(tile_shape, BF16)
+    return pl.pallas_call(
+        collect_kernel,
+        out_shape=(shape, shape),
+        in_specs=whole(1),
+        out_specs=tuple(whole(2)),
+        scratch_shapes=[pltpu.VMEM(rows_array.shape, F32)],
+        compiler_params=vmem_params(),
+        name="collect",
+    )(rows_array)
+
+
+def site_kernel(norm_factor, tile, table, out):
+    both = jnp.concatenate([tile[0], tile[1]], axis=1)
+    momenta = tile.shape[2]
+    for part in range(2):
+        product = jnp.dot(
+            both, table[:, part * momenta : (part + 1) * momenta], preferred_element_type=F32
+        )
+        out[part] = (product * norm_factor).astype(BF16)
+
+
+def to_sites(tile, table, norm_factor):
+    return pl.pallas_call(
+        functools.partial(site_kernel, norm_factor),
+        out_shape=jax.ShapeDtypeStruct(tile.shape, BF16),
+        in_specs=whole(2),
+        out_specs=whole(1)[0],
+        compiler_params=vmem_params(),
+        name="to_sites",
+    )(tile, table)
+
+
+def sigma_kernel(norm_factor, rows, own, crossed, table, inverse, coupling, out, mirror, lines):
+    blocks, _, block_rows, momenta = crossed.shape
+    cols = blocks * block_rows // rows
+    real = jnp.concatenate([crossed[i, 0] for i in range(blocks)], axis=0)
+    imaginary = jnp.concatenate([crossed[i, 1] for i in range(blocks)], axis=0)
+    both = jnp.concatenate([real, -imaginary], axis=1)
+    for part in range(2):
+        product = jnp.dot(
+            both, table[:, part * momenta : (part + 1) * momenta], preferred_element_type=F32
+        )
+        product = (product * norm_factor).astype(BF16).astype(F32)
+        for at in range(momenta // LANES):
+            mirror[part, at] = product[:, at * LANES : (at + 1) * LANES]
+    for pair in range(rows // 2):
+        rights = []
+        for t in (2 * pair, 2 * pair + 1):
+            other_real, other_imaginary = (
+                jnp.concatenate(
+                    [
+                        mirror[part, at, pl.ds(t, cols, stride=rows), :]
+                        for at in range(momenta // LANES)
+                    ],
+                    axis=1,
+                )
+                for part in range(2)
+            )
+            cells = pl.ds(t * cols, cols)
+            self_real, self_imaginary = second_born(
+                own[0, cells, :].astype(F32),
+                own[1, cells, :].astype(F32),
+                other_real,
+                -other_imaginary,
+                coupling[cells, :],
+            )
+            self_real = self_real.astype(BF16)
+            self_imaginary = self_imaginary.astype(BF16)
+            rights.append(jnp.concatenate([self_real, self_imaginary], axis=1))
+            rights.append(jnp.concatenate([self_imaginary, -self_real], axis=1))
+        product = lax.dot_general(
+            inverse[...],
+            jnp.concatenate(rights, axis=0),
+            (((1,), (1,)), ((), ())),
+            preferred_element_type=F32,
+        ) * norm_factor
+        lines[pl.ds(2 * pair, momenta, stride=rows), :] = product[:, : 2 * cols]
+        lines[pl.ds(2 * pair + 1, momenta, stride=rows), :] = product[:, 2 * cols :]
+    out[...] = lines[...].astype(BF16)
+
+
+def to_sigma(own, crossed, table, inverse, coupling, rows, norm_factor):
+    _, cells, momenta = own.shape
+    shape = (momenta * rows, 2 * cells // rows)
+    return pl.pallas_call(
+        functools.partial(sigma_kernel, norm_factor, rows),
+        out_shape=jax.ShapeDtypeStruct(shape, BF16),
+        in_specs=whole(5),
+        out_specs=whole(1)[0],
+        scratch_shapes=[
+            pltpu.VMEM((2, momenta // LANES, cells, LANES), F32),
+            pltpu.VMEM(shape, F32),
+        ],
+        compiler_params=vmem_params(),
+        name="to_sigma",
+    )(own, crossed, table, inverse, coupling)
+
+
+def volterra_kernel(rows, half_ref, own_l, own_g, far_l, far_g, sig_l, sig_g, out):
+    half = half_ref[0]
+    sources = own_l.shape[0]
+    blocks = sources // 2
+    lanes = own_l.shape[2]
+    cols = lanes // 2
+    near = half * cols
+    away = (1 - half) * cols
+    first_times = half * cols + lax.broadcasted_iota(jnp.int32, (cols, lanes), 0)
+    left_lane = lax.broadcasted_iota(jnp.int32, (cols, lanes), 1)
+    left_times = jnp.where(left_lane < cols, near + left_lane, away + left_lane - cols)
+    keep_left = left_times <= first_times
+    row_at = lax.broadcasted_iota(jnp.int32, (lanes, 2 * lanes), 0)
+    inner_times = jnp.where(row_at < cols, near + row_at, away + row_at - cols)
+    lane_at = lax.broadcasted_iota(jnp.int32, (lanes, 2 * lanes), 1)
+    last_times = lane_at // lanes * cols + lane_at % cols
+    keep_right = inner_times <= last_times
+    low_lanes = left_lane < cols
+    pairs = []
+
+    def tall(ref, at, flipped):
+        lines = []
+        for block in range(blocks):
+            parts = []
+            for side in range(2):
+                source = 2 * block + (1 - side if flipped else side)
+                parts.append(ref[source].astype(F32)[at * rows : (at + 1) * rows])
+            lines.append(jnp.concatenate(parts, axis=1))
+        return jnp.concatenate(lines, axis=0)
+
+    def wide(ref, at):
+        near_lines = []
+        far_lines = []
+        for block in range(blocks):
+            near_lines.append(ref[2 * block + half].astype(F32)[at * rows : (at + 1) * rows])
+            far_lines.append(ref[2 * block + 1 - half].astype(F32)[at * rows : (at + 1) * rows])
+        near_part = jnp.concatenate(near_lines, axis=0)
+        far_part = jnp.concatenate(far_lines, axis=0)
+        return (
+            jnp.where(low_lanes, near_part, pltpu.roll(far_part, cols, 1)),
+            jnp.where(low_lanes, pltpu.roll(near_part, cols, 1), far_part),
+        )
+
+    for at in range(2):
+        green_l = jnp.concatenate([tall(own_l, at, False), tall(far_l, at, True)], axis=0)
+        green_g = jnp.concatenate([tall(own_g, at, False), tall(far_g, at, True)], axis=0)
+        advanced = jnp.where(keep_right, green_l - green_g, 0.0).astype(BF16)
+        real_l, imaginary_l = wide(sig_l, at)
+        real_g, imaginary_g = wide(sig_g, at)
+        retarded = jnp.concatenate(
+            [
+                jnp.where(keep_left, real_g - real_l, 0.0),
+                jnp.where(keep_left, imaginary_g - imaginary_l, 0.0),
+            ],
+            axis=0,
+        ).astype(BF16)
+        results = []
+        for real, imaginary, green in (
+            (real_l, imaginary_l, green_l),
+            (real_g, imaginary_g, green_g),
+        ):
+            sigma = jnp.concatenate([real, imaginary], axis=0).astype(BF16)
+            left = jnp.concatenate([retarded, sigma], axis=1)
+            right = jnp.concatenate([green.astype(BF16), advanced], axis=0)
+            product = jnp.dot(left, right, preferred_element_type=F32)
+            sides = []
+            for side in range(2):
+                straight = product[:cols, side * lanes : (side + 1) * lanes]
+                turned = pltpu.roll(product[cols:, side * lanes : (side + 1) * lanes], cols, 1)
+                sides.append((straight + jnp.where(low_lanes, -turned, turned)) * step_size)
+            results.append(sides)
+        pairs.append(results)
+    for block in range(blocks):
+        span = slice(block * rows, (block + 1) * rows)
+        for side in range(2):
+            lines = [pairs[at][g][side][span] for at in range(2) for g in range(2)]
+            out[2 * block + side] = jnp.concatenate(lines, axis=0).astype(BF16)
+
+
+def volterra(half, own, far, sigma, rows):
+    sources, lines, lanes = own[0].shape
+    steps = lines // (2 * rows)
+    spec = pl.BlockSpec((sources, 2 * rows, lanes), lambda p: (0, p, 0))
+    return pl.pallas_call(
+        functools.partial(volterra_kernel, rows),
+        grid=(steps,),
+        out_shape=jax.ShapeDtypeStruct((sources, 2 * lines, lanes), BF16),
+        in_specs=[pl.BlockSpec(memory_space=pltpu.SMEM)] + [spec] * 6,
+        out_specs=pl.BlockSpec((sources, 4 * rows, lanes), lambda p: (0, p, 0)),
+        compiler_params=vmem_params(),
+        name="volterra",
+    )(half, *own, *far, *sigma)
+
+
+def halved_body(green_lesser, green_greater, lattice_map, time_offset):
+    _, rows, cols, momenta = green_lesser.shape
+    half = lax.axis_index("half")
+    line = lax.axis_index("line")
+    side = lax.axis_index("tcol")
+    lines = lax.axis_size("line")
+    sides = lax.axis_size("tcol")
+    group = lines * sides
+    window = rows * lines * lax.axis_size("half")
+    norm_factor = 1.0 / math.sqrt(momenta)
+    greens = (green_lesser, green_greater)
+    corners = [(a, b) for a in range(2) for b in range(2)]
+    opposite = [(2 * a + b, 2 * (1 - a) + 1 - b) for a, b in corners]
+
+    def momentum_blocks(rows_array):
+        shaped = rows_array.reshape(group, rows_array.shape[0] // group, rows_array.shape[1])
+        return lax.all_to_all(shaped, ("line", "tcol"), 0, 0, tiled=True)
+
+    far_tiles = [lax.ppermute(green, ("half", "tcol"), opposite) for green in greens]
+    own_moment = [momentum_blocks(spread(green)) for green in greens]
+    positions = jnp.arange(momenta, dtype=jnp.int32)
+    phases = (lattice_map[:, None] * positions[None, :] % momenta).astype(F32) * (
+        2.0 * math.pi / momenta
+    )
+    cosines = jnp.cos(phases).astype(BF16)
+    sines = jnp.sin(phases).astype(BF16)
+    inverse = jnp.concatenate([cosines, sines], axis=1)
+    table = jnp.concatenate([inverse, jnp.concatenate([-sines, cosines], axis=1)], axis=0)
+    sites = [to_sites(green.reshape(2, rows * cols, momenta), table, norm_factor) for green in greens]
+    time_steps = jnp.arange(window, dtype=jnp.int32)
+    coupling_line = 1.0 + drive_depth * jnp.cos(
+        ((time_offset[0] + time_steps) % PERIOD).astype(F32) * (2.0 * math.pi / PERIOD)
+    )
+    first = lax.dynamic_slice_in_dim(coupling_line, (half * lines + line) * rows, rows)
+    second = lax.dynamic_slice_in_dim(coupling_line, side * cols, cols)
+    coupling = (first[:, None] * second[None, :]).reshape(rows * cols, 1)
+    crossed = []
+    far_moment = []
+    for green, far in zip(greens, far_tiles):
+        chosen = jnp.where(side == half, green, far)
+        sent = chosen.reshape(2, rows, lines, cols // lines, momenta).transpose(2, 0, 1, 3, 4)
+        crossed.append(
+            lax.all_to_all(sent, "line", 0, 0, tiled=True).reshape(
+                lines, 2, rows * cols // lines, momenta
+            )
+        )
+        far_moment.append(momentum_blocks(spread(far)))
+    sigma = [
+        momentum_blocks(
+            to_sigma(sites[g], crossed[1 - g], table, inverse, coupling, rows, norm_factor)
+        )
+        for g in range(2)
+    ]
+    collisions = volterra(half[None], own_moment, far_moment, sigma, rows)
+    returned = lax.all_to_all(collisions, ("line", "tcol"), 0, 0, tiled=True)
+    return collect(returned.reshape(-1, 2 * cols), green_lesser.shape)
+
+
 def solution(mesh):
-    in_specs = (P(None, "trow", "tcol", None), P(None, "trow", "tcol", None), P(), P())
-    out_specs = (P(None, "trow", "tcol", None), P(None, "trow", "tcol", None))
-    return jax.shard_map(body, mesh=mesh, in_specs=in_specs, out_specs=out_specs, check_vma=False)
+    row_parts = mesh.shape["trow"]
+    col_parts = mesh.shape["tcol"]
+
+    def call(green_lesser, green_greater, lattice_map, time_offset):
+        window, window_cols, momenta = green_lesser.shape[1:]
+        rows = window // row_parts
+        cols = window_cols // col_parts
+        halved = (
+            col_parts == 2
+            and row_parts % 2 == 0
+            and window == window_cols
+            and 2 * cols == LANES
+            and cols == rows * (row_parts // 2)
+            and rows % 8 == 0
+            and momenta % (row_parts * LANES // 8) == 0
+        )
+        if halved:
+            devices = mesh.devices.reshape(2, row_parts // 2, col_parts)
+            used = Mesh(devices, ("half", "line", "tcol"))
+            spec = P(None, ("half", "line"), "tcol", None)
+            inner = halved_body
+        else:
+            used = mesh
+            spec = P(None, "trow", "tcol", None)
+            inner = general_body
+        return jax.shard_map(
+            inner, mesh=used, in_specs=(spec, spec, P(), P()), out_specs=(spec, spec), check_vma=False
+        )(green_lesser, green_greater, lattice_map, time_offset)
+
+    return call

time: 606 us -> 292 us (0.48)
  local copies, waits for them, and re-layouts: 172 us -> 10.2 us
  blocking collectives: 142 us -> 49.9 us
  other arithmetic: 53 us -> 12.4 us
  Pallas kernels: 0 us -> 32.4 us
  waiting for transfers between devices: 172 us -> 145 us
  matrix products: 14.1 us -> 0 us
    all_to_all x7, waiting for transfers between devices: 172 us -> 48.4 us  [the longest x5 36.9 us: momentum_blocks(): return lax.all_to_all(shaped, ('line', 'tcol'), 0, 0, tiled=True)]
    ppermute x0 -> x2, waiting for transfers between devices: none -> 96.5 us  [halved_body(): lax.ppermute(green, ('half', 'tcol'), opposite)]
    all_to_all x3 -> x2, blocking collectives: 142 us -> 49.9 us  [the longest x1 30.8 us: halved_body(): returned = lax.all_to_all(collisions, ('line', 'tcol'), 0, 0, tiled=True)]
    reshape x11 -> x0, local copies, waits for them, and re-layouts: 50.4 us -> none  [the longest x5 30.8 us: spread_times(): blocks.reshape(stacked, row_parts, col_parts, local_count, tile_rows, til...]
    pallas_call x0 -> x10, Pallas kernels: none -> 32.4 us  [the longest x1 12.2 us: volterra(): pl.pallas_call(functools.partial(volterra_kernel, rows), grid=(steps,), o...]
    another operation x13 -> x0, local copies, waits for them, and re-layouts: 31.3 us -> none  [the longest x8 14 us: body(): jnp.stack([lesser_out[0], lesser_out[1], greater_out[0], greater_out[1]])]
    sub x6 -> x0, local copies, waits for them, and re-layouts: 16.5 us -> none  [the longest x4 10.8 us: second_born(): square_real = first_real * first_real - first_imaginary * first_imaginary]
    squeeze x9 -> x0, local copies, waits for them, and re-layouts: 16.4 us -> none  [the longest x1 3.09 us: body(): green_moment[3]]
  transfers between devices with their start and end apart: 7 -> 9, of which waited for: 6 -> 6; matrix products, arithmetic and copies ran while one was open for 10% -> 4% of each run, Pallas kernels for 0% -> 5%
where the time goes in v1:
time: 292 us; the launch traced here: 290 us
  waiting for transfers between devices  145 us (50%)
  blocking collectives  49.9 us (17%)
  starting transfers between devices  38.4 us (13%)
  Pallas kernels  32.4 us (11%)
  other arithmetic  12.4 us (4%)
  local copies, waits for them, and re-layouts  10.2 us (3%)
    ppermute x2, waiting for transfers between devices, halved_body(): lax.ppermute(green, ('half', 'tcol'), opposite)  96.5 us
    all_to_all x5, waiting for transfers between devices, momentum_blocks(): return lax.all_to_all(shaped, ('line', 'tcol'), 0, 0, tiled=True)  36.9 us
    all_to_all x1, blocking collectives, halved_body(): returned = lax.all_to_all(collisions, ('line', 'tcol'), 0, 0, tiled=True)  30.8 us
    all_to_all x5, starting transfers between devices, momentum_blocks(): return lax.all_to_all(shaped, ('line', 'tcol'), 0, 0, tiled=True)  25 us
    all_to_all x1, blocking collectives, momentum_blocks(): return lax.all_to_all(shaped, ('line', 'tcol'), 0, 0, tiled=True)  19.1 us
    pallas_call x1, Pallas kernels, volterra(): pl.pallas_call(functools.partial(volterra_kernel, rows), grid=(steps,), o...  12.2 us
    all_to_all x2, waiting for transfers between devices, halved_body(): lax.all_to_all(sent, 'line', 0, 0, tiled=True)  11.5 us
    unnamed x42, local copies, waits for them, and re-layouts  9.89 us
  transfers between devices with their start and end apart: 9, of which 6 were waited for; matrix products, arithmetic and copies ran while one was open for 4% of the time, Pallas kernels for 5%

profile of v1, /device:TPU:0, one launch (start us, length us, event | category | flops | bytes accessed | tf_op | source)
XLA Modules:
  0.0 289.8 jit_solution(16008586938015408192)
XLA Ops:
  0.6 0.0 copy-start.3
  0.7 1.3 copy-done.3
  2.0 1.7 spread.4
  3.6 6.3 %all-to-all-start = ((bf16[16,256,128]{2,1,0:T(8,128)(2,1)}), bf16[16,256,128]{2,1,0:T(8,128)(2,1)S(1)}, u32[]{:S(2)}, u32[]{:S(2)}) async-start(bf16[16,256,128]{2,1,0:T(8,128)(2,1)} %bitcast.1), calls=%async_computation | async-start | bytes 2097152 | tf_op jit(solution)/shard_map/all_to_all | solution.py:477
  9.9 0.0 copy-done.2
  9.9 0.0 copy-start.4
  10.0 0.7 spread.5
  10.7 0.0 copy-start.16
  10.7 1.0 copy-done.16
  11.7 14.5 %all-to-all-done.own_l = bf16[16,256,128]{2,1,0:T(8,128)(2,1)S(1)} async-done(((bf16[16,256,128]{2,1,0:T(8,128)(2,1)}), bf16[16,256,128]{2,1,0:T(8,128)(2,1)S(1)}, u32[]{:S(2)}, u32[]{:S(2)}) %all-to-all-start) | async-done | bytes 1048608 | tf_op jit(solution)/shard_map/all_to_all | solution.py:477
  26.1 4.3 %all-to-all-start.1 = ((bf16[16,256,128]{2,1,0:T(8,128)(2,1)}), bf16[16,256,128]{2,1,0:T(8,128)(2,1)}, u32[]{:S(2)}, u32[]{:S(2)}) async-start(bf16[16,256,128]{2,1,0:T(8,128)(2,1)} %bitcast.32), calls=%async_computation.1 | async-start | bytes 2097152 | tf_op jit(solution)/shard_map/all_to_all | solution.py:477
  30.5 3.8 %collective-permute-start = (bf16[2,8,64,512]{3,2,1,0:T(8,128)(2,1)S(1)}, bf16[2,8,64,512]{3,2,1,0:T(8,128)(2,1)}, u32[]{:S(2)}, u32[]{:S(2)}) collective-permute-start(bf16[2,8,64,512]{3,2,1,0:T(8,128)(2,1)S(1)} %copy-done.4), channel_id=1, source_target_pairs={{0,17},{1,16},{16,1},{17,0},{2,19},{3,18},{18,3},{19,2},{4,21},{5,... | collective-permute-start | bytes 3145736 | tf_op jit(solution)/shard_map/ppermute | solution.py:479
  34.3 49.2 %collective-permute-done.tile = bf16[2,8,64,512]{3,2,1,0:T(8,128)(2,1)} collective-permute-done((bf16[2,8,64,512]{3,2,1,0:T(8,128)(2,1)S(1)}, bf16[2,8,64,512]{3,2,1,0:T(8,128)(2,1)}, u32[]{:S(2)}, u32[]{:S(2)}) %collective-permute-start) | collective-permute-done | bytes 1048608 | tf_op jit(solution)/shard_map/ppermute | solution.py:479
  83.5 1.3 copy_bitcast_fusion
  84.8 0.0 copy-done.6
  84.8 0.0 all-to-all-done.1.own_g
  84.8 3.6 %all-to-all-start.6 = ((bf16[8,2,8,8,512]{4,3,2,1,0:T(8,128)(2,1)}), bf16[8,2,8,8,512]{4,3,2,1,0:T(8,128)(2,1)S(1)}, u32[]{:S(2)}, u32[]{:S(2)}) async-start(bf16[8,2,8,8,512]{4,3,2,1,0:T(8,128)(2,1)} %copy_bitcast_fusion), calls=%async_computation.6 | async-start | bytes 2097152 | tf_op jit(solution)/shard_map/all_to_all | solution.py:503
  88.4 2.4 collective-permute-start.1
  90.8 47.4 %collective-permute-done.1.tile = bf16[2,8,64,512]{3,2,1,0:T(8,128)(2,1)S(1)} collective-permute-done((bf16[2,8,64,512]{3,2,1,0:T(8,128)(2,1)S(1)}, bf16[2,8,64,512]{3,2,1,0:T(8,128)(2,1)S(1)}, u32[]{:S(2)}, u32[]{:S(2)}) %collective-permute-start.1) | collective-permute-done | bytes 1048608 | tf_op jit(solution)/shard_map/ppermute | solution.py:479
  138.2 1.3 copy_bitcast_fusion.1
  139.5 1.0 copy-done.17
  140.5 0.0 all-to-all-done.6
  140.5 3.6 %all-to-all-start.4 = ((bf16[8,2,8,8,512]{4,3,2,1,0:T(8,128)(2,1)}), bf16[8,2,8,8,512]{4,3,2,1,0:T(8,128)(2,1)S(1)}, u32[]{:S(2)}, u32[]{:S(2)}) async-start(bf16[8,2,8,8,512]{4,3,2,1,0:T(8,128)(2,1)} %copy_bitcast_fusion.1), calls=%async_computation.4 | async-start | bytes 2097152 | tf_op jit(solution)/shard_map/all_to_all | solution.py:503
  144.0 1.9 spread.6
  146.0 0.0 copy-done.8
  146.0 0.0 copy-start.19
  146.0 1.0 copy-done.19
  147.0 11.5 %all-to-all-done.4 = bf16[8,2,8,8,512]{4,3,2,1,0:T(8,128)(2,1)S(1)} async-done(((bf16[8,2,8,8,512]{4,3,2,1,0:T(8,128)(2,1)}), bf16[8,2,8,8,512]{4,3,2,1,0:T(8,128)(2,1)S(1)}, u32[]{:S(2)}, u32[]{:S(2)}) %all-to-all-start.4) | async-done | bytes 1048608 | tf_op jit(solution)/shard_map/all_to_all | solution.py:503
  158.4 4.8 %all-to-all-start.2 = ((bf16[16,256,128]{2,1,0:T(8,128)(2,1)}), bf16[16,256,128]{2,1,0:T(8,128)(2,1)S(1)}, u32[]{:S(2)}, u32[]{:S(2)}) async-start(bf16[16,256,128]{2,1,0:T(8,128)(2,1)} %bitcast.33), calls=%async_computation.2 | async-start | bytes 2097152 | tf_op jit(solution)/shard_map/all_to_all | solution.py:477
  163.3 1.2 copy-done.18
  164.5 0.7 spread.7
  165.2 0.9 copy-done.15
  166.2 13.3 %all-to-all-done.2.far_l = bf16[16,256,128]{2,1,0:T(8,128)(2,1)S(1)} async-done(((bf16[16,256,128]{2,1,0:T(8,128)(2,1)}), bf16[16,256,128]{2,1,0:T(8,128)(2,1)S(1)}, u32[]{:S(2)}, u32[]{:S(2)}) %all-to-all-start.2) | async-done | bytes 1048608 | tf_op jit(solution)/shard_map/all_to_all | solution.py:477
  179.5 4.3 %all-to-all-start.3 = ((bf16[16,256,128]{2,1,0:T(8,128)(2,1)}), bf16[16,256,128]{2,1,0:T(8,128)(2,1)}, u32[]{:S(2)}, u32[]{:S(2)}) async-start(bf16[16,256,128]{2,1,0:T(8,128)(2,1)} %bitcast.31), calls=%async_computation.3 | async-start | bytes 2097152 | tf_op jit(solution)/shard_map/all_to_all | solution.py:477
  184.5 0.1 fusion.11
  184.5 0.1 dynamic_slice.6
  184.6 0.1 dynamic_slice.7
  184.7 0.1 broadcast_multiply_fusion
  184.7 0.2 mul.79.coupling
  185.0 4.3 %fusion.6 = bf16[512,512]{1,0:T(8,128)(2,1)S(1)} fusion(s32[512]{0:T(512)S(1)} %copy-done.20), kind=kLoop, calls=%fused_computation.17 | loop fusion | flops 4718592 | bytes 526336 | tf_op jit(solution)/shard_map/neg | solution.py:488
  189.3 4.9 %sine_convert_fusion = (bf16[512,512]{1,0:T(8,128)(2,1)S(1)}, bf16[512,512]{1,0:T(8,128)(2,1)S(1)}) fusion(s32[512]{0:T(512)S(1)} %copy-done.20), kind=kLoop, calls=%fused_computation.12 | loop fusion | flops 4194304 | bytes 1050624 | tf_op jit(solution)/shard_map/convert_element_type | solution.py:486
  194.2 0.3 maximum_maximum_fusion.table
  194.5 0.0 copy-start
  194.5 1.3 to_sites.3.own
  195.7 0.1 copy-done
  195.8 0.1 pad_maximum_fusion.inverse
  196.0 1.1 copy-done.9
  197.1 4.5 %to_sigma.3 = bf16[4096,128]{1,0:T(8,128)(2,1)S(1)} custom-call(bf16[2,512,512]{2,1,0:T(8,128)(2,1)S(1)} %to_sites.3.own, bf16[8,2,64,512]{3,2,1,0:T(8,128)(2,1)S(1)} %bitcast.27, bf16[1024,1024]{1,0:T(8,128)(2,1)} %copy-done, bf16[512,1024]{1,0:T(8,128)(2,1)S(1)} %pad_maximum_fusion.inverse, f32[512,1]{1,0:T(8,128)S(1)} %mul.79.coupling), custom_call_target="tpu_custom_call" | custom-call | tf_op jit(solution)/shard_map/to_sigma/pallas_call | solution.py:353
  201.6 1.1 copy-done.14
  202.7 0.0 all-to-all-done.3.far_g
  202.7 5.2 %all-to-all-start.7 = ((bf16[16,256,128]{2,1,0:T(8,128)(2,1)}), bf16[16,256,128]{2,1,0:T(8,128)(2,1)}, u32[]{:S(2)}, u32[]{:S(2)}) async-start(bf16[16,256,128]{2,1,0:T(8,128)(2,1)} %bitcast.29), calls=%async_computation.7 | async-start | bytes 2097152 | tf_op jit(solution)/shard_map/all_to_all | solution.py:477
  207.9 0.0 copy-done.1
  207.9 0.0 copy-start.5
  207.9 1.2 copy-done.5
  209.1 1.2 to_sites.2.own
  210.4 4.5 %to_sigma.2 = bf16[4096,128]{1,0:T(8,128)(2,1)S(1)} custom-call(bf16[2,512,512]{2,1,0:T(8,128)(2,1)S(1)} %to_sites.2.own, bf16[8,2,64,512]{3,2,1,0:T(8,128)(2,1)S(1)} %bitcast.28, bf16[1024,1024]{1,0:T(8,128)(2,1)} %copy-done, bf16[512,1024]{1,0:T(8,128)(2,1)S(1)} %pad_maximum_fusion.inverse, f32[512,1]{1,0:T(8,128)S(1)} %mul.79.coupling), custom_call_target="tpu_custom_call" | custom-call | tf_op jit(solution)/shard_map/to_sigma/pallas_call | solution.py:353
  215.0 0.0 copy-start.7
  215.0 0.0 copy-start.11
  215.0 9.2 %all-to-all-done.7.sig_g = bf16[16,256,128]{2,1,0:T(8,128)(2,1)} async-done(((bf16[16,256,128]{2,1,0:T(8,128)(2,1)}), bf16[16,256,128]{2,1,0:T(8,128)(2,1)}, u32[]{:S(2)}, u32[]{:S(2)}) %all-to-all-start.7) | async-done | bytes 1048608 | tf_op jit(solution)/shard_map/all_to_all | solution.py:477
  224.1 19.1 %all_to_all.45.sig_l = bf16[16,256,128]{2,1,0:T(8,128)(2,1)S(1)} all-to-all(bf16[16,256,128]{2,1,0:T(8,128)(2,1)S(1)} %bitcast.30), channel_id=1, replica_groups=mesh['half'=2,'line'=8,'tcol'=2] {'line','tcol'}, dimensions={0} | all-to-all | bytes 2097152 | tf_op jit(solution)/shard_map/all_to_all | solution.py:477
  243.2 0.0 copy-done.7
  243.2 12.2 %volterra.1 = bf16[16,512,128]{2,1,0:T(8,128)(2,1)} custom-call(s32[1]{0:T(128)} %bitcast.half_ref, bf16[16,256,128]{2,1,0:T(8,128)(2,1)S(1)} %copy-done.7, bf16[16,256,128]{2,1,0:T(8,128)(2,1)} %all-to-all-done.1.own_g, bf16[16,256,128]{2,1,0:T(8,128)(2,1)S(1)} %copy-done.11, bf16[16,256,128]{2,1,0:T(8,128)(2,1)} %all-to-all-done.3.far_g, ...), custom_call_target="tpu_custom_call" | custom-call | tf_op jit(solution)/shard_map/volterra/pallas_call | solution.py:450
  255.4 30.8 %all_to_all.46 = bf16[16,512,128]{2,1,0:T(8,128)(2,1)S(1)} all-to-all(bf16[16,512,128]{2,1,0:T(8,128)(2,1)} %volterra.1), channel_id=1, replica_groups=mesh['half'=2,'line'=8,'tcol'=2] {'line','tcol'}, dimensions={0} | all-to-all | bytes 4194304 | tf_op jit(solution)/shard_map/all_to_all | solution.py:515
  286.3 3.5 %collect.1 = (bf16[2,8,64,512]{3,2,1,0:T(8,128)(2,1)}, bf16[2,8,64,512]{3,2,1,0:T(8,128)(2,1)}) custom-call(bf16[8192,128]{1,0:T(8,128)(2,1)S(1)} %bitcast.26), custom_call_target="tpu_custom_call" | custom-call | tf_op jit(solution)/shard_map/collect/pallas_call | solution.py:269
  (19 shorter events, 0.0 us)
Async XLA Ops:
  0.6 9.3 %copy-start.2 = (bf16[2,8,64,512]{3,2,1,0:T(8,128)(2,1)S(1)}, bf16[2,8,64,512]{3,2,1,0:T(8,128)(2,1)}, u32[]{:S(2)}) copy-start(bf16[2,8,64,512]{3,2,1,0:T(8,128)(2,1)} %tile.3) | copy-start | bytes 3145732
  0.6 1.3 copy-start.3
  3.6 22.5 %all-to-all-start = ((bf16[16,256,128]{2,1,0:T(8,128)(2,1)}), bf16[16,256,128]{2,1,0:T(8,128)(2,1)S(1)}, u32[]{:S(2)}, u32[]{:S(2)}) async-start(bf16[16,256,128]{2,1,0:T(8,128)(2,1)} %bitcast.1), calls=%async_computation | async-start | bytes 2097152 | tf_op jit(solution)/shard_map/all_to_all | solution.py:477
  9.9 20.5 %copy-start.4 = (bf16[2,8,64,512]{3,2,1,0:T(8,128)(2,1)S(1)}, bf16[2,8,64,512]{3,2,1,0:T(8,128)(2,1)}, u32[]{:S(2)}) copy-start(bf16[2,8,64,512]{3,2,1,0:T(8,128)(2,1)} %tile.2) | copy-start | bytes 3145732
  10.7 1.0 copy-start.16
  26.1 58.7 %copy-start.6 = (bf16[16,256,128]{2,1,0:T(8,128)(2,1)}, bf16[16,256,128]{2,1,0:T(8,128)(2,1)S(1)}, u32[]{:S(2)}) copy-start(bf16[16,256,128]{2,1,0:T(8,128)(2,1)S(1)} %all-to-all-done.own_l) | copy-start | bytes 3145732
  26.1 58.7 %all-to-all-start.1 = ((bf16[16,256,128]{2,1,0:T(8,128)(2,1)}), bf16[16,256,128]{2,1,0:T(8,128)(2,1)}, u32[]{:S(2)}, u32[]{:S(2)}) async-start(bf16[16,256,128]{2,1,0:T(8,128)(2,1)} %bitcast.32), calls=%async_computation.1 | async-start | bytes 2097152 | tf_op jit(solution)/shard_map/all_to_all | solution.py:477
  30.5 53.0 %collective-permute-start = (bf16[2,8,64,512]{3,2,1,0:T(8,128)(2,1)S(1)}, bf16[2,8,64,512]{3,2,1,0:T(8,128)(2,1)}, u32[]{:S(2)}, u32[]{:S(2)}) collective-permute-start(bf16[2,8,64,512]{3,2,1,0:T(8,128)(2,1)S(1)} %copy-done.4), channel_id=1, source_target_pairs={{0,17},{1,16},{16,1},{17,0},{2,19},{3,18},{18,3},{19,2},{4,21},{5,... | collective-permute-start | bytes 3145736 | tf_op jit(solution)/shard_map/ppermute | solution.py:479
  84.8 55.6 %all-to-all-start.6 = ((bf16[8,2,8,8,512]{4,3,2,1,0:T(8,128)(2,1)}), bf16[8,2,8,8,512]{4,3,2,1,0:T(8,128)(2,1)S(1)}, u32[]{:S(2)}, u32[]{:S(2)}) async-start(bf16[8,2,8,8,512]{4,3,2,1,0:T(8,128)(2,1)} %copy_bitcast_fusion), calls=%async_computation.6 | async-start | bytes 2097152 | tf_op jit(solution)/shard_map/all_to_all | solution.py:503
  88.4 49.8 %collective-permute-start.1 = (bf16[2,8,64,512]{3,2,1,0:T(8,128)(2,1)S(1)}, bf16[2,8,64,512]{3,2,1,0:T(8,128)(2,1)S(1)}, u32[]{:S(2)}, u32[]{:S(2)}) collective-permute-start(bf16[2,8,64,512]{3,2,1,0:T(8,128)(2,1)S(1)} %copy-done.2), channel_id=1, source_target_pairs={{0,17},{1,16},{16,1},{17,0},{2,19},{3,18},{18,3},{19,2},{4,21},{5,... | collective-permute-start | bytes 3145736 | tf_op jit(solution)/shard_map/ppermute | solution.py:479
  139.5 1.0 copy-start.17
  140.5 5.5 %copy-start.8 = (bf16[8,2,8,8,512]{4,3,2,1,0:T(8,128)(2,1)}, bf16[8,2,8,8,512]{4,3,2,1,0:T(8,128)(2,1)S(1)}, u32[]{:S(2)}) copy-start(bf16[8,2,8,8,512]{4,3,2,1,0:T(8,128)(2,1)S(1)} %all-to-all-done.6) | copy-start | bytes 3145732
  140.5 17.9 %all-to-all-start.4 = ((bf16[8,2,8,8,512]{4,3,2,1,0:T(8,128)(2,1)}), bf16[8,2,8,8,512]{4,3,2,1,0:T(8,128)(2,1)S(1)}, u32[]{:S(2)}, u32[]{:S(2)}) async-start(bf16[8,2,8,8,512]{4,3,2,1,0:T(8,128)(2,1)} %copy_bitcast_fusion.1), calls=%async_computation.4 | async-start | bytes 2097152 | tf_op jit(solution)/shard_map/all_to_all | solution.py:503
  146.0 1.0 copy-start.19
  158.4 6.8 %copy-start.12 = (bf16[8,2,8,8,512]{4,3,2,1,0:T(8,128)(2,1)}, bf16[8,2,8,8,512]{4,3,2,1,0:T(8,128)(2,1)S(1)}, u32[]{:S(2)}) copy-start(bf16[8,2,8,8,512]{4,3,2,1,0:T(8,128)(2,1)S(1)} %all-to-all-done.4) | copy-start | bytes 3145732
  158.4 21.1 %all-to-all-start.2 = ((bf16[16,256,128]{2,1,0:T(8,128)(2,1)}), bf16[16,256,128]{2,1,0:T(8,128)(2,1)S(1)}, u32[]{:S(2)}, u32[]{:S(2)}) async-start(bf16[16,256,128]{2,1,0:T(8,128)(2,1)} %bitcast.33), calls=%async_computation.2 | async-start | bytes 2097152 | tf_op jit(solution)/shard_map/all_to_all | solution.py:477
  163.3 1.2 copy-start.18
  164.5 20.5 %copy-start.20 = (s32[512]{0:T(512)S(1)}, s32[512]{0:T(512)}, u32[]{:S(2)}) copy-start(s32[512]{0:T(512)} %param.6) | copy-start | bytes 6148
  165.2 1.0 copy-start.15
  179.5 14.7 %copy-start.10 = (bf16[16,256,128]{2,1,0:T(8,128)(2,1)}, bf16[16,256,128]{2,1,0:T(8,128)(2,1)S(1)}, u32[]{:S(2)}) copy-start(bf16[16,256,128]{2,1,0:T(8,128)(2,1)S(1)} %all-to-all-done.2.far_l) | copy-start | bytes 3145732
  179.5 23.2 %all-to-all-start.3 = ((bf16[16,256,128]{2,1,0:T(8,128)(2,1)}), bf16[16,256,128]{2,1,0:T(8,128)(2,1)}, u32[]{:S(2)}, u32[]{:S(2)}) async-start(bf16[16,256,128]{2,1,0:T(8,128)(2,1)} %bitcast.31), calls=%async_computation.3 | async-start | bytes 2097152 | tf_op jit(solution)/shard_map/all_to_all | solution.py:477
  194.5 1.4 copy-start
  195.8 1.2 copy-start.9
  201.6 1.1 copy-start.14
  202.7 5.2 %copy-start.1 = (bf16[1024,1024]{1,0:T(8,128)(2,1)S(1)}, bf16[1024,1024]{1,0:T(8,128)(2,1)}, u32[]{:S(2)}) copy-start(bf16[1024,1024]{1,0:T(8,128)(2,1)} %copy-done) | copy-start | bytes 6291460
  202.7 21.4 %all-to-all-start.7 = ((bf16[16,256,128]{2,1,0:T(8,128)(2,1)}), bf16[16,256,128]{2,1,0:T(8,128)(2,1)}, u32[]{:S(2)}, u32[]{:S(2)}) async-start(bf16[16,256,128]{2,1,0:T(8,128)(2,1)} %bitcast.29), calls=%async_computation.7 | async-start | bytes 2097152 | tf_op jit(solution)/shard_map/all_to_all | solution.py:477
  207.9 1.2 copy-start.5
  209.1 1.3 copy-start.13
  215.0 28.2 %copy-start.7 = (bf16[16,256,128]{2,1,0:T(8,128)(2,1)S(1)}, bf16[16,256,128]{2,1,0:T(8,128)(2,1)}, u32[]{:S(2)}) copy-start(bf16[16,256,128]{2,1,0:T(8,128)(2,1)} %copy-done.6) | copy-start | bytes 3145732
  215.0 28.2 %copy-start.11 = (bf16[16,256,128]{2,1,0:T(8,128)(2,1)S(1)}, bf16[16,256,128]{2,1,0:T(8,128)(2,1)}, u32[]{:S(2)}) copy-start(bf16[16,256,128]{2,1,0:T(8,128)(2,1)} %copy-done.10) | copy-start | bytes 3145732

commit v2 on v0

--- a/solution.py
+++ b/solution.py
@@ -1,9 +1,16 @@
+import functools
 import math
 
 import jax
 import jax.numpy as jnp
 from jax import lax
-from jax.sharding import PartitionSpec as P
+from jax.experimental import pallas as pl
+from jax.experimental.pallas import tpu as pltpu
+from jax.sharding import Mesh, PartitionSpec as P
+
+F32 = jnp.float32
+BF16 = jnp.bfloat16
+LANES = 128
 
 PERIOD = 64
 
@@ -93,7 +100,7 @@
     return (out_real, out_imaginary)
 
 
-def body(green_lesser, green_greater, lattice_map, time_offset):
+def general_body(green_lesser, green_greater, lattice_map, time_offset):
     tile_rows = green_lesser.shape[1]
     tile_cols = green_lesser.shape[2]
     momenta = green_lesser.shape[3]
@@ -217,7 +224,395 @@
     return (out_tiles[0:2], out_tiles[2:4])
 
 
+def vmem_params():
+    return pltpu.CompilerParams(vmem_limit_bytes=48 * 1024 * 1024)
+
+
+def whole(count):
+    return [pl.BlockSpec(memory_space=pltpu.VMEM)] * count
+
+
+def spread_kernel(first, lesser, greater, out, lines):
+    _, rows, _, _ = lesser.shape
+    count = lines.shape[0] // (2 * rows)
+    for g, tile in enumerate((lesser, greater)):
+        for t in range(rows):
+            span = slice(first, first + count)
+            slab = jnp.concatenate([tile[0, t, :, span], tile[1, t, :, span]], axis=0)
+            lines[pl.ds(g * rows + t, count, stride=2 * rows), :] = slab.astype(F32).T
+    out[...] = lines[...].astype(BF16)
+
+
+def spread(tiles, first, count):
+    _, rows, cols, _ = tiles[0].shape
+    shape = (count * 2 * rows, 2 * cols)
+    return pl.pallas_call(
+        functools.partial(spread_kernel, first),
+        out_shape=jax.ShapeDtypeStruct(shape, BF16),
+        in_specs=whole(2),
+        out_specs=whole(1)[0],
+        scratch_shapes=[pltpu.VMEM(shape, F32)],
+        compiler_params=vmem_params(),
+        name="spread",
+    )(*tiles)
+
+
+def collect_kernel(*refs):
+    *parts, lesser, greater, lines = refs
+    _, rows, cols, momenta = lesser.shape
+    count = momenta // len(parts)
+    for at, part in enumerate(parts):
+        lines[...] = part[...].astype(F32)
+        span = slice(at * count, (at + 1) * count)
+        for k in range(2 * rows):
+            slab = lines[pl.ds(k, count, stride=2 * rows), :].T.astype(BF16)
+            out = lesser if k < rows else greater
+            out[0, k % rows, :, span] = slab[:cols]
+            out[1, k % rows, :, span] = slab[cols:]
+
+
+def collect(parts, tile_shape):
+    shape = jax.ShapeDtypeStruct(tile_shape, BF16)
+    return pl.pallas_call(
+        collect_kernel,
+        out_shape=(shape, shape),
+        in_specs=whole(len(parts)),
+        out_specs=tuple(whole(2)),
+        scratch_shapes=[pltpu.VMEM(parts[0].shape, F32)],
+        compiler_params=vmem_params(),
+        name="collect",
+    )(*parts)
+
+
+def site_kernel(norm_factor, lesser, greater, table, out):
+    _, rows, cols, _ = lesser.shape
+    wide = 4 * cols
+    for pair in range(rows // 2):
+        slabs = [
+            jnp.concatenate([tile[0, t], tile[1, t]], axis=1)
+            for t in (2 * pair, 2 * pair + 1)
+            for tile in (lesser, greater)
+        ]
+        product = lax.dot_general(
+            table[...],
+            jnp.concatenate(slabs, axis=0),
+            (((1,), (1,)), ((), ())),
+            preferred_element_type=F32,
+        )
+        out[:, pair * wide : (pair + 1) * wide] = (product * norm_factor).astype(BF16)
+
+
+def to_sites(tiles, table, norm_factor):
+    _, rows, cols, momenta = tiles[0].shape
+    return pl.pallas_call(
+        functools.partial(site_kernel, norm_factor),
+        out_shape=jax.ShapeDtypeStruct((2 * momenta, rows * 2 * cols), BF16),
+        in_specs=whole(3),
+        out_specs=whole(1)[0],
+        compiler_params=vmem_params(),
+        name="to_sites",
+    )(*tiles, table)
+
+
+def cross_kernel(rows, half_ref, own, far, out):
+    half = half_ref[0]
+    blocks = far.shape[0]
+    cols = blocks * rows
+    for at in range(far.shape[1] // (2 * rows)):
+        span = slice(at * 2 * rows, (at + 1) * 2 * rows)
+        for source, offset, target in ((own, half * blocks, half), (far, 0, 1 - half)):
+            loaded = [source[offset + block, span].astype(F32) for block in range(blocks)]
+            stacked = jnp.concatenate(
+                [lines[rows:] for lines in loaded] + [lines[:rows] for lines in loaded], axis=0
+            )
+            turned = stacked.T
+            for block in range(blocks):
+                out[target * blocks + block, span] = jnp.concatenate(
+                    [
+                        turned[block * rows : (block + 1) * rows],
+                        turned[cols + block * rows : cols + (block + 1) * rows],
+                    ],
+                    axis=0,
+                ).astype(BF16)
+
+
+def to_crossed(half, own, far, rows):
+    return pl.pallas_call(
+        functools.partial(cross_kernel, rows),
+        out_shape=jax.ShapeDtypeStruct(own.shape, BF16),
+        in_specs=[pl.BlockSpec(memory_space=pltpu.SMEM)] + whole(2),
+        out_specs=whole(1)[0],
+        compiler_params=vmem_params(),
+        name="to_crossed",
+    )(half, own, far)
+
+
+def self_kernel(norm_factor, parts, *refs):
+    crossed = refs[:parts]
+    own, table, coupling, out, lines = refs[parts:]
+    rows = coupling.shape[0]
+    momenta = own.shape[0] // 2
+    count = momenta // parts
+    for part in range(parts):
+        lines[part] = crossed[part][...].astype(F32)
+    for pair in range(rows // 2):
+        rights = []
+        for t in (2 * pair, 2 * pair + 1):
+            real = [lines[part, pl.ds(t, count, stride=2 * rows), :] for part in range(parts)]
+            imaginary = [
+                -lines[part, pl.ds(rows + t, count, stride=2 * rows), :] for part in range(parts)
+            ]
+            rights.append(jnp.concatenate(real + imaginary, axis=0).astype(BF16))
+        other = jnp.dot(
+            table[...], jnp.concatenate(rights, axis=1), preferred_element_type=F32
+        )
+        other = (other * norm_factor).astype(BF16).astype(F32)
+        for at in range(2):
+            t = 2 * pair + at
+            span = slice(t * LANES, (t + 1) * LANES)
+            self_real, self_imaginary = second_born(
+                own[:momenta, span].astype(F32),
+                own[momenta:, span].astype(F32),
+                other[:momenta, at * LANES : (at + 1) * LANES],
+                -other[momenta:, at * LANES : (at + 1) * LANES],
+                coupling[t : t + 1, :],
+            )
+            out[:momenta, span] = self_real.astype(BF16)
+            out[momenta:, span] = self_imaginary.astype(BF16)
+
+
+def to_self(crossed, own, table, coupling, norm_factor):
+    parts = len(crossed)
+    return pl.pallas_call(
+        functools.partial(self_kernel, norm_factor, parts),
+        out_shape=jax.ShapeDtypeStruct(own.shape, BF16),
+        in_specs=whole(parts + 3),
+        out_specs=whole(1)[0],
+        scratch_shapes=[pltpu.VMEM((parts,) + crossed[0].shape, F32)],
+        compiler_params=vmem_params(),
+        name="to_self",
+    )(*crossed, own, table, coupling)
+
+
+def sigma_kernel(norm_factor, rows, sites, table, out, lines):
+    count = table.shape[0] // 2
+    for pair in range(rows // 2):
+        product = jnp.dot(
+            table[...],
+            sites[:, 2 * pair * LANES : 2 * (pair + 1) * LANES],
+            preferred_element_type=F32,
+        )
+        product = product * norm_factor
+        for at in range(2):
+            for part in range(2):
+                lines[pl.ds(part * rows + 2 * pair + at, count, stride=2 * rows), :] = product[
+                    part * count : (part + 1) * count, at * LANES : (at + 1) * LANES
+                ]
+    out[...] = lines[...].astype(BF16)
+
+
+def to_sigma(sites, table, rows, norm_factor):
+    shape = (table.shape[0] * rows, LANES)
+    return pl.pallas_call(
+        functools.partial(sigma_kernel, norm_factor, rows),
+        out_shape=jax.ShapeDtypeStruct(shape, BF16),
+        in_specs=whole(2),
+        out_specs=whole(1)[0],
+        scratch_shapes=[pltpu.VMEM(shape, F32)],
+        compiler_params=vmem_params(),
+        name="to_sigma",
+    )(sites, table)
+
+
+def volterra_kernel(rows, half_ref, own, far_near, far_away, sigma, out):
+    half = half_ref[0]
+    blocks = far_near.shape[0]
+    lanes = own.shape[2]
+    cols = lanes // 2
+    near = half * cols
+    away = (1 - half) * cols
+    near_at = half * blocks
+    away_at = (1 - half) * blocks
+    first_times = near + lax.broadcasted_iota(jnp.int32, (cols, lanes), 0)
+    left_lane = lax.broadcasted_iota(jnp.int32, (cols, lanes), 1)
+    low_lanes = left_lane < cols
+    left_times = jnp.where(low_lanes, near + left_lane, away + left_lane - cols)
+    keep_left = left_times <= first_times
+    row_at = lax.broadcasted_iota(jnp.int32, (lanes, 2 * lanes), 0)
+    inner_times = jnp.where(row_at < cols, near + row_at, away + row_at - cols)
+    lane_at = lax.broadcasted_iota(jnp.int32, (lanes, 2 * lanes), 1)
+    last_times = jnp.where(lane_at < lanes, near, away) + lane_at % cols
+    keep_right = inner_times <= last_times
+    for at in range(own.shape[1] // (2 * rows)):
+        span = slice(at * 2 * rows, (at + 1) * 2 * rows)
+
+        def stacked(ref, offset):
+            loaded = [ref[offset + block, span].astype(F32) for block in range(blocks)]
+            return [
+                jnp.concatenate([lines[part * rows : (part + 1) * rows] for lines in loaded], axis=0)
+                for part in range(2)
+            ]
+
+        own_near = stacked(own, near_at)
+        own_away = stacked(own, away_at)
+        cross_near = stacked(far_near, 0)
+        cross_away = stacked(far_away, 0)
+        greens = [
+            jnp.concatenate(
+                [
+                    jnp.concatenate([own_near[g], own_away[g]], axis=1),
+                    jnp.concatenate([cross_near[g], cross_away[g]], axis=1),
+                ],
+                axis=0,
+            )
+            for g in range(2)
+        ]
+        advanced = jnp.where(keep_right, greens[0] - greens[1], 0.0).astype(BF16)
+        sigma_near = stacked(sigma, near_at)
+        sigma_away = stacked(sigma, away_at)
+        retarded = []
+        lefts = [[], []]
+        for part in range(2):
+            lesser = jnp.where(
+                low_lanes, sigma_near[part], pltpu.roll(sigma_away[part], cols, 1)
+            )
+            greater = jnp.where(
+                low_lanes, pltpu.roll(sigma_near[part], cols, 1), sigma_away[part]
+            )
+            retarded.append(jnp.where(keep_left, greater - lesser, 0.0))
+            lefts[0].append(lesser)
+            lefts[1].append(greater)
+        retarded = jnp.concatenate(retarded, axis=0).astype(BF16)
+        results = []
+        for g in range(2):
+            left = jnp.concatenate(
+                [retarded, jnp.concatenate(lefts[g], axis=0).astype(BF16)], axis=1
+            )
+            right = jnp.concatenate([greens[g].astype(BF16), advanced], axis=0)
+            product = jnp.dot(left, right, preferred_element_type=F32)
+            sides = []
+            for side in range(2):
+                straight = product[:cols, side * lanes : (side + 1) * lanes]
+                turned = pltpu.roll(product[cols:, side * lanes : (side + 1) * lanes], cols, 1)
+                sides.append((straight + jnp.where(low_lanes, -turned, turned)) * step_size)
+            results.append(sides)
+        for block in range(blocks):
+            piece = slice(block * rows, (block + 1) * rows)
+            for side, offset in enumerate((near_at, away_at)):
+                out[offset + block, span] = jnp.concatenate(
+                    [results[0][side][piece], results[1][side][piece]], axis=0
+                ).astype(BF16)
+
+
+def volterra(half, own, far_near, far_away, sigma, rows):
+    sources, lines, lanes = own.shape
+    blocks = far_near.shape[0]
+    step = 4 * rows
+    spec = pl.BlockSpec((sources, step, lanes), lambda p: (0, p, 0))
+    far_spec = pl.BlockSpec((blocks, step, lanes), lambda p: (0, p, 0))
+    return pl.pallas_call(
+        functools.partial(volterra_kernel, rows),
+        grid=(lines // step,),
+        out_shape=jax.ShapeDtypeStruct(own.shape, BF16),
+        in_specs=[pl.BlockSpec(memory_space=pltpu.SMEM), spec, far_spec, far_spec, spec],
+        out_specs=spec,
+        compiler_params=vmem_params(),
+        name="volterra",
+    )(half, own, far_near, far_away, sigma)
+
+
+PARTS = 2
+
+
+def halved_body(green_lesser, green_greater, lattice_map, time_offset):
+    _, rows, cols, momenta = green_lesser.shape
+    half = lax.axis_index("half")
+    line = lax.axis_index("line")
+    side = lax.axis_index("tcol")
+    lines = lax.axis_size("line")
+    group = lines * lax.axis_size("tcol")
+    window = rows * lines * lax.axis_size("half")
+    norm_factor = 1.0 / math.sqrt(momenta)
+    tiles = (green_lesser, green_greater)
+    count = momenta // PARTS
+    half_at = half[None]
+
+    def exchange(blocks):
+        return lax.all_to_all(blocks, ("tcol", "line"), 0, 0, tiled=True)
+
+    def blocked(rows_array):
+        return rows_array.reshape(group, rows_array.shape[0] // group, rows_array.shape[1])
+
+    def swap(blocks, at):
+        sent = lax.dynamic_slice_in_dim(blocks, at * lines, lines)
+        return lax.ppermute(sent, "half", [(0, 1), (1, 0)])
+
+    own = [exchange(blocked(spread(tiles, part * count, count))) for part in range(PARTS)]
+    far_near = [swap(blocks, 1 - half) for blocks in own]
+    far_away = [swap(blocks, half) for blocks in own]
+
+    positions = jnp.arange(momenta, dtype=jnp.int32)
+    phases = (lattice_map[:, None] * positions[None, :] % momenta).astype(F32) * (
+        2.0 * math.pi / momenta
+    )
+    cosines = jnp.cos(phases).astype(BF16)
+    sines = jnp.sin(phases).astype(BF16)
+    inverse = jnp.concatenate([cosines, sines], axis=1)
+    turned = jnp.concatenate([-sines, cosines], axis=1)
+    table = jnp.concatenate([inverse, turned], axis=0).T
+    sites = to_sites(tiles, table, norm_factor)
+    time_steps = jnp.arange(window, dtype=jnp.int32)
+    coupling_line = 1.0 + drive_depth * jnp.cos(
+        ((time_offset[0] + time_steps) % PERIOD).astype(F32) * (2.0 * math.pi / PERIOD)
+    )
+    first = lax.dynamic_slice_in_dim(coupling_line, (half * lines + line) * rows, rows)
+    second = lax.dynamic_slice_in_dim(coupling_line, side * cols, cols)
+    coupling = first[:, None] * jnp.concatenate([second, second])[None, :]
+
+    crossed = [
+        exchange(to_crossed(half_at, own[part], far_near[part], rows)).reshape(-1, 2 * cols)
+        for part in range(PARTS)
+    ]
+    self_sites = to_self(crossed, sites, table, coupling, norm_factor)
+    returned = []
+    for part in range(PARTS):
+        span = slice(part * count, (part + 1) * count)
+        inverse_part = jnp.concatenate([inverse[span], turned[span]], axis=0)
+        sigma = exchange(blocked(to_sigma(self_sites, inverse_part, rows, norm_factor)))
+        collisions = volterra(half_at, own[part], far_near[part], far_away[part], sigma, rows)
+        returned.append(exchange(collisions).reshape(-1, 2 * cols))
+    return collect(returned, green_lesser.shape)
+
+
 def solution(mesh):
-    in_specs = (P(None, "trow", "tcol", None), P(None, "trow", "tcol", None), P(), P())
-    out_specs = (P(None, "trow", "tcol", None), P(None, "trow", "tcol", None))
-    return jax.shard_map(body, mesh=mesh, in_specs=in_specs, out_specs=out_specs, check_vma=False)
+    row_parts = mesh.shape["trow"]
+    col_parts = mesh.shape["tcol"]
+
+    def call(green_lesser, green_greater, lattice_map, time_offset):
+        window, window_cols, momenta = green_lesser.shape[1:]
+        rows = window // row_parts
+        cols = window_cols // col_parts
+        halved = (
+            col_parts == 2
+            and row_parts % 2 == 0
+            and window == window_cols
+            and 2 * cols == LANES
+            and cols == rows * (row_parts // 2)
+            and rows % 8 == 0
+            and momenta % (PARTS * LANES) == 0
+            and momenta % (PARTS * row_parts * 2) == 0
+        )
+        if halved:
+            devices = mesh.devices.reshape(2, row_parts // 2, col_parts)
+            used = Mesh(devices, ("half", "line", "tcol"))
+            spec = P(None, ("half", "line"), "tcol", None)
+            inner = halved_body
+        else:
+            used = mesh
+            spec = P(None, "trow", "tcol", None)
+            inner = general_body
+        return jax.shard_map(
+            inner, mesh=used, in_specs=(spec, spec, P(), P()), out_specs=(spec, spec), check_vma=False
+        )(green_lesser, green_greater, lattice_map, time_offset)
+
+    return call

time: 606 us -> 254 us (0.42)
  local copies, waits for them, and re-layouts: 172 us -> 20.2 us
  blocking collectives: 142 us -> 23.3 us
  waiting for transfers between devices: 172 us -> 110 us
  other arithmetic: 53 us -> 14.8 us
  Pallas kernels: 0 us -> 29.8 us
  matrix products: 14.1 us -> 0 us
  starting transfers between devices: 44.2 us -> 52.6 us
    all_to_all x7, waiting for transfers between devices: 172 us -> 29.5 us  [exchange(): return lax.all_to_all(blocks, ('tcol', 'line'), 0, 0, tiled=True)]
    all_to_all x3 -> x1, blocking collectives: 142 us -> 23.3 us  [exchange(): return lax.all_to_all(blocks, ('tcol', 'line'), 0, 0, tiled=True)]
    ppermute x0 -> x4, waiting for transfers between devices: none -> 80.9 us  [swap(): return lax.ppermute(sent, 'half', [(0, 1), (1, 0)])]
    reshape x11 -> x0, local copies, waits for them, and re-layouts: 50.4 us -> none  [the longest x5 30.8 us: spread_times(): blocks.reshape(stacked, row_parts, col_parts, local_count, tile_rows, til...]
    another operation x13 -> x0, local copies, waits for them, and re-layouts: 31.3 us -> none  [the longest x8 14 us: body(): jnp.stack([lesser_out[0], lesser_out[1], greater_out[0], greater_out[1]])]
    pallas_call x0 -> x11, Pallas kernels: none -> 29.8 us  [the longest x2 9.24 us: volterra(): pl.pallas_call(functools.partial(volterra_kernel, rows), grid=(lines // s...]
    sub x6 -> x0, local copies, waits for them, and re-layouts: 16.5 us -> none  [the longest x4 10.8 us: second_born(): square_real = first_real * first_real - first_imaginary * first_imaginary]
    squeeze x9 -> x0, local copies, waits for them, and re-layouts: 16.4 us -> none  [the longest x1 3.09 us: body(): green_moment[3]]
  transfers between devices with their start and end apart: 7 -> 11, of which waited for: 6 -> 8; matrix products, arithmetic and copies ran while one was open for 10% -> 8% of each run, Pallas kernels for 0% -> 7%
where the time goes in v2:
time: 254 us; the launch traced here: 253 us
  waiting for transfers between devices  110 us (43%)
  starting transfers between devices  52.6 us (21%)
  Pallas kernels  29.8 us (12%)
  blocking collectives  23.3 us (9%)
  local copies, waits for them, and re-layouts  20.2 us (8%)
  other arithmetic  14.8 us (6%)
    ppermute x4, waiting for transfers between devices, swap(): return lax.ppermute(sent, 'half', [(0, 1), (1, 0)])  80.9 us
    all_to_all x7, starting transfers between devices, exchange(): return lax.all_to_all(blocks, ('tcol', 'line'), 0, 0, tiled=True)  40.6 us
    all_to_all x7, waiting for transfers between devices, exchange(): return lax.all_to_all(blocks, ('tcol', 'line'), 0, 0, tiled=True)  29.5 us
    all_to_all x1, blocking collectives, exchange(): return lax.all_to_all(blocks, ('tcol', 'line'), 0, 0, tiled=True)  23.3 us
    unnamed x52, local copies, waits for them, and re-layouts  14.2 us
    ppermute x4, starting transfers between devices, swap(): return lax.ppermute(sent, 'half', [(0, 1), (1, 0)])  12 us
    pallas_call x2, Pallas kernels, volterra(): pl.pallas_call(functools.partial(volterra_kernel, rows), grid=(lines // s...  9.24 us
    pallas_call x1, Pallas kernels, to_self(): pl.pallas_call(functools.partial(self_kernel, norm_factor, parts), out_sh...  6.81 us
  transfers between devices with their start and end apart: 11, of which 8 were waited for; matrix products, arithmetic and copies ran while one was open for 8% of the time, Pallas kernels for 7%

profile of v2, /device:TPU:0, one launch (start us, length us, event | category | flops | bytes accessed | tf_op | source)
XLA Modules:
  0.0 252.8 jit_solution(2558563428428833621)
XLA Ops:
  0.6 1.2 copy-done.2
  1.9 1.2 copy-done.4
  3.1 0.9 spread.2
  4.0 1.0 copy-done.10
  5.0 6.3 %all-to-all-start = ((bf16[16,256,128]{2,1,0:T(8,128)(2,1)}), bf16[16,256,128]{2,1,0:T(8,128)(2,1)S(1)}, u32[]{:S(2)}, u32[]{:S(2)}) async-start(bf16[16,256,128]{2,1,0:T(8,128)(2,1)} %bitcast.14), calls=%async_computation | async-start | bytes 2097152 | tf_op jit(solution)/shard_map/all_to_all | solution.py:541
  11.3 0.9 spread.3
  12.2 0.0 copy-start.8
  12.2 1.0 copy-done.8
  13.2 14.3 %all-to-all-done.own = bf16[16,256,128]{2,1,0:T(8,128)(2,1)S(1)} async-done(((bf16[16,256,128]{2,1,0:T(8,128)(2,1)}), bf16[16,256,128]{2,1,0:T(8,128)(2,1)S(1)}, u32[]{:S(2)}, u32[]{:S(2)}) %all-to-all-start) | async-done | bytes 1048608 | tf_op jit(solution)/shard_map/all_to_all | solution.py:541
  27.4 3.7 %all-to-all-start.2 = ((bf16[16,256,128]{2,1,0:T(8,128)(2,1)}), bf16[16,256,128]{2,1,0:T(8,128)(2,1)S(1)}, u32[]{:S(2)}, u32[]{:S(2)}) async-start(bf16[16,256,128]{2,1,0:T(8,128)(2,1)} %bitcast.13), calls=%async_computation.2 | async-start | bytes 2097152 | tf_op jit(solution)/shard_map/all_to_all | solution.py:541
  31.1 0.9 constant_dynamic-slice_fusion.2
  32.0 2.6 %collective-permute-start = (bf16[8,256,128]{2,1,0:T(8,128)(2,1)S(1)}, bf16[8,256,128]{2,1,0:T(8,128)(2,1)S(1)}, u32[]{:S(2)}, u32[]{:S(2)}) collective-permute-start(bf16[8,256,128]{2,1,0:T(8,128)(2,1)S(1)} %get-tuple-element.5), channel_id=1, source_target_pairs={{0,16},{16,0},{1,17},{17,1},{2,18},{18,2},{3,19},{19,3},{4,20},{20... | collective-permute-start | bytes 1572872 | tf_op jit(solution)/shard_map/ppermute | solution.py:548
  34.6 19.9 %collective-permute-done.far.far_near = bf16[8,256,128]{2,1,0:T(8,128)(2,1)S(1)} collective-permute-done((bf16[8,256,128]{2,1,0:T(8,128)(2,1)S(1)}, bf16[8,256,128]{2,1,0:T(8,128)(2,1)S(1)}, u32[]{:S(2)}, u32[]{:S(2)}) %collective-permute-start) | collective-permute-done | bytes 524320 | tf_op jit(solution)/shard_map/ppermute | solution.py:548
  54.5 0.4 to_crossed.2
  54.9 1.0 copy-done.12
  55.9 0.8 copy-done.18
  56.7 1.8 all-to-all-done.2.own
  58.5 6.2 %all-to-all-start.1 = ((bf16[16,256,128]{2,1,0:T(8,128)(2,1)}), bf16[16,256,128]{2,1,0:T(8,128)(2,1)}, u32[]{:S(2)}, u32[]{:S(2)}) async-start(bf16[16,256,128]{2,1,0:T(8,128)(2,1)} %copy-done.12), calls=%async_computation.1 | async-start | bytes 2097152 | tf_op jit(solution)/shard_map/all_to_all | solution.py:541
  64.7 0.9 constant_dynamic-slice_fusion
  65.6 3.4 %collective-permute-start.2 = (bf16[8,256,128]{2,1,0:T(8,128)(2,1)S(1)}, bf16[8,256,128]{2,1,0:T(8,128)(2,1)S(1)}, u32[]{:S(2)}, u32[]{:S(2)}) collective-permute-start(bf16[8,256,128]{2,1,0:T(8,128)(2,1)S(1)} %get-tuple-element.3), channel_id=1, source_target_pairs={{0,16},{16,0},{1,17},{17,1},{2,18},{18,2},{3,19},{19,3},{4,20},{20... | collective-permute-start | bytes 1572872 | tf_op jit(solution)/shard_map/ppermute | solution.py:548
  68.9 19.7 %collective-permute-done.2.far.far_near = bf16[8,256,128]{2,1,0:T(8,128)(2,1)S(1)} collective-permute-done((bf16[8,256,128]{2,1,0:T(8,128)(2,1)S(1)}, bf16[8,256,128]{2,1,0:T(8,128)(2,1)S(1)}, u32[]{:S(2)}, u32[]{:S(2)}) %collective-permute-start.2) | collective-permute-done | bytes 524320 | tf_op jit(solution)/shard_map/ppermute | solution.py:548
  88.6 0.4 to_crossed.3
  89.0 0.0 copy-start.11
  89.0 1.0 copy-done.11
  90.0 0.8 copy-done.16
  90.8 1.3 all-to-all-done.1
  92.2 6.9 %all-to-all-start.3 = ((bf16[16,256,128]{2,1,0:T(8,128)(2,1)}), bf16[16,256,128]{2,1,0:T(8,128)(2,1)}, u32[]{:S(2)}, u32[]{:S(2)}) async-start(bf16[16,256,128]{2,1,0:T(8,128)(2,1)} %copy-done.11), calls=%async_computation.3 | async-start | bytes 2097152 | tf_op jit(solution)/shard_map/all_to_all | solution.py:541
  99.1 4.3 %fusion.12 = bf16[512,512]{1,0:T(8,128)(2,1)S(1)} fusion(s32[512]{0:T(512)S(1)} %copy-done.25), kind=kLoop, calls=%fused_computation.25 | loop fusion | flops 4718592 | bytes 526336 | tf_op jit(solution)/shard_map/neg | solution.py:561
  103.4 4.9 %sine_convert_fusion = (bf16[512,512]{1,0:T(8,128)(2,1)S(1)}, bf16[512,512]{1,0:T(8,128)(2,1)S(1)}) fusion(s32[512]{0:T(512)S(1)} %copy-done.25), kind=kLoop, calls=%fused_computation.18 | loop fusion | flops 4194304 | bytes 1050624 | tf_op jit(solution)/shard_map/convert_element_type | solution.py:559
  108.3 0.8 copy-done.21
  109.1 0.2 copy-done.22
  109.3 1.7 maximum_bitcast_fusion
  110.9 4.0 %copy.6.table.refs_3_ = bf16[1024,1024]{1,0:T(8,128)(2,1)} copy(bf16[1024,1024]{0,1:T(8,128)(2,1)} %maximum_bitcast_fusion) | data formatting | bytes 4194304 | tf_op jit(solution)/shard_map/transpose | solution.py:562
  115.0 4.0 %to_sites.1.refs_2_ = bf16[1024,1024]{1,0:T(8,128)(2,1)S(1)} custom-call(bf16[2,8,64,512]{3,2,1,0:T(8,128)(2,1)S(1)} %copy-done.3, bf16[2,8,64,512]{3,2,1,0:T(8,128)(2,1)S(1)} %copy-done.6, bf16[1024,1024]{1,0:T(8,128)(2,1)} %copy.6.table.refs_3_), custom_call_target="tpu_custom_call" | custom-call | tf_op jit(solution)/shard_map/to_sites/pallas_call | solution.py:307
  118.9 1.3 copy-done.7
  120.9 0.1 fusion.17
  121.0 0.1 dynamic_slice.22
  121.1 0.1 dynamic_slice.21
  121.1 0.1 pad_maximum_fusion.2
  121.2 1.3 fusion.10
  122.5 1.0 pad_maximum_fusion.1.table
  123.5 0.1 broadcast_multiply_fusion.refs_4_
  123.6 6.8 %to_self.1.sites = bf16[1024,1024]{1,0:T(8,128)(2,1)S(1)} custom-call(bf16[4096,128]{1,0:T(8,128)(2,1)} %bitcast.2.refs_0_, bf16[4096,128]{1,0:T(8,128)(2,1)} %bitcast.4.refs_1_, bf16[1024,1024]{1,0:T(8,128)(2,1)} %copy-done.7, bf16[1024,1024]{1,0:T(8,128)(2,1)} %copy.6.table.refs_3_, f32[8,128]{1,0:T(8,128)S(1)} %broadcast_multiply_fusion.refs_4_), custom_call_target="tpu_custom_call" | custom-call | tf_op jit(solution)/shard_map/to_self/pallas_call | solution.py:386
  130.4 1.7 to_sigma.2
  132.2 1.0 copy-done.15
  133.1 5.1 %all-to-all-start.4 = ((bf16[16,256,128]{2,1,0:T(8,128)(2,1)}), bf16[16,256,128]{2,1,0:T(8,128)(2,1)}, u32[]{:S(2)}, u32[]{:S(2)}) async-start(bf16[16,256,128]{2,1,0:T(8,128)(2,1)} %bitcast.17), calls=%async_computation.4 | async-start | bytes 2097152 | tf_op jit(solution)/shard_map/all_to_all | solution.py:541
  138.2 1.5 fusion.6.table
  139.7 1.7 to_sigma.3
  141.4 0.0 copy-start.13
  141.4 1.0 copy-done.13
  142.4 12.1 %all-to-all-done.4.sigma = bf16[16,256,128]{2,1,0:T(8,128)(2,1)} async-done(((bf16[16,256,128]{2,1,0:T(8,128)(2,1)}), bf16[16,256,128]{2,1,0:T(8,128)(2,1)}, u32[]{:S(2)}, u32[]{:S(2)}) %all-to-all-start.4) | async-done | bytes 1048608 | tf_op jit(solution)/shard_map/all_to_all | solution.py:541
  154.5 3.7 %all-to-all-start.6 = ((bf16[16,256,128]{2,1,0:T(8,128)(2,1)}), bf16[16,256,128]{2,1,0:T(8,128)(2,1)S(1)}, u32[]{:S(2)}, u32[]{:S(2)}) async-start(bf16[16,256,128]{2,1,0:T(8,128)(2,1)} %bitcast.16), calls=%async_computation.6 | async-start | bytes 2097152 | tf_op jit(solution)/shard_map/all_to_all | solution.py:541
  158.1 3.4 %collective-permute-start.1 = (bf16[8,256,128]{2,1,0:T(8,128)(2,1)S(1)}, bf16[8,256,128]{2,1,0:T(8,128)(2,1)S(1)}, u32[]{:S(2)}, u32[]{:S(2)}) collective-permute-start(bf16[8,256,128]{2,1,0:T(8,128)(2,1)S(1)} %copy-done.24), channel_id=1, source_target_pairs={{0,16},{16,0},{1,17},{17,1},{2,18},{18,2},{3,19},{19,3},{4,20},{20... | collective-permute-start | bytes 1572872 | tf_op jit(solution)/shard_map/ppermute | solution.py:548
  161.6 20.0 %collective-permute-done.1.far_away = bf16[8,256,128]{2,1,0:T(8,128)(2,1)S(1)} collective-permute-done((bf16[8,256,128]{2,1,0:T(8,128)(2,1)S(1)}, bf16[8,256,128]{2,1,0:T(8,128)(2,1)S(1)}, u32[]{:S(2)}, u32[]{:S(2)}) %collective-permute-start.1) | collective-permute-done | bytes 524320 | tf_op jit(solution)/shard_map/ppermute | solution.py:548
  181.6 5.8 %volterra.2 = bf16[16,256,128]{2,1,0:T(8,128)(2,1)S(1)} custom-call(s32[1]{0:T(128)} %bitcast.half_ref, bf16[16,256,128]{2,1,0:T(8,128)(2,1)S(1)} %all-to-all-done.own, bf16[8,256,128]{2,1,0:T(8,128)(2,1)S(1)} %copy-done.19, bf16[8,256,128]{2,1,0:T(8,128)(2,1)S(1)} %collective-permute-done.1.far_away, bf16[16,256,128]{2,1,0:T(8,128)(2,1)} %all-to-all-done.4.sigma), custom_call_target="tpu_custom_call" | custom-call | tf_op jit(solution)/shard_map/volterra/pallas_call | solution.py:513
  187.4 0.0 copy-start.9
  187.4 1.0 copy-done.9
  188.3 8.9 %all-to-all-start.5 = ((bf16[16,256,128]{2,1,0:T(8,128)(2,1)}), bf16[16,256,128]{2,1,0:T(8,128)(2,1)}, u32[]{:S(2)}, u32[]{:S(2)}) async-start(bf16[16,256,128]{2,1,0:T(8,128)(2,1)} %copy-done.9), calls=%async_computation.5 | async-start | bytes 2097152 | tf_op jit(solution)/shard_map/all_to_all | solution.py:541
  197.2 2.6 %collective-permute-start.3 = (bf16[8,256,128]{2,1,0:T(8,128)(2,1)S(1)}, bf16[8,256,128]{2,1,0:T(8,128)(2,1)S(1)}, u32[]{:S(2)}, u32[]{:S(2)}) collective-permute-start(bf16[8,256,128]{2,1,0:T(8,128)(2,1)S(1)} %copy-done.23), channel_id=1, source_target_pairs={{0,16},{16,0},{1,17},{17,1},{2,18},{18,2},{3,19},{19,3},{4,20},{20... | collective-permute-start | bytes 1572872 | tf_op jit(solution)/shard_map/ppermute | solution.py:548
  199.8 21.3 %collective-permute-done.3.far_away = bf16[8,256,128]{2,1,0:T(8,128)(2,1)S(1)} collective-permute-done((bf16[8,256,128]{2,1,0:T(8,128)(2,1)S(1)}, bf16[8,256,128]{2,1,0:T(8,128)(2,1)S(1)}, u32[]{:S(2)}, u32[]{:S(2)}) %collective-permute-start.3) | collective-permute-done | bytes 524320 | tf_op jit(solution)/shard_map/ppermute | solution.py:548
  221.2 1.0 copy-done.17
  222.2 3.5 %volterra.3 = bf16[16,256,128]{2,1,0:T(8,128)(2,1)S(1)} custom-call(s32[1]{0:T(128)} %bitcast.half_ref, bf16[16,256,128]{2,1,0:T(8,128)(2,1)S(1)} %copy-done.1, bf16[8,256,128]{2,1,0:T(8,128)(2,1)S(1)} %copy-done.17, bf16[8,256,128]{2,1,0:T(8,128)(2,1)S(1)} %collective-permute-done.3.far_away, bf16[16,256,128]{2,1,0:T(8,128)(2,1)S(1)} %all-to-all-done.6.sigma), custom_call_target="tpu_custom_call" | custom-call | tf_op jit(solution)/shard_map/volterra/pallas_call | solution.py:513
  225.7 23.3 %all_to_all.40 = bf16[16,256,128]{2,1,0:T(8,128)(2,1)S(1)} all-to-all(bf16[16,256,128]{2,1,0:T(8,128)(2,1)S(1)} %volterra.3), channel_id=1, replica_groups=mesh['half'=2,'line'=8,'tcol'=2] {'tcol','line'}, dimensions={0} | all-to-all | bytes 2097152 | tf_op jit(solution)/shard_map/all_to_all | solution.py:541
  249.0 3.8 %collect.1 = (bf16[2,8,64,512]{3,2,1,0:T(8,128)(2,1)}, bf16[2,8,64,512]{3,2,1,0:T(8,128)(2,1)}) custom-call(bf16[4096,128]{1,0:T(8,128)(2,1)} %bitcast.8.refs_0_, bf16[4096,128]{1,0:T(8,128)(2,1)S(1)} %bitcast.15), custom_call_target="tpu_custom_call" | custom-call | tf_op jit(solution)/shard_map/collect/pallas_call | solution.py:276
  (36 shorter events, 0.1 us)
Async XLA Ops:
  0.6 1.2 copy-start.2
  1.9 1.2 copy-start.4
  3.1 8.2 %copy-start.3 = (bf16[2,8,64,512]{3,2,1,0:T(8,128)(2,1)S(1)}, bf16[2,8,64,512]{3,2,1,0:T(8,128)(2,1)}, u32[]{:S(2)}) copy-start(bf16[2,8,64,512]{3,2,1,0:T(8,128)(2,1)} %lesser.5) | copy-start | bytes 3145732
  3.1 8.2 %copy-start.5 = (bf16[2,8,64,512]{3,2,1,0:T(8,128)(2,1)S(1)}, bf16[2,8,64,512]{3,2,1,0:T(8,128)(2,1)}, u32[]{:S(2)}) copy-start(bf16[2,8,64,512]{3,2,1,0:T(8,128)(2,1)} %greater.5) | copy-start | bytes 3145732
  4.0 1.0 copy-start.10
  5.0 22.5 %all-to-all-start = ((bf16[16,256,128]{2,1,0:T(8,128)(2,1)}), bf16[16,256,128]{2,1,0:T(8,128)(2,1)S(1)}, u32[]{:S(2)}, u32[]{:S(2)}) async-start(bf16[16,256,128]{2,1,0:T(8,128)(2,1)} %bitcast.14), calls=%async_computation | async-start | bytes 2097152 | tf_op jit(solution)/shard_map/all_to_all | solution.py:541
  12.2 1.0 copy-start.8
  27.4 31.0 %all-to-all-start.2 = ((bf16[16,256,128]{2,1,0:T(8,128)(2,1)}), bf16[16,256,128]{2,1,0:T(8,128)(2,1)S(1)}, u32[]{:S(2)}, u32[]{:S(2)}) async-start(bf16[16,256,128]{2,1,0:T(8,128)(2,1)} %bitcast.13), calls=%async_computation.2 | async-start | bytes 2097152 | tf_op jit(solution)/shard_map/all_to_all | solution.py:541
  32.0 22.5 %collective-permute-start = (bf16[8,256,128]{2,1,0:T(8,128)(2,1)S(1)}, bf16[8,256,128]{2,1,0:T(8,128)(2,1)S(1)}, u32[]{:S(2)}, u32[]{:S(2)}) collective-permute-start(bf16[8,256,128]{2,1,0:T(8,128)(2,1)S(1)} %get-tuple-element.5), channel_id=1, source_target_pairs={{0,16},{16,0},{1,17},{17,1},{2,18},{18,2},{3,19},{19,3},{4,20},{20... | collective-permute-start | bytes 1572872 | tf_op jit(solution)/shard_map/ppermute | solution.py:548
  54.9 1.0 copy-start.12
  55.9 0.8 copy-start.18
  58.5 30.1 %copy-start = (bf16[16,256,128]{2,1,0:T(8,128)(2,1)}, bf16[16,256,128]{2,1,0:T(8,128)(2,1)S(1)}, u32[]{:S(2)}) copy-start(bf16[16,256,128]{2,1,0:T(8,128)(2,1)S(1)} %all-to-all-done.2.own) | copy-start | bytes 3145732
  58.5 33.7 %all-to-all-start.1 = ((bf16[16,256,128]{2,1,0:T(8,128)(2,1)}), bf16[16,256,128]{2,1,0:T(8,128)(2,1)}, u32[]{:S(2)}, u32[]{:S(2)}) async-start(bf16[16,256,128]{2,1,0:T(8,128)(2,1)} %copy-done.12), calls=%async_computation.1 | async-start | bytes 2097152 | tf_op jit(solution)/shard_map/all_to_all | solution.py:541
  65.6 33.5 %copy-start.25 = (s32[512]{0:T(512)S(1)}, s32[512]{0:T(512)}, u32[]{:S(2)}) copy-start(s32[512]{0:T(512)} %param.6) | copy-start | bytes 6148
  65.6 23.1 %collective-permute-start.2 = (bf16[8,256,128]{2,1,0:T(8,128)(2,1)S(1)}, bf16[8,256,128]{2,1,0:T(8,128)(2,1)S(1)}, u32[]{:S(2)}, u32[]{:S(2)}) collective-permute-start(bf16[8,256,128]{2,1,0:T(8,128)(2,1)S(1)} %get-tuple-element.3), channel_id=1, source_target_pairs={{0,16},{16,0},{1,17},{17,1},{2,18},{18,2},{3,19},{19,3},{4,20},{20... | collective-permute-start | bytes 1572872 | tf_op jit(solution)/shard_map/ppermute | solution.py:548
  89.0 1.0 copy-start.11
  90.0 0.8 copy-start.16
  92.2 31.4 %all-to-all-start.3 = ((bf16[16,256,128]{2,1,0:T(8,128)(2,1)}), bf16[16,256,128]{2,1,0:T(8,128)(2,1)}, u32[]{:S(2)}, u32[]{:S(2)}) async-start(bf16[16,256,128]{2,1,0:T(8,128)(2,1)} %copy-done.11), calls=%async_computation.3 | async-start | bytes 2097152 | tf_op jit(solution)/shard_map/all_to_all | solution.py:541
  103.4 4.9 %copy-start.20 = (bf16[512,512]{1,0:T(8,128)(2,1)}, bf16[512,512]{1,0:T(8,128)(2,1)S(1)}, u32[]{:S(2)}) copy-start(bf16[512,512]{1,0:T(8,128)(2,1)S(1)} %fusion.12) | copy-start | bytes 1572868
  108.3 0.8 copy-start.21
  108.3 1.0 copy-start.22
  110.9 4.0 %copy-start.6 = (bf16[2,8,64,512]{3,2,1,0:T(8,128)(2,1)S(1)}, bf16[2,8,64,512]{3,2,1,0:T(8,128)(2,1)}, u32[]{:S(2)}) copy-start(bf16[2,8,64,512]{3,2,1,0:T(8,128)(2,1)} %greater.5) | copy-start | bytes 3145732
  118.9 1.3 copy-start.7
  123.6 6.8 %copy-start.14 = (bf16[512,1024]{1,0:T(8,128)(2,1)S(1)}, bf16[512,1024]{1,0:T(8,128)(2,1)}, u32[]{:S(2)}) copy-start(bf16[512,1024]{1,0:T(8,128)(2,1)} %pad_maximum_fusion.1.table) | copy-start | bytes 3145732
  132.2 1.0 copy-start.15
  133.1 21.3 %all-to-all-start.4 = ((bf16[16,256,128]{2,1,0:T(8,128)(2,1)}), bf16[16,256,128]{2,1,0:T(8,128)(2,1)}, u32[]{:S(2)}, u32[]{:S(2)}) async-start(bf16[16,256,128]{2,1,0:T(8,128)(2,1)} %bitcast.17), calls=%async_computation.4 | async-start | bytes 2097152 | tf_op jit(solution)/shard_map/all_to_all | solution.py:541
  141.4 1.0 copy-start.13
  142.4 15.7 %copy-start.24 = (bf16[8,256,128]{2,1,0:T(8,128)(2,1)S(1)}, bf16[8,256,128]{2,1,0:T(8,128)(2,1)}, u32[]{:S(2)}) copy-start(bf16[8,256,128]{2,1,0:T(8,128)(2,1)} %get-tuple-element.4) | copy-start | bytes 1572868
  142.4 39.2 %copy-start.19 = (bf16[8,256,128]{2,1,0:T(8,128)(2,1)S(1)}, bf16[8,256,128]{2,1,0:T(8,128)(2,1)}, u32[]{:S(2)}) copy-start(bf16[8,256,128]{2,1,0:T(8,128)(2,1)} %copy-done.18) | copy-start | bytes 1572868
  154.5 33.9 %all-to-all-start.6 = ((bf16[16,256,128]{2,1,0:T(8,128)(2,1)}), bf16[16,256,128]{2,1,0:T(8,128)(2,1)S(1)}, u32[]{:S(2)}, u32[]{:S(2)}) async-start(bf16[16,256,128]{2,1,0:T(8,128)(2,1)} %bitcast.16), calls=%async_computation.6 | async-start | bytes 2097152 | tf_op jit(solution)/shard_map/all_to_all | solution.py:541
  158.1 23.4 %collective-permute-start.1 = (bf16[8,256,128]{2,1,0:T(8,128)(2,1)S(1)}, bf16[8,256,128]{2,1,0:T(8,128)(2,1)S(1)}, u32[]{:S(2)}, u32[]{:S(2)}) collective-permute-start(bf16[8,256,128]{2,1,0:T(8,128)(2,1)S(1)} %copy-done.24), channel_id=1, source_target_pairs={{0,16},{16,0},{1,17},{17,1},{2,18},{18,2},{3,19},{19,3},{4,20},{20... | collective-permute-start | bytes 1572872 | tf_op jit(solution)/shard_map/ppermute | solution.py:548
  187.4 1.0 copy-start.9
  188.3 8.9 %copy-start.23 = (bf16[8,256,128]{2,1,0:T(8,128)(2,1)S(1)}, bf16[8,256,128]{2,1,0:T(8,128)(2,1)}, u32[]{:S(2)}) copy-start(bf16[8,256,128]{2,1,0:T(8,128)(2,1)} %get-tuple-element.2) | copy-start | bytes 1572868
  188.3 32.8 %copy-start.1 = (bf16[16,256,128]{2,1,0:T(8,128)(2,1)S(1)}, bf16[16,256,128]{2,1,0:T(8,128)(2,1)}, u32[]{:S(2)}) copy-start(bf16[16,256,128]{2,1,0:T(8,128)(2,1)} %copy-done) | copy-start | bytes 3145732
  188.3 37.3 %all-to-all-start.5 = ((bf16[16,256,128]{2,1,0:T(8,128)(2,1)}), bf16[16,256,128]{2,1,0:T(8,128)(2,1)}, u32[]{:S(2)}, u32[]{:S(2)}) async-start(bf16[16,256,128]{2,1,0:T(8,128)(2,1)} %copy-done.9), calls=%async_computation.5 | async-start | bytes 2097152 | tf_op jit(solution)/shard_map/all_to_all | solution.py:541
  197.2 23.9 %collective-permute-start.3 = (bf16[8,256,128]{2,1,0:T(8,128)(2,1)S(1)}, bf16[8,256,128]{2,1,0:T(8,128)(2,1)S(1)}, u32[]{:S(2)}, u32[]{:S(2)}) collective-permute-start(bf16[8,256,128]{2,1,0:T(8,128)(2,1)S(1)} %copy-done.23), channel_id=1, source_target_pairs={{0,16},{16,0},{1,17},{17,1},{2,18},{18,2},{3,19},{19,3},{4,20},{20... | collective-permute-start | bytes 1572872 | tf_op jit(solution)/shard_map/ppermute | solution.py:548
  221.2 1.0 copy-start.17

commit v3 on v2

--- a/solution.py
+++ b/solution.py
@@ -228,11 +228,16 @@
     return pltpu.CompilerParams(vmem_limit_bytes=48 * 1024 * 1024)
 
 
+def unread(arrays):
+    return [pl.BlockSpec(memory_space=pl.ANY)] * len(arrays)
+
+
 def whole(count):
     return [pl.BlockSpec(memory_space=pltpu.VMEM)] * count
 
 
-def spread_kernel(first, lesser, greater, out, lines):
+def spread_kernel(first, lesser, greater, *rest):
+    out, lines = rest[-2:]
     _, rows, _, _ = lesser.shape
     count = lines.shape[0] // (2 * rows)
     for g, tile in enumerate((lesser, greater)):
@@ -243,18 +248,18 @@
     out[...] = lines[...].astype(BF16)
 
 
-def spread(tiles, first, count):
+def spread(tiles, first, count, after):
     _, rows, cols, _ = tiles[0].shape
     shape = (count * 2 * rows, 2 * cols)
     return pl.pallas_call(
         functools.partial(spread_kernel, first),
         out_shape=jax.ShapeDtypeStruct(shape, BF16),
-        in_specs=whole(2),
+        in_specs=whole(2) + unread(after),
         out_specs=whole(1)[0],
         scratch_shapes=[pltpu.VMEM(shape, F32)],
         compiler_params=vmem_params(),
         name="spread",
-    )(*tiles)
+    )(*tiles, *after)
 
 
 def collect_kernel(*refs):
@@ -282,6 +287,41 @@
         compiler_params=vmem_params(),
         name="collect",
     )(*parts)
+
+
+def table_kernel(column_ref, table, *inverse):
+    momenta = column_ref.shape[0]
+    count = momenta // len(inverse)
+    positions = lax.broadcasted_iota(jnp.int32, (momenta, momenta), 1)
+    phases = (column_ref[...] * positions % momenta).astype(F32) * (2.0 * math.pi / momenta)
+    cosines = jnp.cos(phases).astype(BF16)
+    sines = jnp.sin(phases).astype(BF16)
+    for part, ref in enumerate(inverse):
+        span = slice(part * count, (part + 1) * count)
+        ref[:count, :momenta] = cosines[span]
+        ref[:count, momenta:] = sines[span]
+        ref[count:, :momenta] = -sines[span]
+        ref[count:, momenta:] = cosines[span]
+    cosines = cosines.astype(F32).T.astype(BF16)
+    sines = sines.astype(F32).T.astype(BF16)
+    table[:momenta, :momenta] = cosines
+    table[:momenta, momenta:] = -sines
+    table[momenta:, :momenta] = sines
+    table[momenta:, momenta:] = cosines
+
+
+def make_tables(lattice_map, parts):
+    momenta = lattice_map.shape[0]
+    count = momenta // parts
+    shapes = [(2 * momenta, 2 * momenta)] + [(2 * count, 2 * momenta)] * parts
+    return pl.pallas_call(
+        table_kernel,
+        out_shape=tuple(jax.ShapeDtypeStruct(shape, BF16) for shape in shapes),
+        in_specs=whole(1),
+        out_specs=tuple(whole(1 + parts)),
+        compiler_params=vmem_params(),
+        name="make_tables",
+    )(lattice_map[:, None])
 
 
 def site_kernel(norm_factor, lesser, greater, table, out):
@@ -314,7 +354,8 @@
     )(*tiles, table)
 
 
-def cross_kernel(rows, half_ref, own, far, out):
+def cross_kernel(rows, half_ref, own, far, *rest):
+    out = rest[-1]
     half = half_ref[0]
     blocks = far.shape[0]
     cols = blocks * rows
@@ -336,20 +377,21 @@
                 ).astype(BF16)
 
 
-def to_crossed(half, own, far, rows):
+def to_crossed(half, own, far, rows, after):
     return pl.pallas_call(
         functools.partial(cross_kernel, rows),
         out_shape=jax.ShapeDtypeStruct(own.shape, BF16),
-        in_specs=[pl.BlockSpec(memory_space=pltpu.SMEM)] + whole(2),
+        in_specs=[pl.BlockSpec(memory_space=pltpu.SMEM)] + whole(2) + unread(after),
         out_specs=whole(1)[0],
         compiler_params=vmem_params(),
         name="to_crossed",
-    )(half, own, far)
+    )(half, own, far, *after)
 
 
 def self_kernel(norm_factor, parts, *refs):
     crossed = refs[:parts]
-    own, table, coupling, out, lines = refs[parts:]
+    own, table, coupling = refs[parts : parts + 3]
+    out, lines = refs[-2:]
     rows = coupling.shape[0]
     momenta = own.shape[0] // 2
     count = momenta // parts
@@ -381,17 +423,17 @@
             out[momenta:, span] = self_imaginary.astype(BF16)
 
 
-def to_self(crossed, own, table, coupling, norm_factor):
+def to_self(crossed, own, table, coupling, norm_factor, after):
     parts = len(crossed)
     return pl.pallas_call(
         functools.partial(self_kernel, norm_factor, parts),
         out_shape=jax.ShapeDtypeStruct(own.shape, BF16),
-        in_specs=whole(parts + 3),
+        in_specs=whole(parts + 3) + unread(after),
         out_specs=whole(1)[0],
         scratch_shapes=[pltpu.VMEM((parts,) + crossed[0].shape, F32)],
         compiler_params=vmem_params(),
         name="to_self",
-    )(*crossed, own, table, coupling)
+    )(*crossed, own, table, coupling, *after)
 
 
 def sigma_kernel(norm_factor, rows, sites, table, out, lines):
@@ -424,7 +466,8 @@
     )(sites, table)
 
 
-def volterra_kernel(rows, half_ref, own, far_near, far_away, sigma, out):
+def volterra_kernel(rows, half_ref, own, far_near, far_away, sigma, *rest):
+    out = rest[-1]
     half = half_ref[0]
     blocks = far_near.shape[0]
     lanes = own.shape[2]
@@ -504,7 +547,7 @@
                 ).astype(BF16)
 
 
-def volterra(half, own, far_near, far_away, sigma, rows):
+def volterra(half, own, far_near, far_away, sigma, rows, after):
     sources, lines, lanes = own.shape
     blocks = far_near.shape[0]
     step = 4 * rows
@@ -514,11 +557,12 @@
         functools.partial(volterra_kernel, rows),
         grid=(lines // step,),
         out_shape=jax.ShapeDtypeStruct(own.shape, BF16),
-        in_specs=[pl.BlockSpec(memory_space=pltpu.SMEM), spec, far_spec, far_spec, spec],
+        in_specs=[pl.BlockSpec(memory_space=pltpu.SMEM), spec, far_spec, far_spec, spec]
+        + unread(after),
         out_specs=spec,
         compiler_params=vmem_params(),
         name="volterra",
-    )(half, own, far_near, far_away, sigma)
+    )(half, own, far_near, far_away, sigma, *after)
 
 
 PARTS = 2
@@ -547,19 +591,13 @@
         sent = lax.dynamic_slice_in_dim(blocks, at * lines, lines)
         return lax.ppermute(sent, "half", [(0, 1), (1, 0)])
 
-    own = [exchange(blocked(spread(tiles, part * count, count))) for part in range(PARTS)]
+    own = []
+    for part in range(PARTS):
+        own.append(exchange(blocked(spread(tiles, part * count, count, own[-1:]))))
     far_near = [swap(blocks, 1 - half) for blocks in own]
     far_away = [swap(blocks, half) for blocks in own]
 
-    positions = jnp.arange(momenta, dtype=jnp.int32)
-    phases = (lattice_map[:, None] * positions[None, :] % momenta).astype(F32) * (
-        2.0 * math.pi / momenta
-    )
-    cosines = jnp.cos(phases).astype(BF16)
-    sines = jnp.sin(phases).astype(BF16)
-    inverse = jnp.concatenate([cosines, sines], axis=1)
-    turned = jnp.concatenate([-sines, cosines], axis=1)
-    table = jnp.concatenate([inverse, turned], axis=0).T
+    table, *inverse = make_tables(lattice_map, PARTS)
     sites = to_sites(tiles, table, norm_factor)
     time_steps = jnp.arange(window, dtype=jnp.int32)
     coupling_line = 1.0 + drive_depth * jnp.cos(
@@ -570,16 +608,16 @@
     coupling = first[:, None] * jnp.concatenate([second, second])[None, :]
 
     crossed = [
-        exchange(to_crossed(half_at, own[part], far_near[part], rows)).reshape(-1, 2 * cols)
+        exchange(to_crossed(half_at, own[part], far_near[part], rows, [*own, sites])).reshape(-1, 2 * cols)
         for part in range(PARTS)
     ]
-    self_sites = to_self(crossed, sites, table, coupling, norm_factor)
+    self_sites = to_self(crossed, sites, table, coupling, norm_factor, far_away[:1])
     returned = []
     for part in range(PARTS):
-        span = slice(part * count, (part + 1) * count)
-        inverse_part = jnp.concatenate([inverse[span], turned[span]], axis=0)
-        sigma = exchange(blocked(to_sigma(self_sites, inverse_part, rows, norm_factor)))
-        collisions = volterra(half_at, own[part], far_near[part], far_away[part], sigma, rows)
+        sigma = exchange(blocked(to_sigma(self_sites, inverse[part], rows, norm_factor)))
+        collisions = volterra(
+            half_at, own[part], far_near[part], far_away[part], sigma, rows, far_away
+        )
         returned.append(exchange(collisions).reshape(-1, 2 * cols))
     return collect(returned, green_lesser.shape)
 

time: 254 us -> 245 us (0.965)
  blocking collectives: 23.3 us -> 42 us
  waiting for transfers between devices: 110 us -> 94.1 us
  other arithmetic: 14.8 us -> 0.2 us
  Pallas kernels: 29.8 us -> 38.3 us
  starting transfers between devices: 52.6 us -> 44.7 us
    all_to_all x1 -> x2, blocking collectives: 23.3 us -> 42 us  [exchange(): return lax.all_to_all(blocks, ('tcol', 'line'), 0, 0, tiled=True)]
    ppermute x4, waiting for transfers between devices: 80.9 us -> 65.8 us  [swap(): return lax.ppermute(sent, 'half', [(0, 1), (1, 0)])]
    all_to_all x7 -> x6, starting transfers between devices: 40.6 us -> 32.5 us  [exchange(): return lax.all_to_all(blocks, ('tcol', 'line'), 0, 0, tiled=True)]
    unnamed x52 -> x48, local copies, waits for them, and re-layouts: 14.2 us -> 20.1 us
    convert_element_type x1 -> x0, other arithmetic: 4.87 us -> none  [halved_body(): sines = jnp.sin(phases).astype(BF16)]
    pallas_call x0 -> x1, Pallas kernels: none -> 4.54 us  [make_tables(): pl.pallas_call(table_kernel, out_shape=tuple((jax.ShapeDtypeStruct(shape,...]
    neg x1 -> x0, other arithmetic: 4.3 us -> none  [halved_body(): turned = jnp.concatenate([-sines, cosines], axis=1)]
    transpose x1 -> x0, local copies, waits for them, and re-layouts: 4.03 us -> none  [halved_body(): table = jnp.concatenate([inverse, turned], axis=0).T]
  transfers between devices with their start and end apart: 11 -> 10, of which waited for: 8 -> 9; matrix products, arithmetic and copies ran while one was open for 8% -> 1% of each run, Pallas kernels for 7% -> 10%
where the time goes in v3:
time: 245 us; the launch traced here: 243 us
  waiting for transfers between devices  94.1 us (38%)
  starting transfers between devices  44.7 us (18%)
  blocking collectives  42 us (17%)
  Pallas kernels  38.3 us (16%)
  local copies, waits for them, and re-layouts  22.4 us (9%)
    ppermute x4, waiting for transfers between devices, swap(): return lax.ppermute(sent, 'half', [(0, 1), (1, 0)])  65.8 us
    all_to_all x2, blocking collectives, exchange(): return lax.all_to_all(blocks, ('tcol', 'line'), 0, 0, tiled=True)  42 us
    all_to_all x6, starting transfers between devices, exchange(): return lax.all_to_all(blocks, ('tcol', 'line'), 0, 0, tiled=True)  32.5 us
    all_to_all x6, waiting for transfers between devices, exchange(): return lax.all_to_all(blocks, ('tcol', 'line'), 0, 0, tiled=True)  28.4 us
    unnamed x48, local copies, waits for them, and re-layouts  20.1 us
    ppermute x4, starting transfers between devices, swap(): return lax.ppermute(sent, 'half', [(0, 1), (1, 0)])  12.2 us
    pallas_call x2, Pallas kernels, volterra(): pl.pallas_call(functools.partial(volterra_kernel, rows), grid=(lines // s...  11.7 us
    pallas_call x1, Pallas kernels, to_self(): pl.pallas_call(functools.partial(self_kernel, norm_factor, parts), out_sh...  6.49 us
  transfers between devices with their start and end apart: 10, of which 9 were waited for; matrix products, arithmetic and copies ran while one was open for 1% of the time, Pallas kernels for 10%

profile of v3, /device:TPU:0, one launch (start us, length us, event | category | flops | bytes accessed | tf_op | source)
XLA Modules:
  0.0 243.3 jit_solution(7049159805428589169)
XLA Ops:
  0.6 0.0 copy-start.5
  0.6 1.2 copy-done.5
  1.9 1.2 copy-done.7
  3.1 0.9 spread.2
  4.0 22.3 %all_to_all.40.rest_0_.own = bf16[16,256,128]{2,1,0:T(8,128)(2,1)S(1)} all-to-all(bf16[16,256,128]{2,1,0:T(8,128)(2,1)S(1)} %bitcast.12), channel_id=1, replica_groups=mesh['half'=2,'line'=8,'tcol'=2] {'tcol','line'}, dimensions={0} | all-to-all | bytes 2097152 | tf_op jit(solution)/shard_map/all_to_all | solution.py:585
  26.2 0.9 spread.3
  27.2 0.0 copy-start.10
  27.2 1.0 copy-done.10
  28.1 3.8 %all-to-all-start.1 = ((bf16[16,256,128]{2,1,0:T(8,128)(2,1)}), bf16[16,256,128]{2,1,0:T(8,128)(2,1)S(1)}, u32[]{:S(2)}, u32[]{:S(2)}) async-start(bf16[16,256,128]{2,1,0:T(8,128)(2,1)} %bitcast.15), calls=%async_computation.1 | async-start | bytes 2097152 | tf_op jit(solution)/shard_map/all_to_all | solution.py:585
  31.9 1.1 constant_dynamic-slice_fusion.2
  33.0 2.6 %collective-permute-start = (bf16[8,256,128]{2,1,0:T(8,128)(2,1)}, bf16[8,256,128]{2,1,0:T(8,128)(2,1)}, u32[]{:S(2)}, u32[]{:S(2)}) collective-permute-start(bf16[8,256,128]{2,1,0:T(8,128)(2,1)} %get-tuple-element.11), channel_id=1, source_target_pairs={{0,16},{16,0},{1,17},{17,1},{2,18},{18,2},{3,19},{19,3},{4,20},{20... | collective-permute-start | bytes 1572872 | tf_op jit(solution)/shard_map/ppermute | solution.py:592
  35.6 0.1 copy.6.column_ref
  35.7 4.5 %make_tables.1 = (bf16[1024,1024]{1,0:T(8,128)(2,1)S(1)}, bf16[512,1024]{1,0:T(8,128)(2,1)S(1)}, bf16[512,1024]{1,0:T(8,128)(2,1)S(1)}) custom-call(s32[512,1]{1,0:T(8,128)S(1)} %copy.6.column_ref), custom_call_target="tpu_custom_call" | custom-call | tf_op jit(solution)/shard_map/make_tables/pallas_call | solution.py:317
  40.3 1.4 copy-done.9
  41.7 1.0 copy-done.19
  42.7 1.6 copy-done.8
  44.3 3.9 %to_sites.1.rest_2_.refs_2_ = bf16[1024,1024]{1,0:T(8,128)(2,1)S(1)} custom-call(bf16[2,8,64,512]{3,2,1,0:T(8,128)(2,1)S(1)} %copy-done.6, bf16[2,8,64,512]{3,2,1,0:T(8,128)(2,1)S(1)} %copy-done.8, bf16[1024,1024]{1,0:T(8,128)(2,1)} %copy-done.9), custom_call_target="tpu_custom_call" | custom-call | tf_op jit(solution)/shard_map/to_sites/pallas_call | solution.py:347
  48.3 1.3 copy-done
  49.6 5.9 %collective-permute-done.far.far_near = bf16[8,256,128]{2,1,0:T(8,128)(2,1)} collective-permute-done((bf16[8,256,128]{2,1,0:T(8,128)(2,1)}, bf16[8,256,128]{2,1,0:T(8,128)(2,1)}, u32[]{:S(2)}, u32[]{:S(2)}) %collective-permute-start) | collective-permute-done | bytes 524320 | tf_op jit(solution)/shard_map/ppermute | solution.py:592
  55.5 3.7 %all-to-all-done.1.rest_1_.own = bf16[16,256,128]{2,1,0:T(8,128)(2,1)S(1)} async-done(((bf16[16,256,128]{2,1,0:T(8,128)(2,1)}), bf16[16,256,128]{2,1,0:T(8,128)(2,1)S(1)}, u32[]{:S(2)}, u32[]{:S(2)}) %all-to-all-start.1) | async-done | bytes 1048608 | tf_op jit(solution)/shard_map/all_to_all | solution.py:585
  59.2 1.6 copy-done.1
  60.8 2.4 to_crossed.2
  63.2 4.6 %all-to-all-start.2 = ((bf16[16,256,128]{2,1,0:T(8,128)(2,1)}), bf16[16,256,128]{2,1,0:T(8,128)(2,1)S(1)}, u32[]{:S(2)}, u32[]{:S(2)}) async-start(bf16[16,256,128]{2,1,0:T(8,128)(2,1)} %to_crossed.2), calls=%async_computation.2 | async-start | bytes 2097152 | tf_op jit(solution)/shard_map/all_to_all | solution.py:585
  67.7 0.9 constant_dynamic-slice_fusion
  68.7 3.4 %collective-permute-start.2 = (bf16[8,256,128]{2,1,0:T(8,128)(2,1)S(1)}, bf16[8,256,128]{2,1,0:T(8,128)(2,1)S(1)}, u32[]{:S(2)}, u32[]{:S(2)}) collective-permute-start(bf16[8,256,128]{2,1,0:T(8,128)(2,1)S(1)} %get-tuple-element.9), channel_id=1, source_target_pairs={{0,16},{16,0},{1,17},{17,1},{2,18},{18,2},{3,19},{19,3},{4,20},{20... | collective-permute-start | bytes 1572872 | tf_op jit(solution)/shard_map/ppermute | solution.py:592
  72.1 19.7 %collective-permute-done.2.far.far_near = bf16[8,256,128]{2,1,0:T(8,128)(2,1)S(1)} collective-permute-done((bf16[8,256,128]{2,1,0:T(8,128)(2,1)S(1)}, bf16[8,256,128]{2,1,0:T(8,128)(2,1)S(1)}, u32[]{:S(2)}, u32[]{:S(2)}) %collective-permute-start.2) | collective-permute-done | bytes 524320 | tf_op jit(solution)/shard_map/ppermute | solution.py:592
  91.7 1.4 to_crossed.3
  93.1 0.8 copy-done.17
  93.9 1.2 all-to-all-done.2
  95.2 7.1 %all-to-all-start.3 = ((bf16[16,256,128]{2,1,0:T(8,128)(2,1)}), bf16[16,256,128]{2,1,0:T(8,128)(2,1)}, u32[]{:S(2)}, u32[]{:S(2)}) async-start(bf16[16,256,128]{2,1,0:T(8,128)(2,1)} %to_crossed.3), calls=%async_computation.3 | async-start | bytes 2097152 | tf_op jit(solution)/shard_map/all_to_all | solution.py:585
  102.2 3.4 %collective-permute-start.1 = (bf16[8,256,128]{2,1,0:T(8,128)(2,1)}, bf16[8,256,128]{2,1,0:T(8,128)(2,1)S(1)}, u32[]{:S(2)}, u32[]{:S(2)}) collective-permute-start(bf16[8,256,128]{2,1,0:T(8,128)(2,1)} %get-tuple-element.10), channel_id=1, source_target_pairs={{0,16},{16,0},{1,17},{17,1},{2,18},{18,2},{3,19},{19,3},{4,20},{20... | collective-permute-start | bytes 1572872 | tf_op jit(solution)/shard_map/ppermute | solution.py:592
  106.3 0.1 fusion.4
  106.4 0.1 dynamic_slice.22
  106.5 0.1 dynamic_slice.21
  106.6 0.1 pad_maximum_fusion
  106.6 0.1 broadcast_multiply_fusion.refs_4_
  106.7 19.6 %collective-permute-done.1.refs_5_.far_away.rest_0_ = bf16[8,256,128]{2,1,0:T(8,128)(2,1)S(1)} collective-permute-done((bf16[8,256,128]{2,1,0:T(8,128)(2,1)}, bf16[8,256,128]{2,1,0:T(8,128)(2,1)S(1)}, u32[]{:S(2)}, u32[]{:S(2)}) %collective-permute-start.1) | collective-permute-done | bytes 524320 | tf_op jit(solution)/shard_map/ppermute | solution.py:592
  126.3 3.4 %all-to-all-done.3 = bf16[16,256,128]{2,1,0:T(8,128)(2,1)} async-done(((bf16[16,256,128]{2,1,0:T(8,128)(2,1)}), bf16[16,256,128]{2,1,0:T(8,128)(2,1)}, u32[]{:S(2)}, u32[]{:S(2)}) %all-to-all-start.3) | async-done | bytes 1048608 | tf_op jit(solution)/shard_map/all_to_all | solution.py:585
  129.7 1.2 copy-done.16
  130.9 6.5 %to_self.1.sites = bf16[1024,1024]{1,0:T(8,128)(2,1)S(1)} custom-call(bf16[4096,128]{1,0:T(8,128)(2,1)S(1)} %bitcast.18, bf16[4096,128]{1,0:T(8,128)(2,1)} %bitcast.5.refs_1_, bf16[1024,1024]{1,0:T(8,128)(2,1)} %copy-done, bf16[1024,1024]{1,0:T(8,128)(2,1)} %copy-done.9, f32[8,128]{1,0:T(8,128)S(1)} %broadcast_multiply_fusion.refs_4_, ...), custom_call_target="tpu_custom_call" | custom-call | tf_op jit(solution)/shard_map/to_self/pallas_call | solution.py:428
  137.5 1.8 to_sigma.3
  139.2 0.0 copy-start.14
  139.2 1.0 copy-done.14
  140.2 4.7 %all-to-all-start.6 = ((bf16[16,256,128]{2,1,0:T(8,128)(2,1)}), bf16[16,256,128]{2,1,0:T(8,128)(2,1)}, u32[]{:S(2)}, u32[]{:S(2)}) async-start(bf16[16,256,128]{2,1,0:T(8,128)(2,1)} %bitcast.17), calls=%async_computation.6 | async-start | bytes 2097152 | tf_op jit(solution)/shard_map/all_to_all | solution.py:585
  144.9 1.6 copy-done.4
  146.5 1.2 copy-done.20
  147.7 1.7 to_sigma.2
  149.5 0.0 copy-start.11
  149.5 1.0 copy-done.11
  150.4 10.7 %all-to-all-done.6.sigma = bf16[16,256,128]{2,1,0:T(8,128)(2,1)} async-done(((bf16[16,256,128]{2,1,0:T(8,128)(2,1)}), bf16[16,256,128]{2,1,0:T(8,128)(2,1)}, u32[]{:S(2)}, u32[]{:S(2)}) %all-to-all-start.6) | async-done | bytes 1048608 | tf_op jit(solution)/shard_map/all_to_all | solution.py:585
  161.2 4.3 %all-to-all-start.4 = ((bf16[16,256,128]{2,1,0:T(8,128)(2,1)}), bf16[16,256,128]{2,1,0:T(8,128)(2,1)}, u32[]{:S(2)}, u32[]{:S(2)}) async-start(bf16[16,256,128]{2,1,0:T(8,128)(2,1)} %bitcast.16), calls=%async_computation.4 | async-start | bytes 2097152 | tf_op jit(solution)/shard_map/all_to_all | solution.py:585
  165.5 2.8 %collective-permute-start.3 = (bf16[8,256,128]{2,1,0:T(8,128)(2,1)}, bf16[8,256,128]{2,1,0:T(8,128)(2,1)S(1)}, u32[]{:S(2)}, u32[]{:S(2)}) collective-permute-start(bf16[8,256,128]{2,1,0:T(8,128)(2,1)} %get-tuple-element.8), channel_id=1, source_target_pairs={{0,16},{16,0},{1,17},{17,1},{2,18},{18,2},{3,19},{19,3},{4,20},{20... | collective-permute-start | bytes 1572872 | tf_op jit(solution)/shard_map/ppermute | solution.py:592
  168.3 20.6 %collective-permute-done.3.rest_1_.far_away = bf16[8,256,128]{2,1,0:T(8,128)(2,1)S(1)} collective-permute-done((bf16[8,256,128]{2,1,0:T(8,128)(2,1)}, bf16[8,256,128]{2,1,0:T(8,128)(2,1)S(1)}, u32[]{:S(2)}, u32[]{:S(2)}) %collective-permute-start.3) | collective-permute-done | bytes 524320 | tf_op jit(solution)/shard_map/ppermute | solution.py:592
  189.0 1.0 copy-done.18
  190.0 5.8 %volterra.3 = bf16[16,256,128]{2,1,0:T(8,128)(2,1)S(1)} custom-call(s32[1]{0:T(128)} %bitcast.half_ref, bf16[16,256,128]{2,1,0:T(8,128)(2,1)S(1)} %all-to-all-done.1.rest_1_.own, bf16[8,256,128]{2,1,0:T(8,128)(2,1)S(1)} %copy-done.18, bf16[8,256,128]{2,1,0:T(8,128)(2,1)S(1)} %collective-permute-done.3.rest_1_.far_away, ...), custom_call_target="tpu_custom_call" | custom-call | tf_op jit(solution)/shard_map/volterra/pallas_call | solution.py:556
  195.8 0.0 copy-start.12
  195.8 1.0 copy-done.12
  196.8 8.0 %all-to-all-start.7 = ((bf16[16,256,128]{2,1,0:T(8,128)(2,1)}), bf16[16,256,128]{2,1,0:T(8,128)(2,1)S(1)}, u32[]{:S(2)}, u32[]{:S(2)}) async-start(bf16[16,256,128]{2,1,0:T(8,128)(2,1)} %copy-done.12), calls=%async_computation.7 | async-start | bytes 2097152 | tf_op jit(solution)/shard_map/all_to_all | solution.py:585
  204.8 5.9 %volterra.2 = bf16[16,256,128]{2,1,0:T(8,128)(2,1)S(1)} custom-call(s32[1]{0:T(128)} %bitcast.half_ref, bf16[16,256,128]{2,1,0:T(8,128)(2,1)S(1)} %all_to_all.40.rest_0_.own, bf16[8,256,128]{2,1,0:T(8,128)(2,1)} %collective-permute-done.far.far_near, bf16[8,256,128]{2,1,0:T(8,128)(2,1)S(1)} %collective-permute-done.1.refs_5_.far_away.rest_0_, ...), custom_call_target="tpu_custom_call" | custom-call | tf_op jit(solution)/shard_map/volterra/pallas_call | solution.py:556
  210.7 0.0 copy-start.13
  210.7 1.0 copy-done.13
  211.7 9.3 %all-to-all-done.7 = bf16[16,256,128]{2,1,0:T(8,128)(2,1)S(1)} async-done(((bf16[16,256,128]{2,1,0:T(8,128)(2,1)}), bf16[16,256,128]{2,1,0:T(8,128)(2,1)S(1)}, u32[]{:S(2)}, u32[]{:S(2)}) %all-to-all-start.7) | async-done | bytes 1048608 | tf_op jit(solution)/shard_map/all_to_all | solution.py:585
  221.0 19.8 %all_to_all.41 = bf16[16,256,128]{2,1,0:T(8,128)(2,1)S(1)} all-to-all(bf16[16,256,128]{2,1,0:T(8,128)(2,1)} %copy-done.13), channel_id=1, replica_groups=mesh['half'=2,'line'=8,'tcol'=2] {'tcol','line'}, dimensions={0} | all-to-all | bytes 2097152 | tf_op jit(solution)/shard_map/all_to_all | solution.py:585
  240.7 2.6 %collect.1 = (bf16[2,8,64,512]{3,2,1,0:T(8,128)(2,1)}, bf16[2,8,64,512]{3,2,1,0:T(8,128)(2,1)}) custom-call(bf16[4096,128]{1,0:T(8,128)(2,1)S(1)} %bitcast.14, bf16[4096,128]{1,0:T(8,128)(2,1)S(1)} %bitcast.13), custom_call_target="tpu_custom_call" | custom-call | tf_op jit(solution)/shard_map/collect/pallas_call | solution.py:281
  (26 shorter events, 0.0 us)
Async XLA Ops:
  0.6 1.2 copy-start.5
  1.9 1.2 copy-start.7
  27.2 1.0 copy-start.10
  28.1 7.5 %copy-start.23 = (s32[512]{0:T(512)S(1)}, s32[512]{0:T(512)}, u32[]{:S(2)}) copy-start(s32[512]{0:T(512)} %param.6) | copy-start | bytes 6148
  28.1 14.5 %copy-start.6 = (bf16[2,8,64,512]{3,2,1,0:T(8,128)(2,1)S(1)}, bf16[2,8,64,512]{3,2,1,0:T(8,128)(2,1)}, u32[]{:S(2)}) copy-start(bf16[2,8,64,512]{3,2,1,0:T(8,128)(2,1)} %lesser.5) | copy-start | bytes 3145732
  28.1 31.0 %all-to-all-start.1 = ((bf16[16,256,128]{2,1,0:T(8,128)(2,1)}), bf16[16,256,128]{2,1,0:T(8,128)(2,1)S(1)}, u32[]{:S(2)}, u32[]{:S(2)}) async-start(bf16[16,256,128]{2,1,0:T(8,128)(2,1)} %bitcast.15), calls=%async_computation.1 | async-start | bytes 2097152 | tf_op jit(solution)/shard_map/all_to_all | solution.py:585
  33.0 22.5 %collective-permute-start = (bf16[8,256,128]{2,1,0:T(8,128)(2,1)}, bf16[8,256,128]{2,1,0:T(8,128)(2,1)}, u32[]{:S(2)}, u32[]{:S(2)}) collective-permute-start(bf16[8,256,128]{2,1,0:T(8,128)(2,1)} %get-tuple-element.11), channel_id=1, source_target_pairs={{0,16},{16,0},{1,17},{17,1},{2,18},{18,2},{3,19},{19,3},{4,20},{20... | collective-permute-start | bytes 1572872 | tf_op jit(solution)/shard_map/ppermute | solution.py:592
  40.3 1.4 copy-start.9
  41.7 1.0 copy-start.19
  42.7 5.6 %copy-start.21 = (bf16[512,1024]{1,0:T(8,128)(2,1)}, bf16[512,1024]{1,0:T(8,128)(2,1)S(1)}, u32[]{:S(2)}) copy-start(bf16[512,1024]{1,0:T(8,128)(2,1)S(1)} %get-tuple-element.7.table) | copy-start | bytes 3145732
  42.7 1.6 copy-start.8
  48.2 1.3 copy-start
  59.2 1.6 copy-start.1
  63.2 32.0 %all-to-all-start.2 = ((bf16[16,256,128]{2,1,0:T(8,128)(2,1)}), bf16[16,256,128]{2,1,0:T(8,128)(2,1)S(1)}, u32[]{:S(2)}, u32[]{:S(2)}) async-start(bf16[16,256,128]{2,1,0:T(8,128)(2,1)} %to_crossed.2), calls=%async_computation.2 | async-start | bytes 2097152 | tf_op jit(solution)/shard_map/all_to_all | solution.py:585
  67.7 24.0 %copy-start.2 = (bf16[1024,1024]{1,0:T(8,128)(2,1)S(1)}, bf16[1024,1024]{1,0:T(8,128)(2,1)}, u32[]{:S(2)}) copy-start(bf16[1024,1024]{1,0:T(8,128)(2,1)} %copy-done) | copy-start | bytes 6291460
  68.7 23.0 %collective-permute-start.2 = (bf16[8,256,128]{2,1,0:T(8,128)(2,1)S(1)}, bf16[8,256,128]{2,1,0:T(8,128)(2,1)S(1)}, u32[]{:S(2)}, u32[]{:S(2)}) collective-permute-start(bf16[8,256,128]{2,1,0:T(8,128)(2,1)S(1)} %get-tuple-element.9), channel_id=1, source_target_pairs={{0,16},{16,0},{1,17},{17,1},{2,18},{18,2},{3,19},{19,3},{4,20},{20... | collective-permute-start | bytes 1572872 | tf_op jit(solution)/shard_map/ppermute | solution.py:592
  93.1 0.8 copy-start.17
  95.2 7.1 %copy-start.15 = (bf16[16,256,128]{2,1,0:T(8,128)(2,1)}, bf16[16,256,128]{2,1,0:T(8,128)(2,1)S(1)}, u32[]{:S(2)}) copy-start(bf16[16,256,128]{2,1,0:T(8,128)(2,1)S(1)} %all-to-all-done.2) | copy-start | bytes 3145732
  95.2 34.5 %all-to-all-start.3 = ((bf16[16,256,128]{2,1,0:T(8,128)(2,1)}), bf16[16,256,128]{2,1,0:T(8,128)(2,1)}, u32[]{:S(2)}, u32[]{:S(2)}) async-start(bf16[16,256,128]{2,1,0:T(8,128)(2,1)} %to_crossed.3), calls=%async_computation.3 | async-start | bytes 2097152 | tf_op jit(solution)/shard_map/all_to_all | solution.py:585
  102.2 24.0 %collective-permute-start.1 = (bf16[8,256,128]{2,1,0:T(8,128)(2,1)}, bf16[8,256,128]{2,1,0:T(8,128)(2,1)S(1)}, u32[]{:S(2)}, u32[]{:S(2)}) collective-permute-start(bf16[8,256,128]{2,1,0:T(8,128)(2,1)} %get-tuple-element.10), channel_id=1, source_target_pairs={{0,16},{16,0},{1,17},{17,1},{2,18},{18,2},{3,19},{19,3},{4,20},{20... | collective-permute-start | bytes 1572872 | tf_op jit(solution)/shard_map/ppermute | solution.py:592
  129.7 1.2 copy-start.16
  130.9 6.5 %copy-start.22 = (bf16[512,1024]{1,0:T(8,128)(2,1)S(1)}, bf16[512,1024]{1,0:T(8,128)(2,1)}, u32[]{:S(2)}) copy-start(bf16[512,1024]{1,0:T(8,128)(2,1)} %copy-done.21) | copy-start | bytes 3145732
  137.4 1.8 copy-start.3
  139.2 1.0 copy-start.14
  140.2 21.0 %all-to-all-start.6 = ((bf16[16,256,128]{2,1,0:T(8,128)(2,1)}), bf16[16,256,128]{2,1,0:T(8,128)(2,1)}, u32[]{:S(2)}, u32[]{:S(2)}) async-start(bf16[16,256,128]{2,1,0:T(8,128)(2,1)} %bitcast.17), calls=%async_computation.6 | async-start | bytes 2097152 | tf_op jit(solution)/shard_map/all_to_all | solution.py:585
  144.9 1.6 copy-start.4
  146.5 1.2 copy-start.20
  149.5 1.0 copy-start.11
  161.2 35.6 %all-to-all-start.4 = ((bf16[16,256,128]{2,1,0:T(8,128)(2,1)}), bf16[16,256,128]{2,1,0:T(8,128)(2,1)}, u32[]{:S(2)}, u32[]{:S(2)}) async-start(bf16[16,256,128]{2,1,0:T(8,128)(2,1)} %bitcast.16), calls=%async_computation.4 | async-start | bytes 2097152 | tf_op jit(solution)/shard_map/all_to_all | solution.py:585
  165.5 23.5 %collective-permute-start.3 = (bf16[8,256,128]{2,1,0:T(8,128)(2,1)}, bf16[8,256,128]{2,1,0:T(8,128)(2,1)S(1)}, u32[]{:S(2)}, u32[]{:S(2)}) collective-permute-start(bf16[8,256,128]{2,1,0:T(8,128)(2,1)} %get-tuple-element.8), channel_id=1, source_target_pairs={{0,16},{16,0},{1,17},{17,1},{2,18},{18,2},{3,19},{19,3},{4,20},{20... | collective-permute-start | bytes 1572872 | tf_op jit(solution)/shard_map/ppermute | solution.py:592
  189.0 1.0 copy-start.18
  195.8 1.0 copy-start.12
  196.8 24.2 %all-to-all-start.7 = ((bf16[16,256,128]{2,1,0:T(8,128)(2,1)}), bf16[16,256,128]{2,1,0:T(8,128)(2,1)S(1)}, u32[]{:S(2)}, u32[]{:S(2)}) async-start(bf16[16,256,128]{2,1,0:T(8,128)(2,1)} %copy-done.12), calls=%async_computation.7 | async-start | bytes 2097152 | tf_op jit(solution)/shard_map/all_to_all | solution.py:585
  210.7 1.0 copy-start.13

commit v4 on v3

--- a/solution.py
+++ b/solution.py
@@ -236,72 +236,70 @@
     return [pl.BlockSpec(memory_space=pltpu.VMEM)] * count
 
 
-def spread_kernel(first, lesser, greater, *rest):
-    out, lines = rest[-2:]
-    _, rows, _, _ = lesser.shape
-    count = lines.shape[0] // (2 * rows)
+def weight():
+    return pl.CostEstimate(flops=10**11, bytes_accessed=2**20, transcendentals=0)
+
+
+def scalars():
+    return [pl.BlockSpec(memory_space=pltpu.SMEM)]
+
+
+def spread_kernel(lesser, greater, out, lines):
+    _, rows, _, momenta = lesser.shape
     for g, tile in enumerate((lesser, greater)):
         for t in range(rows):
-            span = slice(first, first + count)
-            slab = jnp.concatenate([tile[0, t, :, span], tile[1, t, :, span]], axis=0)
-            lines[pl.ds(g * rows + t, count, stride=2 * rows), :] = slab.astype(F32).T
+            slab = jnp.concatenate([tile[0, t], tile[1, t]], axis=0)
+            lines[pl.ds(g * rows + t, momenta, stride=2 * rows), :] = slab.astype(F32).T
     out[...] = lines[...].astype(BF16)
 
 
-def spread(tiles, first, count, after):
-    _, rows, cols, _ = tiles[0].shape
-    shape = (count * 2 * rows, 2 * cols)
-    return pl.pallas_call(
-        functools.partial(spread_kernel, first),
+def spread(tiles):
+    _, rows, cols, momenta = tiles[0].shape
+    shape = (momenta * 2 * rows, 2 * cols)
+    return pl.pallas_call(
+        spread_kernel,
         out_shape=jax.ShapeDtypeStruct(shape, BF16),
-        in_specs=whole(2) + unread(after),
+        in_specs=whole(2),
         out_specs=whole(1)[0],
         scratch_shapes=[pltpu.VMEM(shape, F32)],
         compiler_params=vmem_params(),
         name="spread",
-    )(*tiles, *after)
-
-
-def collect_kernel(*refs):
-    *parts, lesser, greater, lines = refs
+    )(*tiles)
+
+
+def collect_kernel(rows_ref, lesser, greater, lines):
+    lines[...] = rows_ref[...].astype(F32)
     _, rows, cols, momenta = lesser.shape
-    count = momenta // len(parts)
-    for at, part in enumerate(parts):
-        lines[...] = part[...].astype(F32)
-        span = slice(at * count, (at + 1) * count)
-        for k in range(2 * rows):
-            slab = lines[pl.ds(k, count, stride=2 * rows), :].T.astype(BF16)
-            out = lesser if k < rows else greater
-            out[0, k % rows, :, span] = slab[:cols]
-            out[1, k % rows, :, span] = slab[cols:]
-
-
-def collect(parts, tile_shape):
+    for k in range(2 * rows):
+        slab = lines[pl.ds(k, momenta, stride=2 * rows), :].T.astype(BF16)
+        out = lesser if k < rows else greater
+        out[0, k % rows] = slab[:cols]
+        out[1, k % rows] = slab[cols:]
+
+
+def collect(rows_array, tile_shape):
     shape = jax.ShapeDtypeStruct(tile_shape, BF16)
     return pl.pallas_call(
         collect_kernel,
         out_shape=(shape, shape),
-        in_specs=whole(len(parts)),
+        in_specs=whole(1),
         out_specs=tuple(whole(2)),
-        scratch_shapes=[pltpu.VMEM(parts[0].shape, F32)],
+        scratch_shapes=[pltpu.VMEM(rows_array.shape, F32)],
         compiler_params=vmem_params(),
         name="collect",
-    )(*parts)
-
-
-def table_kernel(column_ref, table, *inverse):
+    )(rows_array)
+
+
+def table_kernel(column_ref, table, inverse):
     momenta = column_ref.shape[0]
-    count = momenta // len(inverse)
     positions = lax.broadcasted_iota(jnp.int32, (momenta, momenta), 1)
     phases = (column_ref[...] * positions % momenta).astype(F32) * (2.0 * math.pi / momenta)
     cosines = jnp.cos(phases).astype(BF16)
     sines = jnp.sin(phases).astype(BF16)
-    for part, ref in enumerate(inverse):
-        span = slice(part * count, (part + 1) * count)
-        ref[:count, :momenta] = cosines[span]
-        ref[:count, momenta:] = sines[span]
-        ref[count:, :momenta] = -sines[span]
-        ref[count:, momenta:] = cosines[span]
+    inverse[:momenta, :momenta] = cosines
+    inverse[:momenta, momenta:] = sines
+    inverse[momenta:, :momenta] = -sines
+    inverse[momenta:, momenta:] = cosines
     cosines = cosines.astype(F32).T.astype(BF16)
     sines = sines.astype(F32).T.astype(BF16)
     table[:momenta, :momenta] = cosines
@@ -310,183 +308,173 @@
     table[momenta:, momenta:] = cosines
 
 
-def make_tables(lattice_map, parts):
+def make_tables(lattice_map):
     momenta = lattice_map.shape[0]
-    count = momenta // parts
-    shapes = [(2 * momenta, 2 * momenta)] + [(2 * count, 2 * momenta)] * parts
+    shape = jax.ShapeDtypeStruct((2 * momenta, 2 * momenta), BF16)
     return pl.pallas_call(
         table_kernel,
-        out_shape=tuple(jax.ShapeDtypeStruct(shape, BF16) for shape in shapes),
+        out_shape=(shape, shape),
         in_specs=whole(1),
-        out_specs=tuple(whole(1 + parts)),
+        out_specs=tuple(whole(2)),
         compiler_params=vmem_params(),
         name="make_tables",
     )(lattice_map[:, None])
 
 
-def site_kernel(norm_factor, lesser, greater, table, out):
-    _, rows, cols, _ = lesser.shape
+def site_kernel(norm_factor, first_ref, lesser, greater, got, table, out):
+    first = first_ref[0]
+    _, _, count, cols, _ = got.shape
     wide = 4 * cols
-    for pair in range(rows // 2):
-        slabs = [
-            jnp.concatenate([tile[0, t], tile[1, t]], axis=1)
-            for t in (2 * pair, 2 * pair + 1)
-            for tile in (lesser, greater)
-        ]
-        product = lax.dot_general(
-            table[...],
-            jnp.concatenate(slabs, axis=0),
-            (((1,), (1,)), ((), ())),
-            preferred_element_type=F32,
-        )
-        out[:, pair * wide : (pair + 1) * wide] = (product * norm_factor).astype(BF16)
-
-
-def to_sites(tiles, table, norm_factor):
-    _, rows, cols, momenta = tiles[0].shape
+    for which in range(2):
+        for pair in range(count // 2):
+            slabs = []
+            for t in (2 * pair, 2 * pair + 1):
+                for g, tile in enumerate((lesser, greater)):
+                    if which == 0:
+                        parts = [tile[c, first + t] for c in range(2)]
+                    else:
+                        parts = [got[g, c, t] for c in range(2)]
+                    slabs.append(jnp.concatenate(parts, axis=1))
+            product = lax.dot_general(
+                table[...],
+                jnp.concatenate(slabs, axis=0),
+                (((1,), (1,)), ((), ())),
+                preferred_element_type=F32,
+            )
+            out[which, :, pair * wide : (pair + 1) * wide] = (product * norm_factor).astype(BF16)
+
+
+def to_sites(first, tiles, got, table, norm_factor):
+    _, _, count, cols, momenta = got.shape
     return pl.pallas_call(
         functools.partial(site_kernel, norm_factor),
-        out_shape=jax.ShapeDtypeStruct((2 * momenta, rows * 2 * cols), BF16),
-        in_specs=whole(3),
+        out_shape=jax.ShapeDtypeStruct((2, 2 * momenta, count * 2 * cols), BF16),
+        in_specs=scalars() + whole(4),
         out_specs=whole(1)[0],
         compiler_params=vmem_params(),
         name="to_sites",
-    )(*tiles, table)
-
-
-def cross_kernel(rows, half_ref, own, far, *rest):
+    )(first, *tiles, got, table)
+
+
+def cross_kernel(rows, blocks, first_ref, source, *rest):
     out = rest[-1]
-    half = half_ref[0]
-    blocks = far.shape[0]
+    first = first_ref[0]
     cols = blocks * rows
-    for at in range(far.shape[1] // (2 * rows)):
-        span = slice(at * 2 * rows, (at + 1) * 2 * rows)
-        for source, offset, target in ((own, half * blocks, half), (far, 0, 1 - half)):
-            loaded = [source[offset + block, span].astype(F32) for block in range(blocks)]
+    count = rows // 2
+    for pair in range(source.shape[1] // (4 * rows)):
+        turned = []
+        for at in (2 * pair, 2 * pair + 1):
+            span = slice(at * 2 * rows, (at + 1) * 2 * rows)
+            loaded = [source[first + block, span].astype(F32) for block in range(blocks)]
             stacked = jnp.concatenate(
                 [lines[rows:] for lines in loaded] + [lines[:rows] for lines in loaded], axis=0
             )
-            turned = stacked.T
+            turned.append(stacked.T)
+        span = slice(pair * 2 * rows, (pair + 1) * 2 * rows)
+        for side in range(2):
             for block in range(blocks):
-                out[target * blocks + block, span] = jnp.concatenate(
+                start = block * rows + side * count
+                out[side * blocks + block, span] = jnp.concatenate(
                     [
-                        turned[block * rows : (block + 1) * rows],
-                        turned[cols + block * rows : cols + (block + 1) * rows],
+                        lines[c * cols + start : c * cols + start + count]
+                        for lines in turned
+                        for c in range(2)
                     ],
                     axis=0,
                 ).astype(BF16)
 
 
-def to_crossed(half, own, far, rows, after):
-    return pl.pallas_call(
-        functools.partial(cross_kernel, rows),
-        out_shape=jax.ShapeDtypeStruct(own.shape, BF16),
-        in_specs=[pl.BlockSpec(memory_space=pltpu.SMEM)] + whole(2) + unread(after),
+def to_crossed(first, source, rows, blocks, after, cost):
+    shape = (2 * blocks, source.shape[1] // 2, source.shape[2])
+    return pl.pallas_call(
+        functools.partial(cross_kernel, rows, blocks),
+        out_shape=jax.ShapeDtypeStruct(shape, BF16),
+        in_specs=scalars() + whole(1) + unread(after),
         out_specs=whole(1)[0],
         compiler_params=vmem_params(),
+        cost_estimate=cost,
         name="to_crossed",
-    )(half, own, far, *after)
-
-
-def self_kernel(norm_factor, parts, *refs):
-    crossed = refs[:parts]
-    own, table, coupling = refs[parts : parts + 3]
-    out, lines = refs[-2:]
-    rows = coupling.shape[0]
-    momenta = own.shape[0] // 2
-    count = momenta // parts
-    for part in range(parts):
-        lines[part] = crossed[part][...].astype(F32)
-    for pair in range(rows // 2):
+    )(first, source, *after)
+
+
+def gate_kernel(*refs):
+    del refs
+
+
+def gate(array, after):
+    return pl.pallas_call(
+        gate_kernel,
+        out_shape=jax.ShapeDtypeStruct(array.shape, array.dtype),
+        in_specs=unread([array, *after]),
+        out_specs=unread([array])[0],
+        input_output_aliases={0: 0},
+        name="gate",
+    )(array, *after)
+
+
+def sigma_kernel(norm_factor, which_ref, crossed, sites, table, inverse, coupling, *rest):
+    out, read, written = rest[-3:]
+    which = which_ref[0]
+    count = coupling.shape[0]
+    momenta = table.shape[0] // 2
+    read[...] = crossed[...].astype(F32)
+    for pair in range(count // 2):
         rights = []
         for t in (2 * pair, 2 * pair + 1):
-            real = [lines[part, pl.ds(t, count, stride=2 * rows), :] for part in range(parts)]
-            imaginary = [
-                -lines[part, pl.ds(rows + t, count, stride=2 * rows), :] for part in range(parts)
-            ]
-            rights.append(jnp.concatenate(real + imaginary, axis=0).astype(BF16))
+            real = read[pl.ds(t, momenta, stride=2 * count), :]
+            imaginary = -read[pl.ds(count + t, momenta, stride=2 * count), :]
+            rights.append(jnp.concatenate([real, imaginary], axis=0).astype(BF16))
         other = jnp.dot(
             table[...], jnp.concatenate(rights, axis=1), preferred_element_type=F32
         )
         other = (other * norm_factor).astype(BF16).astype(F32)
-        for at in range(2):
-            t = 2 * pair + at
-            span = slice(t * LANES, (t + 1) * LANES)
-            self_real, self_imaginary = second_born(
-                own[:momenta, span].astype(F32),
-                own[momenta:, span].astype(F32),
-                other[:momenta, at * LANES : (at + 1) * LANES],
-                -other[momenta:, at * LANES : (at + 1) * LANES],
-                coupling[t : t + 1, :],
-            )
-            out[:momenta, span] = self_real.astype(BF16)
-            out[momenta:, span] = self_imaginary.astype(BF16)
-
-
-def to_self(crossed, own, table, coupling, norm_factor, after):
-    parts = len(crossed)
-    return pl.pallas_call(
-        functools.partial(self_kernel, norm_factor, parts),
-        out_shape=jax.ShapeDtypeStruct(own.shape, BF16),
-        in_specs=whole(parts + 3) + unread(after),
-        out_specs=whole(1)[0],
-        scratch_shapes=[pltpu.VMEM((parts,) + crossed[0].shape, F32)],
-        compiler_params=vmem_params(),
-        name="to_self",
-    )(*crossed, own, table, coupling, *after)
-
-
-def sigma_kernel(norm_factor, rows, sites, table, out, lines):
-    count = table.shape[0] // 2
-    for pair in range(rows // 2):
+        span = slice(2 * pair * LANES, 2 * (pair + 1) * LANES)
+        self_real, self_imaginary = second_born(
+            sites[which, :momenta, span].astype(F32),
+            sites[which, momenta:, span].astype(F32),
+            other[:momenta],
+            -other[momenta:],
+            jnp.concatenate([coupling[t : t + 1] for t in (2 * pair, 2 * pair + 1)], axis=1),
+        )
         product = jnp.dot(
-            table[...],
-            sites[:, 2 * pair * LANES : 2 * (pair + 1) * LANES],
+            inverse[...],
+            jnp.concatenate([self_real, self_imaginary], axis=0).astype(BF16),
             preferred_element_type=F32,
         )
         product = product * norm_factor
         for at in range(2):
             for part in range(2):
-                lines[pl.ds(part * rows + 2 * pair + at, count, stride=2 * rows), :] = product[
-                    part * count : (part + 1) * count, at * LANES : (at + 1) * LANES
+                written[pl.ds(part * count + 2 * pair + at, momenta, stride=2 * count), :] = product[
+                    part * momenta : (part + 1) * momenta, at * LANES : (at + 1) * LANES
                 ]
-    out[...] = lines[...].astype(BF16)
-
-
-def to_sigma(sites, table, rows, norm_factor):
-    shape = (table.shape[0] * rows, LANES)
-    return pl.pallas_call(
-        functools.partial(sigma_kernel, norm_factor, rows),
-        out_shape=jax.ShapeDtypeStruct(shape, BF16),
-        in_specs=whole(2),
+    out[...] = written[...].astype(BF16)
+
+
+def to_sigma(which, crossed, sites, table, inverse, coupling, norm_factor, after):
+    return pl.pallas_call(
+        functools.partial(sigma_kernel, norm_factor),
+        out_shape=jax.ShapeDtypeStruct(crossed.shape, BF16),
+        in_specs=scalars() + whole(5) + unread(after),
         out_specs=whole(1)[0],
-        scratch_shapes=[pltpu.VMEM(shape, F32)],
+        scratch_shapes=[pltpu.VMEM(crossed.shape, F32)] * 2,
         compiler_params=vmem_params(),
         name="to_sigma",
-    )(sites, table)
-
-
-def volterra_kernel(rows, half_ref, own, far_near, far_away, sigma, *rest):
-    out = rest[-1]
+    )(which, crossed, sites, table, inverse, coupling, *after)
+
+
+def rights_kernel(rows, half_ref, own, far_near, far_away, out):
     half = half_ref[0]
     blocks = far_near.shape[0]
     lanes = own.shape[2]
     cols = lanes // 2
     near = half * cols
     away = (1 - half) * cols
-    near_at = half * blocks
-    away_at = (1 - half) * blocks
-    first_times = near + lax.broadcasted_iota(jnp.int32, (cols, lanes), 0)
-    left_lane = lax.broadcasted_iota(jnp.int32, (cols, lanes), 1)
-    low_lanes = left_lane < cols
-    left_times = jnp.where(low_lanes, near + left_lane, away + left_lane - cols)
-    keep_left = left_times <= first_times
     row_at = lax.broadcasted_iota(jnp.int32, (lanes, 2 * lanes), 0)
     inner_times = jnp.where(row_at < cols, near + row_at, away + row_at - cols)
     lane_at = lax.broadcasted_iota(jnp.int32, (lanes, 2 * lanes), 1)
     last_times = jnp.where(lane_at < lanes, near, away) + lane_at % cols
-    keep_right = inner_times <= last_times
-    for at in range(own.shape[1] // (2 * rows)):
+    keep = inner_times <= last_times
+    for at in range(out.shape[0]):
         span = slice(at * 2 * rows, (at + 1) * 2 * rows)
 
         def stacked(ref, offset):
@@ -496,8 +484,8 @@
                 for part in range(2)
             ]
 
-        own_near = stacked(own, near_at)
-        own_away = stacked(own, away_at)
+        own_near = stacked(own, half * blocks)
+        own_away = stacked(own, (1 - half) * blocks)
         cross_near = stacked(far_near, 0)
         cross_away = stacked(far_away, 0)
         greens = [
@@ -510,9 +498,63 @@
             )
             for g in range(2)
         ]
-        advanced = jnp.where(keep_right, greens[0] - greens[1], 0.0).astype(BF16)
-        sigma_near = stacked(sigma, near_at)
-        sigma_away = stacked(sigma, away_at)
+        out[at, :lanes] = greens[0].astype(BF16)
+        out[at, lanes : 2 * lanes] = greens[1].astype(BF16)
+        out[at, 2 * lanes :] = jnp.where(keep, greens[0] - greens[1], 0.0).astype(BF16)
+
+
+def make_rights(half, own, far_near, far_away, rows):
+    sources, lines, lanes = own.shape
+    blocks = far_near.shape[0]
+    step = 4 * rows
+    spec = pl.BlockSpec((sources, step, lanes), lambda p: (0, p, 0))
+    far_spec = pl.BlockSpec((blocks, step, lanes), lambda p: (0, p, 0))
+    return pl.pallas_call(
+        functools.partial(rights_kernel, rows),
+        grid=(lines // step,),
+        out_shape=jax.ShapeDtypeStruct((lines // (2 * rows), 3 * lanes, 2 * lanes), BF16),
+        in_specs=scalars() + [spec, far_spec, far_spec],
+        out_specs=pl.BlockSpec((2, 3 * lanes, 2 * lanes), lambda p: (p, 0, 0)),
+        compiler_params=vmem_params(),
+        cost_estimate=weight(),
+        name="make_rights",
+    )(half, own, far_near, far_away)
+
+
+def volterra_kernel(rows, half_ref, diagonal, cross, rights, out):
+    half = half_ref[0]
+    blocks = diagonal.shape[0] // 2
+    lanes = diagonal.shape[2]
+    cols = lanes // 2
+    count = rows // 2
+    near = half * cols
+    away = (1 - half) * cols
+    first_times = near + lax.broadcasted_iota(jnp.int32, (cols, lanes), 0)
+    left_lane = lax.broadcasted_iota(jnp.int32, (cols, lanes), 1)
+    low_lanes = left_lane < cols
+    left_times = jnp.where(low_lanes, near + left_lane, away + left_lane - cols)
+    keep_left = left_times <= first_times
+    pairs = []
+    for at in range(2):
+        piece = slice(at * rows, (at + 1) * rows)
+
+        def stacked(ref):
+            low = [ref[block].astype(F32)[piece] for block in range(blocks)]
+            high = [ref[blocks + block].astype(F32)[piece] for block in range(blocks)]
+            return [
+                jnp.concatenate(
+                    [
+                        lines[block][part * count : (part + 1) * count]
+                        for block in range(blocks)
+                        for lines in (low, high)
+                    ],
+                    axis=0,
+                )
+                for part in range(2)
+            ]
+
+        sigma_near = stacked(diagonal)
+        sigma_away = stacked(cross)
         retarded = []
         lefts = [[], []]
         for part in range(2):
@@ -531,7 +573,9 @@
             left = jnp.concatenate(
                 [retarded, jnp.concatenate(lefts[g], axis=0).astype(BF16)], axis=1
             )
-            right = jnp.concatenate([greens[g].astype(BF16), advanced], axis=0)
+            right = jnp.concatenate(
+                [rights[at, g * lanes : (g + 1) * lanes], rights[at, 2 * lanes :]], axis=0
+            )
             product = jnp.dot(left, right, preferred_element_type=F32)
             sides = []
             for side in range(2):
@@ -540,32 +584,26 @@
                 sides.append((straight + jnp.where(low_lanes, -turned, turned)) * step_size)
             results.append(sides)
         for block in range(blocks):
-            piece = slice(block * rows, (block + 1) * rows)
-            for side, offset in enumerate((near_at, away_at)):
-                out[offset + block, span] = jnp.concatenate(
-                    [results[0][side][piece], results[1][side][piece]], axis=0
+            lines = slice(block * rows, (block + 1) * rows)
+            for side, offset in enumerate((half * blocks, (1 - half) * blocks)):
+                out[offset + block, at * 2 * rows : (at + 1) * 2 * rows] = jnp.concatenate(
+                    [results[0][side][lines], results[1][side][lines]], axis=0
                 ).astype(BF16)
 
 
-def volterra(half, own, far_near, far_away, sigma, rows, after):
-    sources, lines, lanes = own.shape
-    blocks = far_near.shape[0]
-    step = 4 * rows
-    spec = pl.BlockSpec((sources, step, lanes), lambda p: (0, p, 0))
-    far_spec = pl.BlockSpec((blocks, step, lanes), lambda p: (0, p, 0))
+def volterra(half, diagonal, cross, rights, rows):
+    sources, lines, lanes = diagonal.shape
+    spec = pl.BlockSpec((sources, 2 * rows, lanes), lambda p: (0, p, 0))
     return pl.pallas_call(
         functools.partial(volterra_kernel, rows),
-        grid=(lines // step,),
-        out_shape=jax.ShapeDtypeStruct(own.shape, BF16),
-        in_specs=[pl.BlockSpec(memory_space=pltpu.SMEM), spec, far_spec, far_spec, spec]
-        + unread(after),
-        out_specs=spec,
+        grid=(lines // (2 * rows),),
+        out_shape=jax.ShapeDtypeStruct((sources, 2 * lines, lanes), BF16),
+        in_specs=scalars()
+        + [spec, spec, pl.BlockSpec((2, 3 * lanes, 2 * lanes), lambda p: (p, 0, 0))],
+        out_specs=pl.BlockSpec((sources, 4 * rows, lanes), lambda p: (0, p, 0)),
         compiler_params=vmem_params(),
         name="volterra",
-    )(half, own, far_near, far_away, sigma, *after)
-
-
-PARTS = 2
+    )(half, diagonal, cross, rights)
 
 
 def halved_body(green_lesser, green_greater, lattice_map, time_offset):
@@ -578,8 +616,9 @@
     window = rows * lines * lax.axis_size("half")
     norm_factor = 1.0 / math.sqrt(momenta)
     tiles = (green_lesser, green_greater)
-    count = momenta // PARTS
+    count = rows // 2
     half_at = half[None]
+    trade = [(0, 1), (1, 0)]
 
     def exchange(blocks):
         return lax.all_to_all(blocks, ("tcol", "line"), 0, 0, tiled=True)
@@ -588,38 +627,54 @@
         return rows_array.reshape(group, rows_array.shape[0] // group, rows_array.shape[1])
 
     def swap(blocks, at):
-        sent = lax.dynamic_slice_in_dim(blocks, at * lines, lines)
-        return lax.ppermute(sent, "half", [(0, 1), (1, 0)])
-
-    own = []
-    for part in range(PARTS):
-        own.append(exchange(blocked(spread(tiles, part * count, count, own[-1:]))))
-    far_near = [swap(blocks, 1 - half) for blocks in own]
-    far_away = [swap(blocks, half) for blocks in own]
-
-    table, *inverse = make_tables(lattice_map, PARTS)
-    sites = to_sites(tiles, table, norm_factor)
+        return lax.ppermute(lax.dynamic_slice_in_dim(blocks, at * lines, lines), "half", trade)
+
+    given = jnp.stack(
+        [lax.dynamic_slice_in_dim(tile, (1 - side) * count, count, 1) for tile in tiles]
+    )
+    got = lax.ppermute(given, "tcol", trade)
+    own = exchange(blocked(spread(tiles)))
+    far_near = swap(own, 1 - half)
+    far_away = swap(own, half)
+
+    table, inverse = make_tables(lattice_map)
+    kept = side * count
+    sites = to_sites(kept[None], tiles, got, table, norm_factor)
     time_steps = jnp.arange(window, dtype=jnp.int32)
     coupling_line = 1.0 + drive_depth * jnp.cos(
         ((time_offset[0] + time_steps) % PERIOD).astype(F32) * (2.0 * math.pi / PERIOD)
     )
-    first = lax.dynamic_slice_in_dim(coupling_line, (half * lines + line) * rows, rows)
-    second = lax.dynamic_slice_in_dim(coupling_line, side * cols, cols)
-    coupling = first[:, None] * jnp.concatenate([second, second])[None, :]
-
-    crossed = [
-        exchange(to_crossed(half_at, own[part], far_near[part], rows, [*own, sites])).reshape(-1, 2 * cols)
-        for part in range(PARTS)
-    ]
-    self_sites = to_self(crossed, sites, table, coupling, norm_factor, far_away[:1])
-    returned = []
-    for part in range(PARTS):
-        sigma = exchange(blocked(to_sigma(self_sites, inverse[part], rows, norm_factor)))
-        collisions = volterra(
-            half_at, own[part], far_near[part], far_away[part], sigma, rows, far_away
+    first = lax.dynamic_slice_in_dim(coupling_line, (half * lines + line) * rows + kept, count)
+
+    def phase_sigma(crossed, at, after):
+        second = lax.dynamic_slice_in_dim(coupling_line, at * cols, cols)
+        coupling = first[:, None] * jnp.concatenate([second, second])[None, :]
+        which = (side != at).astype(jnp.int32)[None]
+        return to_sigma(
+            which,
+            crossed.reshape(-1, 2 * cols),
+            sites,
+            table,
+            inverse,
+            coupling,
+            norm_factor,
+            after,
         )
-        returned.append(exchange(collisions).reshape(-1, 2 * cols))
-    return collect(returned, green_lesser.shape)
+
+    crossed = exchange(
+        to_crossed((half * lines)[None], own, rows, lines, [sites], None)
+    )
+    sigma_rows = phase_sigma(crossed, half, [])
+    diagonal = exchange(blocked(sigma_rows))
+    sent = to_crossed(
+        jnp.zeros((1,), jnp.int32), far_near, rows, lines, [sigma_rows], weight()
+    )
+    crossed = exchange(gate(sent, [diagonal]))
+    cross = exchange(blocked(phase_sigma(crossed, 1 - half, [])))
+    rights = make_rights(half_at, own, far_near, far_away, rows)
+    collisions = volterra(half_at, diagonal, cross, rights, rows)
+    returned = exchange(collisions)
+    return collect(returned.reshape(-1, 2 * cols), green_lesser.shape)
 
 
 def solution(mesh):
@@ -637,8 +692,7 @@
             and 2 * cols == LANES
             and cols == rows * (row_parts // 2)
             and rows % 8 == 0
-            and momenta % (PARTS * LANES) == 0
-            and momenta % (PARTS * row_parts * 2) == 0
+            and momenta % (2 * row_parts) == 0 and momenta % LANES == 0
         )
         if halved:
             devices = mesh.devices.reshape(2, row_parts // 2, col_parts)

time: 245 us -> 253 us (1.033)
  waiting for transfers between devices: 94.1 us -> 122 us
  starting transfers between devices: 44.7 us -> 25.8 us
  Pallas kernels: 38.3 us -> 54.7 us
  blocking collectives: 42 us -> 30 us
  local copies, waits for them, and re-layouts: 22.4 us -> 16 us
    all_to_all x6 -> x5, waiting for transfers between devices: 28.4 us -> 54.5 us  [exchange(): return lax.all_to_all(blocks, ('tcol', 'line'), 0, 0, tiled=True)]
    pallas_call x11 -> x10, Pallas kernels: 34.3 us -> 50.4 us  [the longest x2 12.1 us: to_sigma(): pl.pallas_call(functools.partial(sigma_kernel, norm_factor), out_shape=ja...]
    all_to_all x2 -> x1, blocking collectives: 42 us -> 30 us  [exchange(): return lax.all_to_all(blocks, ('tcol', 'line'), 0, 0, tiled=True)]
    all_to_all x6 -> x5, starting transfers between devices: 32.5 us -> 21.3 us  [exchange(): return lax.all_to_all(blocks, ('tcol', 'line'), 0, 0, tiled=True)]
    ppermute x4 -> x3, starting transfers between devices: 12.2 us -> 4.53 us  [the longest x2 2.66 us: swap(): lax.ppermute(lax.dynamic_slice_in_dim(blocks, at * lines, lines), 'half',...]
    unnamed x48 -> x30, local copies, waits for them, and re-layouts: 20.1 us -> 12.5 us
    ppermute x4 -> x3, waiting for transfers between devices: 65.8 us -> 67.5 us  [the longest x1 37.7 us: halved_body(): got = lax.ppermute(given, 'tcol', trade)]
  transfers between devices with their start and end apart: 10 -> 8, of which waited for: 9 -> 7; matrix products, arithmetic and copies ran while one was open for 1% -> 2% of each run, Pallas kernels for 10% -> 13%
where the time goes in v4:
time: 253 us; the launch traced here: 251 us
  waiting for transfers between devices  122 us (48%)
  Pallas kernels  54.7 us (22%)
  blocking collectives  30 us (12%)
  starting transfers between devices  25.8 us (10%)
  local copies, waits for them, and re-layouts  16 us (6%)
    all_to_all x5, waiting for transfers between devices, exchange(): return lax.all_to_all(blocks, ('tcol', 'line'), 0, 0, tiled=True)  54.5 us
    ppermute x1, waiting for transfers between devices, halved_body(): got = lax.ppermute(given, 'tcol', trade)  37.7 us
    all_to_all x1, blocking collectives, exchange(): return lax.all_to_all(blocks, ('tcol', 'line'), 0, 0, tiled=True)  30 us
    ppermute x2, waiting for transfers between devices, swap(): lax.ppermute(lax.dynamic_slice_in_dim(blocks, at * lines, lines), 'half',...  29.8 us
    all_to_all x5, starting transfers between devices, exchange(): return lax.all_to_all(blocks, ('tcol', 'line'), 0, 0, tiled=True)  21.3 us
    unnamed x30, local copies, waits for them, and re-layouts  12.5 us
    pallas_call x2, Pallas kernels, to_sigma(): pl.pallas_call(functools.partial(sigma_kernel, norm_factor), out_shape=ja...  12.1 us
    pallas_call x1, Pallas kernels, volterra(): pl.pallas_call(functools.partial(volterra_kernel, rows), grid=(lines // (...  11.8 us
  transfers between devices with their start and end apart: 8, of which 7 were waited for; matrix products, arithmetic and copies ran while one was open for 2% of the time, Pallas kernels for 13%

profile of v4, /device:TPU:0, one launch (start us, length us, event | category | flops | bytes accessed | tf_op | source)
XLA Modules:
  0.0 251.4 jit_solution(14354563777238003121)
XLA Ops:
  0.6 0.0 copy-start.4
  0.6 1.2 copy-done.4
  1.9 0.0 copy-start.6
  1.9 1.2 copy-done.6
  3.1 3.8 %spread.1 = bf16[8192,128]{1,0:T(8,128)(2,1)} custom-call(bf16[2,8,64,512]{3,2,1,0:T(8,128)(2,1)S(1)} %copy-done.4, bf16[2,8,64,512]{3,2,1,0:T(8,128)(2,1)S(1)} %copy-done.6), custom_call_target="tpu_custom_call" | custom-call | tf_op jit(solution)/shard_map/spread/pallas_call | solution.py:259
  6.9 0.0 copy-start.5
  6.9 0.0 copy-start.7
  6.9 6.5 %all-to-all-start = ((bf16[16,512,128]{2,1,0:T(8,128)(2,1)}), bf16[16,512,128]{2,1,0:T(8,128)(2,1)}, u32[]{:S(2)}, u32[]{:S(2)}) async-start(bf16[16,512,128]{2,1,0:T(8,128)(2,1)} %bitcast.3), calls=%async_computation | async-start | bytes 4194304 | tf_op jit(solution)/shard_map/all_to_all | solution.py:624
  13.4 0.0 copy-done.5
  13.4 0.0 copy-done.7
  13.4 0.0 copy-start.14
  13.4 0.1 dynamic-slice_bitcast_fusion
  13.5 1.1 pad_maximum_fusion
  14.6 1.9 collective-permute-start
  16.5 0.0 copy-done.14
  16.5 0.1 copy.7.column_ref
  16.6 4.5 %make_tables.1 = (bf16[1024,1024]{1,0:T(8,128)(2,1)S(1)}, bf16[1024,1024]{1,0:T(8,128)(2,1)S(1)}) custom-call(s32[512,1]{1,0:T(8,128)S(1)} %copy.7.column_ref), custom_call_target="tpu_custom_call" | custom-call | tf_op jit(solution)/shard_map/make_tables/pallas_call | solution.py:314
  21.2 0.0 copy-start
  21.2 1.3 copy-done
  22.5 0.0 copy-start.3
  22.5 1.3 copy-done.3
  23.8 37.7 %collective-permute-done.got = bf16[2,2,4,64,512]{4,3,2,1,0:T(8,128)(2,1)} collective-permute-done((bf16[2,2,4,64,512]{4,3,2,1,0:T(8,128)(2,1)}, bf16[2,2,4,64,512]{4,3,2,1,0:T(8,128)(2,1)}, u32[]{:S(2)}, u32[]{:S(2)}) %collective-permute-start) | collective-permute-done | bytes 1048608 | tf_op jit(solution)/shard_map/ppermute | solution.py:635
  61.5 0.0 copy-start.8
  61.5 1.2 copy-done.8
  62.8 4.3 %to_sites.1.rest_0_.sites = bf16[2,1024,512]{2,1,0:T(8,128)(2,1)S(1)} custom-call(s32[1]{0:T(128)} %bitcast.4.first_ref, bf16[2,8,64,512]{3,2,1,0:T(8,128)(2,1)S(1)} %copy-done.5, bf16[2,8,64,512]{3,2,1,0:T(8,128)(2,1)S(1)} %copy-done.8, bf16[2,2,4,64,512]{4,3,2,1,0:T(8,128)(2,1)} %collective-permute-done.got, bf16[1024,1024]{1,0:T(8,128)(2,1)} %copy-done), custom_call_target="tpu_custom_call" | custom-call | tf_op jit(solution)/shard_map/to_sites/pallas_call | solution.py:349
  67.0 0.0 all-to-all-done.source.own
  67.0 2.0 to_crossed.2
  69.1 0.0 copy-start.13
  69.1 1.0 copy-done.13
  70.0 3.9 %all-to-all-start.1 = ((bf16[16,256,128]{2,1,0:T(8,128)(2,1)}), bf16[16,256,128]{2,1,0:T(8,128)(2,1)S(1)}, u32[]{:S(2)}, u32[]{:S(2)}) async-start(bf16[16,256,128]{2,1,0:T(8,128)(2,1)} %copy-done.13), calls=%async_computation.1 | async-start | bytes 2097152 | tf_op jit(solution)/shard_map/all_to_all | solution.py:624
  73.9 3.1 %constant_dynamic-slice_fusion = (bf16[8,512,128]{2,1,0:T(8,128)(2,1)}, bf16[8,512,128]{2,1,0:T(8,128)(2,1)}) fusion(bf16[16,512,128]{2,1,0:T(8,128)(2,1)} %all-to-all-done.source.own, s32[]{:T(128)S(6)} %select_n.32, s32[]{:T(128)S(6)} %select_n.30), kind=kLoop, calls=%fused_computation.8 | loop fusion | bytes 4194312 | tf_op jit(solution)/shard_map/dynamic_slice | solution.py:630
  77.0 2.6 %collective-permute-start.1 = (bf16[8,512,128]{2,1,0:T(8,128)(2,1)}, bf16[8,512,128]{2,1,0:T(8,128)(2,1)}, u32[]{:S(2)}, u32[]{:S(2)}) collective-permute-start(bf16[8,512,128]{2,1,0:T(8,128)(2,1)} %get-tuple-element.7), channel_id=1, source_target_pairs={{0,16},{16,0},{1,17},{17,1},{2,18},{18,2},{3,19},{19,3},{4,20},{20... | collective-permute-start | bytes 3145736 | tf_op jit(solution)/shard_map/ppermute | solution.py:630
  80.3 0.1 fusion.4
  80.3 0.1 dynamic_slice.23
  80.4 0.1 fusion.6
  80.5 0.1 pad_maximum_fusion.1
  80.6 0.1 broadcast_multiply_fusion
  80.6 18.4 %all-to-all-done.1 = bf16[16,256,128]{2,1,0:T(8,128)(2,1)S(1)} async-done(((bf16[16,256,128]{2,1,0:T(8,128)(2,1)}), bf16[16,256,128]{2,1,0:T(8,128)(2,1)S(1)}, u32[]{:S(2)}, u32[]{:S(2)}) %all-to-all-start.1) | async-done | bytes 1048608 | tf_op jit(solution)/shard_map/all_to_all | solution.py:624
  99.0 6.1 %to_sigma.2.rest_0_ = bf16[4096,128]{1,0:T(8,128)(2,1)S(1)} custom-call(s32[1]{0:T(128)} %bitcast.1.which_ref, bf16[4096,128]{1,0:T(8,128)(2,1)S(1)} %bitcast.19, bf16[2,1024,512]{2,1,0:T(8,128)(2,1)S(1)} %to_sites.1.rest_0_.sites, bf16[1024,1024]{1,0:T(8,128)(2,1)} %copy-done, bf16[1024,1024]{1,0:T(8,128)(2,1)} %copy-done.3, ...), custom_call_target="tpu_custom_call" | custom-call | tf_op jit(solution)/shard_map/to_sigma/pallas_call | solution.py:454
  105.1 0.0 copy-start.10
  105.1 1.0 copy-done.10
  106.0 3.7 %all-to-all-start.2 = ((bf16[16,256,128]{2,1,0:T(8,128)(2,1)}), bf16[16,256,128]{2,1,0:T(8,128)(2,1)S(1)}, u32[]{:S(2)}, u32[]{:S(2)}) async-start(bf16[16,256,128]{2,1,0:T(8,128)(2,1)} %bitcast.22), calls=%async_computation.2 | async-start | bytes 2097152 | tf_op jit(solution)/shard_map/all_to_all | solution.py:624
  109.7 16.5 %collective-permute-done.1.source.far_near = bf16[8,512,128]{2,1,0:T(8,128)(2,1)} collective-permute-done((bf16[8,512,128]{2,1,0:T(8,128)(2,1)}, bf16[8,512,128]{2,1,0:T(8,128)(2,1)}, u32[]{:S(2)}, u32[]{:S(2)}) %collective-permute-start.1) | collective-permute-done | bytes 1048608 | tf_op jit(solution)/shard_map/ppermute | solution.py:630
  126.2 0.0 copy-start.11
  126.2 1.2 copy-done.11
  127.4 1.6 to_crossed.3.refs_0_
  129.1 0.0 copy-start.12
  129.1 1.0 copy-done.12
  130.1 8.9 %all-to-all-done.2.refs_1_.diagonal = bf16[16,256,128]{2,1,0:T(8,128)(2,1)S(1)} async-done(((bf16[16,256,128]{2,1,0:T(8,128)(2,1)}), bf16[16,256,128]{2,1,0:T(8,128)(2,1)S(1)}, u32[]{:S(2)}, u32[]{:S(2)}) %all-to-all-start.2) | async-done | bytes 1048608 | tf_op jit(solution)/shard_map/all_to_all | solution.py:624
  139.1 1.0 copy-done.1
  140.0 3.7 %all-to-all-start.3 = ((bf16[16,256,128]{2,1,0:T(8,128)(2,1)}), bf16[16,256,128]{2,1,0:T(8,128)(2,1)S(1)}, u32[]{:S(2)}, u32[]{:S(2)}) async-start(bf16[16,256,128]{2,1,0:T(8,128)(2,1)} %gate.1), calls=%async_computation.3 | async-start | bytes 2097152 | tf_op jit(solution)/shard_map/all_to_all | solution.py:624
  143.7 0.1 collective-permute-start.2
  143.8 25.1 %all-to-all-done.3 = bf16[16,256,128]{2,1,0:T(8,128)(2,1)S(1)} async-done(((bf16[16,256,128]{2,1,0:T(8,128)(2,1)}), bf16[16,256,128]{2,1,0:T(8,128)(2,1)S(1)}, u32[]{:S(2)}, u32[]{:S(2)}) %all-to-all-start.3) | async-done | bytes 1048608 | tf_op jit(solution)/shard_map/all_to_all | solution.py:624
  168.9 6.1 %to_sigma.3 = bf16[4096,128]{1,0:T(8,128)(2,1)S(1)} custom-call(s32[1]{0:T(128)} %bitcast.11.which_ref, bf16[4096,128]{1,0:T(8,128)(2,1)S(1)} %bitcast.20, bf16[2,1024,512]{2,1,0:T(8,128)(2,1)S(1)} %to_sites.1.rest_0_.sites, bf16[1024,1024]{1,0:T(8,128)(2,1)} %copy-done, bf16[1024,1024]{1,0:T(8,128)(2,1)} %copy-done.3, f32[4,128]{1,0:T(4,128)S(1)} %get-tuple-element.8.coupling), custom_call_target="tpu_custom_call" | custom-call | tf_op jit(solution)/shard_map/to_sigma/pallas_call | solution.py:454
  174.9 0.0 copy-start.9
  174.9 1.0 copy-done.9
  175.9 3.7 %all-to-all-start.4 = ((bf16[16,256,128]{2,1,0:T(8,128)(2,1)}), bf16[16,256,128]{2,1,0:T(8,128)(2,1)S(1)}, u32[]{:S(2)}, u32[]{:S(2)}) async-start(bf16[16,256,128]{2,1,0:T(8,128)(2,1)} %bitcast.21), calls=%async_computation.4 | async-start | bytes 2097152 | tf_op jit(solution)/shard_map/all_to_all | solution.py:624
  179.6 13.3 %collective-permute-done.2.far_away = bf16[8,512,128]{2,1,0:T(8,128)(2,1)} collective-permute-done((bf16[8,512,128]{2,1,0:T(8,128)(2,1)}, bf16[8,512,128]{2,1,0:T(8,128)(2,1)}, u32[]{:S(2)}, u32[]{:S(2)}) %collective-permute-start.2) | collective-permute-done | bytes 1048608 | tf_op jit(solution)/shard_map/ppermute | solution.py:630
  192.9 11.0 %make_rights.1.rights = bf16[32,384,256]{2,1,0:T(8,128)(2,1)} custom-call(s32[1]{0:T(128)} %bitcast.half_ref, bf16[16,512,128]{2,1,0:T(8,128)(2,1)} %all-to-all-done.source.own, bf16[8,512,128]{2,1,0:T(8,128)(2,1)} %collective-permute-done.1.source.far_near, bf16[8,512,128]{2,1,0:T(8,128)(2,1)} %collective-permute-done.2.far_away), custom_call_target="tpu_custom_call" | custom-call | flops 99999997952 | bytes 1048576 | tf_op jit(solution)/shard_map/make_rights/pallas_call | solution.py:512
  203.9 2.1 all-to-all-done.4.cross
  206.0 0.0 copy-done.2
  206.0 11.8 %volterra.1 = bf16[16,512,128]{2,1,0:T(8,128)(2,1)S(1)} custom-call(s32[1]{0:T(128)} %bitcast.half_ref, bf16[16,256,128]{2,1,0:T(8,128)(2,1)S(1)} %copy-done.2, bf16[16,256,128]{2,1,0:T(8,128)(2,1)S(1)} %all-to-all-done.4.cross, bf16[32,384,256]{2,1,0:T(8,128)(2,1)} %make_rights.1.rights), custom_call_target="tpu_custom_call" | custom-call | tf_op jit(solution)/shard_map/volterra/pallas_call | solution.py:597
  217.8 30.0 %all_to_all.30 = bf16[16,512,128]{2,1,0:T(8,128)(2,1)S(1)} all-to-all(bf16[16,512,128]{2,1,0:T(8,128)(2,1)S(1)} %volterra.1), channel_id=1, replica_groups=mesh['half'=2,'line'=8,'tcol'=2] {'tcol','line'}, dimensions={0} | all-to-all | bytes 4194304 | tf_op jit(solution)/shard_map/all_to_all | solution.py:624
  247.9 3.5 %collect.1 = (bf16[2,8,64,512]{3,2,1,0:T(8,128)(2,1)}, bf16[2,8,64,512]{3,2,1,0:T(8,128)(2,1)}) custom-call(bf16[8192,128]{1,0:T(8,128)(2,1)S(1)} %bitcast.18), custom_call_target="tpu_custom_call" | custom-call | tf_op jit(solution)/shard_map/collect/pallas_call | solution.py:282
  (3 shorter events, 0.0 us)
Async XLA Ops:
  0.6 1.2 copy-start.4
  1.9 1.2 copy-start.6
  6.9 6.5 %copy-start.5 = (bf16[2,8,64,512]{3,2,1,0:T(8,128)(2,1)S(1)}, bf16[2,8,64,512]{3,2,1,0:T(8,128)(2,1)}, u32[]{:S(2)}) copy-start(bf16[2,8,64,512]{3,2,1,0:T(8,128)(2,1)} %lesser.3) | copy-start | bytes 3145732
  6.9 6.5 %copy-start.7 = (bf16[2,8,64,512]{3,2,1,0:T(8,128)(2,1)S(1)}, bf16[2,8,64,512]{3,2,1,0:T(8,128)(2,1)}, u32[]{:S(2)}) copy-start(bf16[2,8,64,512]{3,2,1,0:T(8,128)(2,1)} %greater.3) | copy-start | bytes 3145732
  6.9 60.1 %all-to-all-start = ((bf16[16,512,128]{2,1,0:T(8,128)(2,1)}), bf16[16,512,128]{2,1,0:T(8,128)(2,1)}, u32[]{:S(2)}, u32[]{:S(2)}) async-start(bf16[16,512,128]{2,1,0:T(8,128)(2,1)} %bitcast.3), calls=%async_computation | async-start | bytes 4194304 | tf_op jit(solution)/shard_map/all_to_all | solution.py:624
  13.4 3.0 %copy-start.14 = (s32[512]{0:T(512)S(1)}, s32[512]{0:T(512)}, u32[]{:S(2)}) copy-start(s32[512]{0:T(512)} %param.6) | copy-start | bytes 6148
  14.6 46.9 %collective-permute-start = (bf16[2,2,4,64,512]{4,3,2,1,0:T(8,128)(2,1)}, bf16[2,2,4,64,512]{4,3,2,1,0:T(8,128)(2,1)}, u32[]{:S(2)}, u32[]{:S(2)}) collective-permute-start(bf16[2,2,4,64,512]{4,3,2,1,0:T(8,128)(2,1)} %pad_maximum_fusion), channel_id=1, source_target_pairs={{0,1},{1,0},{2,3},{3,2},{4,5},{5,4},{6,7},{7,6},{8,9},{9,8},{10,11... | collective-permute-start | bytes 3145736 | tf_op jit(solution)/shard_map/ppermute | solution.py:635
  21.2 1.4 copy-start
  22.5 1.3 copy-start.3
  61.5 1.2 copy-start.8
  69.1 1.0 copy-start.13
  70.0 29.0 %all-to-all-start.1 = ((bf16[16,256,128]{2,1,0:T(8,128)(2,1)}), bf16[16,256,128]{2,1,0:T(8,128)(2,1)S(1)}, u32[]{:S(2)}, u32[]{:S(2)}) async-start(bf16[16,256,128]{2,1,0:T(8,128)(2,1)} %copy-done.13), calls=%async_computation.1 | async-start | bytes 2097152 | tf_op jit(solution)/shard_map/all_to_all | solution.py:624
  77.0 49.2 %collective-permute-start.1 = (bf16[8,512,128]{2,1,0:T(8,128)(2,1)}, bf16[8,512,128]{2,1,0:T(8,128)(2,1)}, u32[]{:S(2)}, u32[]{:S(2)}) collective-permute-start(bf16[8,512,128]{2,1,0:T(8,128)(2,1)} %get-tuple-element.7), channel_id=1, source_target_pairs={{0,16},{16,0},{1,17},{17,1},{2,18},{18,2},{3,19},{19,3},{4,20},{20... | collective-permute-start | bytes 3145736 | tf_op jit(solution)/shard_map/ppermute | solution.py:630
  105.1 1.0 copy-start.10
  106.0 33.0 %all-to-all-start.2 = ((bf16[16,256,128]{2,1,0:T(8,128)(2,1)}), bf16[16,256,128]{2,1,0:T(8,128)(2,1)S(1)}, u32[]{:S(2)}, u32[]{:S(2)}) async-start(bf16[16,256,128]{2,1,0:T(8,128)(2,1)} %bitcast.22), calls=%async_computation.2 | async-start | bytes 2097152 | tf_op jit(solution)/shard_map/all_to_all | solution.py:624
  126.2 1.2 copy-start.11
  129.1 1.0 copy-start.12
  139.1 1.0 copy-start.1
  140.0 28.9 %all-to-all-start.3 = ((bf16[16,256,128]{2,1,0:T(8,128)(2,1)}), bf16[16,256,128]{2,1,0:T(8,128)(2,1)S(1)}, u32[]{:S(2)}, u32[]{:S(2)}) async-start(bf16[16,256,128]{2,1,0:T(8,128)(2,1)} %gate.1), calls=%async_computation.3 | async-start | bytes 2097152 | tf_op jit(solution)/shard_map/all_to_all | solution.py:624
  143.7 49.2 %collective-permute-start.2 = (bf16[8,512,128]{2,1,0:T(8,128)(2,1)}, bf16[8,512,128]{2,1,0:T(8,128)(2,1)}, u32[]{:S(2)}, u32[]{:S(2)}) collective-permute-start(bf16[8,512,128]{2,1,0:T(8,128)(2,1)} %get-tuple-element.6), channel_id=1, source_target_pairs={{0,16},{16,0},{1,17},{17,1},{2,18},{18,2},{3,19},{19,3},{4,20},{20... | collective-permute-start | bytes 3145736 | tf_op jit(solution)/shard_map/ppermute | solution.py:630
  174.9 1.0 copy-start.9
  175.9 30.1 %all-to-all-start.4 = ((bf16[16,256,128]{2,1,0:T(8,128)(2,1)}), bf16[16,256,128]{2,1,0:T(8,128)(2,1)S(1)}, u32[]{:S(2)}, u32[]{:S(2)}) async-start(bf16[16,256,128]{2,1,0:T(8,128)(2,1)} %bitcast.21), calls=%async_computation.4 | async-start | bytes 2097152 | tf_op jit(solution)/shard_map/all_to_all | solution.py:624
  192.9 13.1 %copy-start.2 = (bf16[16,256,128]{2,1,0:T(8,128)(2,1)S(1)}, bf16[16,256,128]{2,1,0:T(8,128)(2,1)}, u32[]{:S(2)}) copy-start(bf16[16,256,128]{2,1,0:T(8,128)(2,1)} %copy-done.1) | copy-start | bytes 3145732

commit v5 on v4

--- a/solution.py
+++ b/solution.py
@@ -244,25 +244,35 @@
     return [pl.BlockSpec(memory_space=pltpu.SMEM)]
 
 
-def spread_kernel(lesser, greater, out, lines):
-    _, rows, _, momenta = lesser.shape
-    for g, tile in enumerate((lesser, greater)):
-        for t in range(rows):
-            slab = jnp.concatenate([tile[0, t], tile[1, t]], axis=0)
-            lines[pl.ds(g * rows + t, momenta, stride=2 * rows), :] = slab.astype(F32).T
-    out[...] = lines[...].astype(BF16)
-
-
-def spread(tiles):
+def spread_kernel(*refs):
+    *tiles, out, lines = refs
+    _, rows, _, momenta = tiles[0].shape
+    blocks, height, _ = out.shape
+    height = height // len(tiles)
+    wide = momenta // 2
+    for g, tile in enumerate(tiles):
+        for first in range(0, momenta, wide):
+            for t in range(rows):
+                span = slice(first, first + wide)
+                slab = jnp.concatenate([tile[0, t, :, span], tile[1, t, :, span]], axis=0)
+                lines[pl.ds(first * rows + t, wide, stride=rows), :] = slab.astype(F32).T
+        for block in range(blocks):
+            out[block, g * height : (g + 1) * height] = lines[
+                block * height : (block + 1) * height
+            ].astype(BF16)
+
+
+def spread(tiles, blocks, cost):
     _, rows, cols, momenta = tiles[0].shape
-    shape = (momenta * 2 * rows, 2 * cols)
+    lines = momenta * rows
     return pl.pallas_call(
         spread_kernel,
-        out_shape=jax.ShapeDtypeStruct(shape, BF16),
-        in_specs=whole(2),
+        out_shape=jax.ShapeDtypeStruct((blocks, len(tiles) * lines // blocks, 2 * cols), BF16),
+        in_specs=whole(len(tiles)),
         out_specs=whole(1)[0],
-        scratch_shapes=[pltpu.VMEM(shape, F32)],
-        compiler_params=vmem_params(),
+        scratch_shapes=[pltpu.VMEM((lines, 2 * cols), F32)],
+        compiler_params=vmem_params(),
+        cost_estimate=cost,
         name="spread",
     )(*tiles)
 
@@ -321,80 +331,75 @@
     )(lattice_map[:, None])
 
 
-def site_kernel(norm_factor, first_ref, lesser, greater, got, table, out):
-    first = first_ref[0]
-    _, _, count, cols, _ = got.shape
+def site_kernel(norm_factor, lesser, greater, table, out):
+    _, rows, cols, _ = lesser.shape
     wide = 4 * cols
-    for which in range(2):
-        for pair in range(count // 2):
-            slabs = []
-            for t in (2 * pair, 2 * pair + 1):
-                for g, tile in enumerate((lesser, greater)):
-                    if which == 0:
-                        parts = [tile[c, first + t] for c in range(2)]
-                    else:
-                        parts = [got[g, c, t] for c in range(2)]
-                    slabs.append(jnp.concatenate(parts, axis=1))
-            product = lax.dot_general(
-                table[...],
-                jnp.concatenate(slabs, axis=0),
-                (((1,), (1,)), ((), ())),
-                preferred_element_type=F32,
-            )
-            out[which, :, pair * wide : (pair + 1) * wide] = (product * norm_factor).astype(BF16)
-
-
-def to_sites(first, tiles, got, table, norm_factor):
-    _, _, count, cols, momenta = got.shape
+    for pair in range(rows // 2):
+        slabs = [
+            jnp.concatenate([tile[0, t], tile[1, t]], axis=1)
+            for t in (2 * pair, 2 * pair + 1)
+            for tile in (lesser, greater)
+        ]
+        product = lax.dot_general(
+            table[...],
+            jnp.concatenate(slabs, axis=0),
+            (((1,), (1,)), ((), ())),
+            preferred_element_type=F32,
+        )
+        out[:, pair * wide : (pair + 1) * wide] = (product * norm_factor).astype(BF16)
+
+
+def to_sites(tiles, table, norm_factor):
+    _, rows, cols, momenta = tiles[0].shape
     return pl.pallas_call(
         functools.partial(site_kernel, norm_factor),
-        out_shape=jax.ShapeDtypeStruct((2, 2 * momenta, count * 2 * cols), BF16),
-        in_specs=scalars() + whole(4),
+        out_shape=jax.ShapeDtypeStruct((2 * momenta, rows * 2 * cols), BF16),
+        in_specs=whole(3),
         out_specs=whole(1)[0],
         compiler_params=vmem_params(),
         name="to_sites",
-    )(first, *tiles, got, table)
-
-
-def cross_kernel(rows, blocks, first_ref, source, *rest):
+    )(*tiles, table)
+
+
+def cross_kernel(rows, half_ref, own, far_l, near_g, *rest):
     out = rest[-1]
-    first = first_ref[0]
+    half = half_ref[0]
+    blocks = near_g.shape[0]
     cols = blocks * rows
-    count = rows // 2
-    for pair in range(source.shape[1] // (4 * rows)):
-        turned = []
-        for at in (2 * pair, 2 * pair + 1):
-            span = slice(at * 2 * rows, (at + 1) * 2 * rows)
-            loaded = [source[first + block, span].astype(F32) for block in range(blocks)]
-            stacked = jnp.concatenate(
-                [lines[rows:] for lines in loaded] + [lines[:rows] for lines in loaded], axis=0
-            )
-            turned.append(stacked.T)
-        span = slice(pair * 2 * rows, (pair + 1) * 2 * rows)
-        for side in range(2):
-            for block in range(blocks):
-                start = block * rows + side * count
-                out[side * blocks + block, span] = jnp.concatenate(
-                    [
-                        lines[c * cols + start : c * cols + start + count]
-                        for lines in turned
-                        for c in range(2)
-                    ],
-                    axis=0,
-                ).astype(BF16)
-
-
-def to_crossed(first, source, rows, blocks, after, cost):
-    shape = (2 * blocks, source.shape[1] // 2, source.shape[2])
-    return pl.pallas_call(
-        functools.partial(cross_kernel, rows, blocks),
-        out_shape=jax.ShapeDtypeStruct(shape, BF16),
-        in_specs=scalars() + whole(1) + unread(after),
+    height = near_g.shape[1]
+    here = half * blocks
+    for pair in range(height // (2 * rows)):
+        low = slice(pair * 2 * rows, (pair + 1) * 2 * rows)
+        high = slice(height + pair * 2 * rows, height + (pair + 1) * 2 * rows)
+        for lesser, greater, target in (
+            ([own[here + b, low] for b in range(blocks)], [own[here + b, high] for b in range(blocks)], half),
+            ([far_l[here + b, low] for b in range(blocks)], [near_g[b, low] for b in range(blocks)], 1 - half),
+        ):
+            loaded = [lines.astype(F32) for lines in greater + lesser]
+            for at in range(2):
+                turned = jnp.concatenate(
+                    [lines[at * rows : (at + 1) * rows] for lines in loaded], axis=0
+                ).T
+                start = (2 * pair + at) * 2 * rows
+                for block in range(blocks):
+                    out[target * blocks + block, start : start + 2 * rows] = jnp.concatenate(
+                        [
+                            turned[block * rows : (block + 1) * rows],
+                            turned[cols + block * rows : cols + (block + 1) * rows],
+                        ],
+                        axis=0,
+                    ).astype(BF16)
+
+
+def to_crossed(half, own, far_l, near_g, rows, after):
+    return pl.pallas_call(
+        functools.partial(cross_kernel, rows),
+        out_shape=jax.ShapeDtypeStruct(own.shape, BF16),
+        in_specs=scalars() + whole(3) + unread(after),
         out_specs=whole(1)[0],
         compiler_params=vmem_params(),
-        cost_estimate=cost,
         name="to_crossed",
-    )(first, source, *after)
+    )(half, own, far_l, near_g, *after)
 
 
 def gate_kernel(*refs):
@@ -412,9 +417,7 @@
     )(array, *after)
 
 
-def sigma_kernel(norm_factor, which_ref, crossed, sites, table, inverse, coupling, *rest):
-    out, read, written = rest[-3:]
-    which = which_ref[0]
+def sigma_kernel(norm_factor, crossed, sites, table, inverse, coupling, out, read, written):
     count = coupling.shape[0]
     momenta = table.shape[0] // 2
     read[...] = crossed[...].astype(F32)
@@ -430,8 +433,8 @@
         other = (other * norm_factor).astype(BF16).astype(F32)
         span = slice(2 * pair * LANES, 2 * (pair + 1) * LANES)
         self_real, self_imaginary = second_born(
-            sites[which, :momenta, span].astype(F32),
-            sites[which, momenta:, span].astype(F32),
+            sites[:momenta, span].astype(F32),
+            sites[momenta:, span].astype(F32),
             other[:momenta],
             -other[momenta:],
             jnp.concatenate([coupling[t : t + 1] for t in (2 * pair, 2 * pair + 1)], axis=1),
@@ -450,22 +453,22 @@
     out[...] = written[...].astype(BF16)
 
 
-def to_sigma(which, crossed, sites, table, inverse, coupling, norm_factor, after):
+def to_sigma(crossed, sites, table, inverse, coupling, norm_factor):
     return pl.pallas_call(
         functools.partial(sigma_kernel, norm_factor),
         out_shape=jax.ShapeDtypeStruct(crossed.shape, BF16),
-        in_specs=scalars() + whole(5) + unread(after),
+        in_specs=whole(5),
         out_specs=whole(1)[0],
         scratch_shapes=[pltpu.VMEM(crossed.shape, F32)] * 2,
         compiler_params=vmem_params(),
         name="to_sigma",
-    )(which, crossed, sites, table, inverse, coupling, *after)
-
-
-def rights_kernel(rows, half_ref, own, far_near, far_away, out):
+    )(crossed, sites, table, inverse, coupling)
+
+
+def rights_kernel(rows, half_ref, own_l, own_g, far_l, near_g, away_g, out):
     half = half_ref[0]
-    blocks = far_near.shape[0]
-    lanes = own.shape[2]
+    blocks = near_g.shape[0]
+    lanes = own_l.shape[2]
     cols = lanes // 2
     near = half * cols
     away = (1 - half) * cols
@@ -474,87 +477,83 @@
     lane_at = lax.broadcasted_iota(jnp.int32, (lanes, 2 * lanes), 1)
     last_times = jnp.where(lane_at < lanes, near, away) + lane_at % cols
     keep = inner_times <= last_times
-    for at in range(out.shape[0]):
-        span = slice(at * 2 * rows, (at + 1) * 2 * rows)
+    here = half * blocks
+    there = (1 - half) * blocks
+    for pair in range(out.shape[0] // 2):
+        span = slice(pair * 2 * rows, (pair + 1) * 2 * rows)
 
         def stacked(ref, offset):
             loaded = [ref[offset + block, span].astype(F32) for block in range(blocks)]
             return [
-                jnp.concatenate([lines[part * rows : (part + 1) * rows] for lines in loaded], axis=0)
-                for part in range(2)
+                jnp.concatenate([lines[at * rows : (at + 1) * rows] for lines in loaded], axis=0)
+                for at in range(2)
             ]
 
-        own_near = stacked(own, half * blocks)
-        own_away = stacked(own, (1 - half) * blocks)
-        cross_near = stacked(far_near, 0)
-        cross_away = stacked(far_away, 0)
-        greens = [
-            jnp.concatenate(
-                [
-                    jnp.concatenate([own_near[g], own_away[g]], axis=1),
-                    jnp.concatenate([cross_near[g], cross_away[g]], axis=1),
-                ],
-                axis=0,
-            )
-            for g in range(2)
+        parts = [
+            [[stacked(own_l, here), stacked(own_l, there)], [stacked(far_l, here), stacked(far_l, there)]],
+            [[stacked(own_g, here), stacked(own_g, there)], [stacked(near_g, 0), stacked(away_g, 0)]],
         ]
-        out[at, :lanes] = greens[0].astype(BF16)
-        out[at, lanes : 2 * lanes] = greens[1].astype(BF16)
-        out[at, 2 * lanes :] = jnp.where(keep, greens[0] - greens[1], 0.0).astype(BF16)
-
-
-def make_rights(half, own, far_near, far_away, rows):
-    sources, lines, lanes = own.shape
-    blocks = far_near.shape[0]
-    step = 4 * rows
-    spec = pl.BlockSpec((sources, step, lanes), lambda p: (0, p, 0))
-    far_spec = pl.BlockSpec((blocks, step, lanes), lambda p: (0, p, 0))
+        for at in range(2):
+            greens = [
+                jnp.concatenate(
+                    [jnp.concatenate([side[at] for side in line], axis=1) for line in part], axis=0
+                )
+                for part in parts
+            ]
+            out[2 * pair + at, :lanes] = greens[0].astype(BF16)
+            out[2 * pair + at, lanes : 2 * lanes] = greens[1].astype(BF16)
+            out[2 * pair + at, 2 * lanes :] = jnp.where(keep, greens[0] - greens[1], 0.0).astype(BF16)
+
+
+STEPS = 4
+
+
+def make_rights(half, own, far_l, near_g, away_g, rows):
+    sources, lines, lanes = far_l.shape
+    blocks = near_g.shape[0]
+    step = lines // STEPS
+    momenta = step // rows
+    lesser = pl.BlockSpec((sources, step, lanes), lambda p: (0, p, 0))
+    greater = pl.BlockSpec((sources, step, lanes), lambda p: (0, STEPS + p, 0))
+    half_spec = pl.BlockSpec((blocks, step, lanes), lambda p: (0, p, 0))
     return pl.pallas_call(
         functools.partial(rights_kernel, rows),
-        grid=(lines // step,),
-        out_shape=jax.ShapeDtypeStruct((lines // (2 * rows), 3 * lanes, 2 * lanes), BF16),
-        in_specs=scalars() + [spec, far_spec, far_spec],
-        out_specs=pl.BlockSpec((2, 3 * lanes, 2 * lanes), lambda p: (p, 0, 0)),
+        grid=(STEPS,),
+        out_shape=jax.ShapeDtypeStruct((lines // rows, 3 * lanes, 2 * lanes), BF16),
+        in_specs=scalars() + [lesser, greater, lesser, half_spec, half_spec],
+        out_specs=pl.BlockSpec((momenta, 3 * lanes, 2 * lanes), lambda p: (p, 0, 0)),
         compiler_params=vmem_params(),
         cost_estimate=weight(),
         name="make_rights",
-    )(half, own, far_near, far_away)
-
-
-def volterra_kernel(rows, half_ref, diagonal, cross, rights, out):
+    )(half, own, own, far_l, near_g, away_g)
+
+
+def volterra_kernel(rows, half_ref, sigma, rights, out):
     half = half_ref[0]
-    blocks = diagonal.shape[0] // 2
-    lanes = diagonal.shape[2]
+    blocks = sigma.shape[0] // 2
+    lanes = sigma.shape[2]
     cols = lanes // 2
-    count = rows // 2
     near = half * cols
     away = (1 - half) * cols
+    here = half * blocks
+    there = (1 - half) * blocks
     first_times = near + lax.broadcasted_iota(jnp.int32, (cols, lanes), 0)
     left_lane = lax.broadcasted_iota(jnp.int32, (cols, lanes), 1)
     low_lanes = left_lane < cols
     left_times = jnp.where(low_lanes, near + left_lane, away + left_lane - cols)
     keep_left = left_times <= first_times
-    pairs = []
-    for at in range(2):
-        piece = slice(at * rows, (at + 1) * rows)
-
-        def stacked(ref):
-            low = [ref[block].astype(F32)[piece] for block in range(blocks)]
-            high = [ref[blocks + block].astype(F32)[piece] for block in range(blocks)]
+    for at in range(rights.shape[0]):
+        span = slice(at * 2 * rows, (at + 1) * 2 * rows)
+
+        def stacked(offset):
+            loaded = [sigma[offset + block, span].astype(F32) for block in range(blocks)]
             return [
-                jnp.concatenate(
-                    [
-                        lines[block][part * count : (part + 1) * count]
-                        for block in range(blocks)
-                        for lines in (low, high)
-                    ],
-                    axis=0,
-                )
+                jnp.concatenate([lines[part * rows : (part + 1) * rows] for lines in loaded], axis=0)
                 for part in range(2)
             ]
 
-        sigma_near = stacked(diagonal)
-        sigma_away = stacked(cross)
+        sigma_near = stacked(here)
+        sigma_away = stacked(there)
         retarded = []
         lefts = [[], []]
         for part in range(2):
@@ -585,25 +584,27 @@
             results.append(sides)
         for block in range(blocks):
             lines = slice(block * rows, (block + 1) * rows)
-            for side, offset in enumerate((half * blocks, (1 - half) * blocks)):
-                out[offset + block, at * 2 * rows : (at + 1) * 2 * rows] = jnp.concatenate(
+            for side, offset in enumerate((here, there)):
+                out[offset + block, span] = jnp.concatenate(
                     [results[0][side][lines], results[1][side][lines]], axis=0
                 ).astype(BF16)
 
 
-def volterra(half, diagonal, cross, rights, rows):
-    sources, lines, lanes = diagonal.shape
-    spec = pl.BlockSpec((sources, 2 * rows, lanes), lambda p: (0, p, 0))
+def volterra(half, sigma, rights, rows):
+    sources, lines, lanes = sigma.shape
+    step = lines // STEPS
+    momenta = step // (2 * rows)
+    spec = pl.BlockSpec((sources, step, lanes), lambda p: (0, p, 0))
     return pl.pallas_call(
         functools.partial(volterra_kernel, rows),
-        grid=(lines // (2 * rows),),
-        out_shape=jax.ShapeDtypeStruct((sources, 2 * lines, lanes), BF16),
+        grid=(STEPS,),
+        out_shape=jax.ShapeDtypeStruct(sigma.shape, BF16),
         in_specs=scalars()
-        + [spec, spec, pl.BlockSpec((2, 3 * lanes, 2 * lanes), lambda p: (p, 0, 0))],
-        out_specs=pl.BlockSpec((sources, 4 * rows, lanes), lambda p: (0, p, 0)),
+        + [spec, pl.BlockSpec((momenta, 3 * lanes, 2 * lanes), lambda p: (p, 0, 0))],
+        out_specs=spec,
         compiler_params=vmem_params(),
         name="volterra",
-    )(half, diagonal, cross, rights)
+    )(half, sigma, rights)
 
 
 def halved_body(green_lesser, green_greater, lattice_map, time_offset):
@@ -616,63 +617,44 @@
     window = rows * lines * lax.axis_size("half")
     norm_factor = 1.0 / math.sqrt(momenta)
     tiles = (green_lesser, green_greater)
-    count = rows // 2
     half_at = half[None]
-    trade = [(0, 1), (1, 0)]
+    height = momenta * rows // group
 
     def exchange(blocks):
         return lax.all_to_all(blocks, ("tcol", "line"), 0, 0, tiled=True)
 
-    def blocked(rows_array):
-        return rows_array.reshape(group, rows_array.shape[0] // group, rows_array.shape[1])
-
-    def swap(blocks, at):
-        return lax.ppermute(lax.dynamic_slice_in_dim(blocks, at * lines, lines), "half", trade)
-
-    given = jnp.stack(
-        [lax.dynamic_slice_in_dim(tile, (1 - side) * count, count, 1) for tile in tiles]
-    )
-    got = lax.ppermute(given, "tcol", trade)
-    own = exchange(blocked(spread(tiles)))
-    far_near = swap(own, 1 - half)
-    far_away = swap(own, half)
+    def swap(array):
+        return lax.ppermute(array, "half", [(0, 1), (1, 0)])
+
+    def greater_blocks(at):
+        zero = jnp.zeros((), jnp.int32)
+        return lax.dynamic_slice(
+            own, (at * lines, zero + height, zero), (lines, height, 2 * cols)
+        )
+
+    far_tile = swap(green_lesser)
+    own = exchange(spread(tiles, group, None))
+    far_l = exchange(gate(spread([far_tile], group, weight()), [own]))
+    near_g = swap(greater_blocks(1 - half))
+    away_g = swap(greater_blocks(half))
 
     table, inverse = make_tables(lattice_map)
-    kept = side * count
-    sites = to_sites(kept[None], tiles, got, table, norm_factor)
+    sites = to_sites(tiles, table, norm_factor)
     time_steps = jnp.arange(window, dtype=jnp.int32)
     coupling_line = 1.0 + drive_depth * jnp.cos(
         ((time_offset[0] + time_steps) % PERIOD).astype(F32) * (2.0 * math.pi / PERIOD)
     )
-    first = lax.dynamic_slice_in_dim(coupling_line, (half * lines + line) * rows + kept, count)
-
-    def phase_sigma(crossed, at, after):
-        second = lax.dynamic_slice_in_dim(coupling_line, at * cols, cols)
-        coupling = first[:, None] * jnp.concatenate([second, second])[None, :]
-        which = (side != at).astype(jnp.int32)[None]
-        return to_sigma(
-            which,
-            crossed.reshape(-1, 2 * cols),
-            sites,
-            table,
-            inverse,
-            coupling,
-            norm_factor,
-            after,
-        )
-
-    crossed = exchange(
-        to_crossed((half * lines)[None], own, rows, lines, [sites], None)
-    )
-    sigma_rows = phase_sigma(crossed, half, [])
-    diagonal = exchange(blocked(sigma_rows))
-    sent = to_crossed(
-        jnp.zeros((1,), jnp.int32), far_near, rows, lines, [sigma_rows], weight()
-    )
-    crossed = exchange(gate(sent, [diagonal]))
-    cross = exchange(blocked(phase_sigma(crossed, 1 - half, [])))
-    rights = make_rights(half_at, own, far_near, far_away, rows)
-    collisions = volterra(half_at, diagonal, cross, rights, rows)
+    first = lax.dynamic_slice_in_dim(coupling_line, (half * lines + line) * rows, rows)
+    second = lax.dynamic_slice_in_dim(coupling_line, side * cols, cols)
+    coupling = first[:, None] * jnp.concatenate([second, second])[None, :]
+
+    crossed = exchange(to_crossed(half_at, own, far_l, near_g, rows, [sites]))
+    sigma_rows = to_sigma(
+        crossed.reshape(-1, 2 * cols), sites, table, inverse, coupling, norm_factor
+    )
+    sigma = exchange(sigma_rows.reshape(crossed.shape))
+    rights = make_rights(half_at, own, far_l, near_g, away_g, rows)
+    collisions = volterra(half_at, sigma, rights, rows)
     returned = exchange(collisions)
     return collect(returned.reshape(-1, 2 * cols), green_lesser.shape)
 
@@ -692,7 +674,8 @@
             and 2 * cols == LANES
             and cols == rows * (row_parts // 2)
             and rows % 8 == 0
-            and momenta % (2 * row_parts) == 0 and momenta % LANES == 0
+            and momenta % (2 * row_parts * STEPS) == 0
+            and momenta % LANES == 0
         )
         if halved:
             devices = mesh.devices.reshape(2, row_parts // 2, col_parts)

time: 253 us -> 229 us (0.905)
  Pallas kernels: 54.7 us -> 37.8 us
  starting transfers between devices: 25.8 us -> 22.5 us
    ppermute x3, waiting for transfers between devices: 67.5 us -> 47.9 us  [swap(): return lax.ppermute(array, 'half', [(0, 1), (1, 0)])]
    all_to_all x5 -> x4, waiting for transfers between devices: 54.5 us -> 72.1 us  [exchange(): return lax.all_to_all(blocks, ('tcol', 'line'), 0, 0, tiled=True)]
    pallas_call x5, Pallas kernels: 30.3 us -> 14.9 us  [the longest x1 5.26 us: volterra(): pl.pallas_call(functools.partial(volterra_kernel, rows), grid=(STEPS,), o...]
    all_to_all x5 -> x4, starting transfers between devices: 21.3 us -> 17.7 us  [exchange(): return lax.all_to_all(blocks, ('tcol', 'line'), 0, 0, tiled=True)]
    unnamed x30 -> x28, local copies, waits for them, and re-layouts: 12.5 us -> 15.3 us
    pallas_call x2 -> x1, Pallas kernels: 12.1 us -> 10.9 us  [to_sigma(): pl.pallas_call(functools.partial(sigma_kernel, norm_factor), out_shape=ja...]
  transfers between devices with their start and end apart: 8 -> 7, of which waited for: 7 -> 5; matrix products, arithmetic and copies ran while one was open for 2% -> 1% of each run, Pallas kernels for 13% -> 12%
where the time goes in v5:
time: 229 us
  waiting for transfers between devices  120 us (52%)
  Pallas kernels  37.8 us (17%)
  blocking collectives  30 us (13%)
  starting transfers between devices  22.5 us (10%)
  local copies, waits for them, and re-layouts  16.7 us (7%)
    all_to_all x4, waiting for transfers between devices, exchange(): return lax.all_to_all(blocks, ('tcol', 'line'), 0, 0, tiled=True)  72.1 us
    ppermute x3, waiting for transfers between devices, swap(): return lax.ppermute(array, 'half', [(0, 1), (1, 0)])  47.9 us
    all_to_all x1, blocking collectives, exchange(): return lax.all_to_all(blocks, ('tcol', 'line'), 0, 0, tiled=True)  30 us
    all_to_all x4, starting transfers between devices, exchange(): return lax.all_to_all(blocks, ('tcol', 'line'), 0, 0, tiled=True)  17.7 us
    unnamed x28, local copies, waits for them, and re-layouts  15.3 us
    pallas_call x1, Pallas kernels, to_sigma(): pl.pallas_call(functools.partial(sigma_kernel, norm_factor), out_shape=ja...  10.9 us
    pallas_call x1, Pallas kernels, volterra(): pl.pallas_call(functools.partial(volterra_kernel, rows), grid=(STEPS,), o...  5.26 us
    pallas_call x1, Pallas kernels, make_rights(): pl.pallas_call(functools.partial(rights_kernel, rows), grid=(STEPS,), out...  5.24 us
  transfers between devices with their start and end apart: 7, of which 5 were waited for; matrix products, arithmetic and copies ran while one was open for 1% of the time, Pallas kernels for 12%

profile of v5, /device:TPU:0, one launch (start us, length us, event | category | flops | bytes accessed | tf_op | source)
XLA Modules:
  0.0 228.7 jit_solution(16908128694031105162)
XLA Ops:
  0.6 4.1 %collective-permute-start = (bf16[2,8,64,512]{3,2,1,0:T(8,128)(2,1)}, bf16[2,8,64,512]{3,2,1,0:T(8,128)(2,1)}, u32[]{:S(2)}, u32[]{:S(2)}) collective-permute-start(bf16[2,8,64,512]{3,2,1,0:T(8,128)(2,1)} %lesser.1), channel_id=1, source_target_pairs={{0,16},{16,0},{1,17},{17,1},{2,18},{18,2},{3,19},{19,3},{4,20},{20... | collective-permute-start | bytes 3145736 | tf_op jit(solution)/shard_map/ppermute | solution.py:627
  4.7 0.0 copy-start.8
  4.7 1.3 copy-done.8
  6.0 0.0 copy-start.10
  6.0 1.2 copy-done.10
  7.2 1.0 spread.2
  8.2 0.0 copy-start.5
  8.2 1.3 copy-done.5
  9.5 4.8 %all-to-all-start = ((bf16[16,512,128]{2,1,0:T(8,128)(2,1)}), bf16[16,512,128]{2,1,0:T(8,128)(2,1)S(1)}, u32[]{:S(2)}, u32[]{:S(2)}) async-start(bf16[16,512,128]{2,1,0:T(8,128)(2,1)} %copy-done.5), calls=%async_computation | async-start | bytes 4194304 | tf_op jit(solution)/shard_map/all_to_all | solution.py:624
  14.4 36.4 %collective-permute-done.refs_0_ = bf16[2,8,64,512]{3,2,1,0:T(8,128)(2,1)} collective-permute-done((bf16[2,8,64,512]{3,2,1,0:T(8,128)(2,1)}, bf16[2,8,64,512]{3,2,1,0:T(8,128)(2,1)}, u32[]{:S(2)}, u32[]{:S(2)}) %collective-permute-start) | collective-permute-done | bytes 1048608 | tf_op jit(solution)/shard_map/ppermute | solution.py:627
  50.8 1.7 spread.3.refs_0_
  52.5 0.0 copy-start.7
  52.5 1.0 copy-done.7
  53.5 11.1 %all-to-all-done.refs_1_.own.own_l.own_g = bf16[16,512,128]{2,1,0:T(8,128)(2,1)S(1)} async-done(((bf16[16,512,128]{2,1,0:T(8,128)(2,1)}), bf16[16,512,128]{2,1,0:T(8,128)(2,1)S(1)}, u32[]{:S(2)}, u32[]{:S(2)}) %all-to-all-start) | async-done | bytes 2097184 | tf_op jit(solution)/shard_map/all_to_all | solution.py:624
  64.6 0.0 copy-start
  64.6 1.3 copy-done
  65.9 0.0 copy-start.1
  65.9 0.0 copy-start.13
  65.9 3.8 %all-to-all-start.1 = ((bf16[16,256,128]{2,1,0:T(8,128)(2,1)}), bf16[16,256,128]{2,1,0:T(8,128)(2,1)S(1)}, u32[]{:S(2)}, u32[]{:S(2)}) async-start(bf16[16,256,128]{2,1,0:T(8,128)(2,1)} %gate.1), calls=%async_computation.1 | async-start | bytes 2097152 | tf_op jit(solution)/shard_map/all_to_all | solution.py:624
  69.7 0.0 copy-done.1
  69.7 1.1 constant_dynamic-slice_fusion
  70.8 0.0 collective-permute-start.1
  70.8 0.0 copy-done.13
  70.8 0.1 copy.7.column_ref
  71.0 4.5 %make_tables.1 = (bf16[1024,1024]{1,0:T(8,128)(2,1)S(1)}, bf16[1024,1024]{1,0:T(8,128)(2,1)S(1)}) custom-call(s32[512,1]{1,0:T(8,128)S(1)} %copy.7.column_ref), custom_call_target="tpu_custom_call" | custom-call | tf_op jit(solution)/shard_map/make_tables/pallas_call | solution.py:324
  75.5 0.0 copy-start.3
  75.5 1.3 copy-done.3
  76.9 0.0 copy-start.12
  76.9 1.4 copy-done.12
  78.2 0.0 copy-start.9
  78.2 1.2 copy-done.9
  79.4 0.0 copy-start.11
  79.4 1.2 copy-done.11
  80.7 3.9 %to_sites.1.rest_0_.sites = bf16[1024,1024]{1,0:T(8,128)(2,1)S(1)} custom-call(bf16[2,8,64,512]{3,2,1,0:T(8,128)(2,1)S(1)} %copy-done.9, bf16[2,8,64,512]{3,2,1,0:T(8,128)(2,1)S(1)} %copy-done.11, bf16[1024,1024]{1,0:T(8,128)(2,1)} %copy-done.3), custom_call_target="tpu_custom_call" | custom-call | tf_op jit(solution)/shard_map/to_sites/pallas_call | solution.py:354
  84.6 0.0 copy-start.2
  84.6 1.3 copy-done.2
  85.9 11.5 %collective-permute-done.1.near_g = bf16[8,256,128]{2,1,0:T(8,128)(2,1)} collective-permute-done((bf16[8,256,128]{2,1,0:T(8,128)(2,1)}, bf16[8,256,128]{2,1,0:T(8,128)(2,1)}, u32[]{:S(2)}, u32[]{:S(2)}) %collective-permute-start.1) | collective-permute-done | bytes 524320 | tf_op jit(solution)/shard_map/ppermute | solution.py:627
  97.4 0.0 all-to-all-done.1.far_l
  97.4 1.7 to_crossed.1
  99.1 0.0 copy-start.6
  99.1 1.4 copy-done.6
  100.5 4.6 %all-to-all-start.2 = ((bf16[16,512,128]{2,1,0:T(8,128)(2,1)}), bf16[16,512,128]{2,1,0:T(8,128)(2,1)}, u32[]{:S(2)}, u32[]{:S(2)}) async-start(bf16[16,512,128]{2,1,0:T(8,128)(2,1)} %copy-done.6), calls=%async_computation.2 | async-start | bytes 4194304 | tf_op jit(solution)/shard_map/all_to_all | solution.py:624
  105.2 0.7 collective-permute-start.2
  106.5 0.1 fusion.4
  106.6 0.1 dynamic_slice.14
  106.7 0.1 dynamic_slice.13
  106.7 0.1 pad_maximum_fusion
  106.8 0.1 broadcast_multiply_fusion.coupling
  106.9 36.9 %all-to-all-done.2 = bf16[16,512,128]{2,1,0:T(8,128)(2,1)} async-done(((bf16[16,512,128]{2,1,0:T(8,128)(2,1)}), bf16[16,512,128]{2,1,0:T(8,128)(2,1)}, u32[]{:S(2)}, u32[]{:S(2)}) %all-to-all-start.2) | async-done | bytes 2097184 | tf_op jit(solution)/shard_map/all_to_all | solution.py:624
  143.8 10.9 %to_sigma.1 = bf16[8192,128]{1,0:T(8,128)(2,1)S(1)} custom-call(bf16[8192,128]{1,0:T(8,128)(2,1)} %bitcast.2.crossed, bf16[1024,1024]{1,0:T(8,128)(2,1)} %copy-done.2, bf16[1024,1024]{1,0:T(8,128)(2,1)} %copy-done.3, bf16[1024,1024]{1,0:T(8,128)(2,1)} %copy-done.12, f32[8,128]{1,0:T(8,128)S(1)} %broadcast_multiply_fusion.coupling), custom_call_target="tpu_custom_call" | custom-call | tf_op jit(solution)/shard_map/to_sigma/pallas_call | solution.py:457
  154.7 0.0 copy-start.4
  154.7 1.4 copy-done.4
  156.1 4.4 %all-to-all-start.3 = ((bf16[16,512,128]{2,1,0:T(8,128)(2,1)}), bf16[16,512,128]{2,1,0:T(8,128)(2,1)}, u32[]{:S(2)}, u32[]{:S(2)}) async-start(bf16[16,512,128]{2,1,0:T(8,128)(2,1)} %bitcast.7), calls=%async_computation.3 | async-start | bytes 4194304 | tf_op jit(solution)/shard_map/all_to_all | solution.py:624
  160.5 0.0 collective-permute-done.2.away_g
  160.6 5.2 %make_rights.1.rights = bf16[32,384,256]{2,1,0:T(8,128)(2,1)} custom-call(s32[1]{0:T(128)} %bitcast.half_ref, bf16[16,512,128]{2,1,0:T(8,128)(2,1)S(1)} %copy-done.1, bf16[16,512,128]{2,1,0:T(8,128)(2,1)S(1)} %copy-done.1, bf16[16,256,128]{2,1,0:T(8,128)(2,1)S(1)} %all-to-all-done.1.far_l, bf16[8,256,128]{2,1,0:T(8,128)(2,1)} %collective-permute-done.1.near_g, ...), custom_call_target="tpu_custom_call" | custom-call | flops 99999997952 | bytes 1048576 | tf_op jit(solution)/shard_map/make_rights/pallas_call | solution.py:519
  165.8 24.1 %all-to-all-done.3.sigma = bf16[16,512,128]{2,1,0:T(8,128)(2,1)} async-done(((bf16[16,512,128]{2,1,0:T(8,128)(2,1)}), bf16[16,512,128]{2,1,0:T(8,128)(2,1)}, u32[]{:S(2)}, u32[]{:S(2)}) %all-to-all-start.3) | async-done | bytes 2097184 | tf_op jit(solution)/shard_map/all_to_all | solution.py:624
  189.9 5.3 %volterra.1 = bf16[16,512,128]{2,1,0:T(8,128)(2,1)S(1)} custom-call(s32[1]{0:T(128)} %bitcast.half_ref, bf16[16,512,128]{2,1,0:T(8,128)(2,1)} %all-to-all-done.3.sigma, bf16[32,384,256]{2,1,0:T(8,128)(2,1)} %make_rights.1.rights), custom_call_target="tpu_custom_call" | custom-call | tf_op jit(solution)/shard_map/volterra/pallas_call | solution.py:598
  195.1 30.0 %all_to_all.25 = bf16[16,512,128]{2,1,0:T(8,128)(2,1)S(1)} all-to-all(bf16[16,512,128]{2,1,0:T(8,128)(2,1)S(1)} %volterra.1), channel_id=1, replica_groups=mesh['half'=2,'line'=8,'tcol'=2] {'tcol','line'}, dimensions={0} | all-to-all | bytes 4194304 | tf_op jit(solution)/shard_map/all_to_all | solution.py:624
  225.2 3.5 %collect.1 = (bf16[2,8,64,512]{3,2,1,0:T(8,128)(2,1)}, bf16[2,8,64,512]{3,2,1,0:T(8,128)(2,1)}) custom-call(bf16[8192,128]{1,0:T(8,128)(2,1)S(1)} %bitcast.8), custom_call_target="tpu_custom_call" | custom-call | tf_op jit(solution)/shard_map/collect/pallas_call | solution.py:292
  (1 shorter events, 0.0 us)
Async XLA Ops:
  0.6 50.1 %collective-permute-start = (bf16[2,8,64,512]{3,2,1,0:T(8,128)(2,1)}, bf16[2,8,64,512]{3,2,1,0:T(8,128)(2,1)}, u32[]{:S(2)}, u32[]{:S(2)}) collective-permute-start(bf16[2,8,64,512]{3,2,1,0:T(8,128)(2,1)} %lesser.1), channel_id=1, source_target_pairs={{0,16},{16,0},{1,17},{17,1},{2,18},{18,2},{3,19},{19,3},{4,20},{20... | collective-permute-start | bytes 3145736 | tf_op jit(solution)/shard_map/ppermute | solution.py:627
  4.7 1.3 copy-start.8
  6.0 1.2 copy-start.10
  8.2 1.3 copy-start.5
  9.5 55.1 %all-to-all-start = ((bf16[16,512,128]{2,1,0:T(8,128)(2,1)}), bf16[16,512,128]{2,1,0:T(8,128)(2,1)S(1)}, u32[]{:S(2)}, u32[]{:S(2)}) async-start(bf16[16,512,128]{2,1,0:T(8,128)(2,1)} %copy-done.5), calls=%async_computation | async-start | bytes 4194304 | tf_op jit(solution)/shard_map/all_to_all | solution.py:624
  52.5 1.0 copy-start.7
  64.6 1.3 copy-start
  65.9 3.8 %copy-start.1 = (bf16[16,512,128]{2,1,0:T(8,128)(2,1)S(1)}, bf16[16,512,128]{2,1,0:T(8,128)(2,1)}, u32[]{:S(2)}) copy-start(bf16[16,512,128]{2,1,0:T(8,128)(2,1)} %copy-done) | copy-start | bytes 6291460
  65.9 4.9 %copy-start.13 = (s32[512]{0:T(512)S(1)}, s32[512]{0:T(512)}, u32[]{:S(2)}) copy-start(s32[512]{0:T(512)} %param.6) | copy-start | bytes 6148
  65.9 31.5 %all-to-all-start.1 = ((bf16[16,256,128]{2,1,0:T(8,128)(2,1)}), bf16[16,256,128]{2,1,0:T(8,128)(2,1)S(1)}, u32[]{:S(2)}, u32[]{:S(2)}) async-start(bf16[16,256,128]{2,1,0:T(8,128)(2,1)} %gate.1), calls=%async_computation.1 | async-start | bytes 2097152 | tf_op jit(solution)/shard_map/all_to_all | solution.py:624
  70.8 26.6 %collective-permute-start.1 = (bf16[8,256,128]{2,1,0:T(8,128)(2,1)}, bf16[8,256,128]{2,1,0:T(8,128)(2,1)}, u32[]{:S(2)}, u32[]{:S(2)}) collective-permute-start(bf16[8,256,128]{2,1,0:T(8,128)(2,1)} %get-tuple-element.7), channel_id=1, source_target_pairs={{0,16},{16,0},{1,17},{17,1},{2,18},{18,2},{3,19},{19,3},{4,20},{20... | collective-permute-start | bytes 1572872 | tf_op jit(solution)/shard_map/ppermute | solution.py:627
  75.5 1.3 copy-start.3
  76.9 1.4 copy-start.12
  78.2 1.2 copy-start.9
  79.4 1.2 copy-start.11
  84.6 1.3 copy-start.2
  99.1 1.4 copy-start.6
  100.5 43.3 %all-to-all-start.2 = ((bf16[16,512,128]{2,1,0:T(8,128)(2,1)}), bf16[16,512,128]{2,1,0:T(8,128)(2,1)}, u32[]{:S(2)}, u32[]{:S(2)}) async-start(bf16[16,512,128]{2,1,0:T(8,128)(2,1)} %copy-done.6), calls=%async_computation.2 | async-start | bytes 4194304 | tf_op jit(solution)/shard_map/all_to_all | solution.py:624
  105.2 55.4 %collective-permute-start.2 = (bf16[8,256,128]{2,1,0:T(8,128)(2,1)}, bf16[8,256,128]{2,1,0:T(8,128)(2,1)}, u32[]{:S(2)}, u32[]{:S(2)}) collective-permute-start(bf16[8,256,128]{2,1,0:T(8,128)(2,1)} %get-tuple-element.6), channel_id=1, source_target_pairs={{0,16},{16,0},{1,17},{17,1},{2,18},{18,2},{3,19},{19,3},{4,20},{20... | collective-permute-start | bytes 1572872 | tf_op jit(solution)/shard_map/ppermute | solution.py:627
  154.7 1.4 copy-start.4
  156.1 33.8 %all-to-all-start.3 = ((bf16[16,512,128]{2,1,0:T(8,128)(2,1)}), bf16[16,512,128]{2,1,0:T(8,128)(2,1)}, u32[]{:S(2)}, u32[]{:S(2)}) async-start(bf16[16,512,128]{2,1,0:T(8,128)(2,1)} %bitcast.7), calls=%async_computation.3 | async-start | bytes 4194304 | tf_op jit(solution)/shard_map/all_to_all | solution.py:624

commit v6 on v5

--- a/solution.py
+++ b/solution.py
@@ -244,60 +244,62 @@
     return [pl.BlockSpec(memory_space=pltpu.SMEM)]
 
 
-def spread_kernel(*refs):
-    *tiles, out, lines = refs
-    _, rows, _, momenta = tiles[0].shape
-    blocks, height, _ = out.shape
-    height = height // len(tiles)
-    wide = momenta // 2
-    for g, tile in enumerate(tiles):
-        for first in range(0, momenta, wide):
-            for t in range(rows):
-                span = slice(first, first + wide)
-                slab = jnp.concatenate([tile[0, t, :, span], tile[1, t, :, span]], axis=0)
-                lines[pl.ds(first * rows + t, wide, stride=rows), :] = slab.astype(F32).T
+def spread_kernel(first, lesser, greater, *rest):
+    out, lines = rest[-2:]
+    _, rows, _, _ = lesser.shape
+    count = lines.shape[0] // (2 * rows)
+    for g, tile in enumerate((lesser, greater)):
+        for t in range(rows):
+            span = slice(first, first + count)
+            slab = jnp.concatenate([tile[0, t, :, span], tile[1, t, :, span]], axis=0)
+            lines[pl.ds(g * rows + t, count, stride=2 * rows), :] = slab.astype(F32).T
+    out[...] = lines[...].astype(BF16)
+
+
+def spread(tiles, first, count, after):
+    _, rows, cols, _ = tiles[0].shape
+    shape = (count * 2 * rows, 2 * cols)
+    return pl.pallas_call(
+        functools.partial(spread_kernel, first),
+        out_shape=jax.ShapeDtypeStruct(shape, BF16),
+        in_specs=whole(2) + unread(after),
+        out_specs=whole(1)[0],
+        scratch_shapes=[pltpu.VMEM(shape, F32)],
+        compiler_params=vmem_params(),
+        name="spread",
+    )(*tiles, *after)
+
+
+def collect_kernel(parts, blocks_ref, lesser, greater, lines):
+    _, rows, cols, momenta = lesser.shape
+    blocks, height, _ = blocks_ref.shape
+    height = height // parts
+    for part in range(parts):
         for block in range(blocks):
-            out[block, g * height : (g + 1) * height] = lines[
-                block * height : (block + 1) * height
-            ].astype(BF16)
-
-
-def spread(tiles, blocks, cost):
-    _, rows, cols, momenta = tiles[0].shape
-    lines = momenta * rows
-    return pl.pallas_call(
-        spread_kernel,
-        out_shape=jax.ShapeDtypeStruct((blocks, len(tiles) * lines // blocks, 2 * cols), BF16),
-        in_specs=whole(len(tiles)),
-        out_specs=whole(1)[0],
-        scratch_shapes=[pltpu.VMEM((lines, 2 * cols), F32)],
-        compiler_params=vmem_params(),
-        cost_estimate=cost,
-        name="spread",
-    )(*tiles)
-
-
-def collect_kernel(rows_ref, lesser, greater, lines):
-    lines[...] = rows_ref[...].astype(F32)
-    _, rows, cols, momenta = lesser.shape
-    for k in range(2 * rows):
-        slab = lines[pl.ds(k, momenta, stride=2 * rows), :].T.astype(BF16)
-        out = lesser if k < rows else greater
-        out[0, k % rows] = slab[:cols]
-        out[1, k % rows] = slab[cols:]
-
-
-def collect(rows_array, tile_shape):
+            lines[block * height : (block + 1) * height] = blocks_ref[
+                block, part * height : (part + 1) * height
+            ].astype(F32)
+        count = momenta // parts
+        span = slice(part * count, (part + 1) * count)
+        for k in range(2 * rows):
+            slab = lines[pl.ds(k, count, stride=2 * rows), :].T.astype(BF16)
+            out = lesser if k < rows else greater
+            out[0, k % rows, :, span] = slab[:cols]
+            out[1, k % rows, :, span] = slab[cols:]
+
+
+def collect(blocks, tile_shape):
     shape = jax.ShapeDtypeStruct(tile_shape, BF16)
-    return pl.pallas_call(
-        collect_kernel,
+    lines = blocks.shape[0] * blocks.shape[1] // PARTS
+    return pl.pallas_call(
+        functools.partial(collect_kernel, PARTS),
         out_shape=(shape, shape),
         in_specs=whole(1),
         out_specs=tuple(whole(2)),
-        scratch_shapes=[pltpu.VMEM(rows_array.shape, F32)],
+        scratch_shapes=[pltpu.VMEM((lines, blocks.shape[2]), F32)],
         compiler_params=vmem_params(),
         name="collect",
-    )(rows_array)
+    )(blocks)
 
 
 def table_kernel(column_ref, table, inverse):
@@ -361,45 +363,39 @@
     )(*tiles, table)
 
 
-def cross_kernel(rows, half_ref, own, far_l, near_g, *rest):
+def cross_kernel(rows, half_ref, own, far, *rest):
     out = rest[-1]
     half = half_ref[0]
-    blocks = near_g.shape[0]
+    blocks = far.shape[0]
     cols = blocks * rows
-    height = near_g.shape[1]
-    here = half * blocks
-    for pair in range(height // (2 * rows)):
-        low = slice(pair * 2 * rows, (pair + 1) * 2 * rows)
-        high = slice(height + pair * 2 * rows, height + (pair + 1) * 2 * rows)
-        for lesser, greater, target in (
-            ([own[here + b, low] for b in range(blocks)], [own[here + b, high] for b in range(blocks)], half),
-            ([far_l[here + b, low] for b in range(blocks)], [near_g[b, low] for b in range(blocks)], 1 - half),
-        ):
-            loaded = [lines.astype(F32) for lines in greater + lesser]
-            for at in range(2):
-                turned = jnp.concatenate(
-                    [lines[at * rows : (at + 1) * rows] for lines in loaded], axis=0
-                ).T
-                start = (2 * pair + at) * 2 * rows
-                for block in range(blocks):
-                    out[target * blocks + block, start : start + 2 * rows] = jnp.concatenate(
-                        [
-                            turned[block * rows : (block + 1) * rows],
-                            turned[cols + block * rows : cols + (block + 1) * rows],
-                        ],
-                        axis=0,
-                    ).astype(BF16)
-
-
-def to_crossed(half, own, far_l, near_g, rows, after):
+    for at in range(far.shape[1] // (2 * rows)):
+        span = slice(at * 2 * rows, (at + 1) * 2 * rows)
+        for source, offset, target in ((own, half * blocks, half), (far, 0, 1 - half)):
+            loaded = [source[offset + block, span].astype(F32) for block in range(blocks)]
+            stacked = jnp.concatenate(
+                [lines[rows:] for lines in loaded] + [lines[:rows] for lines in loaded], axis=0
+            )
+            turned = stacked.T
+            for block in range(blocks):
+                out[target * blocks + block, span] = jnp.concatenate(
+                    [
+                        turned[block * rows : (block + 1) * rows],
+                        turned[cols + block * rows : cols + (block + 1) * rows],
+                    ],
+                    axis=0,
+                ).astype(BF16)
+
+
+def to_crossed(half, own, far, rows, after, cost):
     return pl.pallas_call(
         functools.partial(cross_kernel, rows),
         out_shape=jax.ShapeDtypeStruct(own.shape, BF16),
-        in_specs=scalars() + whole(3) + unread(after),
+        in_specs=[pl.BlockSpec(memory_space=pltpu.SMEM)] + whole(2) + unread(after),
         out_specs=whole(1)[0],
         compiler_params=vmem_params(),
+        cost_estimate=cost,
         name="to_crossed",
-    )(half, own, far_l, near_g, *after)
+    )(half, own, far, *after)
 
 
 def gate_kernel(*refs):
@@ -417,10 +413,14 @@
     )(array, *after)
 
 
-def sigma_kernel(norm_factor, crossed, sites, table, inverse, coupling, out, read, written):
+def sigma_kernel(norm_factor, parts, *refs):
+    crossed = refs[:parts]
+    sites, table, inverse, coupling, out, read, written = refs[parts:]
     count = coupling.shape[0]
     momenta = table.shape[0] // 2
-    read[...] = crossed[...].astype(F32)
+    for part in range(parts):
+        lines = crossed[part].shape[0]
+        read[part * lines : (part + 1) * lines] = crossed[part][...].astype(F32)
     for pair in range(count // 2):
         rights = []
         for t in (2 * pair, 2 * pair + 1):
@@ -450,25 +450,35 @@
                 written[pl.ds(part * count + 2 * pair + at, momenta, stride=2 * count), :] = product[
                     part * momenta : (part + 1) * momenta, at * LANES : (at + 1) * LANES
                 ]
-    out[...] = written[...].astype(BF16)
-
-
-def to_sigma(crossed, sites, table, inverse, coupling, norm_factor):
-    return pl.pallas_call(
-        functools.partial(sigma_kernel, norm_factor),
-        out_shape=jax.ShapeDtypeStruct(crossed.shape, BF16),
-        in_specs=whole(5),
+    blocks, height, _ = out.shape
+    height = height // parts
+    for part in range(parts):
+        for block in range(blocks):
+            start = (part * blocks + block) * height
+            out[block, part * height : (part + 1) * height] = written[
+                start : start + height
+            ].astype(BF16)
+
+
+def to_sigma(crossed, sites, table, inverse, coupling, norm_factor, blocks):
+    parts = len(crossed)
+    lines, lanes = crossed[0].shape
+    return pl.pallas_call(
+        functools.partial(sigma_kernel, norm_factor, parts),
+        out_shape=jax.ShapeDtypeStruct((blocks, parts * lines // blocks, lanes), BF16),
+        in_specs=whole(parts + 4),
         out_specs=whole(1)[0],
-        scratch_shapes=[pltpu.VMEM(crossed.shape, F32)] * 2,
+        scratch_shapes=[pltpu.VMEM((parts * lines, lanes), F32)] * 2,
         compiler_params=vmem_params(),
         name="to_sigma",
-    )(crossed, sites, table, inverse, coupling)
-
-
-def rights_kernel(rows, half_ref, own_l, own_g, far_l, near_g, away_g, out):
+    )(*crossed, sites, table, inverse, coupling)
+
+
+def rights_kernel(rows, half_ref, own, near_ref, away_ref, *rest):
+    out = rest[-1]
     half = half_ref[0]
-    blocks = near_g.shape[0]
-    lanes = own_l.shape[2]
+    blocks = near_ref.shape[0]
+    lanes = own.shape[2]
     cols = lanes // 2
     near = half * cols
     away = (1 - half) * cols
@@ -477,55 +487,64 @@
     lane_at = lax.broadcasted_iota(jnp.int32, (lanes, 2 * lanes), 1)
     last_times = jnp.where(lane_at < lanes, near, away) + lane_at % cols
     keep = inner_times <= last_times
-    here = half * blocks
-    there = (1 - half) * blocks
-    for pair in range(out.shape[0] // 2):
-        span = slice(pair * 2 * rows, (pair + 1) * 2 * rows)
-
-        def stacked(ref, offset):
-            loaded = [ref[offset + block, span].astype(F32) for block in range(blocks)]
+    for at in range(out.shape[0]):
+        span = slice(at * 2 * rows, (at + 1) * 2 * rows)
+
+        def stacked(read):
+            loaded = [read(block).astype(F32) for block in range(blocks)]
             return [
-                jnp.concatenate([lines[at * rows : (at + 1) * rows] for lines in loaded], axis=0)
-                for at in range(2)
+                jnp.concatenate([lines[g * rows : (g + 1) * rows] for lines in loaded], axis=0)
+                for g in range(2)
             ]
 
-        parts = [
-            [[stacked(own_l, here), stacked(own_l, there)], [stacked(far_l, here), stacked(far_l, there)]],
-            [[stacked(own_g, here), stacked(own_g, there)], [stacked(near_g, 0), stacked(away_g, 0)]],
+        own_near = stacked(lambda block: own[half * blocks + block, span])
+        own_away = stacked(lambda block: own[(1 - half) * blocks + block, span])
+        far_near = stacked(lambda block: near_ref[block, span])
+        far_away = stacked(lambda block: away_ref[0, block, span])
+        greens = [
+            jnp.concatenate(
+                [
+                    jnp.concatenate([own_near[g], own_away[g]], axis=1),
+                    jnp.concatenate([far_near[g], far_away[g]], axis=1),
+                ],
+                axis=0,
+            )
+            for g in range(2)
         ]
-        for at in range(2):
-            greens = [
-                jnp.concatenate(
-                    [jnp.concatenate([side[at] for side in line], axis=1) for line in part], axis=0
-                )
-                for part in parts
-            ]
-            out[2 * pair + at, :lanes] = greens[0].astype(BF16)
-            out[2 * pair + at, lanes : 2 * lanes] = greens[1].astype(BF16)
-            out[2 * pair + at, 2 * lanes :] = jnp.where(keep, greens[0] - greens[1], 0.0).astype(BF16)
+        out[at, :lanes] = greens[0].astype(BF16)
+        out[at, lanes : 2 * lanes] = greens[1].astype(BF16)
+        out[at, 2 * lanes :] = jnp.where(keep, greens[0] - greens[1], 0.0).astype(BF16)
 
 
 STEPS = 4
-
-
-def make_rights(half, own, far_l, near_g, away_g, rows):
-    sources, lines, lanes = far_l.shape
-    blocks = near_g.shape[0]
-    step = lines // STEPS
-    momenta = step // rows
-    lesser = pl.BlockSpec((sources, step, lanes), lambda p: (0, p, 0))
-    greater = pl.BlockSpec((sources, step, lanes), lambda p: (0, STEPS + p, 0))
-    half_spec = pl.BlockSpec((blocks, step, lanes), lambda p: (0, p, 0))
+PARTS = 2
+
+
+def make_rights(half, own, far_near, far_away, rows, part, before):
+    sources, lines, lanes = own.shape
+    blocks = far_near.shape[0]
+    steps = STEPS // PARTS
+    step = lines // steps
+    momenta = step // (2 * rows)
     return pl.pallas_call(
         functools.partial(rights_kernel, rows),
-        grid=(STEPS,),
-        out_shape=jax.ShapeDtypeStruct((lines // rows, 3 * lanes, 2 * lanes), BF16),
-        in_specs=scalars() + [lesser, greater, lesser, half_spec, half_spec],
-        out_specs=pl.BlockSpec((momenta, 3 * lanes, 2 * lanes), lambda p: (p, 0, 0)),
+        grid=(steps,),
+        out_shape=jax.ShapeDtypeStruct((STEPS * momenta, 3 * lanes, 2 * lanes), BF16),
+        in_specs=scalars()
+        + [
+            pl.BlockSpec((sources, step, lanes), lambda p: (0, p, 0)),
+            pl.BlockSpec((blocks, step, lanes), lambda p: (0, p, 0)),
+            pl.BlockSpec((1, blocks, step, lanes), lambda p: (part, 0, p, 0)),
+        ]
+        + unread(before),
+        out_specs=pl.BlockSpec(
+            (momenta, 3 * lanes, 2 * lanes), lambda p: (part * steps + p, 0, 0)
+        ),
+        input_output_aliases={4: 0} if before else {},
         compiler_params=vmem_params(),
         cost_estimate=weight(),
         name="make_rights",
-    )(half, own, own, far_l, near_g, away_g)
+    )(half, own, far_near, far_away, *before)
 
 
 def volterra_kernel(rows, half_ref, sigma, rights, out):
@@ -618,25 +637,22 @@
     norm_factor = 1.0 / math.sqrt(momenta)
     tiles = (green_lesser, green_greater)
     half_at = half[None]
-    height = momenta * rows // group
+    count = momenta // PARTS
 
     def exchange(blocks):
         return lax.all_to_all(blocks, ("tcol", "line"), 0, 0, tiled=True)
 
+    def blocked(rows_array):
+        return rows_array.reshape(group, rows_array.shape[0] // group, rows_array.shape[1])
+
     def swap(array):
         return lax.ppermute(array, "half", [(0, 1), (1, 0)])
 
-    def greater_blocks(at):
-        zero = jnp.zeros((), jnp.int32)
-        return lax.dynamic_slice(
-            own, (at * lines, zero + height, zero), (lines, height, 2 * cols)
-        )
-
-    far_tile = swap(green_lesser)
-    own = exchange(spread(tiles, group, None))
-    far_l = exchange(gate(spread([far_tile], group, weight()), [own]))
-    near_g = swap(greater_blocks(1 - half))
-    away_g = swap(greater_blocks(half))
+    own = []
+    far_near = []
+    for part in range(PARTS):
+        own.append(exchange(blocked(spread(tiles, part * count, count, own[-1:]))))
+        far_near.append(swap(lax.dynamic_slice_in_dim(own[-1], (1 - half) * lines, lines)))
 
     table, inverse = make_tables(lattice_map)
     sites = to_sites(tiles, table, norm_factor)
@@ -648,15 +664,41 @@
     second = lax.dynamic_slice_in_dim(coupling_line, side * cols, cols)
     coupling = first[:, None] * jnp.concatenate([second, second])[None, :]
 
-    crossed = exchange(to_crossed(half_at, own, far_l, near_g, rows, [sites]))
-    sigma_rows = to_sigma(
-        crossed.reshape(-1, 2 * cols), sites, table, inverse, coupling, norm_factor
-    )
-    sigma = exchange(sigma_rows.reshape(crossed.shape))
-    rights = make_rights(half_at, own, far_l, near_g, away_g, rows)
-    collisions = volterra(half_at, sigma, rights, rows)
-    returned = exchange(collisions)
-    return collect(returned.reshape(-1, 2 * cols), green_lesser.shape)
+    sent = []
+    for part in range(PARTS):
+        sent.append(
+            to_crossed(
+                half_at,
+                own[part],
+                far_near[part],
+                rows,
+                [sites, own[-1]] + sent[-1:],
+                weight() if part > 0 else None,
+            )
+        )
+    crossed = [exchange(blocks) for blocks in sent]
+    kept = jnp.stack(
+        [lax.dynamic_slice_in_dim(blocks, half * lines, lines) for blocks in own]
+    )
+    far_away = swap(gate(kept, crossed))
+    sigma = exchange(
+        to_sigma(
+            [blocks.reshape(-1, 2 * cols) for blocks in crossed],
+            sites,
+            table,
+            inverse,
+            coupling,
+            norm_factor,
+            group,
+        )
+    )
+    rights = []
+    for part in range(PARTS):
+        rights = [
+            make_rights(half_at, own[part], far_near[part], far_away, rows, part, rights)
+        ]
+    returned = exchange(volterra(half_at, sigma, rights[0], rows))
+    return collect(returned, green_lesser.shape)
 
 
 def solution(mesh):
@@ -675,7 +717,7 @@
             and cols == rows * (row_parts // 2)
             and rows % 8 == 0
             and momenta % (2 * row_parts * STEPS) == 0
-            and momenta % LANES == 0
+            and momenta % (PARTS * LANES) == 0
         )
         if halved:
             devices = mesh.devices.reshape(2, row_parts // 2, col_parts)

time: 229 us -> 228 us (level)
  waiting for transfers between devices: 120 us -> 93.4 us
  blocking collectives: 30 us -> 52.3 us
  Pallas kernels: 37.8 us -> 40.4 us
    all_to_all x1 -> x2, blocking collectives: 30 us -> 52.3 us  [exchange(): return lax.all_to_all(blocks, ('tcol', 'line'), 0, 0, tiled=True)]
    ppermute x3, waiting for transfers between devices: 47.9 us -> 28.6 us  [swap(): return lax.ppermute(array, 'half', [(0, 1), (1, 0)])]
    all_to_all x4, waiting for transfers between devices: 72.1 us -> 64.8 us  [exchange(): return lax.all_to_all(blocks, ('tcol', 'line'), 0, 0, tiled=True)]
    unnamed x28 -> x38, local copies, waits for them, and re-layouts: 15.3 us -> 14.2 us
    pallas_call x5 -> x6, Pallas kernels: 22.4 us -> 23.3 us  [the longest x1 12 us: to_sigma(): pl.pallas_call(functools.partial(sigma_kernel, norm_factor, parts), out_s...]
  transfers between devices with their start and end apart: 7 -> 7, of which waited for: 5 -> 6; matrix products, arithmetic and copies ran while one was open for 1% -> 2% of each run, Pallas kernels for 12% -> 13%
where the time goes in v6:
time: 228 us; the launch traced here: 227 us
  waiting for transfers between devices  93.4 us (41%)
  blocking collectives  52.3 us (23%)
  Pallas kernels  40.4 us (18%)
  starting transfers between devices  21.8 us (10%)
  local copies, waits for them, and re-layouts  16.7 us (7%)
    all_to_all x4, waiting for transfers between devices, exchange(): return lax.all_to_all(blocks, ('tcol', 'line'), 0, 0, tiled=True)  64.8 us
    all_to_all x2, blocking collectives, exchange(): return lax.all_to_all(blocks, ('tcol', 'line'), 0, 0, tiled=True)  52.3 us
    ppermute x3, waiting for transfers between devices, swap(): return lax.ppermute(array, 'half', [(0, 1), (1, 0)])  28.6 us
    all_to_all x4, starting transfers between devices, exchange(): return lax.all_to_all(blocks, ('tcol', 'line'), 0, 0, tiled=True)  16.3 us
    unnamed x38, local copies, waits for them, and re-layouts  14.2 us
    pallas_call x1, Pallas kernels, to_sigma(): pl.pallas_call(functools.partial(sigma_kernel, norm_factor, parts), out_s...  12 us
    pallas_call x2, Pallas kernels, make_rights(): pl.pallas_call(functools.partial(rights_kernel, rows), grid=(steps,), out...  5.92 us
    ppermute x3, starting transfers between devices, swap(): return lax.ppermute(array, 'half', [(0, 1), (1, 0)])  5.51 us
  transfers between devices with their start and end apart: 7, of which 6 were waited for; matrix products, arithmetic and copies ran while one was open for 2% of the time, Pallas kernels for 13%

profile of v6, /device:TPU:0, one launch (start us, length us, event | category | flops | bytes accessed | tf_op | source)
XLA Modules:
  0.0 227.4 jit_solution(11843028680956113974)
XLA Ops:
  0.6 0.0 copy-start.3
  0.6 1.2 copy-done.3
  1.9 0.0 copy-start.5
  1.9 1.2 copy-done.5
  3.1 0.9 spread.2
  4.0 22.3 %all_to_all.30.rest_0_.own = bf16[16,256,128]{2,1,0:T(8,128)(2,1)S(1)} all-to-all(bf16[16,256,128]{2,1,0:T(8,128)(2,1)S(1)} %bitcast.13), channel_id=1, replica_groups=mesh['half'=2,'line'=8,'tcol'=2] {'tcol','line'}, dimensions={0} | all-to-all | bytes 2097152 | tf_op jit(solution)/shard_map/all_to_all | solution.py:643
  26.2 1.9 spread.3
  28.1 3.7 %all-to-all-start.1 = ((bf16[16,256,128]{2,1,0:T(8,128)(2,1)}), bf16[16,256,128]{2,1,0:T(8,128)(2,1)S(1)}, u32[]{:S(2)}, u32[]{:S(2)}) async-start(bf16[16,256,128]{2,1,0:T(8,128)(2,1)} %bitcast.3), calls=%async_computation.1 | async-start | bytes 2097152 | tf_op jit(solution)/shard_map/all_to_all | solution.py:643
  31.8 0.0 copy-start.18
  31.8 1.1 dynamic-slice_bitcast_fusion.1
  32.9 2.6 %collective-permute-start = (bf16[8,256,128]{2,1,0:T(8,128)(2,1)}, bf16[8,256,128]{2,1,0:T(8,128)(2,1)}, u32[]{:S(2)}, u32[]{:S(2)}) collective-permute-start(bf16[8,256,128]{2,1,0:T(8,128)(2,1)} %get-tuple-element.7), channel_id=1, source_target_pairs={{0,16},{16,0},{1,17},{17,1},{2,18},{18,2},{3,19},{19,3},{4,20},{20... | collective-permute-start | bytes 1572872 | tf_op jit(solution)/shard_map/ppermute | solution.py:649
  35.5 23.6 %all-to-all-done.1.rest_1_.own = bf16[16,256,128]{2,1,0:T(8,128)(2,1)S(1)} async-done(((bf16[16,256,128]{2,1,0:T(8,128)(2,1)}), bf16[16,256,128]{2,1,0:T(8,128)(2,1)S(1)}, u32[]{:S(2)}, u32[]{:S(2)}) %all-to-all-start.1) | async-done | bytes 1048608 | tf_op jit(solution)/shard_map/all_to_all | solution.py:643
  59.0 0.0 copy-start.7
  59.0 1.1 dynamic-slice_bitcast_fusion
  60.1 0.0 collective-permute-start.1
  60.1 0.0 copy-done.18
  60.1 0.1 copy.8.column_ref
  60.3 4.5 %make_tables.1 = (bf16[1024,1024]{1,0:T(8,128)(2,1)S(1)}, bf16[1024,1024]{1,0:T(8,128)(2,1)S(1)}) custom-call(s32[512,1]{1,0:T(8,128)S(1)} %copy.8.column_ref), custom_call_target="tpu_custom_call" | custom-call | tf_op jit(solution)/shard_map/make_tables/pallas_call | solution.py:326
  64.8 0.0 copy-done.7
  64.9 0.0 copy-start.11
  64.9 1.4 copy-done.11
  66.2 1.4 copy-done.14
  67.6 1.2 copy-done.4
  68.8 1.2 copy-done.6
  70.0 4.0 %to_sites.1.rest_0_.refs_2_ = bf16[1024,1024]{1,0:T(8,128)(2,1)S(1)} custom-call(bf16[2,8,64,512]{3,2,1,0:T(8,128)(2,1)S(1)} %copy-done.4, bf16[2,8,64,512]{3,2,1,0:T(8,128)(2,1)S(1)} %copy-done.6, bf16[1024,1024]{1,0:T(8,128)(2,1)} %copy-done.11), custom_call_target="tpu_custom_call" | custom-call | tf_op jit(solution)/shard_map/to_sites/pallas_call | solution.py:356
  74.1 0.0 copy-start
  74.1 0.0 collective-permute-done.far.near_ref
  74.1 0.0 copy-done.8
  74.1 1.8 to_crossed.2.rest_2_
  75.9 0.0 copy-start.12
  75.9 1.0 copy-done.12
  76.9 4.4 %all-to-all-start.2 = ((bf16[16,256,128]{2,1,0:T(8,128)(2,1)}), bf16[16,256,128]{2,1,0:T(8,128)(2,1)}, u32[]{:S(2)}, u32[]{:S(2)}) async-start(bf16[16,256,128]{2,1,0:T(8,128)(2,1)} %copy-done.12), calls=%async_computation.2 | async-start | bytes 2097152 | tf_op jit(solution)/shard_map/all_to_all | solution.py:643
  81.3 2.2 collective-permute-done.1.far.near_ref
  83.4 0.0 copy-done
  83.4 1.2 copy-done.9
  84.7 1.2 copy-done.13
  85.9 1.4 to_crossed.3
  87.3 0.0 copy-start.15
  87.3 1.0 copy-done.15
  88.3 9.2 %all-to-all-done.2.refs_1_ = bf16[16,256,128]{2,1,0:T(8,128)(2,1)} async-done(((bf16[16,256,128]{2,1,0:T(8,128)(2,1)}), bf16[16,256,128]{2,1,0:T(8,128)(2,1)}, u32[]{:S(2)}, u32[]{:S(2)}) %all-to-all-start.2) | async-done | bytes 1048608 | tf_op jit(solution)/shard_map/all_to_all | solution.py:643
  97.5 3.8 %all-to-all-start.3 = ((bf16[16,256,128]{2,1,0:T(8,128)(2,1)}), bf16[16,256,128]{2,1,0:T(8,128)(2,1)S(1)}, u32[]{:S(2)}, u32[]{:S(2)}) async-start(bf16[16,256,128]{2,1,0:T(8,128)(2,1)} %copy-done.15), calls=%async_computation.3 | async-start | bytes 2097152 | tf_op jit(solution)/shard_map/all_to_all | solution.py:643
  101.3 0.0 copy-done.16
  101.3 0.0 copy-done.17
  101.3 1.1 pad_maximum_fusion.refs_0_
  102.4 14.9 %all-to-all-done.3.refs_2_ = bf16[16,256,128]{2,1,0:T(8,128)(2,1)S(1)} async-done(((bf16[16,256,128]{2,1,0:T(8,128)(2,1)}), bf16[16,256,128]{2,1,0:T(8,128)(2,1)S(1)}, u32[]{:S(2)}, u32[]{:S(2)}) %all-to-all-start.3) | async-done | bytes 1048608 | tf_op jit(solution)/shard_map/all_to_all | solution.py:643
  117.3 1.0 copy-done.1
  118.2 2.9 %collective-permute-start.2 = (bf16[2,8,256,128]{3,2,1,0:T(8,128)(2,1)}, bf16[2,8,256,128]{3,2,1,0:T(8,128)(2,1)S(1)}, u32[]{:S(2)}, u32[]{:S(2)}) collective-permute-start(bf16[2,8,256,128]{3,2,1,0:T(8,128)(2,1)} %gate.1), channel_id=1, source_target_pairs={{0,16},{16,0},{1,17},{17,1},{2,18},{18,2},{3,19},{19,3},{4,20},{20... | collective-permute-start | bytes 3145736 | tf_op jit(solution)/shard_map/ppermute | solution.py:649
  121.8 0.1 fusion.4
  121.9 0.1 dynamic_slice.21
  121.9 0.1 dynamic_slice.20
  122.0 0.1 pad_maximum_fusion.1
  122.1 0.1 broadcast_multiply_fusion.refs_5_
  122.2 1.2 copy-done.2
  123.4 12.0 %to_sigma.1 = bf16[16,512,128]{2,1,0:T(8,128)(2,1)} custom-call(bf16[4096,128]{1,0:T(8,128)(2,1)} %bitcast.4.refs_0_, bf16[4096,128]{1,0:T(8,128)(2,1)S(1)} %bitcast.12, bf16[1024,1024]{1,0:T(8,128)(2,1)} %copy-done, bf16[1024,1024]{1,0:T(8,128)(2,1)} %copy-done.11, bf16[1024,1024]{1,0:T(8,128)(2,1)} %copy-done.14, f32[8,128]{1,0:T(8,128)S(1)} %broadcast_multiply_fusion.refs_5_), custom_call_target="tpu_custom_call" | custom-call | tf_op jit(solution)/shard_map/to_sigma/pallas_call | solution.py:466
  135.4 4.4 %all-to-all-start.4 = ((bf16[16,512,128]{2,1,0:T(8,128)(2,1)}), bf16[16,512,128]{2,1,0:T(8,128)(2,1)}, u32[]{:S(2)}, u32[]{:S(2)}) async-start(bf16[16,512,128]{2,1,0:T(8,128)(2,1)} %to_sigma.1), calls=%async_computation.4 | async-start | bytes 4194304 | tf_op jit(solution)/shard_map/all_to_all | solution.py:643
  139.9 0.0 copy-start.10
  139.9 26.5 %collective-permute-done.2.away_ref = bf16[2,8,256,128]{3,2,1,0:T(8,128)(2,1)S(1)} collective-permute-done((bf16[2,8,256,128]{3,2,1,0:T(8,128)(2,1)}, bf16[2,8,256,128]{3,2,1,0:T(8,128)(2,1)S(1)}, u32[]{:S(2)}, u32[]{:S(2)}) %collective-permute-start.2) | collective-permute-done | bytes 1048608 | tf_op jit(solution)/shard_map/ppermute | solution.py:649
  166.4 2.9 %make_rights.2.rest_0_ = bf16[32,384,256]{2,1,0:T(8,128)(2,1)} custom-call(s32[1]{0:T(128)} %bitcast.half_ref, bf16[16,256,128]{2,1,0:T(8,128)(2,1)S(1)} %all_to_all.30.rest_0_.own, bf16[8,256,128]{2,1,0:T(8,128)(2,1)} %collective-permute-done.far.near_ref, bf16[2,8,256,128]{3,2,1,0:T(8,128)(2,1)S(1)} %collective-permute-done.2.away_ref), custom_call_target="tpu_custom_call" | custom-call | flops 99999997952 | bytes 1048576 | tf_op jit(solution)/shard_map/make_rights/pallas_call | solution.py:529
  169.3 0.0 copy-done.10
  169.3 3.0 %make_rights.3.rights = bf16[32,384,256]{2,1,0:T(8,128)(2,1)} custom-call(s32[1]{0:T(128)} %bitcast.half_ref, bf16[16,256,128]{2,1,0:T(8,128)(2,1)S(1)} %copy-done.10, bf16[8,256,128]{2,1,0:T(8,128)(2,1)} %collective-permute-done.1.far.near_ref, bf16[2,8,256,128]{3,2,1,0:T(8,128)(2,1)S(1)} %collective-permute-done.2.away_ref, ...), custom_call_target="tpu_custom_call", output_to_operand_aliasing={{}: (4, {})} | custom-call | flops 99999997952 | bytes 1048576 | tf_op jit(solution)/shard_map/make_rights/pallas_call | solution.py:529
  172.3 17.2 %all-to-all-done.4.sigma = bf16[16,512,128]{2,1,0:T(8,128)(2,1)} async-done(((bf16[16,512,128]{2,1,0:T(8,128)(2,1)}), bf16[16,512,128]{2,1,0:T(8,128)(2,1)}, u32[]{:S(2)}, u32[]{:S(2)}) %all-to-all-start.4) | async-done | bytes 2097184 | tf_op jit(solution)/shard_map/all_to_all | solution.py:643
  189.5 5.3 %volterra.1 = bf16[16,512,128]{2,1,0:T(8,128)(2,1)S(1)} custom-call(s32[1]{0:T(128)} %bitcast.half_ref, bf16[16,512,128]{2,1,0:T(8,128)(2,1)} %all-to-all-done.4.sigma, bf16[32,384,256]{2,1,0:T(8,128)(2,1)} %make_rights.3.rights), custom_call_target="tpu_custom_call" | custom-call | tf_op jit(solution)/shard_map/volterra/pallas_call | solution.py:617
  194.7 30.0 %all_to_all.31.blocks_ref = bf16[16,512,128]{2,1,0:T(8,128)(2,1)S(1)} all-to-all(bf16[16,512,128]{2,1,0:T(8,128)(2,1)S(1)} %volterra.1), channel_id=1, replica_groups=mesh['half'=2,'line'=8,'tcol'=2] {'tcol','line'}, dimensions={0} | all-to-all | bytes 4194304 | tf_op jit(solution)/shard_map/all_to_all | solution.py:643
  224.8 2.6 %collect.1 = (bf16[2,8,64,512]{3,2,1,0:T(8,128)(2,1)}, bf16[2,8,64,512]{3,2,1,0:T(8,128)(2,1)}) custom-call(bf16[16,512,128]{2,1,0:T(8,128)(2,1)S(1)} %all_to_all.31.blocks_ref), custom_call_target="tpu_custom_call" | custom-call | tf_op jit(solution)/shard_map/collect/pallas_call | solution.py:294
  (11 shorter events, 0.0 us)
Async XLA Ops:
  0.6 1.2 copy-start.3
  1.9 1.2 copy-start.5
  28.1 30.9 %all-to-all-start.1 = ((bf16[16,256,128]{2,1,0:T(8,128)(2,1)}), bf16[16,256,128]{2,1,0:T(8,128)(2,1)S(1)}, u32[]{:S(2)}, u32[]{:S(2)}) async-start(bf16[16,256,128]{2,1,0:T(8,128)(2,1)} %bitcast.3), calls=%async_computation.1 | async-start | bytes 2097152 | tf_op jit(solution)/shard_map/all_to_all | solution.py:643
  31.8 28.4 %copy-start.18 = (s32[512]{0:T(512)S(1)}, s32[512]{0:T(512)}, u32[]{:S(2)}) copy-start(s32[512]{0:T(512)} %param.6) | copy-start | bytes 6148
  32.9 41.2 %collective-permute-start = (bf16[8,256,128]{2,1,0:T(8,128)(2,1)}, bf16[8,256,128]{2,1,0:T(8,128)(2,1)}, u32[]{:S(2)}, u32[]{:S(2)}) collective-permute-start(bf16[8,256,128]{2,1,0:T(8,128)(2,1)} %get-tuple-element.7), channel_id=1, source_target_pairs={{0,16},{16,0},{1,17},{17,1},{2,18},{18,2},{3,19},{19,3},{4,20},{20... | collective-permute-start | bytes 1572872 | tf_op jit(solution)/shard_map/ppermute | solution.py:649
  59.0 5.8 %copy-start.7 = (bf16[16,256,128]{2,1,0:T(8,128)(2,1)}, bf16[16,256,128]{2,1,0:T(8,128)(2,1)S(1)}, u32[]{:S(2)}) copy-start(bf16[16,256,128]{2,1,0:T(8,128)(2,1)S(1)} %all-to-all-done.1.rest_1_.own) | copy-start | bytes 3145732
  60.1 23.3 %collective-permute-start.1 = (bf16[8,256,128]{2,1,0:T(8,128)(2,1)}, bf16[8,256,128]{2,1,0:T(8,128)(2,1)}, u32[]{:S(2)}, u32[]{:S(2)}) collective-permute-start(bf16[8,256,128]{2,1,0:T(8,128)(2,1)} %get-tuple-element.9), channel_id=1, source_target_pairs={{0,16},{16,0},{1,17},{17,1},{2,18},{18,2},{3,19},{19,3},{4,20},{20... | collective-permute-start | bytes 1572872 | tf_op jit(solution)/shard_map/ppermute | solution.py:649
  64.9 1.4 copy-start.11
  66.2 1.4 copy-start.14
  67.6 1.2 copy-start.4
  68.8 1.2 copy-start.6
  70.0 4.1 %copy-start.8 = (bf16[16,256,128]{2,1,0:T(8,128)(2,1)S(1)}, bf16[16,256,128]{2,1,0:T(8,128)(2,1)}, u32[]{:S(2)}) copy-start(bf16[16,256,128]{2,1,0:T(8,128)(2,1)} %copy-done.7) | copy-start | bytes 3145732
  74.1 9.3 %copy-start = (bf16[1024,1024]{1,0:T(8,128)(2,1)}, bf16[1024,1024]{1,0:T(8,128)(2,1)S(1)}, u32[]{:S(2)}) copy-start(bf16[1024,1024]{1,0:T(8,128)(2,1)S(1)} %to_sites.1.rest_0_.refs_2_) | copy-start | bytes 6291460
  75.9 1.0 copy-start.12
  76.9 20.5 %all-to-all-start.2 = ((bf16[16,256,128]{2,1,0:T(8,128)(2,1)}), bf16[16,256,128]{2,1,0:T(8,128)(2,1)}, u32[]{:S(2)}, u32[]{:S(2)}) async-start(bf16[16,256,128]{2,1,0:T(8,128)(2,1)} %copy-done.12), calls=%async_computation.2 | async-start | bytes 2097152 | tf_op jit(solution)/shard_map/all_to_all | solution.py:643
  83.4 1.2 copy-start.9
  84.7 1.2 copy-start.13
  87.3 1.0 copy-start.15
  88.3 13.0 %copy-start.16 = (bf16[1,8,256,128]{3,2,1,0:T(8,128)(2,1)S(1)}, bf16[1,8,256,128]{3,2,1,0:T(8,128)(2,1)}, u32[]{:S(2)}) copy-start(bf16[1,8,256,128]{3,2,1,0:T(8,128)(2,1)} %get-tuple-element.6) | copy-start | bytes 1572868
  88.3 13.0 %copy-start.17 = (bf16[1,8,256,128]{3,2,1,0:T(8,128)(2,1)S(1)}, bf16[1,8,256,128]{3,2,1,0:T(8,128)(2,1)}, u32[]{:S(2)}) copy-start(bf16[1,8,256,128]{3,2,1,0:T(8,128)(2,1)} %get-tuple-element.8) | copy-start | bytes 1572868
  97.5 19.8 %all-to-all-start.3 = ((bf16[16,256,128]{2,1,0:T(8,128)(2,1)}), bf16[16,256,128]{2,1,0:T(8,128)(2,1)S(1)}, u32[]{:S(2)}, u32[]{:S(2)}) async-start(bf16[16,256,128]{2,1,0:T(8,128)(2,1)} %copy-done.15), calls=%async_computation.3 | async-start | bytes 2097152 | tf_op jit(solution)/shard_map/all_to_all | solution.py:643
  117.3 1.0 copy-start.1
  118.2 48.1 %collective-permute-start.2 = (bf16[2,8,256,128]{3,2,1,0:T(8,128)(2,1)}, bf16[2,8,256,128]{3,2,1,0:T(8,128)(2,1)S(1)}, u32[]{:S(2)}, u32[]{:S(2)}) collective-permute-start(bf16[2,8,256,128]{3,2,1,0:T(8,128)(2,1)} %gate.1), channel_id=1, source_target_pairs={{0,16},{16,0},{1,17},{17,1},{2,18},{18,2},{3,19},{19,3},{4,20},{20... | collective-permute-start | bytes 3145736 | tf_op jit(solution)/shard_map/ppermute | solution.py:649
  122.2 1.2 copy-start.2
  135.4 54.0 %all-to-all-start.4 = ((bf16[16,512,128]{2,1,0:T(8,128)(2,1)}), bf16[16,512,128]{2,1,0:T(8,128)(2,1)}, u32[]{:S(2)}, u32[]{:S(2)}) async-start(bf16[16,512,128]{2,1,0:T(8,128)(2,1)} %to_sigma.1), calls=%async_computation.4 | async-start | bytes 4194304 | tf_op jit(solution)/shard_map/all_to_all | solution.py:643
  139.9 29.4 %copy-start.10 = (bf16[16,256,128]{2,1,0:T(8,128)(2,1)S(1)}, bf16[16,256,128]{2,1,0:T(8,128)(2,1)}, u32[]{:S(2)}) copy-start(bf16[16,256,128]{2,1,0:T(8,128)(2,1)} %copy-done.7) | copy-start | bytes 3145732

commit v7 on v6

--- a/solution.py
+++ b/solution.py
@@ -648,12 +648,6 @@
     def swap(array):
         return lax.ppermute(array, "half", [(0, 1), (1, 0)])
 
-    own = []
-    far_near = []
-    for part in range(PARTS):
-        own.append(exchange(blocked(spread(tiles, part * count, count, own[-1:]))))
-        far_near.append(swap(lax.dynamic_slice_in_dim(own[-1], (1 - half) * lines, lines)))
-
     table, inverse = make_tables(lattice_map)
     sites = to_sites(tiles, table, norm_factor)
     time_steps = jnp.arange(window, dtype=jnp.int32)
@@ -663,6 +657,12 @@
     first = lax.dynamic_slice_in_dim(coupling_line, (half * lines + line) * rows, rows)
     second = lax.dynamic_slice_in_dim(coupling_line, side * cols, cols)
     coupling = first[:, None] * jnp.concatenate([second, second])[None, :]
+
+    spread_parts = [spread(tiles, part * count, count, []) for part in range(PARTS)]
+    own = [exchange(blocked(spread_parts[0]))]
+    for rows_array in spread_parts[1:]:
+        own.append(exchange(gate(blocked(rows_array), [own[-1], sites, coupling])))
+    far_near = [swap(lax.dynamic_slice_in_dim(blocks, (1 - half) * lines, lines)) for blocks in own]
 
     sent = []
     for part in range(PARTS):
@@ -672,7 +672,7 @@
                 own[part],
                 far_near[part],
                 rows,
-                [sites, own[-1]] + sent[-1:],
+                own[-1:] + sent[-1:],
                 weight() if part > 0 else None,
             )
         )
@@ -680,7 +680,7 @@
     kept = jnp.stack(
         [lax.dynamic_slice_in_dim(blocks, half * lines, lines) for blocks in own]
     )
-    far_away = swap(gate(kept, crossed))
+    far_away = swap(gate(kept, sent[-1:]))
     sigma = exchange(
         to_sigma(
             [blocks.reshape(-1, 2 * cols) for blocks in crossed],

time: 228 us -> 224 us (0.982)
  blocking collectives: 52.3 us -> 30 us
  waiting for transfers between devices: 93.4 us -> 110 us
  starting transfers between devices: 21.8 us -> 26.1 us
  Pallas kernels: 40.4 us -> 37.6 us
    all_to_all x2 -> x1, blocking collectives: 52.3 us -> 30 us  [exchange(): return lax.all_to_all(blocks, ('tcol', 'line'), 0, 0, tiled=True)]
    ppermute x3, waiting for transfers between devices: 28.6 us -> 49.4 us  [swap(): return lax.ppermute(array, 'half', [(0, 1), (1, 0)])]
    all_to_all x4 -> x5, starting transfers between devices: 16.3 us -> 23.5 us  [exchange(): return lax.all_to_all(blocks, ('tcol', 'line'), 0, 0, tiled=True)]
    all_to_all x4 -> x5, waiting for transfers between devices: 64.8 us -> 60.9 us  [exchange(): return lax.all_to_all(blocks, ('tcol', 'line'), 0, 0, tiled=True)]
    ppermute x3, starting transfers between devices: 5.51 us -> 2.6 us  [swap(): return lax.ppermute(array, 'half', [(0, 1), (1, 0)])]
    unnamed x38 -> x36, local copies, waits for them, and re-layouts: 14.2 us -> 12.4 us
  transfers between devices with their start and end apart: 7 -> 8, of which waited for: 6 -> 5; matrix products, arithmetic and copies ran while one was open for 2% -> 2% of each run, Pallas kernels for 13% -> 8%
where the time goes in v7:
time: 224 us; the launch traced here: 223 us
  waiting for transfers between devices  110 us (49%)
  Pallas kernels  37.6 us (17%)
  blocking collectives  30 us (13%)
  starting transfers between devices  26.1 us (12%)
  local copies, waits for them, and re-layouts  14.7 us (7%)
  other arithmetic  3.16 us (1%)
    all_to_all x5, waiting for transfers between devices, exchange(): return lax.all_to_all(blocks, ('tcol', 'line'), 0, 0, tiled=True)  60.9 us
    ppermute x3, waiting for transfers between devices, swap(): return lax.ppermute(array, 'half', [(0, 1), (1, 0)])  49.4 us
    all_to_all x1, blocking collectives, exchange(): return lax.all_to_all(blocks, ('tcol', 'line'), 0, 0, tiled=True)  30 us
    all_to_all x5, starting transfers between devices, exchange(): return lax.all_to_all(blocks, ('tcol', 'line'), 0, 0, tiled=True)  23.5 us
    unnamed x36, local copies, waits for them, and re-layouts  12.4 us
    pallas_call x1, Pallas kernels, to_sigma(): pl.pallas_call(functools.partial(sigma_kernel, norm_factor, parts), out_s...  11.9 us
    pallas_call x2, Pallas kernels, make_rights(): pl.pallas_call(functools.partial(rights_kernel, rows), grid=(steps,), out...  6.05 us
    pallas_call x1, Pallas kernels, volterra(): pl.pallas_call(functools.partial(volterra_kernel, rows), grid=(STEPS,), o...  4.99 us
  transfers between devices with their start and end apart: 8, of which 5 were waited for; matrix products, arithmetic and copies ran while one was open for 2% of the time, Pallas kernels for 8%

profile of v7, /device:TPU:0, one launch (start us, length us, event | category | flops | bytes accessed | tf_op | source)
XLA Modules:
  0.0 223.4 jit_solution(3068983097291597331)
XLA Ops:
  0.6 0.0 copy-start.3
  0.6 1.2 copy-done.3
  1.9 1.2 copy-done.5
  3.1 0.9 spread.2
  4.0 0.0 copy-start.9
  4.0 1.0 copy-done.9
  5.0 6.3 %all-to-all-start = ((bf16[16,256,128]{2,1,0:T(8,128)(2,1)}), bf16[16,256,128]{2,1,0:T(8,128)(2,1)S(1)}, u32[]{:S(2)}, u32[]{:S(2)}) async-start(bf16[16,256,128]{2,1,0:T(8,128)(2,1)} %bitcast.13), calls=%async_computation | async-start | bytes 2097152 | tf_op jit(solution)/shard_map/all_to_all | solution.py:643
  11.3 0.0 copy-start.17
  11.3 0.0 copy-done.4
  11.3 0.0 copy-done.6
  11.3 0.9 spread.3
  12.2 0.0 copy-start.7
  12.2 1.0 copy-done.7
  13.8 0.1 fusion.4
  13.9 0.1 dynamic_slice.20
  14.0 0.1 dynamic_slice.19
  14.0 0.0 copy-done.17
  14.0 0.1 copy.9.column_ref
  14.2 4.5 %make_tables.1 = (bf16[1024,1024]{1,0:T(8,128)(2,1)S(1)}, bf16[1024,1024]{1,0:T(8,128)(2,1)S(1)}) custom-call(s32[512,1]{1,0:T(8,128)S(1)} %copy.9.column_ref), custom_call_target="tpu_custom_call" | custom-call | tf_op jit(solution)/shard_map/make_tables/pallas_call | solution.py:326
  18.7 0.0 copy-start.8
  18.8 1.4 copy-done.8
  20.1 1.4 copy-done.13
  21.5 4.0 %to_sites.1.refs_2_ = bf16[1024,1024]{1,0:T(8,128)(2,1)S(1)} custom-call(bf16[2,8,64,512]{3,2,1,0:T(8,128)(2,1)S(1)} %copy-done.4, bf16[2,8,64,512]{3,2,1,0:T(8,128)(2,1)S(1)} %copy-done.6, bf16[1024,1024]{1,0:T(8,128)(2,1)} %copy-done.8), custom_call_target="tpu_custom_call" | custom-call | tf_op jit(solution)/shard_map/to_sites/pallas_call | solution.py:356
  25.5 0.0 copy-start
  25.5 1.3 copy-done
  26.8 0.1 pad_maximum_fusion.1
  26.9 0.7 broadcast_multiply_fusion.refs_3_.refs_5_
  27.6 0.0 all-to-all-done.refs_1_.own
  27.6 1.0 copy-done.1
  28.5 5.2 %all-to-all-start.1 = ((bf16[16,256,128]{2,1,0:T(8,128)(2,1)}), bf16[16,256,128]{2,1,0:T(8,128)(2,1)S(1)}, u32[]{:S(2)}, u32[]{:S(2)}) async-start(bf16[16,256,128]{2,1,0:T(8,128)(2,1)} %gate.2), calls=%async_computation.1 | async-start | bytes 2097152 | tf_op jit(solution)/shard_map/all_to_all | solution.py:643
  33.8 0.0 copy-done.2
  33.8 0.9 dynamic-slice_bitcast_fusion.1
  34.7 2.6 %collective-permute-start = (bf16[8,256,128]{2,1,0:T(8,128)(2,1)S(1)}, bf16[8,256,128]{2,1,0:T(8,128)(2,1)S(1)}, u32[]{:S(2)}, u32[]{:S(2)}) collective-permute-start(bf16[8,256,128]{2,1,0:T(8,128)(2,1)S(1)} %get-tuple-element.7), channel_id=1, source_target_pairs={{0,16},{16,0},{1,17},{17,1},{2,18},{18,2},{3,19},{19,3},{4,20},{20... | collective-permute-start | bytes 1572872 | tf_op jit(solution)/shard_map/ppermute | solution.py:649
  37.3 23.9 %all-to-all-done.1.rest_0_.own = bf16[16,256,128]{2,1,0:T(8,128)(2,1)S(1)} async-done(((bf16[16,256,128]{2,1,0:T(8,128)(2,1)}), bf16[16,256,128]{2,1,0:T(8,128)(2,1)S(1)}, u32[]{:S(2)}, u32[]{:S(2)}) %all-to-all-start.1) | async-done | bytes 1048608 | tf_op jit(solution)/shard_map/all_to_all | solution.py:643
  61.2 1.1 dynamic-slice_bitcast_fusion
  62.3 0.0 collective-permute-start.1
  62.3 0.0 collective-permute-done.far.near_ref
  62.3 0.4 to_crossed.2.rest_1_
  62.6 0.0 copy-start.11
  62.7 1.0 copy-done.11
  63.6 0.0 copy-done.14
  63.6 3.7 %all-to-all-start.2 = ((bf16[16,256,128]{2,1,0:T(8,128)(2,1)}), bf16[16,256,128]{2,1,0:T(8,128)(2,1)S(1)}, u32[]{:S(2)}, u32[]{:S(2)}) async-start(bf16[16,256,128]{2,1,0:T(8,128)(2,1)} %copy-done.11), calls=%async_computation.2 | async-start | bytes 2097152 | tf_op jit(solution)/shard_map/all_to_all | solution.py:643
  67.3 0.0 copy-start.12
  67.3 2.4 %pad_maximum_fusion.refs_0_ = bf16[2,8,256,128]{3,2,1,0:T(8,128)(2,1)} fusion(bf16[1,8,256,128]{3,2,1,0:T(8,128)(2,1)} %get-tuple-element.8, bf16[1,8,256,128]{3,2,1,0:T(8,128)(2,1)} %get-tuple-element.6), kind=kLoop, calls=%fused_computation | loop fusion | flops 524288 | bytes 2097152 | tf_op jit(solution)/shard_map/stack | solution.py:680
  69.7 15.9 %collective-permute-done.1.far.near_ref = bf16[8,256,128]{2,1,0:T(8,128)(2,1)} collective-permute-done((bf16[8,256,128]{2,1,0:T(8,128)(2,1)}, bf16[8,256,128]{2,1,0:T(8,128)(2,1)}, u32[]{:S(2)}, u32[]{:S(2)}) %collective-permute-start.1) | collective-permute-done | bytes 524320 | tf_op jit(solution)/shard_map/ppermute | solution.py:649
  85.6 0.0 copy-done.12
  85.6 1.4 to_crossed.3.refs_1_
  87.0 0.0 copy-start.10
  87.0 1.0 copy-done.10
  88.0 0.0 collective-permute-start.2
  88.0 10.8 %all-to-all-done.2 = bf16[16,256,128]{2,1,0:T(8,128)(2,1)S(1)} async-done(((bf16[16,256,128]{2,1,0:T(8,128)(2,1)}), bf16[16,256,128]{2,1,0:T(8,128)(2,1)S(1)}, u32[]{:S(2)}, u32[]{:S(2)}) %all-to-all-start.2) | async-done | bytes 1048608 | tf_op jit(solution)/shard_map/all_to_all | solution.py:643
  98.7 4.5 %all-to-all-start.3 = ((bf16[16,256,128]{2,1,0:T(8,128)(2,1)}), bf16[16,256,128]{2,1,0:T(8,128)(2,1)}, u32[]{:S(2)}, u32[]{:S(2)}) async-start(bf16[16,256,128]{2,1,0:T(8,128)(2,1)} %copy-done.10), calls=%async_computation.3 | async-start | bytes 2097152 | tf_op jit(solution)/shard_map/all_to_all | solution.py:643
  103.3 33.5 %collective-permute-done.2.away_ref = bf16[2,8,256,128]{3,2,1,0:T(8,128)(2,1)} collective-permute-done((bf16[2,8,256,128]{3,2,1,0:T(8,128)(2,1)}, bf16[2,8,256,128]{3,2,1,0:T(8,128)(2,1)}, u32[]{:S(2)}, u32[]{:S(2)}) %collective-permute-start.2) | collective-permute-done | bytes 1048608 | tf_op jit(solution)/shard_map/ppermute | solution.py:649
  136.7 1.0 copy-done.15
  137.8 2.9 %make_rights.2.rest_0_ = bf16[32,384,256]{2,1,0:T(8,128)(2,1)} custom-call(s32[1]{0:T(128)} %bitcast.half_ref, bf16[16,256,128]{2,1,0:T(8,128)(2,1)S(1)} %copy-done.2, bf16[8,256,128]{2,1,0:T(8,128)(2,1)S(1)} %copy-done.15, bf16[2,8,256,128]{3,2,1,0:T(8,128)(2,1)} %collective-permute-done.2.away_ref), custom_call_target="tpu_custom_call" | custom-call | flops 99999997952 | bytes 1048576 | tf_op jit(solution)/shard_map/make_rights/pallas_call | solution.py:529
  140.7 0.0 all-to-all-done.3
  140.7 0.0 copy-done.16
  140.7 11.9 %to_sigma.1 = bf16[16,512,128]{2,1,0:T(8,128)(2,1)} custom-call(bf16[4096,128]{1,0:T(8,128)(2,1)S(1)} %bitcast.14, bf16[4096,128]{1,0:T(8,128)(2,1)} %bitcast.6.refs_1_, bf16[1024,1024]{1,0:T(8,128)(2,1)} %copy-done, bf16[1024,1024]{1,0:T(8,128)(2,1)} %copy-done.8, bf16[1024,1024]{1,0:T(8,128)(2,1)} %copy-done.13, f32[8,128]{1,0:T(8,128)S(1)} %copy-done.16), custom_call_target="tpu_custom_call" | custom-call | tf_op jit(solution)/shard_map/to_sigma/pallas_call | solution.py:466
  152.7 3.8 %all-to-all-start.4 = ((bf16[16,512,128]{2,1,0:T(8,128)(2,1)}), bf16[16,512,128]{2,1,0:T(8,128)(2,1)S(1)}, u32[]{:S(2)}, u32[]{:S(2)}) async-start(bf16[16,512,128]{2,1,0:T(8,128)(2,1)} %to_sigma.1), calls=%async_computation.4 | async-start | bytes 4194304 | tf_op jit(solution)/shard_map/all_to_all | solution.py:643
  156.4 3.1 %make_rights.3.rights = bf16[32,384,256]{2,1,0:T(8,128)(2,1)} custom-call(s32[1]{0:T(128)} %bitcast.half_ref, bf16[16,256,128]{2,1,0:T(8,128)(2,1)S(1)} %all-to-all-done.1.rest_0_.own, bf16[8,256,128]{2,1,0:T(8,128)(2,1)} %collective-permute-done.1.far.near_ref, ...), custom_call_target="tpu_custom_call", output_to_operand_aliasing={{}: (4, {})} | custom-call | flops 99999997952 | bytes 1048576 | tf_op jit(solution)/shard_map/make_rights/pallas_call | solution.py:529
  159.5 26.2 %all-to-all-done.4.sigma = bf16[16,512,128]{2,1,0:T(8,128)(2,1)S(1)} async-done(((bf16[16,512,128]{2,1,0:T(8,128)(2,1)}), bf16[16,512,128]{2,1,0:T(8,128)(2,1)S(1)}, u32[]{:S(2)}, u32[]{:S(2)}) %all-to-all-start.4) | async-done | bytes 2097184 | tf_op jit(solution)/shard_map/all_to_all | solution.py:643
  185.8 5.0 %volterra.1 = bf16[16,512,128]{2,1,0:T(8,128)(2,1)S(1)} custom-call(s32[1]{0:T(128)} %bitcast.half_ref, bf16[16,512,128]{2,1,0:T(8,128)(2,1)S(1)} %all-to-all-done.4.sigma, bf16[32,384,256]{2,1,0:T(8,128)(2,1)} %make_rights.3.rights), custom_call_target="tpu_custom_call" | custom-call | tf_op jit(solution)/shard_map/volterra/pallas_call | solution.py:617
  190.8 30.0 %all_to_all.30.blocks_ref = bf16[16,512,128]{2,1,0:T(8,128)(2,1)S(1)} all-to-all(bf16[16,512,128]{2,1,0:T(8,128)(2,1)S(1)} %volterra.1), channel_id=1, replica_groups=mesh['half'=2,'line'=8,'tcol'=2] {'tcol','line'}, dimensions={0} | all-to-all | bytes 4194304 | tf_op jit(solution)/shard_map/all_to_all | solution.py:643
  220.8 2.6 %collect.1 = (bf16[2,8,64,512]{3,2,1,0:T(8,128)(2,1)}, bf16[2,8,64,512]{3,2,1,0:T(8,128)(2,1)}) custom-call(bf16[16,512,128]{2,1,0:T(8,128)(2,1)S(1)} %all_to_all.30.blocks_ref), custom_call_target="tpu_custom_call" | custom-call | tf_op jit(solution)/shard_map/collect/pallas_call | solution.py:294
  (11 shorter events, 0.0 us)
Async XLA Ops:
  0.6 1.2 copy-start.3
  1.9 1.2 copy-start.5
  3.1 8.2 %copy-start.4 = (bf16[2,8,64,512]{3,2,1,0:T(8,128)(2,1)S(1)}, bf16[2,8,64,512]{3,2,1,0:T(8,128)(2,1)}, u32[]{:S(2)}) copy-start(bf16[2,8,64,512]{3,2,1,0:T(8,128)(2,1)} %lesser.5) | copy-start | bytes 3145732
  3.1 8.2 %copy-start.6 = (bf16[2,8,64,512]{3,2,1,0:T(8,128)(2,1)S(1)}, bf16[2,8,64,512]{3,2,1,0:T(8,128)(2,1)}, u32[]{:S(2)}) copy-start(bf16[2,8,64,512]{3,2,1,0:T(8,128)(2,1)} %greater.5) | copy-start | bytes 3145732
  4.0 1.0 copy-start.9
  5.0 22.6 %all-to-all-start = ((bf16[16,256,128]{2,1,0:T(8,128)(2,1)}), bf16[16,256,128]{2,1,0:T(8,128)(2,1)S(1)}, u32[]{:S(2)}, u32[]{:S(2)}) async-start(bf16[16,256,128]{2,1,0:T(8,128)(2,1)} %bitcast.13), calls=%async_computation | async-start | bytes 2097152 | tf_op jit(solution)/shard_map/all_to_all | solution.py:643
  11.3 2.8 %copy-start.17 = (s32[512]{0:T(512)S(1)}, s32[512]{0:T(512)}, u32[]{:S(2)}) copy-start(s32[512]{0:T(512)} %param.6) | copy-start | bytes 6148
  12.2 1.0 copy-start.7
  18.7 1.4 copy-start.8
  20.1 1.4 copy-start.13
  25.5 1.4 copy-start
  27.6 1.0 copy-start.1
  28.5 5.3 %copy-start.2 = (bf16[16,256,128]{2,1,0:T(8,128)(2,1)S(1)}, bf16[16,256,128]{2,1,0:T(8,128)(2,1)}, u32[]{:S(2)}) copy-start(bf16[16,256,128]{2,1,0:T(8,128)(2,1)} %copy-done.1) | copy-start | bytes 3145732
  28.5 32.7 %all-to-all-start.1 = ((bf16[16,256,128]{2,1,0:T(8,128)(2,1)}), bf16[16,256,128]{2,1,0:T(8,128)(2,1)S(1)}, u32[]{:S(2)}, u32[]{:S(2)}) async-start(bf16[16,256,128]{2,1,0:T(8,128)(2,1)} %gate.2), calls=%async_computation.1 | async-start | bytes 2097152 | tf_op jit(solution)/shard_map/all_to_all | solution.py:643
  34.7 27.6 %collective-permute-start = (bf16[8,256,128]{2,1,0:T(8,128)(2,1)S(1)}, bf16[8,256,128]{2,1,0:T(8,128)(2,1)S(1)}, u32[]{:S(2)}, u32[]{:S(2)}) collective-permute-start(bf16[8,256,128]{2,1,0:T(8,128)(2,1)S(1)} %get-tuple-element.7), channel_id=1, source_target_pairs={{0,16},{16,0},{1,17},{17,1},{2,18},{18,2},{3,19},{19,3},{4,20},{20... | collective-permute-start | bytes 1572872 | tf_op jit(solution)/shard_map/ppermute | solution.py:649
  62.3 23.3 %collective-permute-start.1 = (bf16[8,256,128]{2,1,0:T(8,128)(2,1)}, bf16[8,256,128]{2,1,0:T(8,128)(2,1)}, u32[]{:S(2)}, u32[]{:S(2)}) collective-permute-start(bf16[8,256,128]{2,1,0:T(8,128)(2,1)} %get-tuple-element.9), channel_id=1, source_target_pairs={{0,16},{16,0},{1,17},{17,1},{2,18},{18,2},{3,19},{19,3},{4,20},{20... | collective-permute-start | bytes 1572872 | tf_op jit(solution)/shard_map/ppermute | solution.py:649
  62.3 1.4 copy-start.14
  62.6 1.0 copy-start.11
  63.6 35.1 %all-to-all-start.2 = ((bf16[16,256,128]{2,1,0:T(8,128)(2,1)}), bf16[16,256,128]{2,1,0:T(8,128)(2,1)S(1)}, u32[]{:S(2)}, u32[]{:S(2)}) async-start(bf16[16,256,128]{2,1,0:T(8,128)(2,1)} %copy-done.11), calls=%async_computation.2 | async-start | bytes 2097152 | tf_op jit(solution)/shard_map/all_to_all | solution.py:643
  67.3 18.3 %copy-start.12 = (bf16[16,256,128]{2,1,0:T(8,128)(2,1)S(1)}, bf16[16,256,128]{2,1,0:T(8,128)(2,1)}, u32[]{:S(2)}) copy-start(bf16[16,256,128]{2,1,0:T(8,128)(2,1)} %copy-done.11) | copy-start | bytes 3145732
  87.0 1.0 copy-start.10
  88.0 48.8 %collective-permute-start.2 = (bf16[2,8,256,128]{3,2,1,0:T(8,128)(2,1)}, bf16[2,8,256,128]{3,2,1,0:T(8,128)(2,1)}, u32[]{:S(2)}, u32[]{:S(2)}) collective-permute-start(bf16[2,8,256,128]{3,2,1,0:T(8,128)(2,1)} %gate.3), channel_id=1, source_target_pairs={{0,16},{16,0},{1,17},{17,1},{2,18},{18,2},{3,19},{19,3},{4,20},{20... | collective-permute-start | bytes 3145736 | tf_op jit(solution)/shard_map/ppermute | solution.py:649
  98.7 42.0 %all-to-all-start.3 = ((bf16[16,256,128]{2,1,0:T(8,128)(2,1)}), bf16[16,256,128]{2,1,0:T(8,128)(2,1)}, u32[]{:S(2)}, u32[]{:S(2)}) async-start(bf16[16,256,128]{2,1,0:T(8,128)(2,1)} %copy-done.10), calls=%async_computation.3 | async-start | bytes 2097152 | tf_op jit(solution)/shard_map/all_to_all | solution.py:643
  136.7 1.0 copy-start.15
  137.8 3.0 %copy-start.16 = (f32[8,128]{1,0:T(8,128)S(1)}, f32[8,128]{1,0:T(8,128)}, u32[]{:S(2)}) copy-start(f32[8,128]{1,0:T(8,128)} %broadcast_multiply_fusion.refs_3_.refs_5_) | copy-start | bytes 12292
  152.7 33.1 %all-to-all-start.4 = ((bf16[16,512,128]{2,1,0:T(8,128)(2,1)}), bf16[16,512,128]{2,1,0:T(8,128)(2,1)S(1)}, u32[]{:S(2)}, u32[]{:S(2)}) async-start(bf16[16,512,128]{2,1,0:T(8,128)(2,1)} %to_sigma.1), calls=%async_computation.4 | async-start | bytes 4194304 | tf_op jit(solution)/shard_map/all_to_all | solution.py:643

commit v8 on v7

--- a/solution.py
+++ b/solution.py
@@ -413,25 +413,58 @@
     )(array, *after)
 
 
+def mirrored_term(table, part, parts, read, pair, count):
+    momenta = table.shape[1] // 2
+    wide = momenta // parts
+    rights = []
+    for t in (2 * pair, 2 * pair + 1):
+        real = read[pl.ds(t, wide, stride=2 * count), :]
+        imaginary = -read[pl.ds(count + t, wide, stride=2 * count), :]
+        rights.append(jnp.concatenate([real, imaginary], axis=0).astype(BF16))
+    columns = jnp.concatenate(
+        [
+            table[:, part * wide : (part + 1) * wide],
+            table[:, momenta + part * wide : momenta + (part + 1) * wide],
+        ],
+        axis=1,
+    )
+    return jnp.dot(columns, jnp.concatenate(rights, axis=1), preferred_element_type=F32)
+
+
+def mirror_kernel(part, parts, count, crossed, table, out, read):
+    read[...] = crossed[...].astype(F32)
+    wide = 2 * crossed.shape[1]
+    for pair in range(count // 2):
+        out[:, pair * wide : (pair + 1) * wide] = mirrored_term(
+            table, part, parts, read, pair, count
+        )
+
+
+def to_mirror(crossed, table, part, parts, count):
+    lines, lanes = crossed.shape
+    return pl.pallas_call(
+        functools.partial(mirror_kernel, part, parts, count),
+        out_shape=jax.ShapeDtypeStruct((table.shape[0], count * lanes), F32),
+        in_specs=whole(2),
+        out_specs=whole(1)[0],
+        scratch_shapes=[pltpu.VMEM((lines, lanes), F32)],
+        compiler_params=vmem_params(),
+        name="to_mirror",
+    )(crossed, table)
+
+
 def sigma_kernel(norm_factor, parts, *refs):
-    crossed = refs[:parts]
-    sites, table, inverse, coupling, out, read, written = refs[parts:]
+    mirrors = refs[: parts - 1]
+    crossed, sites, table, inverse, coupling, out, read, written = refs[parts - 1 :]
     count = coupling.shape[0]
     momenta = table.shape[0] // 2
-    for part in range(parts):
-        lines = crossed[part].shape[0]
-        read[part * lines : (part + 1) * lines] = crossed[part][...].astype(F32)
+    read[...] = crossed[...].astype(F32)
     for pair in range(count // 2):
-        rights = []
-        for t in (2 * pair, 2 * pair + 1):
-            real = read[pl.ds(t, momenta, stride=2 * count), :]
-            imaginary = -read[pl.ds(count + t, momenta, stride=2 * count), :]
-            rights.append(jnp.concatenate([real, imaginary], axis=0).astype(BF16))
-        other = jnp.dot(
-            table[...], jnp.concatenate(rights, axis=1), preferred_element_type=F32
-        )
+        span = slice(2 * pair * LANES, 2 * (pair + 1) * LANES)
+        other = mirrored_term(table, parts - 1, parts, read, pair, count)
+        for mirror in mirrors:
+            other = other + mirror[:, span]
         other = (other * norm_factor).astype(BF16).astype(F32)
-        span = slice(2 * pair * LANES, 2 * (pair + 1) * LANES)
         self_real, self_imaginary = second_born(
             sites[:momenta, span].astype(F32),
             sites[momenta:, span].astype(F32),
@@ -460,18 +493,18 @@
             ].astype(BF16)
 
 
-def to_sigma(crossed, sites, table, inverse, coupling, norm_factor, blocks):
-    parts = len(crossed)
-    lines, lanes = crossed[0].shape
+def to_sigma(mirrors, crossed, sites, table, inverse, coupling, norm_factor, blocks):
+    parts = len(mirrors) + 1
+    lines, lanes = crossed.shape
     return pl.pallas_call(
         functools.partial(sigma_kernel, norm_factor, parts),
         out_shape=jax.ShapeDtypeStruct((blocks, parts * lines // blocks, lanes), BF16),
         in_specs=whole(parts + 4),
         out_specs=whole(1)[0],
-        scratch_shapes=[pltpu.VMEM((parts * lines, lanes), F32)] * 2,
+        scratch_shapes=[pltpu.VMEM((lines, lanes), F32), pltpu.VMEM((parts * lines, lanes), F32)],
         compiler_params=vmem_params(),
         name="to_sigma",
-    )(*crossed, sites, table, inverse, coupling)
+    )(*mirrors, crossed, sites, table, inverse, coupling)
 
 
 def rights_kernel(rows, half_ref, own, near_ref, away_ref, *rest):
@@ -540,7 +573,7 @@
         out_specs=pl.BlockSpec(
             (momenta, 3 * lanes, 2 * lanes), lambda p: (part * steps + p, 0, 0)
         ),
-        input_output_aliases={4: 0} if before else {},
+        input_output_aliases={4: 0} if part > 0 else {},
         compiler_params=vmem_params(),
         cost_estimate=weight(),
         name="make_rights",
@@ -680,22 +713,19 @@
     kept = jnp.stack(
         [lax.dynamic_slice_in_dim(blocks, half * lines, lines) for blocks in own]
     )
-    far_away = swap(gate(kept, sent[-1:]))
-    sigma = exchange(
-        to_sigma(
-            [blocks.reshape(-1, 2 * cols) for blocks in crossed],
-            sites,
-            table,
-            inverse,
-            coupling,
-            norm_factor,
-            group,
-        )
-    )
+    far_away = swap(gate(kept, sent[-1:] + crossed[:-1]))
+    flat = [blocks.reshape(-1, 2 * cols) for blocks in crossed]
+    mirrors = [to_mirror(flat[part], table, part, PARTS, rows) for part in range(PARTS - 1)]
+    sigma_rows = to_sigma(
+        mirrors, flat[-1], sites, table, inverse, coupling, norm_factor, group
+    )
+    sigma = exchange(sigma_rows)
     rights = []
     for part in range(PARTS):
         rights = [
-            make_rights(half_at, own[part], far_near[part], far_away, rows, part, rights)
+            make_rights(
+                half_at, own[part], far_near[part], far_away, rows, part, rights + [sigma_rows]
+            )
         ]
     returned = exchange(volterra(half_at, sigma, rights[0], rows))
     return collect(returned, green_lesser.shape)

time: 224 us -> 216 us (0.964)
  waiting for transfers between devices: 110 us -> 91.8 us
  starting transfers between devices: 26.1 us -> 30.9 us
  Pallas kernels: 37.6 us -> 40.7 us
  local copies, waits for them, and re-layouts: 14.7 us -> 17.8 us
    ppermute x3, waiting for transfers between devices: 49.4 us -> 25.5 us  [swap(): return lax.ppermute(array, 'half', [(0, 1), (1, 0)])]
    all_to_all x5, waiting for transfers between devices: 60.9 us -> 66.4 us  [exchange(): return lax.all_to_all(blocks, ('tcol', 'line'), 0, 0, tiled=True)]
    ppermute x3, starting transfers between devices: 2.6 us -> 6.6 us  [swap(): return lax.ppermute(array, 'half', [(0, 1), (1, 0)])]
    pallas_call x0 -> x1, Pallas kernels: none -> 3.47 us  [to_mirror(): pl.pallas_call(functools.partial(mirror_kernel, part, parts, count), out_...]
    unnamed x36 -> x52, local copies, waits for them, and re-layouts: 12.4 us -> 15.5 us
  transfers between devices with their start and end apart: 8 -> 8, of which waited for: 5 -> 6; matrix products, arithmetic and copies ran while one was open for 2% -> 2% of each run, Pallas kernels for 8% -> 15%
where the time goes in v8:
time: 216 us; the launch traced here: 215 us
  waiting for transfers between devices  91.8 us (42%)
  Pallas kernels  40.7 us (19%)
  starting transfers between devices  30.9 us (14%)
  blocking collectives  30 us (14%)
  local copies, waits for them, and re-layouts  17.8 us (8%)
    all_to_all x5, waiting for transfers between devices, exchange(): return lax.all_to_all(blocks, ('tcol', 'line'), 0, 0, tiled=True)  66.4 us
    all_to_all x1, blocking collectives, exchange(): return lax.all_to_all(blocks, ('tcol', 'line'), 0, 0, tiled=True)  30 us
    ppermute x3, waiting for transfers between devices, swap(): return lax.ppermute(array, 'half', [(0, 1), (1, 0)])  25.5 us
    all_to_all x5, starting transfers between devices, exchange(): return lax.all_to_all(blocks, ('tcol', 'line'), 0, 0, tiled=True)  24.3 us
    unnamed x52, local copies, waits for them, and re-layouts  15.5 us
    pallas_call x1, Pallas kernels, to_sigma(): pl.pallas_call(functools.partial(sigma_kernel, norm_factor, parts), out_s...  11.2 us
    ppermute x3, starting transfers between devices, swap(): return lax.ppermute(array, 'half', [(0, 1), (1, 0)])  6.6 us
    pallas_call x2, Pallas kernels, make_rights(): pl.pallas_call(functools.partial(rights_kernel, rows), grid=(steps,), out...  6.03 us
  transfers between devices with their start and end apart: 8, of which 6 were waited for; matrix products, arithmetic and copies ran while one was open for 2% of the time, Pallas kernels for 15%

profile of v8, /device:TPU:0, one launch (start us, length us, event | category | flops | bytes accessed | tf_op | source)
XLA Modules:
  0.0 214.7 jit_solution(13042202742064862815)
XLA Ops:
  0.6 0.0 copy-start.6
  0.6 1.2 copy-done.6
  1.9 1.2 copy-done.8
  3.1 0.9 spread.2
  4.0 0.0 copy-start.15
  4.0 1.0 copy-done.15
  5.0 6.3 %all-to-all-start = ((bf16[16,256,128]{2,1,0:T(8,128)(2,1)}), bf16[16,256,128]{2,1,0:T(8,128)(2,1)S(1)}, u32[]{:S(2)}, u32[]{:S(2)}) async-start(bf16[16,256,128]{2,1,0:T(8,128)(2,1)} %bitcast.14), calls=%async_computation | async-start | bytes 2097152 | tf_op jit(solution)/shard_map/all_to_all | solution.py:676
  11.3 0.0 copy-start.25
  11.3 0.0 copy-done.7
  11.3 0.0 copy-done.9
  11.3 0.9 spread.3
  12.2 0.0 copy-start.10
  12.2 1.0 copy-done.10
  13.8 0.1 fusion.4
  13.9 0.1 dynamic_slice.19
  14.0 0.1 dynamic_slice.20
  14.0 0.0 copy-done.25
  14.0 0.1 copy.9.column_ref
  14.2 4.5 %make_tables.1 = (bf16[1024,1024]{1,0:T(8,128)(2,1)S(1)}, bf16[1024,1024]{1,0:T(8,128)(2,1)S(1)}) custom-call(s32[512,1]{1,0:T(8,128)S(1)} %copy.9.column_ref), custom_call_target="tpu_custom_call" | custom-call | tf_op jit(solution)/shard_map/make_tables/pallas_call | solution.py:326
  18.7 0.0 copy-start
  18.8 1.4 copy-done
  20.1 1.4 copy-done.19
  21.5 3.9 %to_sites.1.refs_2_ = bf16[1024,1024]{1,0:T(8,128)(2,1)S(1)} custom-call(bf16[2,8,64,512]{3,2,1,0:T(8,128)(2,1)S(1)} %copy-done.7, bf16[2,8,64,512]{3,2,1,0:T(8,128)(2,1)S(1)} %copy-done.9, bf16[1024,1024]{1,0:T(8,128)(2,1)} %copy-done), custom_call_target="tpu_custom_call" | custom-call | tf_op jit(solution)/shard_map/to_sites/pallas_call | solution.py:356
  25.5 0.0 copy-start.2
  25.5 1.4 copy-done.2
  26.9 0.1 pad_maximum_fusion.1
  26.9 0.7 broadcast_multiply_fusion.refs_3_.refs_5_
  27.6 0.0 all-to-all-done.refs_1_.own
  27.6 1.0 copy-done.4
  28.6 5.2 %all-to-all-start.1 = ((bf16[16,256,128]{2,1,0:T(8,128)(2,1)}), bf16[16,256,128]{2,1,0:T(8,128)(2,1)S(1)}, u32[]{:S(2)}, u32[]{:S(2)}) async-start(bf16[16,256,128]{2,1,0:T(8,128)(2,1)} %gate.2), calls=%async_computation.1 | async-start | bytes 2097152 | tf_op jit(solution)/shard_map/all_to_all | solution.py:676
  33.8 0.0 copy-done.5
  33.9 0.9 dynamic-slice_bitcast_fusion.1
  34.7 2.6 %collective-permute-start = (bf16[8,256,128]{2,1,0:T(8,128)(2,1)S(1)}, bf16[8,256,128]{2,1,0:T(8,128)(2,1)S(1)}, u32[]{:S(2)}, u32[]{:S(2)}) collective-permute-start(bf16[8,256,128]{2,1,0:T(8,128)(2,1)S(1)} %get-tuple-element.7), channel_id=1, source_target_pairs={{0,16},{16,0},{1,17},{17,1},{2,18},{18,2},{3,19},{19,3},{4,20},{20... | collective-permute-start | bytes 1572872 | tf_op jit(solution)/shard_map/ppermute | solution.py:682
  37.3 23.9 %all-to-all-done.1.rest_0_.own = bf16[16,256,128]{2,1,0:T(8,128)(2,1)S(1)} async-done(((bf16[16,256,128]{2,1,0:T(8,128)(2,1)}), bf16[16,256,128]{2,1,0:T(8,128)(2,1)S(1)}, u32[]{:S(2)}, u32[]{:S(2)}) %all-to-all-start.1) | async-done | bytes 1048608 | tf_op jit(solution)/shard_map/all_to_all | solution.py:676
  61.3 1.1 dynamic-slice_bitcast_fusion
  62.4 0.0 collective-permute-start.1
  62.4 0.0 collective-permute-done.far.near_ref
  62.4 0.4 to_crossed.2.rest_1_
  62.8 0.0 copy-start.17
  62.8 1.0 copy-done.17
  63.8 3.7 %all-to-all-start.2 = ((bf16[16,256,128]{2,1,0:T(8,128)(2,1)}), bf16[16,256,128]{2,1,0:T(8,128)(2,1)S(1)}, u32[]{:S(2)}, u32[]{:S(2)}) async-start(bf16[16,256,128]{2,1,0:T(8,128)(2,1)} %copy-done.17), calls=%async_computation.2 | async-start | bytes 2097152 | tf_op jit(solution)/shard_map/all_to_all | solution.py:676
  67.4 18.3 %collective-permute-done.1.far.near_ref = bf16[8,256,128]{2,1,0:T(8,128)(2,1)} collective-permute-done((bf16[8,256,128]{2,1,0:T(8,128)(2,1)}, bf16[8,256,128]{2,1,0:T(8,128)(2,1)}, u32[]{:S(2)}, u32[]{:S(2)}) %collective-permute-start.1) | collective-permute-done | bytes 524320 | tf_op jit(solution)/shard_map/ppermute | solution.py:682
  85.7 1.2 copy-done.18
  86.9 1.4 to_crossed.3.refs_1_
  88.3 0.0 copy-start.16
  88.4 1.0 copy-done.16
  89.3 5.4 %all-to-all-done.2.refs_2_ = bf16[16,256,128]{2,1,0:T(8,128)(2,1)S(1)} async-done(((bf16[16,256,128]{2,1,0:T(8,128)(2,1)}), bf16[16,256,128]{2,1,0:T(8,128)(2,1)S(1)}, u32[]{:S(2)}, u32[]{:S(2)}) %all-to-all-start.2) | async-done | bytes 1048608 | tf_op jit(solution)/shard_map/all_to_all | solution.py:676
  94.7 4.5 %all-to-all-start.3 = ((bf16[16,256,128]{2,1,0:T(8,128)(2,1)}), bf16[16,256,128]{2,1,0:T(8,128)(2,1)}, u32[]{:S(2)}, u32[]{:S(2)}) async-start(bf16[16,256,128]{2,1,0:T(8,128)(2,1)} %copy-done.16), calls=%async_computation.3 | async-start | bytes 2097152 | tf_op jit(solution)/shard_map/all_to_all | solution.py:676
  99.3 1.1 pad_maximum_fusion.refs_0_
  100.4 4.0 %collective-permute-start.2 = (bf16[2,8,256,128]{3,2,1,0:T(8,128)(2,1)}, bf16[2,8,256,128]{3,2,1,0:T(8,128)(2,1)}, u32[]{:S(2)}, u32[]{:S(2)}) collective-permute-start(bf16[2,8,256,128]{3,2,1,0:T(8,128)(2,1)} %gate.3), channel_id=1, source_target_pairs={{0,16},{16,0},{1,17},{17,1},{2,18},{18,2},{3,19},{19,3},{4,20},{20... | collective-permute-start | bytes 3145736 | tf_op jit(solution)/shard_map/ppermute | solution.py:682
  104.4 1.2 copy-done.12
  105.6 3.5 %to_mirror.1.refs_0_ = f32[1024,1024]{1,0:T(8,128)} custom-call(bf16[4096,128]{1,0:T(8,128)(2,1)S(1)} %bitcast.13, bf16[1024,1024]{1,0:T(8,128)(2,1)S(1)} %copy-done.1), custom_call_target="tpu_custom_call" | custom-call | tf_op jit(solution)/shard_map/to_mirror/pallas_call | solution.py:445
  109.1 17.3 %all-to-all-done.3 = bf16[16,256,128]{2,1,0:T(8,128)(2,1)} async-done(((bf16[16,256,128]{2,1,0:T(8,128)(2,1)}), bf16[16,256,128]{2,1,0:T(8,128)(2,1)}, u32[]{:S(2)}, u32[]{:S(2)}) %all-to-all-start.3) | async-done | bytes 1048608 | tf_op jit(solution)/shard_map/all_to_all | solution.py:676
  126.3 0.0 copy-done.22
  126.3 1.6 copy-done.3
  127.9 11.2 %to_sigma.1.rest_0_.rest_1_ = bf16[16,512,128]{2,1,0:T(8,128)(2,1)} custom-call(f32[1024,1024]{1,0:T(8,128)} %to_mirror.1.refs_0_, bf16[4096,128]{1,0:T(8,128)(2,1)} %bitcast.6.refs_1_, bf16[1024,1024]{1,0:T(8,128)(2,1)S(1)} %copy-done.3, bf16[1024,1024]{1,0:T(8,128)(2,1)} %copy-done, bf16[1024,1024]{1,0:T(8,128)(2,1)} %copy-done.19, f32[8,128]{1,0:T(8,128)S(1)} %copy-done.22), custom_call_target="tpu_custom_call" | custom-call | tf_op jit(solution)/shard_map/to_sigma/pallas_call | solution.py:499
  139.2 4.6 %all-to-all-start.4 = ((bf16[16,512,128]{2,1,0:T(8,128)(2,1)}), bf16[16,512,128]{2,1,0:T(8,128)(2,1)}, u32[]{:S(2)}, u32[]{:S(2)}) async-start(bf16[16,512,128]{2,1,0:T(8,128)(2,1)} %to_sigma.1.rest_0_.rest_1_), calls=%async_computation.4 | async-start | bytes 4194304 | tf_op jit(solution)/shard_map/all_to_all | solution.py:676
  143.8 7.2 %collective-permute-done.2.away_ref = bf16[2,8,256,128]{3,2,1,0:T(8,128)(2,1)} collective-permute-done((bf16[2,8,256,128]{3,2,1,0:T(8,128)(2,1)}, bf16[2,8,256,128]{3,2,1,0:T(8,128)(2,1)}, u32[]{:S(2)}, u32[]{:S(2)}) %collective-permute-start.2) | collective-permute-done | bytes 1048608 | tf_op jit(solution)/shard_map/ppermute | solution.py:682
  151.0 3.0 %make_rights.2.rest_0_ = bf16[32,384,256]{2,1,0:T(8,128)(2,1)} custom-call(s32[1]{0:T(128)} %bitcast.half_ref, bf16[16,256,128]{2,1,0:T(8,128)(2,1)S(1)} %copy-done.5, bf16[8,256,128]{2,1,0:T(8,128)(2,1)S(1)} %copy-done.21, bf16[2,8,256,128]{3,2,1,0:T(8,128)(2,1)} %collective-permute-done.2.away_ref, bf16[16,512,128]{2,1,0:T(8,128)(2,1)} %to_sigma.1.rest_0_.rest_1_), custom_call_target="tpu_custom_call" | custom-call | flops 99999997952 | bytes 1048576 | tf_op jit(solution)/shard_map/make_rights/pallas_call | solution.py:562
  153.9 3.1 %make_rights.3.rights = bf16[32,384,256]{2,1,0:T(8,128)(2,1)} custom-call(s32[1]{0:T(128)} %bitcast.half_ref, bf16[16,256,128]{2,1,0:T(8,128)(2,1)S(1)} %copy-done.14, bf16[8,256,128]{2,1,0:T(8,128)(2,1)} %collective-permute-done.1.far.near_ref, bf16[2,8,256,128]{3,2,1,0:T(8,128)(2,1)} %collective-permute-done.2.away_ref, ...), custom_call_target="tpu_custom_call", output_to_operand_aliasing={{}: (4, {})} | custom-call | flops 99999997952 | bytes 1048576 | tf_op jit(solution)/shard_map/make_rights/pallas_call | solution.py:562
  157.0 19.8 %all-to-all-done.4.sigma = bf16[16,512,128]{2,1,0:T(8,128)(2,1)} async-done(((bf16[16,512,128]{2,1,0:T(8,128)(2,1)}), bf16[16,512,128]{2,1,0:T(8,128)(2,1)}, u32[]{:S(2)}, u32[]{:S(2)}) %all-to-all-start.4) | async-done | bytes 2097184 | tf_op jit(solution)/shard_map/all_to_all | solution.py:676
  176.8 5.3 %volterra.1 = bf16[16,512,128]{2,1,0:T(8,128)(2,1)S(1)} custom-call(s32[1]{0:T(128)} %bitcast.half_ref, bf16[16,512,128]{2,1,0:T(8,128)(2,1)} %all-to-all-done.4.sigma, bf16[32,384,256]{2,1,0:T(8,128)(2,1)} %make_rights.3.rights), custom_call_target="tpu_custom_call" | custom-call | tf_op jit(solution)/shard_map/volterra/pallas_call | solution.py:650
  182.0 30.0 %all_to_all.30.blocks_ref = bf16[16,512,128]{2,1,0:T(8,128)(2,1)S(1)} all-to-all(bf16[16,512,128]{2,1,0:T(8,128)(2,1)S(1)} %volterra.1), channel_id=1, replica_groups=mesh['half'=2,'line'=8,'tcol'=2] {'tcol','line'}, dimensions={0} | all-to-all | bytes 4194304 | tf_op jit(solution)/shard_map/all_to_all | solution.py:676
  212.1 2.6 %collect.1 = (bf16[2,8,64,512]{3,2,1,0:T(8,128)(2,1)}, bf16[2,8,64,512]{3,2,1,0:T(8,128)(2,1)}) custom-call(bf16[16,512,128]{2,1,0:T(8,128)(2,1)S(1)} %all_to_all.30.blocks_ref), custom_call_target="tpu_custom_call" | custom-call | tf_op jit(solution)/shard_map/collect/pallas_call | solution.py:294
  (28 shorter events, 0.0 us)
Async XLA Ops:
  0.6 1.2 copy-start.6
  1.9 1.2 copy-start.8
  3.1 8.2 %copy-start.7 = (bf16[2,8,64,512]{3,2,1,0:T(8,128)(2,1)S(1)}, bf16[2,8,64,512]{3,2,1,0:T(8,128)(2,1)}, u32[]{:S(2)}) copy-start(bf16[2,8,64,512]{3,2,1,0:T(8,128)(2,1)} %lesser.5) | copy-start | bytes 3145732
  3.1 8.2 %copy-start.9 = (bf16[2,8,64,512]{3,2,1,0:T(8,128)(2,1)S(1)}, bf16[2,8,64,512]{3,2,1,0:T(8,128)(2,1)}, u32[]{:S(2)}) copy-start(bf16[2,8,64,512]{3,2,1,0:T(8,128)(2,1)} %greater.5) | copy-start | bytes 3145732
  4.0 1.0 copy-start.15
  5.0 22.6 %all-to-all-start = ((bf16[16,256,128]{2,1,0:T(8,128)(2,1)}), bf16[16,256,128]{2,1,0:T(8,128)(2,1)S(1)}, u32[]{:S(2)}, u32[]{:S(2)}) async-start(bf16[16,256,128]{2,1,0:T(8,128)(2,1)} %bitcast.14), calls=%async_computation | async-start | bytes 2097152 | tf_op jit(solution)/shard_map/all_to_all | solution.py:676
  11.3 2.8 %copy-start.25 = (s32[512]{0:T(512)S(1)}, s32[512]{0:T(512)}, u32[]{:S(2)}) copy-start(s32[512]{0:T(512)} %param.6) | copy-start | bytes 6148
  12.2 1.0 copy-start.10
  18.7 1.4 copy-start
  20.1 1.4 copy-start.19
  25.5 1.4 copy-start.2
  27.6 1.0 copy-start.4
  28.6 5.3 %copy-start.5 = (bf16[16,256,128]{2,1,0:T(8,128)(2,1)S(1)}, bf16[16,256,128]{2,1,0:T(8,128)(2,1)}, u32[]{:S(2)}) copy-start(bf16[16,256,128]{2,1,0:T(8,128)(2,1)} %copy-done.4) | copy-start | bytes 3145732
  28.6 32.7 %all-to-all-start.1 = ((bf16[16,256,128]{2,1,0:T(8,128)(2,1)}), bf16[16,256,128]{2,1,0:T(8,128)(2,1)S(1)}, u32[]{:S(2)}, u32[]{:S(2)}) async-start(bf16[16,256,128]{2,1,0:T(8,128)(2,1)} %gate.2), calls=%async_computation.1 | async-start | bytes 2097152 | tf_op jit(solution)/shard_map/all_to_all | solution.py:676
  34.7 27.7 %collective-permute-start = (bf16[8,256,128]{2,1,0:T(8,128)(2,1)S(1)}, bf16[8,256,128]{2,1,0:T(8,128)(2,1)S(1)}, u32[]{:S(2)}, u32[]{:S(2)}) collective-permute-start(bf16[8,256,128]{2,1,0:T(8,128)(2,1)S(1)} %get-tuple-element.7), channel_id=1, source_target_pairs={{0,16},{16,0},{1,17},{17,1},{2,18},{18,2},{3,19},{19,3},{4,20},{20... | collective-permute-start | bytes 1572872 | tf_op jit(solution)/shard_map/ppermute | solution.py:682
  61.3 24.4 %copy-start.13 = (bf16[16,256,128]{2,1,0:T(8,128)(2,1)}, bf16[16,256,128]{2,1,0:T(8,128)(2,1)S(1)}, u32[]{:S(2)}) copy-start(bf16[16,256,128]{2,1,0:T(8,128)(2,1)S(1)} %all-to-all-done.1.rest_0_.own) | copy-start | bytes 3145732
  62.4 23.3 %collective-permute-start.1 = (bf16[8,256,128]{2,1,0:T(8,128)(2,1)}, bf16[8,256,128]{2,1,0:T(8,128)(2,1)}, u32[]{:S(2)}, u32[]{:S(2)}) collective-permute-start(bf16[8,256,128]{2,1,0:T(8,128)(2,1)} %get-tuple-element.9), channel_id=1, source_target_pairs={{0,16},{16,0},{1,17},{17,1},{2,18},{18,2},{3,19},{19,3},{4,20},{20... | collective-permute-start | bytes 1572872 | tf_op jit(solution)/shard_map/ppermute | solution.py:682
  62.4 1.4 copy-start.20
  62.8 1.0 copy-start.17
  63.8 30.9 %all-to-all-start.2 = ((bf16[16,256,128]{2,1,0:T(8,128)(2,1)}), bf16[16,256,128]{2,1,0:T(8,128)(2,1)S(1)}, u32[]{:S(2)}, u32[]{:S(2)}) async-start(bf16[16,256,128]{2,1,0:T(8,128)(2,1)} %copy-done.17), calls=%async_computation.2 | async-start | bytes 2097152 | tf_op jit(solution)/shard_map/all_to_all | solution.py:676
  85.7 1.2 copy-start.18
  88.3 1.0 copy-start.16
  89.3 9.9 %copy-start.23 = (bf16[1,8,256,128]{3,2,1,0:T(8,128)(2,1)S(1)}, bf16[1,8,256,128]{3,2,1,0:T(8,128)(2,1)}, u32[]{:S(2)}) copy-start(bf16[1,8,256,128]{3,2,1,0:T(8,128)(2,1)} %get-tuple-element.6) | copy-start | bytes 1572868
  89.3 9.9 %copy-start.24 = (bf16[1,8,256,128]{3,2,1,0:T(8,128)(2,1)S(1)}, bf16[1,8,256,128]{3,2,1,0:T(8,128)(2,1)}, u32[]{:S(2)}) copy-start(bf16[1,8,256,128]{3,2,1,0:T(8,128)(2,1)} %get-tuple-element.8) | copy-start | bytes 1572868
  94.7 4.5 %copy-start.11 = (bf16[16,256,128]{2,1,0:T(8,128)(2,1)}, bf16[16,256,128]{2,1,0:T(8,128)(2,1)S(1)}, u32[]{:S(2)}) copy-start(bf16[16,256,128]{2,1,0:T(8,128)(2,1)S(1)} %all-to-all-done.2.refs_2_) | copy-start | bytes 3145732
  94.7 31.6 %all-to-all-start.3 = ((bf16[16,256,128]{2,1,0:T(8,128)(2,1)}), bf16[16,256,128]{2,1,0:T(8,128)(2,1)}, u32[]{:S(2)}, u32[]{:S(2)}) async-start(bf16[16,256,128]{2,1,0:T(8,128)(2,1)} %copy-done.16), calls=%async_computation.3 | async-start | bytes 2097152 | tf_op jit(solution)/shard_map/all_to_all | solution.py:676
  100.4 4.0 %copy-start.1 = (bf16[1024,1024]{1,0:T(8,128)(2,1)S(1)}, bf16[1024,1024]{1,0:T(8,128)(2,1)}, u32[]{:S(2)}) copy-start(bf16[1024,1024]{1,0:T(8,128)(2,1)} %copy-done) | copy-start | bytes 6291460
  100.4 50.6 %collective-permute-start.2 = (bf16[2,8,256,128]{3,2,1,0:T(8,128)(2,1)}, bf16[2,8,256,128]{3,2,1,0:T(8,128)(2,1)}, u32[]{:S(2)}, u32[]{:S(2)}) collective-permute-start(bf16[2,8,256,128]{3,2,1,0:T(8,128)(2,1)} %gate.3), channel_id=1, source_target_pairs={{0,16},{16,0},{1,17},{17,1},{2,18},{18,2},{3,19},{19,3},{4,20},{20... | collective-permute-start | bytes 3145736 | tf_op jit(solution)/shard_map/ppermute | solution.py:682
  104.4 1.2 copy-start.12
  105.6 20.7 %copy-start.22 = (f32[8,128]{1,0:T(8,128)S(1)}, f32[8,128]{1,0:T(8,128)}, u32[]{:S(2)}) copy-start(f32[8,128]{1,0:T(8,128)} %broadcast_multiply_fusion.refs_3_.refs_5_) | copy-start | bytes 12292
  126.3 1.6 copy-start.3
  139.2 11.8 %copy-start.21 = (bf16[8,256,128]{2,1,0:T(8,128)(2,1)S(1)}, bf16[8,256,128]{2,1,0:T(8,128)(2,1)}, u32[]{:S(2)}) copy-start(bf16[8,256,128]{2,1,0:T(8,128)(2,1)} %copy-done.20) | copy-start | bytes 1572868
  139.2 37.6 %all-to-all-start.4 = ((bf16[16,512,128]{2,1,0:T(8,128)(2,1)}), bf16[16,512,128]{2,1,0:T(8,128)(2,1)}, u32[]{:S(2)}, u32[]{:S(2)}) async-start(bf16[16,512,128]{2,1,0:T(8,128)(2,1)} %to_sigma.1.rest_0_.rest_1_), calls=%async_computation.4 | async-start | bytes 4194304 | tf_op jit(solution)/shard_map/all_to_all | solution.py:676
  143.7 10.2 %copy-start.14 = (bf16[16,256,128]{2,1,0:T(8,128)(2,1)S(1)}, bf16[16,256,128]{2,1,0:T(8,128)(2,1)}, u32[]{:S(2)}) copy-start(bf16[16,256,128]{2,1,0:T(8,128)(2,1)} %copy-done.13) | copy-start | bytes 3145732

commit v9 on v8

--- a/solution.py
+++ b/solution.py
@@ -224,12 +224,16 @@
     return (out_tiles[0:2], out_tiles[2:4])
 
 
-def vmem_params():
-    return pltpu.CompilerParams(vmem_limit_bytes=48 * 1024 * 1024)
+def vmem_params(mebibytes):
+    return pltpu.CompilerParams(vmem_limit_bytes=mebibytes * 1024 * 1024)
 
 
 def unread(arrays):
     return [pl.BlockSpec(memory_space=pl.ANY)] * len(arrays)
+
+
+def token(array):
+    return lax.slice(array, (0,) * array.ndim, (1,) * (array.ndim - 2) + (16, LANES))
 
 
 def whole(count):
@@ -261,11 +265,11 @@
     shape = (count * 2 * rows, 2 * cols)
     return pl.pallas_call(
         functools.partial(spread_kernel, first),
-        out_shape=jax.ShapeDtypeStruct(shape, BF16),
+        out_shape=pltpu.HBM(shape, BF16),
         in_specs=whole(2) + unread(after),
         out_specs=whole(1)[0],
         scratch_shapes=[pltpu.VMEM(shape, F32)],
-        compiler_params=vmem_params(),
+        compiler_params=vmem_params(14),
         name="spread",
     )(*tiles, *after)
 
@@ -297,7 +301,7 @@
         in_specs=whole(1),
         out_specs=tuple(whole(2)),
         scratch_shapes=[pltpu.VMEM((lines, blocks.shape[2]), F32)],
-        compiler_params=vmem_params(),
+        compiler_params=vmem_params(20),
         name="collect",
     )(blocks)
 
@@ -328,7 +332,7 @@
         out_shape=(shape, shape),
         in_specs=whole(1),
         out_specs=tuple(whole(2)),
-        compiler_params=vmem_params(),
+        compiler_params=vmem_params(20),
         name="make_tables",
     )(lattice_map[:, None])
 
@@ -358,7 +362,7 @@
         out_shape=jax.ShapeDtypeStruct((2 * momenta, rows * 2 * cols), BF16),
         in_specs=whole(3),
         out_specs=whole(1)[0],
-        compiler_params=vmem_params(),
+        compiler_params=vmem_params(20),
         name="to_sites",
     )(*tiles, table)
 
@@ -389,10 +393,10 @@
 def to_crossed(half, own, far, rows, after, cost):
     return pl.pallas_call(
         functools.partial(cross_kernel, rows),
-        out_shape=jax.ShapeDtypeStruct(own.shape, BF16),
+        out_shape=pltpu.HBM(own.shape, BF16),
         in_specs=[pl.BlockSpec(memory_space=pltpu.SMEM)] + whole(2) + unread(after),
         out_specs=whole(1)[0],
-        compiler_params=vmem_params(),
+        compiler_params=vmem_params(10),
         cost_estimate=cost,
         name="to_crossed",
     )(half, own, far, *after)
@@ -448,7 +452,7 @@
         in_specs=whole(2),
         out_specs=whole(1)[0],
         scratch_shapes=[pltpu.VMEM((lines, lanes), F32)],
-        compiler_params=vmem_params(),
+        compiler_params=vmem_params(18),
         name="to_mirror",
     )(crossed, table)
 
@@ -502,7 +506,7 @@
         in_specs=whole(parts + 4),
         out_specs=whole(1)[0],
         scratch_shapes=[pltpu.VMEM((lines, lanes), F32), pltpu.VMEM((parts * lines, lanes), F32)],
-        compiler_params=vmem_params(),
+        compiler_params=vmem_params(34),
         name="to_sigma",
     )(*mirrors, crossed, sites, table, inverse, coupling)
 
@@ -574,7 +578,7 @@
             (momenta, 3 * lanes, 2 * lanes), lambda p: (part * steps + p, 0, 0)
         ),
         input_output_aliases={4: 0} if part > 0 else {},
-        compiler_params=vmem_params(),
+        compiler_params=vmem_params(14),
         cost_estimate=weight(),
         name="make_rights",
     )(half, own, far_near, far_away, *before)
@@ -654,7 +658,7 @@
         in_specs=scalars()
         + [spec, pl.BlockSpec((momenta, 3 * lanes, 2 * lanes), lambda p: (p, 0, 0))],
         out_specs=spec,
-        compiler_params=vmem_params(),
+        compiler_params=vmem_params(14),
         name="volterra",
     )(half, sigma, rights)
 
@@ -694,7 +698,7 @@
     spread_parts = [spread(tiles, part * count, count, []) for part in range(PARTS)]
     own = [exchange(blocked(spread_parts[0]))]
     for rows_array in spread_parts[1:]:
-        own.append(exchange(gate(blocked(rows_array), [own[-1], sites, coupling])))
+        own.append(exchange(gate(blocked(rows_array), [token(own[-1]), token(sites), coupling])))
     far_near = [swap(lax.dynamic_slice_in_dim(blocks, (1 - half) * lines, lines)) for blocks in own]
 
     sent = []
@@ -705,7 +709,7 @@
                 own[part],
                 far_near[part],
                 rows,
-                own[-1:] + sent[-1:],
+                [token(blocks) for blocks in own[-1:] + sent[-1:]],
                 weight() if part > 0 else None,
             )
         )
@@ -713,7 +717,7 @@
     kept = jnp.stack(
         [lax.dynamic_slice_in_dim(blocks, half * lines, lines) for blocks in own]
     )
-    far_away = swap(gate(kept, sent[-1:] + crossed[:-1]))
+    far_away = swap(gate(kept, [token(blocks) for blocks in sent[-1:] + crossed[:-1]]))
     flat = [blocks.reshape(-1, 2 * cols) for blocks in crossed]
     mirrors = [to_mirror(flat[part], table, part, PARTS, rows) for part in range(PARTS - 1)]
     sigma_rows = to_sigma(
@@ -724,7 +728,7 @@
     for part in range(PARTS):
         rights = [
             make_rights(
-                half_at, own[part], far_near[part], far_away, rows, part, rights + [sigma_rows]
+                half_at, own[part], far_near[part], far_away, rows, part, rights + [token(sigma_rows)]
             )
         ]
     returned = exchange(volterra(half_at, sigma, rights[0], rows))

time: 216 us -> 222 us (1.028)
  local copies, waits for them, and re-layouts: 17.8 us -> 30.5 us
  Pallas kernels: 40.7 us -> 36 us
  starting transfers between devices: 30.9 us -> 27.4 us
    unnamed x52 -> x34, local copies, waits for them, and re-layouts: 15.5 us -> 21.7 us
    pallas_call x4, Pallas kernels: 3.58 us -> 8.84 us  [the longest x2 5.09 us: to_crossed(): pl.pallas_call(functools.partial(cross_kernel, rows), out_shape=pltpu.HBM...]
    slice x0 -> x7, local copies, waits for them, and re-layouts: none -> 5.09 us  [token(): lax.slice(array, (0,) * array.ndim, (1,) * (array.ndim - 2) + (16, LANES))]
    ppermute x3, waiting for transfers between devices: 25.5 us -> 30.6 us  [swap(): return lax.ppermute(array, 'half', [(0, 1), (1, 0)])]
    all_to_all x5, waiting for transfers between devices: 66.4 us -> 61.6 us  [exchange(): return lax.all_to_all(blocks, ('tcol', 'line'), 0, 0, tiled=True)]
    ppermute x3, starting transfers between devices: 6.6 us -> 2.59 us  [swap(): return lax.ppermute(array, 'half', [(0, 1), (1, 0)])]
    pallas_call x1, Pallas kernels: 11.2 us -> 7.3 us  [to_sigma(): pl.pallas_call(functools.partial(sigma_kernel, norm_factor, parts), out_s...]
    pallas_call x2, Pallas kernels: 6.03 us -> 3.6 us  [make_rights(): pl.pallas_call(functools.partial(rights_kernel, rows), grid=(steps,), out...]
  transfers between devices with their start and end apart: 8 -> 8, of which waited for: 6 -> 6; matrix products, arithmetic and copies ran while one was open for 2% -> 5% of each run, Pallas kernels for 15% -> 12%
where the time goes in v9:
time: 222 us; the launch traced here: 221 us
  waiting for transfers between devices  92.2 us (42%)
  Pallas kernels  36 us (16%)
  local copies, waits for them, and re-layouts  30.5 us (14%)
  blocking collectives  30 us (14%)
  starting transfers between devices  27.4 us (12%)
  other arithmetic  3.06 us (1%)
    all_to_all x5, waiting for transfers between devices, exchange(): return lax.all_to_all(blocks, ('tcol', 'line'), 0, 0, tiled=True)  61.6 us
    ppermute x3, waiting for transfers between devices, swap(): return lax.ppermute(array, 'half', [(0, 1), (1, 0)])  30.6 us
    all_to_all x1, blocking collectives, exchange(): return lax.all_to_all(blocks, ('tcol', 'line'), 0, 0, tiled=True)  30 us
    all_to_all x5, starting transfers between devices, exchange(): return lax.all_to_all(blocks, ('tcol', 'line'), 0, 0, tiled=True)  24.8 us
    unnamed x34, local copies, waits for them, and re-layouts  21.7 us
    pallas_call x1, Pallas kernels, to_sigma(): pl.pallas_call(functools.partial(sigma_kernel, norm_factor, parts), out_s...  7.3 us
    slice x7, local copies, waits for them, and re-layouts, token(): lax.slice(array, (0,) * array.ndim, (1,) * (array.ndim - 2) + (16, LANES))  5.09 us
    pallas_call x2, Pallas kernels, to_crossed(): pl.pallas_call(functools.partial(cross_kernel, rows), out_shape=pltpu.HBM...  5.09 us
  transfers between devices with their start and end apart: 8, of which 6 were waited for; matrix products, arithmetic and copies ran while one was open for 5% of the time, Pallas kernels for 12%

profile of v9, /device:TPU:0, one launch (start us, length us, event | category | flops | bytes accessed | tf_op | source)
XLA Modules:
  0.0 220.6 jit_solution(6634160627179398452)
XLA Ops:
  0.6 0.0 copy-start.2
  0.6 1.2 copy-done.2
  1.9 1.2 copy-done.5
  3.1 1.9 spread.2
  5.0 6.3 %all-to-all-start = ((bf16[16,256,128]{2,1,0:T(8,128)(2,1)}), bf16[16,256,128]{2,1,0:T(8,128)(2,1)S(1)}, u32[]{:S(2)}, u32[]{:S(2)}) async-start(bf16[16,256,128]{2,1,0:T(8,128)(2,1)} %bitcast.13), calls=%async_computation | async-start | bytes 2097152 | tf_op jit(solution)/shard_map/all_to_all | solution.py:680
  11.3 0.0 copy-start.16
  11.3 0.0 copy-done.3
  11.3 0.0 copy-done.6
  11.3 1.9 spread.3
  13.8 0.1 fusion.4
  13.9 0.1 dynamic_slice.20
  14.0 0.1 dynamic_slice.19
  14.0 0.0 copy-done.16
  14.0 0.1 copy.9.column_ref
  14.2 4.5 %make_tables.1 = (bf16[1024,1024]{1,0:T(8,128)(2,1)S(1)}, bf16[1024,1024]{1,0:T(8,128)(2,1)S(1)}) custom-call(s32[512,1]{1,0:T(8,128)S(1)} %copy.9.column_ref), custom_call_target="tpu_custom_call" | custom-call | tf_op jit(solution)/shard_map/make_tables/pallas_call | solution.py:330
  18.7 0.0 copy-start.13
  18.7 1.3 copy-done.13
  20.1 1.2 copy-done.4
  21.3 1.2 copy-done.7
  22.5 2.4 %to_sites.1.refs_2_ = bf16[1024,1024]{1,0:T(8,128)(2,1)S(1)} custom-call(bf16[2,8,64,512]{3,2,1,0:T(8,128)(2,1)S(1)} %copy-done.4, bf16[2,8,64,512]{3,2,1,0:T(8,128)(2,1)S(1)} %copy-done.7, bf16[1024,1024]{1,0:T(8,128)(2,1)S(1)} %get-tuple-element.4.table.refs_3_), custom_call_target="tpu_custom_call" | custom-call | tf_op jit(solution)/shard_map/to_sites/pallas_call | solution.py:360
  24.9 0.6 slice.31.refs_2_
  25.5 1.3 copy-done.8
  26.8 0.1 pad_maximum_fusion.1
  26.9 0.7 broadcast_multiply_fusion.refs_3_.refs_5_
  27.6 0.0 all-to-all-done.own
  27.6 0.6 slice.30.refs_1_
  28.2 5.2 %all-to-all-start.1 = ((bf16[16,256,128]{2,1,0:T(8,128)(2,1)}), bf16[16,256,128]{2,1,0:T(8,128)(2,1)}, u32[]{:S(2)}, u32[]{:S(2)}) async-start(bf16[16,256,128]{2,1,0:T(8,128)(2,1)} %gate.2), calls=%async_computation.1 | async-start | bytes 2097152 | tf_op jit(solution)/shard_map/all_to_all | solution.py:680
  33.4 1.1 dynamic-slice_bitcast_fusion.1
  34.4 2.6 %collective-permute-start = (bf16[8,256,128]{2,1,0:T(8,128)(2,1)}, bf16[8,256,128]{2,1,0:T(8,128)(2,1)}, u32[]{:S(2)}, u32[]{:S(2)}) collective-permute-start(bf16[8,256,128]{2,1,0:T(8,128)(2,1)} %get-tuple-element.7), channel_id=1, source_target_pairs={{0,16},{16,0},{1,17},{17,1},{2,18},{18,2},{3,19},{19,3},{4,20},{20... | collective-permute-start | bytes 1572872 | tf_op jit(solution)/shard_map/ppermute | solution.py:686
  37.0 23.7 %all-to-all-done.1.own = bf16[16,256,128]{2,1,0:T(8,128)(2,1)} async-done(((bf16[16,256,128]{2,1,0:T(8,128)(2,1)}), bf16[16,256,128]{2,1,0:T(8,128)(2,1)}, u32[]{:S(2)}, u32[]{:S(2)}) %all-to-all-start.1) | async-done | bytes 1048608 | tf_op jit(solution)/shard_map/all_to_all | solution.py:680
  60.7 2.3 %dynamic-slice_bitcast_fusion = (bf16[1,8,256,128]{3,2,1,0:T(8,128)(2,1)}, bf16[8,256,128]{2,1,0:T(8,128)(2,1)}) fusion(bf16[16,256,128]{2,1,0:T(8,128)(2,1)} %all-to-all-done.1.own, s32[]{:T(128)S(6)} %select_n.25, s32[]{:T(128)S(6)} %select_n.21), kind=kLoop, calls=%fused_computation.1 | loop fusion | bytes 2097160 | tf_op jit(solution)/shard_map/stack | solution.py:717
  62.9 0.0 collective-permute-start.1
  62.9 0.7 slice.32.rest_0_
  63.6 0.0 collective-permute-done.far.near_ref
  63.6 2.4 %to_crossed.2 = bf16[16,256,128]{2,1,0:T(8,128)(2,1)} custom-call(s32[1]{0:T(128)} %bitcast.half_ref, bf16[16,256,128]{2,1,0:T(8,128)(2,1)S(1)} %all-to-all-done.own, bf16[8,256,128]{2,1,0:T(8,128)(2,1)} %collective-permute-done.far.near_ref, bf16[1,16,128]{2,1,0:T(8,128)(2,1)S(1)} %slice.32.rest_0_), custom_call_target="tpu_custom_call" | custom-call | tf_op jit(solution)/shard_map/to_crossed/pallas_call | solution.py:394
  66.0 0.7 slice.33.rest_1_
  66.7 4.4 %all-to-all-start.2 = ((bf16[16,256,128]{2,1,0:T(8,128)(2,1)}), bf16[16,256,128]{2,1,0:T(8,128)(2,1)}, u32[]{:S(2)}, u32[]{:S(2)}) async-start(bf16[16,256,128]{2,1,0:T(8,128)(2,1)} %to_crossed.2), calls=%async_computation.2 | async-start | bytes 2097152 | tf_op jit(solution)/shard_map/all_to_all | solution.py:680
  71.1 15.2 %collective-permute-done.1.far.near_ref = bf16[8,256,128]{2,1,0:T(8,128)(2,1)} collective-permute-done((bf16[8,256,128]{2,1,0:T(8,128)(2,1)}, bf16[8,256,128]{2,1,0:T(8,128)(2,1)}, u32[]{:S(2)}, u32[]{:S(2)}) %collective-permute-start.1) | collective-permute-done | bytes 524320 | tf_op jit(solution)/shard_map/ppermute | solution.py:686
  86.3 2.7 %to_crossed.3 = bf16[16,256,128]{2,1,0:T(8,128)(2,1)} custom-call(s32[1]{0:T(128)} %bitcast.half_ref, bf16[16,256,128]{2,1,0:T(8,128)(2,1)} %all-to-all-done.1.own, bf16[8,256,128]{2,1,0:T(8,128)(2,1)} %collective-permute-done.1.far.near_ref, bf16[1,16,128]{2,1,0:T(8,128)(2,1)S(1)} %slice.32.rest_0_, bf16[1,16,128]{2,1,0:T(8,128)(2,1)S(1)} %slice.33.rest_1_), custom_call_target="tpu_custom_call" | custom-call | flops 99999997952 | bytes 1048576 | tf_op jit(solution)/shard_map/to_crossed/pallas_call | solution.py:394
  89.0 9.4 %all-to-all-done.2 = bf16[16,256,128]{2,1,0:T(8,128)(2,1)} async-done(((bf16[16,256,128]{2,1,0:T(8,128)(2,1)}), bf16[16,256,128]{2,1,0:T(8,128)(2,1)}, u32[]{:S(2)}, u32[]{:S(2)}) %all-to-all-start.2) | async-done | bytes 1048608 | tf_op jit(solution)/shard_map/all_to_all | solution.py:680
  98.4 4.5 %all-to-all-start.3 = ((bf16[16,256,128]{2,1,0:T(8,128)(2,1)}), bf16[16,256,128]{2,1,0:T(8,128)(2,1)}, u32[]{:S(2)}, u32[]{:S(2)}) async-start(bf16[16,256,128]{2,1,0:T(8,128)(2,1)} %to_crossed.3), calls=%async_computation.3 | async-start | bytes 2097152 | tf_op jit(solution)/shard_map/all_to_all | solution.py:680
  102.9 2.3 %pad_maximum_fusion.refs_0_ = bf16[2,8,256,128]{3,2,1,0:T(8,128)(2,1)} fusion(bf16[1,8,256,128]{3,2,1,0:T(8,128)(2,1)} %get-tuple-element.8, bf16[1,8,256,128]{3,2,1,0:T(8,128)(2,1)} %get-tuple-element.6), kind=kLoop, calls=%fused_computation | loop fusion | flops 524288 | bytes 2097152 | tf_op jit(solution)/shard_map/stack | solution.py:717
  105.2 1.3 slice.34.refs_1_
  106.5 1.3 slice.35.refs_2_
  107.7 0.0 collective-permute-start.2
  107.7 2.7 %to_mirror.1.refs_0_ = f32[1024,1024]{1,0:T(8,128)S(1)} custom-call(bf16[4096,128]{1,0:T(8,128)(2,1)} %bitcast.5.crossed, bf16[1024,1024]{1,0:T(8,128)(2,1)S(1)} %get-tuple-element.4.table.refs_3_), custom_call_target="tpu_custom_call" | custom-call | tf_op jit(solution)/shard_map/to_mirror/pallas_call | solution.py:449
  110.5 2.0 copy-done
  112.4 10.4 %all-to-all-done.3 = bf16[16,256,128]{2,1,0:T(8,128)(2,1)} async-done(((bf16[16,256,128]{2,1,0:T(8,128)(2,1)}), bf16[16,256,128]{2,1,0:T(8,128)(2,1)}, u32[]{:S(2)}, u32[]{:S(2)}) %all-to-all-start.3) | async-done | bytes 1048608 | tf_op jit(solution)/shard_map/all_to_all | solution.py:680
  122.8 2.2 copy-done.1
  125.0 1.6 copy-done.9
  126.6 1.6 copy-done.14
  128.2 7.3 %to_sigma.1 = bf16[16,512,128]{2,1,0:T(8,128)(2,1)S(1)} custom-call(f32[1024,1024]{1,0:T(8,128)S(1)} %copy-done.1, bf16[4096,128]{1,0:T(8,128)(2,1)} %bitcast.6.refs_1_, bf16[1024,1024]{1,0:T(8,128)(2,1)S(1)} %copy-done.9, bf16[1024,1024]{1,0:T(8,128)(2,1)S(1)} %get-tuple-element.4.table.refs_3_, bf16[1024,1024]{1,0:T(8,128)(2,1)S(1)} %copy-done.14, ...), custom_call_target="tpu_custom_call" | custom-call | tf_op jit(solution)/shard_map/to_sigma/pallas_call | solution.py:503
  135.5 1.3 copy-done.10
  136.9 4.4 %all-to-all-start.4 = ((bf16[16,512,128]{2,1,0:T(8,128)(2,1)}), bf16[16,512,128]{2,1,0:T(8,128)(2,1)}, u32[]{:S(2)}, u32[]{:S(2)}) async-start(bf16[16,512,128]{2,1,0:T(8,128)(2,1)} %copy-done.10), calls=%async_computation.4 | async-start | bytes 4194304 | tf_op jit(solution)/shard_map/all_to_all | solution.py:680
  141.3 15.3 %collective-permute-done.2.away_ref = bf16[2,8,256,128]{3,2,1,0:T(8,128)(2,1)} collective-permute-done((bf16[2,8,256,128]{3,2,1,0:T(8,128)(2,1)}, bf16[2,8,256,128]{3,2,1,0:T(8,128)(2,1)}, u32[]{:S(2)}, u32[]{:S(2)}) %collective-permute-start.2) | collective-permute-done | bytes 1048608 | tf_op jit(solution)/shard_map/ppermute | solution.py:686
  156.7 1.7 make_rights.2.rest_0_
  158.4 1.9 make_rights.3.rights
  160.3 0.0 copy-start.11
  160.3 2.7 %copy-done.11 = bf16[32,384,256]{2,1,0:T(8,128)(2,1)} copy-done((bf16[32,384,256]{2,1,0:T(8,128)(2,1)}, bf16[32,384,256]{2,1,0:T(8,128)(2,1)S(1)}, u32[]{:S(2)}) %copy-start.11) | copy-done | bytes 6291480
  162.9 18.1 %all-to-all-done.4.sigma = bf16[16,512,128]{2,1,0:T(8,128)(2,1)} async-done(((bf16[16,512,128]{2,1,0:T(8,128)(2,1)}), bf16[16,512,128]{2,1,0:T(8,128)(2,1)}, u32[]{:S(2)}, u32[]{:S(2)}) %all-to-all-start.4) | async-done | bytes 2097184 | tf_op jit(solution)/shard_map/all_to_all | solution.py:680
  181.1 2.8 %copy-done.12 = bf16[32,384,256]{2,1,0:T(8,128)(2,1)S(1)} copy-done((bf16[32,384,256]{2,1,0:T(8,128)(2,1)S(1)}, bf16[32,384,256]{2,1,0:T(8,128)(2,1)}, u32[]{:S(2)}) %copy-start.12) | copy-done | bytes 6291480
  183.9 4.1 %volterra.1 = bf16[16,512,128]{2,1,0:T(8,128)(2,1)S(1)} custom-call(s32[1]{0:T(128)} %bitcast.half_ref, bf16[16,512,128]{2,1,0:T(8,128)(2,1)} %all-to-all-done.4.sigma, bf16[32,384,256]{2,1,0:T(8,128)(2,1)S(1)} %copy-done.12), custom_call_target="tpu_custom_call" | custom-call | tf_op jit(solution)/shard_map/volterra/pallas_call | solution.py:654
  188.0 30.0 %all_to_all.30.blocks_ref = bf16[16,512,128]{2,1,0:T(8,128)(2,1)S(1)} all-to-all(bf16[16,512,128]{2,1,0:T(8,128)(2,1)S(1)} %volterra.1), channel_id=1, replica_groups=mesh['half'=2,'line'=8,'tcol'=2] {'tcol','line'}, dimensions={0} | all-to-all | bytes 4194304 | tf_op jit(solution)/shard_map/all_to_all | solution.py:680
  218.0 2.6 %collect.1 = (bf16[2,8,64,512]{3,2,1,0:T(8,128)(2,1)}, bf16[2,8,64,512]{3,2,1,0:T(8,128)(2,1)}) custom-call(bf16[16,512,128]{2,1,0:T(8,128)(2,1)S(1)} %all_to_all.30.blocks_ref), custom_call_target="tpu_custom_call" | custom-call | tf_op jit(solution)/shard_map/collect/pallas_call | solution.py:298
  (17 shorter events, 0.0 us)
Async XLA Ops:
  0.6 1.2 copy-start.2
  1.9 1.2 copy-start.5
  3.1 8.2 %copy-start.3 = (bf16[2,8,64,512]{3,2,1,0:T(8,128)(2,1)S(1)}, bf16[2,8,64,512]{3,2,1,0:T(8,128)(2,1)}, u32[]{:S(2)}) copy-start(bf16[2,8,64,512]{3,2,1,0:T(8,128)(2,1)} %lesser.5) | copy-start | bytes 3145732
  3.1 8.2 %copy-start.6 = (bf16[2,8,64,512]{3,2,1,0:T(8,128)(2,1)S(1)}, bf16[2,8,64,512]{3,2,1,0:T(8,128)(2,1)}, u32[]{:S(2)}) copy-start(bf16[2,8,64,512]{3,2,1,0:T(8,128)(2,1)} %greater.5) | copy-start | bytes 3145732
  5.0 22.6 %all-to-all-start = ((bf16[16,256,128]{2,1,0:T(8,128)(2,1)}), bf16[16,256,128]{2,1,0:T(8,128)(2,1)S(1)}, u32[]{:S(2)}, u32[]{:S(2)}) async-start(bf16[16,256,128]{2,1,0:T(8,128)(2,1)} %bitcast.13), calls=%async_computation | async-start | bytes 2097152 | tf_op jit(solution)/shard_map/all_to_all | solution.py:680
  11.3 2.8 %copy-start.16 = (s32[512]{0:T(512)S(1)}, s32[512]{0:T(512)}, u32[]{:S(2)}) copy-start(s32[512]{0:T(512)} %param.6) | copy-start | bytes 6148
  18.7 1.4 copy-start.13
  20.1 1.2 copy-start.4
  21.3 1.2 copy-start.7
  25.5 1.3 copy-start.8
  28.2 32.5 %all-to-all-start.1 = ((bf16[16,256,128]{2,1,0:T(8,128)(2,1)}), bf16[16,256,128]{2,1,0:T(8,128)(2,1)}, u32[]{:S(2)}, u32[]{:S(2)}) async-start(bf16[16,256,128]{2,1,0:T(8,128)(2,1)} %gate.2), calls=%async_computation.1 | async-start | bytes 2097152 | tf_op jit(solution)/shard_map/all_to_all | solution.py:680
  34.4 29.2 %collective-permute-start = (bf16[8,256,128]{2,1,0:T(8,128)(2,1)}, bf16[8,256,128]{2,1,0:T(8,128)(2,1)}, u32[]{:S(2)}, u32[]{:S(2)}) collective-permute-start(bf16[8,256,128]{2,1,0:T(8,128)(2,1)} %get-tuple-element.7), channel_id=1, source_target_pairs={{0,16},{16,0},{1,17},{17,1},{2,18},{18,2},{3,19},{19,3},{4,20},{20... | collective-permute-start | bytes 1572872 | tf_op jit(solution)/shard_map/ppermute | solution.py:686
  62.9 23.3 %collective-permute-start.1 = (bf16[8,256,128]{2,1,0:T(8,128)(2,1)}, bf16[8,256,128]{2,1,0:T(8,128)(2,1)}, u32[]{:S(2)}, u32[]{:S(2)}) collective-permute-start(bf16[8,256,128]{2,1,0:T(8,128)(2,1)} %get-tuple-element.9), channel_id=1, source_target_pairs={{0,16},{16,0},{1,17},{17,1},{2,18},{18,2},{3,19},{19,3},{4,20},{20... | collective-permute-start | bytes 1572872 | tf_op jit(solution)/shard_map/ppermute | solution.py:686
  66.7 31.7 %all-to-all-start.2 = ((bf16[16,256,128]{2,1,0:T(8,128)(2,1)}), bf16[16,256,128]{2,1,0:T(8,128)(2,1)}, u32[]{:S(2)}, u32[]{:S(2)}) async-start(bf16[16,256,128]{2,1,0:T(8,128)(2,1)} %to_crossed.2), calls=%async_computation.2 | async-start | bytes 2097152 | tf_op jit(solution)/shard_map/all_to_all | solution.py:680
  98.4 24.5 %all-to-all-start.3 = ((bf16[16,256,128]{2,1,0:T(8,128)(2,1)}), bf16[16,256,128]{2,1,0:T(8,128)(2,1)}, u32[]{:S(2)}, u32[]{:S(2)}) async-start(bf16[16,256,128]{2,1,0:T(8,128)(2,1)} %to_crossed.3), calls=%async_computation.3 | async-start | bytes 2097152 | tf_op jit(solution)/shard_map/all_to_all | solution.py:680
  107.7 48.9 %collective-permute-start.2 = (bf16[2,8,256,128]{3,2,1,0:T(8,128)(2,1)}, bf16[2,8,256,128]{3,2,1,0:T(8,128)(2,1)}, u32[]{:S(2)}, u32[]{:S(2)}) collective-permute-start(bf16[2,8,256,128]{3,2,1,0:T(8,128)(2,1)} %gate.3), channel_id=1, source_target_pairs={{0,16},{16,0},{1,17},{17,1},{2,18},{18,2},{3,19},{19,3},{4,20},{20... | collective-permute-start | bytes 3145736 | tf_op jit(solution)/shard_map/ppermute | solution.py:686
  107.7 15.1 %copy-start.15 = (f32[8,128]{1,0:T(8,128)S(1)}, f32[8,128]{1,0:T(8,128)}, u32[]{:S(2)}) copy-start(f32[8,128]{1,0:T(8,128)} %broadcast_multiply_fusion.refs_3_.refs_5_) | copy-start | bytes 12292
  110.4 2.0 copy-start
  122.8 2.2 copy-start.1
  125.0 1.6 copy-start.9
  126.6 1.6 copy-start.14
  135.5 1.3 copy-start.10
  136.9 44.2 %all-to-all-start.4 = ((bf16[16,512,128]{2,1,0:T(8,128)(2,1)}), bf16[16,512,128]{2,1,0:T(8,128)(2,1)}, u32[]{:S(2)}, u32[]{:S(2)}) async-start(bf16[16,512,128]{2,1,0:T(8,128)(2,1)} %copy-done.10), calls=%async_computation.4 | async-start | bytes 4194304 | tf_op jit(solution)/shard_map/all_to_all | solution.py:680
  160.3 2.7 %copy-start.11 = (bf16[32,384,256]{2,1,0:T(8,128)(2,1)}, bf16[32,384,256]{2,1,0:T(8,128)(2,1)S(1)}, u32[]{:S(2)}) copy-start(bf16[32,384,256]{2,1,0:T(8,128)(2,1)S(1)} %make_rights.3.rights) | copy-start | bytes 18874372
  181.1 2.8 %copy-start.12 = (bf16[32,384,256]{2,1,0:T(8,128)(2,1)S(1)}, bf16[32,384,256]{2,1,0:T(8,128)(2,1)}, u32[]{:S(2)}) copy-start(bf16[32,384,256]{2,1,0:T(8,128)(2,1)} %copy-done.11) | copy-start | bytes 18874372

commit v10 on v8

--- a/solution.py
+++ b/solution.py
@@ -224,8 +224,8 @@
     return (out_tiles[0:2], out_tiles[2:4])
 
 
-def vmem_params():
-    return pltpu.CompilerParams(vmem_limit_bytes=48 * 1024 * 1024)
+def vmem_params(mebibytes=48):
+    return pltpu.CompilerParams(vmem_limit_bytes=mebibytes * 1024 * 1024)
 
 
 def unread(arrays):
@@ -244,30 +244,29 @@
     return [pl.BlockSpec(memory_space=pltpu.SMEM)]
 
 
-def spread_kernel(first, lesser, greater, *rest):
-    out, lines = rest[-2:]
-    _, rows, _, _ = lesser.shape
-    count = lines.shape[0] // (2 * rows)
+def spread_kernel(lesser, greater, out, lines):
+    _, rows, _, count = lesser.shape
     for g, tile in enumerate((lesser, greater)):
         for t in range(rows):
-            span = slice(first, first + count)
-            slab = jnp.concatenate([tile[0, t, :, span], tile[1, t, :, span]], axis=0)
+            slab = jnp.concatenate([tile[0, t], tile[1, t]], axis=0)
             lines[pl.ds(g * rows + t, count, stride=2 * rows), :] = slab.astype(F32).T
     out[...] = lines[...].astype(BF16)
 
 
-def spread(tiles, first, count, after):
+def spread(tiles, first, count):
     _, rows, cols, _ = tiles[0].shape
-    shape = (count * 2 * rows, 2 * cols)
-    return pl.pallas_call(
-        functools.partial(spread_kernel, first),
-        out_shape=jax.ShapeDtypeStruct(shape, BF16),
-        in_specs=whole(2) + unread(after),
-        out_specs=whole(1)[0],
-        scratch_shapes=[pltpu.VMEM(shape, F32)],
-        compiler_params=vmem_params(),
+    height = 2 * rows * LANES
+    tile_spec = pl.BlockSpec((2, rows, cols, LANES), lambda p: (0, 0, 0, first // LANES + p))
+    return pl.pallas_call(
+        spread_kernel,
+        grid=(count // LANES,),
+        out_shape=pltpu.HBM((count * 2 * rows, 2 * cols), BF16),
+        in_specs=[tile_spec, tile_spec],
+        out_specs=pl.BlockSpec((height, 2 * cols), lambda p: (p, 0)),
+        scratch_shapes=[pltpu.VMEM((height, 2 * cols), F32)],
+        compiler_params=vmem_params(58),
         name="spread",
-    )(*tiles, *after)
+    )(*tiles)
 
 
 def collect_kernel(parts, blocks_ref, lesser, greater, lines):
@@ -364,7 +363,8 @@
 
 
 def cross_kernel(rows, half_ref, own, far, *rest):
-    out = rest[-1]
+    out, mark = rest[-2:]
+    mark[...] = jnp.zeros_like(mark)
     half = half_ref[0]
     blocks = far.shape[0]
     cols = blocks * rows
@@ -387,11 +387,20 @@
 
 
 def to_crossed(half, own, far, rows, after, cost):
+    sources, lines, lanes = own.shape
+    blocks = far.shape[0]
+    step = lines // STEPS
+    spec = pl.BlockSpec((sources, step, lanes), lambda p: (0, p, 0))
+    far_spec = pl.BlockSpec((blocks, step, lanes), lambda p: (0, p, 0))
     return pl.pallas_call(
         functools.partial(cross_kernel, rows),
-        out_shape=jax.ShapeDtypeStruct(own.shape, BF16),
-        in_specs=[pl.BlockSpec(memory_space=pltpu.SMEM)] + whole(2) + unread(after),
-        out_specs=whole(1)[0],
+        grid=(STEPS,),
+        out_shape=(
+            pltpu.HBM(own.shape, BF16),
+            jax.ShapeDtypeStruct((8, LANES), F32),
+        ),
+        in_specs=scalars() + [spec, far_spec] + unread(after),
+        out_specs=(spec, pl.BlockSpec((8, LANES), lambda p: (0, 0))),
         compiler_params=vmem_params(),
         cost_estimate=cost,
         name="to_crossed",
@@ -413,31 +422,30 @@
     )(array, *after)
 
 
-def mirrored_term(table, part, parts, read, pair, count):
-    momenta = table.shape[1] // 2
-    wide = momenta // parts
+def mirrored_term(columns, read, first, count):
+    wide = columns.shape[1] // 2
     rights = []
-    for t in (2 * pair, 2 * pair + 1):
+    for t in (first, first + 1):
         real = read[pl.ds(t, wide, stride=2 * count), :]
         imaginary = -read[pl.ds(count + t, wide, stride=2 * count), :]
         rights.append(jnp.concatenate([real, imaginary], axis=0).astype(BF16))
-    columns = jnp.concatenate(
-        [
-            table[:, part * wide : (part + 1) * wide],
-            table[:, momenta + part * wide : momenta + (part + 1) * wide],
-        ],
-        axis=1,
-    )
     return jnp.dot(columns, jnp.concatenate(rights, axis=1), preferred_element_type=F32)
 
 
 def mirror_kernel(part, parts, count, crossed, table, out, read):
     read[...] = crossed[...].astype(F32)
     wide = 2 * crossed.shape[1]
+    momenta = table.shape[1] // 2
+    width = momenta // parts
+    columns = jnp.concatenate(
+        [
+            table[:, part * width : (part + 1) * width],
+            table[:, momenta + part * width : momenta + (part + 1) * width],
+        ],
+        axis=1,
+    )
     for pair in range(count // 2):
-        out[:, pair * wide : (pair + 1) * wide] = mirrored_term(
-            table, part, parts, read, pair, count
-        )
+        out[:, pair * wide : (pair + 1) * wide] = mirrored_term(columns, read, 2 * pair, count)
 
 
 def to_mirror(crossed, table, part, parts, count):
@@ -455,56 +463,78 @@
 
 def sigma_kernel(norm_factor, parts, *refs):
     mirrors = refs[: parts - 1]
-    crossed, sites, table, inverse, coupling, out, read, written = refs[parts - 1 :]
+    crossed, sites, cosines, sines, inverse, coupling, out, read, written = refs[parts - 1 :]
     count = coupling.shape[0]
-    momenta = table.shape[0] // 2
-    read[...] = crossed[...].astype(F32)
-    for pair in range(count // 2):
-        span = slice(2 * pair * LANES, 2 * (pair + 1) * LANES)
-        other = mirrored_term(table, parts - 1, parts, read, pair, count)
-        for mirror in mirrors:
-            other = other + mirror[:, span]
-        other = (other * norm_factor).astype(BF16).astype(F32)
-        self_real, self_imaginary = second_born(
-            sites[:momenta, span].astype(F32),
-            sites[momenta:, span].astype(F32),
-            other[:momenta],
-            -other[momenta:],
-            jnp.concatenate([coupling[t : t + 1] for t in (2 * pair, 2 * pair + 1)], axis=1),
-        )
-        product = jnp.dot(
-            inverse[...],
-            jnp.concatenate([self_real, self_imaginary], axis=0).astype(BF16),
-            preferred_element_type=F32,
-        )
-        product = product * norm_factor
-        for at in range(2):
-            for part in range(2):
-                written[pl.ds(part * count + 2 * pair + at, momenta, stride=2 * count), :] = product[
-                    part * momenta : (part + 1) * momenta, at * LANES : (at + 1) * LANES
-                ]
-    blocks, height, _ = out.shape
-    height = height // parts
-    for part in range(parts):
-        for block in range(blocks):
-            start = (part * blocks + block) * height
-            out[block, part * height : (part + 1) * height] = written[
-                start : start + height
-            ].astype(BF16)
+    momenta = cosines.shape[0] // 2
+    step = pl.program_id(0)
+
+    @pl.when(step == 0)
+    def _():
+        read[...] = crossed[...].astype(F32)
+
+    first = 2 * step
+    columns = jnp.concatenate([cosines[...], sines[...]], axis=1)
+    other = mirrored_term(columns, read, first, count)
+    for mirror in mirrors:
+        other = other + mirror[...]
+    other = (other * norm_factor).astype(BF16).astype(F32)
+    self_real, self_imaginary = second_born(
+        sites[:momenta].astype(F32),
+        sites[momenta:].astype(F32),
+        other[:momenta],
+        -other[momenta:],
+        jnp.concatenate([coupling[pl.ds(first, 1), :], coupling[pl.ds(first + 1, 1), :]], axis=1),
+    )
+    product = jnp.dot(
+        inverse[...],
+        jnp.concatenate([self_real, self_imaginary], axis=0).astype(BF16),
+        preferred_element_type=F32,
+    )
+    product = product * norm_factor
+    for at in range(2):
+        for part in range(2):
+            written[pl.ds(part * count + first + at, momenta, stride=2 * count), :] = product[
+                part * momenta : (part + 1) * momenta, at * LANES : (at + 1) * LANES
+            ]
+
+    @pl.when(step == count // 2 - 1)
+    def _():
+        blocks, height, _ = out.shape
+        height = height // parts
+        for part in range(parts):
+            for block in range(blocks):
+                start = (part * blocks + block) * height
+                out[block, part * height : (part + 1) * height] = written[
+                    start : start + height
+                ].astype(BF16)
 
 
 def to_sigma(mirrors, crossed, sites, table, inverse, coupling, norm_factor, blocks):
     parts = len(mirrors) + 1
     lines, lanes = crossed.shape
+    size = table.shape[0]
+    width = size // (2 * parts)
+    shape = (blocks, parts * lines // blocks, lanes)
+    by_step = pl.BlockSpec((size, 2 * lanes), lambda p: (0, p))
+    fixed = lambda array: pl.BlockSpec(array.shape, lambda p: (0, 0))
     return pl.pallas_call(
         functools.partial(sigma_kernel, norm_factor, parts),
-        out_shape=jax.ShapeDtypeStruct((blocks, parts * lines // blocks, lanes), BF16),
-        in_specs=whole(parts + 4),
-        out_specs=whole(1)[0],
+        grid=(coupling.shape[0] // 2,),
+        out_shape=pltpu.HBM(shape, BF16),
+        in_specs=[by_step] * (parts - 1)
+        + [
+            fixed(crossed),
+            by_step,
+            pl.BlockSpec((size, width), lambda p: (0, parts - 1)),
+            pl.BlockSpec((size, width), lambda p: (0, 2 * parts - 1)),
+            fixed(inverse),
+            fixed(coupling),
+        ],
+        out_specs=pl.BlockSpec(shape, lambda p: (0, 0, 0)),
         scratch_shapes=[pltpu.VMEM((lines, lanes), F32), pltpu.VMEM((parts * lines, lanes), F32)],
-        compiler_params=vmem_params(),
+        compiler_params=vmem_params(58),
         name="to_sigma",
-    )(*mirrors, crossed, sites, table, inverse, coupling)
+    )(*mirrors, crossed, sites, table, table, inverse, coupling)
 
 
 def rights_kernel(rows, half_ref, own, near_ref, away_ref, *rest):
@@ -691,29 +721,30 @@
     second = lax.dynamic_slice_in_dim(coupling_line, side * cols, cols)
     coupling = first[:, None] * jnp.concatenate([second, second])[None, :]
 
-    spread_parts = [spread(tiles, part * count, count, []) for part in range(PARTS)]
+    spread_parts = [spread(tiles, part * count, count) for part in range(PARTS)]
     own = [exchange(blocked(spread_parts[0]))]
     for rows_array in spread_parts[1:]:
-        own.append(exchange(gate(blocked(rows_array), [own[-1], sites, coupling])))
+        own.append(exchange(gate(blocked(rows_array), [sites, coupling])))
     far_near = [swap(lax.dynamic_slice_in_dim(blocks, (1 - half) * lines, lines)) for blocks in own]
 
     sent = []
+    marks = []
     for part in range(PARTS):
-        sent.append(
-            to_crossed(
-                half_at,
-                own[part],
-                far_near[part],
-                rows,
-                own[-1:] + sent[-1:],
-                weight() if part > 0 else None,
-            )
+        blocks, mark = to_crossed(
+            half_at,
+            own[part],
+            far_near[part],
+            rows,
+            own[-1:] + marks[-1:],
+            weight() if part > 0 else None,
         )
+        sent.append(blocks)
+        marks.append(mark)
     crossed = [exchange(blocks) for blocks in sent]
     kept = jnp.stack(
         [lax.dynamic_slice_in_dim(blocks, half * lines, lines) for blocks in own]
     )
-    far_away = swap(gate(kept, sent[-1:] + crossed[:-1]))
+    far_away = swap(gate(kept, marks[-1:] + crossed[:-1]))
     flat = [blocks.reshape(-1, 2 * cols) for blocks in crossed]
     mirrors = [to_mirror(flat[part], table, part, PARTS, rows) for part in range(PARTS - 1)]
     sigma_rows = to_sigma(

time: 216 us -> 216 us (level)
  local copies, waits for them, and re-layouts: 17.8 us -> 9.48 us
  starting transfers between devices: 30.9 us -> 39.2 us
  Pallas kernels: 40.7 us -> 47.1 us
  waiting for transfers between devices: 91.8 us -> 86.3 us
    all_to_all x5, starting transfers between devices: 24.3 us -> 36 us  [exchange(): return lax.all_to_all(blocks, ('tcol', 'line'), 0, 0, tiled=True)]
    ppermute x3, waiting for transfers between devices: 25.5 us -> 14.4 us  [swap(): return lax.ppermute(array, 'half', [(0, 1), (1, 0)])]
    unnamed x52 -> x42, local copies, waits for them, and re-layouts: 15.5 us -> 7.01 us
    pallas_call x5, Pallas kernels: 14.8 us -> 21.2 us  [the longest x1 11.8 us: to_sigma(): pl.pallas_call(functools.partial(sigma_kernel, norm_factor, parts), grid=...]
    all_to_all x5, waiting for transfers between devices: 66.4 us -> 71.9 us  [exchange(): return lax.all_to_all(blocks, ('tcol', 'line'), 0, 0, tiled=True)]
    ppermute x3, starting transfers between devices: 6.6 us -> 3.27 us  [swap(): return lax.ppermute(array, 'half', [(0, 1), (1, 0)])]
  transfers between devices with their start and end apart: 8 -> 8, of which waited for: 6 -> 6; matrix products, arithmetic and copies ran while one was open for 2% -> 2% of each run, Pallas kernels for 15% -> 17%
where the time goes in v10:
time: 216 us; the launch traced here: 215 us
  waiting for transfers between devices  86.3 us (40%)
  Pallas kernels  47.1 us (22%)
  starting transfers between devices  39.2 us (18%)
  blocking collectives  30 us (14%)
  local copies, waits for them, and re-layouts  9.48 us (4%)
    all_to_all x5, waiting for transfers between devices, exchange(): return lax.all_to_all(blocks, ('tcol', 'line'), 0, 0, tiled=True)  71.9 us
    all_to_all x5, starting transfers between devices, exchange(): return lax.all_to_all(blocks, ('tcol', 'line'), 0, 0, tiled=True)  36 us
    all_to_all x1, blocking collectives, exchange(): return lax.all_to_all(blocks, ('tcol', 'line'), 0, 0, tiled=True)  30 us
    ppermute x3, waiting for transfers between devices, swap(): return lax.ppermute(array, 'half', [(0, 1), (1, 0)])  14.4 us
    pallas_call x1, Pallas kernels, to_sigma(): pl.pallas_call(functools.partial(sigma_kernel, norm_factor, parts), grid=...  11.8 us
    unnamed x42, local copies, waits for them, and re-layouts  7.01 us
    pallas_call x2, Pallas kernels, make_rights(): pl.pallas_call(functools.partial(rights_kernel, rows), grid=(steps,), out...  6.02 us
    pallas_call x2, Pallas kernels, spread(): pl.pallas_call(spread_kernel, grid=(count // LANES,), out_shape=pltpu.HBM...  5.44 us
  transfers between devices with their start and end apart: 8, of which 6 were waited for; matrix products, arithmetic and copies ran while one was open for 2% of the time, Pallas kernels for 17%

profile of v10, /device:TPU:0, one launch (start us, length us, event | category | flops | bytes accessed | tf_op | source)
XLA Modules:
  0.0 215.4 jit_solution(7455780467549975183)
XLA Ops:
  0.6 2.6 %spread.2 = bf16[4096,128]{1,0:T(8,128)(2,1)} custom-call(bf16[2,8,64,512]{3,2,1,0:T(8,128)(2,1)} %lesser.5, bf16[2,8,64,512]{3,2,1,0:T(8,128)(2,1)} %greater.5), custom_call_target="tpu_custom_call" | custom-call | tf_op jit(solution)/shard_map/spread/pallas_call | solution.py:260
  3.3 6.3 %all-to-all-start = ((bf16[16,256,128]{2,1,0:T(8,128)(2,1)}), bf16[16,256,128]{2,1,0:T(8,128)(2,1)S(1)}, u32[]{:S(2)}, u32[]{:S(2)}) async-start(bf16[16,256,128]{2,1,0:T(8,128)(2,1)} %bitcast.14), calls=%async_computation | async-start | bytes 2097152 | tf_op jit(solution)/shard_map/all_to_all | solution.py:706
  9.6 0.0 copy-start.20
  9.6 0.0 copy-start.3
  9.6 0.0 copy-start.4
  9.6 2.8 %spread.3 = bf16[4096,128]{1,0:T(8,128)(2,1)} custom-call(bf16[2,8,64,512]{3,2,1,0:T(8,128)(2,1)} %lesser.5, bf16[2,8,64,512]{3,2,1,0:T(8,128)(2,1)} %greater.5), custom_call_target="tpu_custom_call" | custom-call | tf_op jit(solution)/shard_map/spread/pallas_call | solution.py:260
  13.1 0.1 fusion.4
  13.1 0.1 dynamic_slice.19
  13.2 0.1 dynamic_slice.20
  13.3 0.0 copy-done.20
  13.3 0.1 copy.9.column_ref
  13.4 4.5 %make_tables.1 = (bf16[1024,1024]{1,0:T(8,128)(2,1)S(1)}, bf16[1024,1024]{1,0:T(8,128)(2,1)S(1)}) custom-call(s32[512,1]{1,0:T(8,128)S(1)} %copy.9.column_ref), custom_call_target="tpu_custom_call" | custom-call | tf_op jit(solution)/shard_map/make_tables/pallas_call | solution.py:325
  18.0 0.0 copy-start
  18.0 1.4 copy-done
  19.3 1.4 copy-done.12
  20.7 0.0 copy-done.3
  20.7 0.0 copy-done.4
  20.7 4.0 %to_sites.1.refs_1_.refs_2_ = bf16[1024,1024]{1,0:T(8,128)(2,1)S(1)} custom-call(bf16[2,8,64,512]{3,2,1,0:T(8,128)(2,1)S(1)} %copy-done.3, bf16[2,8,64,512]{3,2,1,0:T(8,128)(2,1)S(1)} %copy-done.4, bf16[1024,1024]{1,0:T(8,128)(2,1)} %copy-done), custom_call_target="tpu_custom_call" | custom-call | tf_op jit(solution)/shard_map/to_sites/pallas_call | solution.py:355
  24.7 0.0 copy-start.2
  24.7 1.4 copy-done.2
  26.1 0.1 pad_maximum_fusion.1
  26.2 0.7 broadcast_multiply_fusion.refs_2_.refs_6_
  26.8 0.0 all-to-all-done.own
  26.8 5.1 %all-to-all-start.1 = ((bf16[16,256,128]{2,1,0:T(8,128)(2,1)}), bf16[16,256,128]{2,1,0:T(8,128)(2,1)S(1)}, u32[]{:S(2)}, u32[]{:S(2)}) async-start(bf16[16,256,128]{2,1,0:T(8,128)(2,1)} %gate.2), calls=%async_computation.1 | async-start | bytes 2097152 | tf_op jit(solution)/shard_map/all_to_all | solution.py:706
  32.0 1.1 dynamic-slice_bitcast_fusion.1
  33.0 2.6 %collective-permute-start = (bf16[8,256,128]{2,1,0:T(8,128)(2,1)}, bf16[8,256,128]{2,1,0:T(8,128)(2,1)S(1)}, u32[]{:S(2)}, u32[]{:S(2)}) collective-permute-start(bf16[8,256,128]{2,1,0:T(8,128)(2,1)} %get-tuple-element.15), channel_id=1, source_target_pairs={{0,16},{16,0},{1,17},{17,1},{2,18},{18,2},{3,19},{19,3},{4,20},{20... | collective-permute-start | bytes 1572872 | tf_op jit(solution)/shard_map/ppermute | solution.py:712
  35.6 23.6 %all-to-all-done.1.rest_0_.own = bf16[16,256,128]{2,1,0:T(8,128)(2,1)S(1)} async-done(((bf16[16,256,128]{2,1,0:T(8,128)(2,1)}), bf16[16,256,128]{2,1,0:T(8,128)(2,1)S(1)}, u32[]{:S(2)}, u32[]{:S(2)}) %all-to-all-start.1) | async-done | bytes 1048608 | tf_op jit(solution)/shard_map/all_to_all | solution.py:706
  59.2 1.1 dynamic-slice_bitcast_fusion
  60.3 0.0 collective-permute-start.1
  60.3 0.0 collective-permute-done.far.near_ref
  60.3 0.0 copy-done.7
  60.4 2.0 to_crossed.2
  62.4 0.0 copy-done.13
  62.4 15.3 %all-to-all-start.2 = ((bf16[16,256,128]{2,1,0:T(8,128)(2,1)}), bf16[16,256,128]{2,1,0:T(8,128)(2,1)S(1)}, u32[]{:S(2)}, u32[]{:S(2)}) async-start(bf16[16,256,128]{2,1,0:T(8,128)(2,1)} %get-tuple-element.9), calls=%async_computation.2 | async-start | bytes 2097152 | tf_op jit(solution)/shard_map/all_to_all | solution.py:706
  77.7 6.0 %collective-permute-done.1.far.near_ref = bf16[8,256,128]{2,1,0:T(8,128)(2,1)S(1)} collective-permute-done((bf16[8,256,128]{2,1,0:T(8,128)(2,1)}, bf16[8,256,128]{2,1,0:T(8,128)(2,1)S(1)}, u32[]{:S(2)}, u32[]{:S(2)}) %collective-permute-start.1) | collective-permute-done | bytes 524320 | tf_op jit(solution)/shard_map/ppermute | solution.py:712
  83.7 0.0 copy-done.9
  83.7 2.0 to_crossed.3
  85.7 0.0 copy-done.16
  85.7 0.6 copy-done.15
  86.3 10.4 %all-to-all-done.2.refs_2_ = bf16[16,256,128]{2,1,0:T(8,128)(2,1)S(1)} async-done(((bf16[16,256,128]{2,1,0:T(8,128)(2,1)}), bf16[16,256,128]{2,1,0:T(8,128)(2,1)S(1)}, u32[]{:S(2)}, u32[]{:S(2)}) %all-to-all-start.2) | async-done | bytes 1048608 | tf_op jit(solution)/shard_map/all_to_all | solution.py:706
  96.7 4.5 %all-to-all-start.3 = ((bf16[16,256,128]{2,1,0:T(8,128)(2,1)}), bf16[16,256,128]{2,1,0:T(8,128)(2,1)}, u32[]{:S(2)}, u32[]{:S(2)}) async-start(bf16[16,256,128]{2,1,0:T(8,128)(2,1)} %get-tuple-element.11), calls=%async_computation.3 | async-start | bytes 2097152 | tf_op jit(solution)/shard_map/all_to_all | solution.py:706
  101.2 0.0 copy-done.18
  101.3 0.0 copy-done.19
  101.3 1.1 pad_maximum_fusion.refs_0_
  102.3 0.0 copy-done.5
  102.3 0.7 collective-permute-start.2
  103.0 0.9 copy-done.1
  103.9 0.3 copy-done.6
  104.2 3.5 %to_mirror.1.refs_0_ = f32[1024,1024]{1,0:T(8,128)} custom-call(bf16[4096,128]{1,0:T(8,128)(2,1)S(1)} %bitcast.12, bf16[1024,1024]{1,0:T(8,128)(2,1)S(1)} %copy-done.1), custom_call_target="tpu_custom_call" | custom-call | tf_op jit(solution)/shard_map/to_mirror/pallas_call | solution.py:453
  107.7 18.8 %all-to-all-done.3 = bf16[16,256,128]{2,1,0:T(8,128)(2,1)} async-done(((bf16[16,256,128]{2,1,0:T(8,128)(2,1)}), bf16[16,256,128]{2,1,0:T(8,128)(2,1)}, u32[]{:S(2)}, u32[]{:S(2)}) %all-to-all-start.3) | async-done | bytes 1048608 | tf_op jit(solution)/shard_map/all_to_all | solution.py:706
  126.5 11.8 %to_sigma.1.rest_0_.rest_1_ = bf16[16,512,128]{2,1,0:T(8,128)(2,1)} custom-call(f32[1024,1024]{1,0:T(8,128)} %to_mirror.1.refs_0_, bf16[4096,128]{1,0:T(8,128)(2,1)} %bitcast.6.refs_1_, bf16[1024,1024]{1,0:T(8,128)(2,1)} %copy-done.2, bf16[1024,1024]{1,0:T(8,128)(2,1)} %copy-done, bf16[1024,1024]{1,0:T(8,128)(2,1)} %copy-done, ...), custom_call_target="tpu_custom_call" | custom-call | tf_op jit(solution)/shard_map/to_sigma/pallas_call | solution.py:520
  138.2 4.7 %all-to-all-start.4 = ((bf16[16,512,128]{2,1,0:T(8,128)(2,1)}), bf16[16,512,128]{2,1,0:T(8,128)(2,1)}, u32[]{:S(2)}, u32[]{:S(2)}) async-start(bf16[16,512,128]{2,1,0:T(8,128)(2,1)} %to_sigma.1.rest_0_.rest_1_), calls=%async_computation.4 | async-start | bytes 4194304 | tf_op jit(solution)/shard_map/all_to_all | solution.py:706
  143.0 0.0 copy-start.10
  143.0 8.4 %collective-permute-done.2.away_ref = bf16[2,8,256,128]{3,2,1,0:T(8,128)(2,1)} collective-permute-done((bf16[2,8,256,128]{3,2,1,0:T(8,128)(2,1)}, bf16[2,8,256,128]{3,2,1,0:T(8,128)(2,1)}, u32[]{:S(2)}, u32[]{:S(2)}) %collective-permute-start.2) | collective-permute-done | bytes 1048608 | tf_op jit(solution)/shard_map/ppermute | solution.py:712
  151.3 0.0 copy-done.8
  151.3 0.0 copy-done.11
  151.3 1.0 copy-done.14
  152.4 3.0 %make_rights.2.rest_0_ = bf16[32,384,256]{2,1,0:T(8,128)(2,1)} custom-call(s32[1]{0:T(128)} %bitcast.half_ref, bf16[16,256,128]{2,1,0:T(8,128)(2,1)S(1)} %copy-done.8, bf16[8,256,128]{2,1,0:T(8,128)(2,1)S(1)} %copy-done.14, bf16[2,8,256,128]{3,2,1,0:T(8,128)(2,1)} %collective-permute-done.2.away_ref, bf16[16,512,128]{2,1,0:T(8,128)(2,1)S(1)} %copy-done.11), custom_call_target="tpu_custom_call" | custom-call | flops 99999997952 | bytes 1048576 | tf_op jit(solution)/shard_map/make_rights/pallas_call | solution.py:592
  155.4 0.0 copy-done.10
  155.4 3.0 %make_rights.3.rights = bf16[32,384,256]{2,1,0:T(8,128)(2,1)} custom-call(s32[1]{0:T(128)} %bitcast.half_ref, bf16[16,256,128]{2,1,0:T(8,128)(2,1)S(1)} %copy-done.10, bf16[8,256,128]{2,1,0:T(8,128)(2,1)S(1)} %copy-done.17, bf16[2,8,256,128]{3,2,1,0:T(8,128)(2,1)} %collective-permute-done.2.away_ref, ...), custom_call_target="tpu_custom_call", output_to_operand_aliasing={{}: (4, {})} | custom-call | flops 99999997952 | bytes 1048576 | tf_op jit(solution)/shard_map/make_rights/pallas_call | solution.py:592
  158.4 19.1 %all-to-all-done.4.sigma = bf16[16,512,128]{2,1,0:T(8,128)(2,1)} async-done(((bf16[16,512,128]{2,1,0:T(8,128)(2,1)}), bf16[16,512,128]{2,1,0:T(8,128)(2,1)}, u32[]{:S(2)}, u32[]{:S(2)}) %all-to-all-start.4) | async-done | bytes 2097184 | tf_op jit(solution)/shard_map/all_to_all | solution.py:706
  177.5 5.3 %volterra.1 = bf16[16,512,128]{2,1,0:T(8,128)(2,1)S(1)} custom-call(s32[1]{0:T(128)} %bitcast.half_ref, bf16[16,512,128]{2,1,0:T(8,128)(2,1)} %all-to-all-done.4.sigma, bf16[32,384,256]{2,1,0:T(8,128)(2,1)} %make_rights.3.rights), custom_call_target="tpu_custom_call" | custom-call | tf_op jit(solution)/shard_map/volterra/pallas_call | solution.py:680
  182.8 30.0 %all_to_all.30.blocks_ref = bf16[16,512,128]{2,1,0:T(8,128)(2,1)S(1)} all-to-all(bf16[16,512,128]{2,1,0:T(8,128)(2,1)S(1)} %volterra.1), channel_id=1, replica_groups=mesh['half'=2,'line'=8,'tcol'=2] {'tcol','line'}, dimensions={0} | all-to-all | bytes 4194304 | tf_op jit(solution)/shard_map/all_to_all | solution.py:706
  212.8 2.6 %collect.1 = (bf16[2,8,64,512]{3,2,1,0:T(8,128)(2,1)}, bf16[2,8,64,512]{3,2,1,0:T(8,128)(2,1)}) custom-call(bf16[16,512,128]{2,1,0:T(8,128)(2,1)S(1)} %all_to_all.30.blocks_ref), custom_call_target="tpu_custom_call" | custom-call | tf_op jit(solution)/shard_map/collect/pallas_call | solution.py:293
  (18 shorter events, 0.0 us)
Async XLA Ops:
  3.3 23.6 %all-to-all-start = ((bf16[16,256,128]{2,1,0:T(8,128)(2,1)}), bf16[16,256,128]{2,1,0:T(8,128)(2,1)S(1)}, u32[]{:S(2)}, u32[]{:S(2)}) async-start(bf16[16,256,128]{2,1,0:T(8,128)(2,1)} %bitcast.14), calls=%async_computation | async-start | bytes 2097152 | tf_op jit(solution)/shard_map/all_to_all | solution.py:706
  9.6 3.7 %copy-start.20 = (s32[512]{0:T(512)S(1)}, s32[512]{0:T(512)}, u32[]{:S(2)}) copy-start(s32[512]{0:T(512)} %param.6) | copy-start | bytes 6148
  9.6 11.2 %copy-start.3 = (bf16[2,8,64,512]{3,2,1,0:T(8,128)(2,1)S(1)}, bf16[2,8,64,512]{3,2,1,0:T(8,128)(2,1)}, u32[]{:S(2)}) copy-start(bf16[2,8,64,512]{3,2,1,0:T(8,128)(2,1)} %lesser.5) | copy-start | bytes 3145732
  9.6 11.1 %copy-start.4 = (bf16[2,8,64,512]{3,2,1,0:T(8,128)(2,1)S(1)}, bf16[2,8,64,512]{3,2,1,0:T(8,128)(2,1)}, u32[]{:S(2)}) copy-start(bf16[2,8,64,512]{3,2,1,0:T(8,128)(2,1)} %greater.5) | copy-start | bytes 3145732
  18.0 1.4 copy-start
  19.3 1.4 copy-start.12
  24.7 1.4 copy-start.2
  26.8 33.5 %copy-start.7 = (bf16[16,256,128]{2,1,0:T(8,128)(2,1)}, bf16[16,256,128]{2,1,0:T(8,128)(2,1)S(1)}, u32[]{:S(2)}) copy-start(bf16[16,256,128]{2,1,0:T(8,128)(2,1)S(1)} %all-to-all-done.own) | copy-start | bytes 3145732
  26.8 32.4 %all-to-all-start.1 = ((bf16[16,256,128]{2,1,0:T(8,128)(2,1)}), bf16[16,256,128]{2,1,0:T(8,128)(2,1)S(1)}, u32[]{:S(2)}, u32[]{:S(2)}) async-start(bf16[16,256,128]{2,1,0:T(8,128)(2,1)} %gate.2), calls=%async_computation.1 | async-start | bytes 2097152 | tf_op jit(solution)/shard_map/all_to_all | solution.py:706
  33.0 27.3 %collective-permute-start = (bf16[8,256,128]{2,1,0:T(8,128)(2,1)}, bf16[8,256,128]{2,1,0:T(8,128)(2,1)S(1)}, u32[]{:S(2)}, u32[]{:S(2)}) collective-permute-start(bf16[8,256,128]{2,1,0:T(8,128)(2,1)} %get-tuple-element.15), channel_id=1, source_target_pairs={{0,16},{16,0},{1,17},{17,1},{2,18},{18,2},{3,19},{19,3},{4,20},{20... | collective-permute-start | bytes 1572872 | tf_op jit(solution)/shard_map/ppermute | solution.py:712
  59.2 24.5 %copy-start.9 = (bf16[16,256,128]{2,1,0:T(8,128)(2,1)}, bf16[16,256,128]{2,1,0:T(8,128)(2,1)S(1)}, u32[]{:S(2)}) copy-start(bf16[16,256,128]{2,1,0:T(8,128)(2,1)S(1)} %all-to-all-done.1.rest_0_.own) | copy-start | bytes 3145732
  60.3 23.3 %collective-permute-start.1 = (bf16[8,256,128]{2,1,0:T(8,128)(2,1)}, bf16[8,256,128]{2,1,0:T(8,128)(2,1)S(1)}, u32[]{:S(2)}, u32[]{:S(2)}) collective-permute-start(bf16[8,256,128]{2,1,0:T(8,128)(2,1)} %get-tuple-element.17), channel_id=1, source_target_pairs={{0,16},{16,0},{1,17},{17,1},{2,18},{18,2},{3,19},{19,3},{4,20},{20... | collective-permute-start | bytes 1572872 | tf_op jit(solution)/shard_map/ppermute | solution.py:712
  60.3 2.0 copy-start.13
  62.4 34.4 %all-to-all-start.2 = ((bf16[16,256,128]{2,1,0:T(8,128)(2,1)}), bf16[16,256,128]{2,1,0:T(8,128)(2,1)S(1)}, u32[]{:S(2)}, u32[]{:S(2)}) async-start(bf16[16,256,128]{2,1,0:T(8,128)(2,1)} %get-tuple-element.9), calls=%async_computation.2 | async-start | bytes 2097152 | tf_op jit(solution)/shard_map/all_to_all | solution.py:706
  83.7 2.0 copy-start.16
  85.7 0.6 copy-start.15
  86.3 15.0 %copy-start.18 = (bf16[1,8,256,128]{3,2,1,0:T(8,128)(2,1)S(1)}, bf16[1,8,256,128]{3,2,1,0:T(8,128)(2,1)}, u32[]{:S(2)}) copy-start(bf16[1,8,256,128]{3,2,1,0:T(8,128)(2,1)} %get-tuple-element.14) | copy-start | bytes 1572868
  86.3 15.0 %copy-start.19 = (bf16[1,8,256,128]{3,2,1,0:T(8,128)(2,1)S(1)}, bf16[1,8,256,128]{3,2,1,0:T(8,128)(2,1)}, u32[]{:S(2)}) copy-start(bf16[1,8,256,128]{3,2,1,0:T(8,128)(2,1)} %get-tuple-element.16) | copy-start | bytes 1572868
  96.7 5.6 %copy-start.5 = (bf16[16,256,128]{2,1,0:T(8,128)(2,1)}, bf16[16,256,128]{2,1,0:T(8,128)(2,1)S(1)}, u32[]{:S(2)}) copy-start(bf16[16,256,128]{2,1,0:T(8,128)(2,1)S(1)} %all-to-all-done.2.refs_2_) | copy-start | bytes 3145732
  96.7 29.8 %all-to-all-start.3 = ((bf16[16,256,128]{2,1,0:T(8,128)(2,1)}), bf16[16,256,128]{2,1,0:T(8,128)(2,1)}, u32[]{:S(2)}, u32[]{:S(2)}) async-start(bf16[16,256,128]{2,1,0:T(8,128)(2,1)} %get-tuple-element.11), calls=%async_computation.3 | async-start | bytes 2097152 | tf_op jit(solution)/shard_map/all_to_all | solution.py:706
  102.3 1.6 copy-start.1
  102.3 1.9 copy-start.6
  102.3 49.0 %collective-permute-start.2 = (bf16[2,8,256,128]{3,2,1,0:T(8,128)(2,1)}, bf16[2,8,256,128]{3,2,1,0:T(8,128)(2,1)}, u32[]{:S(2)}, u32[]{:S(2)}) collective-permute-start(bf16[2,8,256,128]{3,2,1,0:T(8,128)(2,1)} %gate.3), channel_id=1, source_target_pairs={{0,16},{16,0},{1,17},{17,1},{2,18},{18,2},{3,19},{19,3},{4,20},{20... | collective-permute-start | bytes 3145736 | tf_op jit(solution)/shard_map/ppermute | solution.py:712
  138.2 13.1 %copy-start.8 = (bf16[16,256,128]{2,1,0:T(8,128)(2,1)S(1)}, bf16[16,256,128]{2,1,0:T(8,128)(2,1)}, u32[]{:S(2)}) copy-start(bf16[16,256,128]{2,1,0:T(8,128)(2,1)} %copy-done.7) | copy-start | bytes 3145732
  138.2 13.1 %copy-start.11 = (bf16[16,512,128]{2,1,0:T(8,128)(2,1)S(1)}, bf16[16,512,128]{2,1,0:T(8,128)(2,1)}, u32[]{:S(2)}) copy-start(bf16[16,512,128]{2,1,0:T(8,128)(2,1)} %to_sigma.1.rest_0_.rest_1_) | copy-start | bytes 6291460
  138.2 39.3 %all-to-all-start.4 = ((bf16[16,512,128]{2,1,0:T(8,128)(2,1)}), bf16[16,512,128]{2,1,0:T(8,128)(2,1)}, u32[]{:S(2)}, u32[]{:S(2)}) async-start(bf16[16,512,128]{2,1,0:T(8,128)(2,1)} %to_sigma.1.rest_0_.rest_1_), calls=%async_computation.4 | async-start | bytes 4194304 | tf_op jit(solution)/shard_map/all_to_all | solution.py:706
  143.0 12.4 %copy-start.10 = (bf16[16,256,128]{2,1,0:T(8,128)(2,1)S(1)}, bf16[16,256,128]{2,1,0:T(8,128)(2,1)}, u32[]{:S(2)}) copy-start(bf16[16,256,128]{2,1,0:T(8,128)(2,1)} %copy-done.9) | copy-start | bytes 3145732
  151.3 1.0 copy-start.14
  152.4 3.0 %copy-start.17 = (bf16[8,256,128]{2,1,0:T(8,128)(2,1)S(1)}, bf16[8,256,128]{2,1,0:T(8,128)(2,1)}, u32[]{:S(2)}) copy-start(bf16[8,256,128]{2,1,0:T(8,128)(2,1)} %copy-done.16) | copy-start | bytes 1572868

commit v11 on v10

--- a/solution.py
+++ b/solution.py
@@ -269,33 +269,31 @@
     )(*tiles)
 
 
-def collect_kernel(parts, blocks_ref, lesser, greater, lines):
-    _, rows, cols, momenta = lesser.shape
+def collect_kernel(blocks_ref, lesser, greater, lines):
+    _, rows, cols, count = lesser.shape
     blocks, height, _ = blocks_ref.shape
-    height = height // parts
-    for part in range(parts):
-        for block in range(blocks):
-            lines[block * height : (block + 1) * height] = blocks_ref[
-                block, part * height : (part + 1) * height
-            ].astype(F32)
-        count = momenta // parts
-        span = slice(part * count, (part + 1) * count)
-        for k in range(2 * rows):
-            slab = lines[pl.ds(k, count, stride=2 * rows), :].T.astype(BF16)
-            out = lesser if k < rows else greater
-            out[0, k % rows, :, span] = slab[:cols]
-            out[1, k % rows, :, span] = slab[cols:]
+    for block in range(blocks):
+        lines[block * height : (block + 1) * height] = blocks_ref[block].astype(F32)
+    for k in range(2 * rows):
+        slab = lines[pl.ds(k, count, stride=2 * rows), :].T.astype(BF16)
+        out = lesser if k < rows else greater
+        out[0, k % rows] = slab[:cols]
+        out[1, k % rows] = slab[cols:]
 
 
 def collect(blocks, tile_shape):
     shape = jax.ShapeDtypeStruct(tile_shape, BF16)
-    lines = blocks.shape[0] * blocks.shape[1] // PARTS
-    return pl.pallas_call(
-        functools.partial(collect_kernel, PARTS),
+    sources, lines, lanes = blocks.shape
+    height = lines // PARTS
+    block_shape = tile_shape[:3] + (tile_shape[3] // PARTS,)
+    tile_spec = pl.BlockSpec(block_shape, lambda p: (0, 0, 0, p))
+    return pl.pallas_call(
+        collect_kernel,
+        grid=(PARTS,),
         out_shape=(shape, shape),
-        in_specs=whole(1),
-        out_specs=tuple(whole(2)),
-        scratch_shapes=[pltpu.VMEM((lines, blocks.shape[2]), F32)],
+        in_specs=[pl.BlockSpec((sources, height, lanes), lambda p: (0, p, 0))],
+        out_specs=(tile_spec, tile_spec),
+        scratch_shapes=[pltpu.VMEM((sources * height, lanes), F32)],
         compiler_params=vmem_params(),
         name="collect",
     )(blocks)
@@ -332,7 +330,8 @@
     )(lattice_map[:, None])
 
 
-def site_kernel(norm_factor, lesser, greater, table, out):
+def site_kernel(norm_factor, lesser, greater, table, *rest):
+    out = rest[-1]
     _, rows, cols, _ = lesser.shape
     wide = 4 * cols
     for pair in range(rows // 2):
@@ -350,16 +349,16 @@
         out[:, pair * wide : (pair + 1) * wide] = (product * norm_factor).astype(BF16)
 
 
-def to_sites(tiles, table, norm_factor):
+def to_sites(tiles, table, norm_factor, after):
     _, rows, cols, momenta = tiles[0].shape
     return pl.pallas_call(
         functools.partial(site_kernel, norm_factor),
         out_shape=jax.ShapeDtypeStruct((2 * momenta, rows * 2 * cols), BF16),
-        in_specs=whole(3),
+        in_specs=whole(3) + unread(after),
         out_specs=whole(1)[0],
-        compiler_params=vmem_params(),
+        compiler_params=vmem_params(24),
         name="to_sites",
-    )(*tiles, table)
+    )(*tiles, table, *after)
 
 
 def cross_kernel(rows, half_ref, own, far, *rest):
@@ -432,109 +431,95 @@
     return jnp.dot(columns, jnp.concatenate(rights, axis=1), preferred_element_type=F32)
 
 
-def mirror_kernel(part, parts, count, crossed, table, out, read):
-    read[...] = crossed[...].astype(F32)
-    wide = 2 * crossed.shape[1]
+def part_columns(table, part, parts):
     momenta = table.shape[1] // 2
     width = momenta // parts
-    columns = jnp.concatenate(
+    return jnp.concatenate(
         [
             table[:, part * width : (part + 1) * width],
             table[:, momenta + part * width : momenta + (part + 1) * width],
         ],
         axis=1,
     )
+
+
+def mirror_kernel(part, parts, count, crossed, table, inverse, out, columns, handed, read):
+    read[...] = crossed[...].astype(F32)
+    wide = 2 * crossed.shape[1]
+    own = part_columns(table, part, parts)
     for pair in range(count // 2):
-        out[:, pair * wide : (pair + 1) * wide] = mirrored_term(columns, read, 2 * pair, count)
-
-
-def to_mirror(crossed, table, part, parts, count):
-    lines, lanes = crossed.shape
-    return pl.pallas_call(
-        functools.partial(mirror_kernel, part, parts, count),
-        out_shape=jax.ShapeDtypeStruct((table.shape[0], count * lanes), F32),
-        in_specs=whole(2),
-        out_specs=whole(1)[0],
-        scratch_shapes=[pltpu.VMEM((lines, lanes), F32)],
-        compiler_params=vmem_params(),
-        name="to_mirror",
-    )(crossed, table)
-
-
-def sigma_kernel(norm_factor, parts, *refs):
-    mirrors = refs[: parts - 1]
-    crossed, sites, cosines, sines, inverse, coupling, out, read, written = refs[parts - 1 :]
-    count = coupling.shape[0]
-    momenta = cosines.shape[0] // 2
-    step = pl.program_id(0)
-
-    @pl.when(step == 0)
-    def _():
-        read[...] = crossed[...].astype(F32)
-
-    first = 2 * step
-    columns = jnp.concatenate([cosines[...], sines[...]], axis=1)
-    other = mirrored_term(columns, read, first, count)
-    for mirror in mirrors:
-        other = other + mirror[...]
-    other = (other * norm_factor).astype(BF16).astype(F32)
-    self_real, self_imaginary = second_born(
-        sites[:momenta].astype(F32),
-        sites[momenta:].astype(F32),
-        other[:momenta],
-        -other[momenta:],
-        jnp.concatenate([coupling[pl.ds(first, 1), :], coupling[pl.ds(first + 1, 1), :]], axis=1),
-    )
-    product = jnp.dot(
-        inverse[...],
-        jnp.concatenate([self_real, self_imaginary], axis=0).astype(BF16),
-        preferred_element_type=F32,
-    )
-    product = product * norm_factor
-    for at in range(2):
-        for part in range(2):
-            written[pl.ds(part * count + first + at, momenta, stride=2 * count), :] = product[
-                part * momenta : (part + 1) * momenta, at * LANES : (at + 1) * LANES
-            ]
-
-    @pl.when(step == count // 2 - 1)
-    def _():
-        blocks, height, _ = out.shape
-        height = height // parts
-        for part in range(parts):
-            for block in range(blocks):
-                start = (part * blocks + block) * height
-                out[block, part * height : (part + 1) * height] = written[
-                    start : start + height
-                ].astype(BF16)
-
-
-def to_sigma(mirrors, crossed, sites, table, inverse, coupling, norm_factor, blocks):
-    parts = len(mirrors) + 1
+        out[:, pair * wide : (pair + 1) * wide] = mirrored_term(own, read, 2 * pair, count)
+    columns[...] = part_columns(table, parts - 1, parts)
+    handed[...] = inverse[...]
+
+
+def to_mirror(crossed, table, inverse, part, parts, count):
     lines, lanes = crossed.shape
     size = table.shape[0]
-    width = size // (2 * parts)
-    shape = (blocks, parts * lines // blocks, lanes)
-    by_step = pl.BlockSpec((size, 2 * lanes), lambda p: (0, p))
-    fixed = lambda array: pl.BlockSpec(array.shape, lambda p: (0, 0))
-    return pl.pallas_call(
-        functools.partial(sigma_kernel, norm_factor, parts),
-        grid=(coupling.shape[0] // 2,),
-        out_shape=pltpu.HBM(shape, BF16),
-        in_specs=[by_step] * (parts - 1)
-        + [
-            fixed(crossed),
-            by_step,
-            pl.BlockSpec((size, width), lambda p: (0, parts - 1)),
-            pl.BlockSpec((size, width), lambda p: (0, 2 * parts - 1)),
-            fixed(inverse),
-            fixed(coupling),
-        ],
-        out_specs=pl.BlockSpec(shape, lambda p: (0, 0, 0)),
-        scratch_shapes=[pltpu.VMEM((lines, lanes), F32), pltpu.VMEM((parts * lines, lanes), F32)],
-        compiler_params=vmem_params(58),
+    return pl.pallas_call(
+        functools.partial(mirror_kernel, part, parts, count),
+        out_shape=(
+            jax.ShapeDtypeStruct((size, count * lanes), F32),
+            jax.ShapeDtypeStruct((size, size // parts), BF16),
+            jax.ShapeDtypeStruct((size, size), BF16),
+        ),
+        in_specs=whole(3),
+        out_specs=tuple(whole(3)),
+        scratch_shapes=[pltpu.VMEM((lines, lanes), F32)],
+        compiler_params=vmem_params(24),
+        name="to_mirror",
+    )(crossed, table, inverse)
+
+
+def sigma_kernel(
+    norm_factor, mirror, crossed, sites, columns, inverse, coupling, out, read, written
+):
+    count = coupling.shape[0]
+    momenta = inverse.shape[0] // 2
+    read[...] = crossed[...].astype(F32)
+    for first in range(0, count, 2):
+        span = slice(first * LANES, (first + 2) * LANES)
+        other = mirrored_term(columns[...], read, first, count) + mirror[:, span]
+        other = (other * norm_factor).astype(BF16).astype(F32)
+        self_real, self_imaginary = second_born(
+            sites[:momenta, span].astype(F32),
+            sites[momenta:, span].astype(F32),
+            other[:momenta],
+            -other[momenta:],
+            jnp.concatenate([coupling[t : t + 1] for t in (first, first + 1)], axis=1),
+        )
+        product = jnp.dot(
+            inverse[...],
+            jnp.concatenate([self_real, self_imaginary], axis=0).astype(BF16),
+            preferred_element_type=F32,
+        )
+        product = product * norm_factor
+        for at in range(2):
+            for part in range(2):
+                written[pl.ds(part * count + first + at, momenta, stride=2 * count), :] = product[
+                    part * momenta : (part + 1) * momenta, at * LANES : (at + 1) * LANES
+                ]
+    blocks, height, _ = out.shape
+    height = height // PARTS
+    for part in range(PARTS):
+        for block in range(blocks):
+            start = (part * blocks + block) * height
+            out[block, part * height : (part + 1) * height] = written[
+                start : start + height
+            ].astype(BF16)
+
+
+def to_sigma(mirror, crossed, sites, columns, inverse, coupling, norm_factor, blocks):
+    lines, lanes = crossed.shape
+    return pl.pallas_call(
+        functools.partial(sigma_kernel, norm_factor),
+        out_shape=pltpu.HBM((blocks, PARTS * lines // blocks, lanes), BF16),
+        in_specs=whole(6),
+        out_specs=whole(1)[0],
+        scratch_shapes=[pltpu.VMEM((lines, lanes), F32), pltpu.VMEM((PARTS * lines, lanes), F32)],
+        compiler_params=vmem_params(34),
         name="to_sigma",
-    )(*mirrors, crossed, sites, table, table, inverse, coupling)
+    )(mirror, crossed, sites, columns, inverse, coupling)
 
 
 def rights_kernel(rows, half_ref, own, near_ref, away_ref, *rest):
@@ -712,7 +697,6 @@
         return lax.ppermute(array, "half", [(0, 1), (1, 0)])
 
     table, inverse = make_tables(lattice_map)
-    sites = to_sites(tiles, table, norm_factor)
     time_steps = jnp.arange(window, dtype=jnp.int32)
     coupling_line = 1.0 + drive_depth * jnp.cos(
         ((time_offset[0] + time_steps) % PERIOD).astype(F32) * (2.0 * math.pi / PERIOD)
@@ -724,7 +708,7 @@
     spread_parts = [spread(tiles, part * count, count) for part in range(PARTS)]
     own = [exchange(blocked(spread_parts[0]))]
     for rows_array in spread_parts[1:]:
-        own.append(exchange(gate(blocked(rows_array), [sites, coupling])))
+        own.append(exchange(gate(blocked(rows_array), [table, coupling])))
     far_near = [swap(lax.dynamic_slice_in_dim(blocks, (1 - half) * lines, lines)) for blocks in own]
 
     sent = []
@@ -746,10 +730,9 @@
     )
     far_away = swap(gate(kept, marks[-1:] + crossed[:-1]))
     flat = [blocks.reshape(-1, 2 * cols) for blocks in crossed]
-    mirrors = [to_mirror(flat[part], table, part, PARTS, rows) for part in range(PARTS - 1)]
-    sigma_rows = to_sigma(
-        mirrors, flat[-1], sites, table, inverse, coupling, norm_factor, group
-    )
+    sites = to_sites(tiles, table, norm_factor, marks[-1:])
+    mirror, columns, handed = to_mirror(flat[0], table, inverse, 0, PARTS, rows)
+    sigma_rows = to_sigma(mirror, flat[1], sites, columns, handed, coupling, norm_factor, group)
     sigma = exchange(sigma_rows)
     rights = []
     for part in range(PARTS):

time: 216 us -> 212 us (0.981)
  local copies, waits for them, and re-layouts: 9.48 us -> 19.5 us
  Pallas kernels: 47.1 us -> 40.4 us
  waiting for transfers between devices: 86.3 us -> 80.6 us
    unnamed x42 -> x58, local copies, waits for them, and re-layouts: 7.01 us -> 17.1 us
    all_to_all x5, waiting for transfers between devices: 71.9 us -> 68.6 us  [exchange(): return lax.all_to_all(blocks, ('tcol', 'line'), 0, 0, tiled=True)]
    pallas_call x2, Pallas kernels: 14.4 us -> 11.3 us  [the longest x1 8.65 us: to_sigma(): pl.pallas_call(functools.partial(sigma_kernel, norm_factor), out_shape=pl...]
    ppermute x3, waiting for transfers between devices: 14.4 us -> 12 us  [swap(): return lax.ppermute(array, 'half', [(0, 1), (1, 0)])]
  transfers between devices with their start and end apart: 8 -> 8, of which waited for: 6 -> 7; matrix products, arithmetic and copies ran while one was open for 2% -> 2% of each run, Pallas kernels for 17% -> 14%
where the time goes in v11:
time: 212 us
  waiting for transfers between devices  80.6 us (38%)
  Pallas kernels  40.4 us (19%)
  starting transfers between devices  37.6 us (18%)
  blocking collectives  30 us (14%)
  local copies, waits for them, and re-layouts  19.5 us (9%)
    all_to_all x5, waiting for transfers between devices, exchange(): return lax.all_to_all(blocks, ('tcol', 'line'), 0, 0, tiled=True)  68.6 us
    all_to_all x5, starting transfers between devices, exchange(): return lax.all_to_all(blocks, ('tcol', 'line'), 0, 0, tiled=True)  34.4 us
    all_to_all x1, blocking collectives, exchange(): return lax.all_to_all(blocks, ('tcol', 'line'), 0, 0, tiled=True)  30 us
    unnamed x58, local copies, waits for them, and re-layouts  17.1 us
    ppermute x3, waiting for transfers between devices, swap(): return lax.ppermute(array, 'half', [(0, 1), (1, 0)])  12 us
    pallas_call x1, Pallas kernels, to_sigma(): pl.pallas_call(functools.partial(sigma_kernel, norm_factor), out_shape=pl...  8.65 us
    pallas_call x2, Pallas kernels, make_rights(): pl.pallas_call(functools.partial(rights_kernel, rows), grid=(steps,), out...  6.01 us
    pallas_call x2, Pallas kernels, spread(): pl.pallas_call(spread_kernel, grid=(count // LANES,), out_shape=pltpu.HBM...  5.3 us
  transfers between devices with their start and end apart: 8, of which 7 were waited for; matrix products, arithmetic and copies ran while one was open for 2% of the time, Pallas kernels for 14%

profile of v11, /device:TPU:0, one launch (start us, length us, event | category | flops | bytes accessed | tf_op | source)
XLA Modules:
  0.0 211.5 jit_solution(10376406161427839137)
XLA Ops:
  0.6 2.6 %spread.2 = bf16[4096,128]{1,0:T(8,128)(2,1)} custom-call(bf16[2,8,64,512]{3,2,1,0:T(8,128)(2,1)} %lesser.5, bf16[2,8,64,512]{3,2,1,0:T(8,128)(2,1)} %greater.5), custom_call_target="tpu_custom_call" | custom-call | tf_op jit(solution)/shard_map/spread/pallas_call | solution.py:260
  3.3 6.3 %all-to-all-start = ((bf16[16,256,128]{2,1,0:T(8,128)(2,1)}), bf16[16,256,128]{2,1,0:T(8,128)(2,1)S(1)}, u32[]{:S(2)}, u32[]{:S(2)}) async-start(bf16[16,256,128]{2,1,0:T(8,128)(2,1)} %bitcast.14), calls=%async_computation | async-start | bytes 2097152 | tf_op jit(solution)/shard_map/all_to_all | solution.py:691
  9.6 0.0 copy-start.28
  9.6 2.7 %spread.3 = bf16[4096,128]{1,0:T(8,128)(2,1)} custom-call(bf16[2,8,64,512]{3,2,1,0:T(8,128)(2,1)} %lesser.5, bf16[2,8,64,512]{3,2,1,0:T(8,128)(2,1)} %greater.5), custom_call_target="tpu_custom_call" | custom-call | tf_op jit(solution)/shard_map/spread/pallas_call | solution.py:260
  12.2 0.0 copy-done.28
  12.2 0.1 copy.9.column_ref
  12.4 4.5 %make_tables.1 = (bf16[1024,1024]{1,0:T(8,128)(2,1)S(1)}, bf16[1024,1024]{1,0:T(8,128)(2,1)S(1)}) custom-call(s32[512,1]{1,0:T(8,128)S(1)} %copy.9.column_ref), custom_call_target="tpu_custom_call" | custom-call | tf_op jit(solution)/shard_map/make_tables/pallas_call | solution.py:323
  16.9 0.0 copy-start
  16.9 1.4 copy-done
  18.3 1.3 copy-done.15
  20.3 0.1 fusion.4
  20.4 0.1 dynamic_slice.20
  20.5 0.1 dynamic_slice.19
  20.5 0.1 pad_maximum_fusion.1
  20.6 0.7 broadcast_multiply_fusion.refs_2_.coupling
  21.3 4.5 %all-to-all-done.own = bf16[16,256,128]{2,1,0:T(8,128)(2,1)S(1)} async-done(((bf16[16,256,128]{2,1,0:T(8,128)(2,1)}), bf16[16,256,128]{2,1,0:T(8,128)(2,1)S(1)}, u32[]{:S(2)}, u32[]{:S(2)}) %all-to-all-start) | async-done | bytes 1048608 | tf_op jit(solution)/shard_map/all_to_all | solution.py:691
  25.8 3.7 %all-to-all-start.1 = ((bf16[16,256,128]{2,1,0:T(8,128)(2,1)}), bf16[16,256,128]{2,1,0:T(8,128)(2,1)S(1)}, u32[]{:S(2)}, u32[]{:S(2)}) async-start(bf16[16,256,128]{2,1,0:T(8,128)(2,1)} %gate.2), calls=%async_computation.1 | async-start | bytes 2097152 | tf_op jit(solution)/shard_map/all_to_all | solution.py:691
  29.4 1.0 dynamic-slice_bitcast_fusion.1
  30.5 2.6 %collective-permute-start = (bf16[8,256,128]{2,1,0:T(8,128)(2,1)}, bf16[8,256,128]{2,1,0:T(8,128)(2,1)S(1)}, u32[]{:S(2)}, u32[]{:S(2)}) collective-permute-start(bf16[8,256,128]{2,1,0:T(8,128)(2,1)} %get-tuple-element.21), channel_id=1, source_target_pairs={{0,16},{16,0},{1,17},{17,1},{2,18},{18,2},{3,19},{19,3},{4,20},{20... | collective-permute-start | bytes 1572872 | tf_op jit(solution)/shard_map/ppermute | solution.py:697
  33.1 23.6 %all-to-all-done.1.rest_0_.own = bf16[16,256,128]{2,1,0:T(8,128)(2,1)S(1)} async-done(((bf16[16,256,128]{2,1,0:T(8,128)(2,1)}), bf16[16,256,128]{2,1,0:T(8,128)(2,1)S(1)}, u32[]{:S(2)}, u32[]{:S(2)}) %all-to-all-start.1) | async-done | bytes 1048608 | tf_op jit(solution)/shard_map/all_to_all | solution.py:691
  56.7 1.1 dynamic-slice_bitcast_fusion
  57.8 0.0 collective-permute-start.1
  57.8 0.0 collective-permute-done.far.near_ref
  57.8 0.0 copy-done.6
  57.8 2.0 to_crossed.2
  59.8 0.0 copy-done.19
  59.8 15.3 %all-to-all-start.2 = ((bf16[16,256,128]{2,1,0:T(8,128)(2,1)}), bf16[16,256,128]{2,1,0:T(8,128)(2,1)S(1)}, u32[]{:S(2)}, u32[]{:S(2)}) async-start(bf16[16,256,128]{2,1,0:T(8,128)(2,1)} %get-tuple-element.12), calls=%async_computation.2 | async-start | bytes 2097152 | tf_op jit(solution)/shard_map/all_to_all | solution.py:691
  75.1 5.9 %collective-permute-done.1.far.near_ref = bf16[8,256,128]{2,1,0:T(8,128)(2,1)S(1)} collective-permute-done((bf16[8,256,128]{2,1,0:T(8,128)(2,1)}, bf16[8,256,128]{2,1,0:T(8,128)(2,1)S(1)}, u32[]{:S(2)}, u32[]{:S(2)}) %collective-permute-start.1) | collective-permute-done | bytes 524320 | tf_op jit(solution)/shard_map/ppermute | solution.py:697
  81.0 0.0 copy-done.8
  81.0 2.0 to_crossed.3
  83.0 0.6 copy-done.22
  83.6 10.5 %all-to-all-done.2.refs_2_ = bf16[16,256,128]{2,1,0:T(8,128)(2,1)S(1)} async-done(((bf16[16,256,128]{2,1,0:T(8,128)(2,1)}), bf16[16,256,128]{2,1,0:T(8,128)(2,1)S(1)}, u32[]{:S(2)}, u32[]{:S(2)}) %all-to-all-start.2) | async-done | bytes 1048608 | tf_op jit(solution)/shard_map/all_to_all | solution.py:691
  94.1 4.5 %all-to-all-start.3 = ((bf16[16,256,128]{2,1,0:T(8,128)(2,1)}), bf16[16,256,128]{2,1,0:T(8,128)(2,1)}, u32[]{:S(2)}, u32[]{:S(2)}) async-start(bf16[16,256,128]{2,1,0:T(8,128)(2,1)} %get-tuple-element.16), calls=%async_computation.3 | async-start | bytes 2097152 | tf_op jit(solution)/shard_map/all_to_all | solution.py:691
  98.7 0.0 copy-done.4
  98.7 0.0 copy-done.26
  98.7 0.0 copy-done.27
  98.7 1.1 pad_maximum_fusion.refs_0_
  99.8 0.6 collective-permute-start.2
  100.3 1.0 copy-done.1
  101.3 0.3 copy-done.2
  101.6 1.2 copy-done.3
  102.8 2.4 %to_sites.1.sites = bf16[1024,1024]{1,0:T(8,128)(2,1)S(1)} custom-call(bf16[2,8,64,512]{3,2,1,0:T(8,128)(2,1)S(1)} %copy-done.2, bf16[2,8,64,512]{3,2,1,0:T(8,128)(2,1)S(1)} %copy-done.3, bf16[1024,1024]{1,0:T(8,128)(2,1)S(1)} %copy-done.1, f32[8,128]{1,0:T(8,128)S(1)} %copy-done.23), custom_call_target="tpu_custom_call" | custom-call | tf_op jit(solution)/shard_map/to_sites/pallas_call | solution.py:354
  105.2 1.4 copy-done.11
  106.6 0.0 copy-done.5
  106.6 1.7 to_mirror.1
  108.3 0.0 copy-start.13
  108.3 2.1 copy-done.13
  110.4 1.3 copy-done.17
  111.7 12.1 %all-to-all-done.3 = bf16[16,256,128]{2,1,0:T(8,128)(2,1)} async-done(((bf16[16,256,128]{2,1,0:T(8,128)(2,1)}), bf16[16,256,128]{2,1,0:T(8,128)(2,1)}, u32[]{:S(2)}, u32[]{:S(2)}) %all-to-all-start.3) | async-done | bytes 1048608 | tf_op jit(solution)/shard_map/all_to_all | solution.py:691
  123.9 1.6 copy-done.12
  125.5 2.2 %copy-done.14 = f32[1024,1024]{1,0:T(8,128)S(1)} copy-done((f32[1024,1024]{1,0:T(8,128)S(1)}, f32[1024,1024]{1,0:T(8,128)}, u32[]{:S(2)}) %copy-start.14) | copy-done | bytes 4194328
  127.6 1.6 copy-done.18
  129.2 8.7 %to_sigma.1.rest_0_.rest_1_ = bf16[16,512,128]{2,1,0:T(8,128)(2,1)} custom-call(f32[1024,1024]{1,0:T(8,128)S(1)} %copy-done.14, bf16[4096,128]{1,0:T(8,128)(2,1)} %bitcast.6.crossed, bf16[1024,1024]{1,0:T(8,128)(2,1)S(1)} %copy-done.12, bf16[1024,512]{1,0:T(8,128)(2,1)S(1)} %get-tuple-element.18.columns, bf16[1024,1024]{1,0:T(8,128)(2,1)S(1)} %copy-done.18, ...), custom_call_target="tpu_custom_call" | custom-call | tf_op jit(solution)/shard_map/to_sigma/pallas_call | solution.py:514
  137.9 4.7 %all-to-all-start.4 = ((bf16[16,512,128]{2,1,0:T(8,128)(2,1)}), bf16[16,512,128]{2,1,0:T(8,128)(2,1)}, u32[]{:S(2)}, u32[]{:S(2)}) async-start(bf16[16,512,128]{2,1,0:T(8,128)(2,1)} %to_sigma.1.rest_0_.rest_1_), calls=%async_computation.4 | async-start | bytes 4194304 | tf_op jit(solution)/shard_map/all_to_all | solution.py:691
  142.6 6.1 %collective-permute-done.2.away_ref = bf16[2,8,256,128]{3,2,1,0:T(8,128)(2,1)} collective-permute-done((bf16[2,8,256,128]{3,2,1,0:T(8,128)(2,1)}, bf16[2,8,256,128]{3,2,1,0:T(8,128)(2,1)}, u32[]{:S(2)}, u32[]{:S(2)}) %collective-permute-start.2) | collective-permute-done | bytes 1048608 | tf_op jit(solution)/shard_map/ppermute | solution.py:697
  148.7 0.0 copy-done.10
  148.7 1.0 copy-done.20
  149.7 3.0 %make_rights.2.rest_0_ = bf16[32,384,256]{2,1,0:T(8,128)(2,1)} custom-call(s32[1]{0:T(128)} %bitcast.half_ref, bf16[16,256,128]{2,1,0:T(8,128)(2,1)S(1)} %copy-done.7, bf16[8,256,128]{2,1,0:T(8,128)(2,1)S(1)} %copy-done.20, bf16[2,8,256,128]{3,2,1,0:T(8,128)(2,1)} %collective-permute-done.2.away_ref, bf16[16,512,128]{2,1,0:T(8,128)(2,1)S(1)} %copy-done.10), custom_call_target="tpu_custom_call" | custom-call | flops 99999997952 | bytes 1048576 | tf_op jit(solution)/shard_map/make_rights/pallas_call | solution.py:577
  152.7 0.0 copy-done.9
  152.7 3.0 %make_rights.3.rights = bf16[32,384,256]{2,1,0:T(8,128)(2,1)} custom-call(s32[1]{0:T(128)} %bitcast.half_ref, bf16[16,256,128]{2,1,0:T(8,128)(2,1)S(1)} %copy-done.9, bf16[8,256,128]{2,1,0:T(8,128)(2,1)S(1)} %copy-done.25, bf16[2,8,256,128]{3,2,1,0:T(8,128)(2,1)} %collective-permute-done.2.away_ref, ...), custom_call_target="tpu_custom_call", output_to_operand_aliasing={{}: (4, {})} | custom-call | flops 99999997952 | bytes 1048576 | tf_op jit(solution)/shard_map/make_rights/pallas_call | solution.py:577
  155.8 17.9 %all-to-all-done.4.sigma = bf16[16,512,128]{2,1,0:T(8,128)(2,1)} async-done(((bf16[16,512,128]{2,1,0:T(8,128)(2,1)}), bf16[16,512,128]{2,1,0:T(8,128)(2,1)}, u32[]{:S(2)}, u32[]{:S(2)}) %all-to-all-start.4) | async-done | bytes 2097184 | tf_op jit(solution)/shard_map/all_to_all | solution.py:691
  173.6 5.3 %volterra.1 = bf16[16,512,128]{2,1,0:T(8,128)(2,1)S(1)} custom-call(s32[1]{0:T(128)} %bitcast.half_ref, bf16[16,512,128]{2,1,0:T(8,128)(2,1)} %all-to-all-done.4.sigma, bf16[32,384,256]{2,1,0:T(8,128)(2,1)} %make_rights.3.rights), custom_call_target="tpu_custom_call" | custom-call | tf_op jit(solution)/shard_map/volterra/pallas_call | solution.py:665
  178.9 30.0 %all_to_all.30.blocks_ref = bf16[16,512,128]{2,1,0:T(8,128)(2,1)S(1)} all-to-all(bf16[16,512,128]{2,1,0:T(8,128)(2,1)S(1)} %volterra.1), channel_id=1, replica_groups=mesh['half'=2,'line'=8,'tcol'=2] {'tcol','line'}, dimensions={0} | all-to-all | bytes 4194304 | tf_op jit(solution)/shard_map/all_to_all | solution.py:691
  208.9 2.6 %collect.1 = (bf16[2,8,64,512]{3,2,1,0:T(8,128)(2,1)}, bf16[2,8,64,512]{3,2,1,0:T(8,128)(2,1)}) custom-call(bf16[16,512,128]{2,1,0:T(8,128)(2,1)S(1)} %all_to_all.30.blocks_ref), custom_call_target="tpu_custom_call" | custom-call | tf_op jit(solution)/shard_map/collect/pallas_call | solution.py:290
  (34 shorter events, 0.1 us)
Async XLA Ops:
  3.3 22.5 %all-to-all-start = ((bf16[16,256,128]{2,1,0:T(8,128)(2,1)}), bf16[16,256,128]{2,1,0:T(8,128)(2,1)S(1)}, u32[]{:S(2)}, u32[]{:S(2)}) async-start(bf16[16,256,128]{2,1,0:T(8,128)(2,1)} %bitcast.14), calls=%async_computation | async-start | bytes 2097152 | tf_op jit(solution)/shard_map/all_to_all | solution.py:691
  9.6 2.7 %copy-start.28 = (s32[512]{0:T(512)S(1)}, s32[512]{0:T(512)}, u32[]{:S(2)}) copy-start(s32[512]{0:T(512)} %param.6) | copy-start | bytes 6148
  16.9 1.4 copy-start
  18.3 1.3 copy-start.15
  25.8 32.0 %copy-start.6 = (bf16[16,256,128]{2,1,0:T(8,128)(2,1)}, bf16[16,256,128]{2,1,0:T(8,128)(2,1)S(1)}, u32[]{:S(2)}) copy-start(bf16[16,256,128]{2,1,0:T(8,128)(2,1)S(1)} %all-to-all-done.own) | copy-start | bytes 3145732
  25.8 30.9 %all-to-all-start.1 = ((bf16[16,256,128]{2,1,0:T(8,128)(2,1)}), bf16[16,256,128]{2,1,0:T(8,128)(2,1)S(1)}, u32[]{:S(2)}, u32[]{:S(2)}) async-start(bf16[16,256,128]{2,1,0:T(8,128)(2,1)} %gate.2), calls=%async_computation.1 | async-start | bytes 2097152 | tf_op jit(solution)/shard_map/all_to_all | solution.py:691
  30.5 27.3 %collective-permute-start = (bf16[8,256,128]{2,1,0:T(8,128)(2,1)}, bf16[8,256,128]{2,1,0:T(8,128)(2,1)S(1)}, u32[]{:S(2)}, u32[]{:S(2)}) collective-permute-start(bf16[8,256,128]{2,1,0:T(8,128)(2,1)} %get-tuple-element.21), channel_id=1, source_target_pairs={{0,16},{16,0},{1,17},{17,1},{2,18},{18,2},{3,19},{19,3},{4,20},{20... | collective-permute-start | bytes 1572872 | tf_op jit(solution)/shard_map/ppermute | solution.py:697
  56.7 24.3 %copy-start.8 = (bf16[16,256,128]{2,1,0:T(8,128)(2,1)}, bf16[16,256,128]{2,1,0:T(8,128)(2,1)S(1)}, u32[]{:S(2)}) copy-start(bf16[16,256,128]{2,1,0:T(8,128)(2,1)S(1)} %all-to-all-done.1.rest_0_.own) | copy-start | bytes 3145732
  57.8 23.2 %collective-permute-start.1 = (bf16[8,256,128]{2,1,0:T(8,128)(2,1)}, bf16[8,256,128]{2,1,0:T(8,128)(2,1)S(1)}, u32[]{:S(2)}, u32[]{:S(2)}) collective-permute-start(bf16[8,256,128]{2,1,0:T(8,128)(2,1)} %get-tuple-element.23), channel_id=1, source_target_pairs={{0,16},{16,0},{1,17},{17,1},{2,18},{18,2},{3,19},{19,3},{4,20},{20... | collective-permute-start | bytes 1572872 | tf_op jit(solution)/shard_map/ppermute | solution.py:697
  57.8 2.0 copy-start.19
  59.8 34.3 %all-to-all-start.2 = ((bf16[16,256,128]{2,1,0:T(8,128)(2,1)}), bf16[16,256,128]{2,1,0:T(8,128)(2,1)S(1)}, u32[]{:S(2)}, u32[]{:S(2)}) async-start(bf16[16,256,128]{2,1,0:T(8,128)(2,1)} %get-tuple-element.12), calls=%async_computation.2 | async-start | bytes 2097152 | tf_op jit(solution)/shard_map/all_to_all | solution.py:691
  81.0 2.0 copy-start.24
  83.0 0.6 copy-start.22
  83.6 15.1 %copy-start.26 = (bf16[1,8,256,128]{3,2,1,0:T(8,128)(2,1)S(1)}, bf16[1,8,256,128]{3,2,1,0:T(8,128)(2,1)}, u32[]{:S(2)}) copy-start(bf16[1,8,256,128]{3,2,1,0:T(8,128)(2,1)} %get-tuple-element.20) | copy-start | bytes 1572868
  83.6 15.1 %copy-start.27 = (bf16[1,8,256,128]{3,2,1,0:T(8,128)(2,1)S(1)}, bf16[1,8,256,128]{3,2,1,0:T(8,128)(2,1)}, u32[]{:S(2)}) copy-start(bf16[1,8,256,128]{3,2,1,0:T(8,128)(2,1)} %get-tuple-element.22) | copy-start | bytes 1572868
  94.1 4.5 %copy-start.4 = (bf16[16,256,128]{2,1,0:T(8,128)(2,1)}, bf16[16,256,128]{2,1,0:T(8,128)(2,1)S(1)}, u32[]{:S(2)}) copy-start(bf16[16,256,128]{2,1,0:T(8,128)(2,1)S(1)} %all-to-all-done.2.refs_2_) | copy-start | bytes 3145732
  94.1 29.7 %all-to-all-start.3 = ((bf16[16,256,128]{2,1,0:T(8,128)(2,1)}), bf16[16,256,128]{2,1,0:T(8,128)(2,1)}, u32[]{:S(2)}, u32[]{:S(2)}) async-start(bf16[16,256,128]{2,1,0:T(8,128)(2,1)} %get-tuple-element.16), calls=%async_computation.3 | async-start | bytes 2097152 | tf_op jit(solution)/shard_map/all_to_all | solution.py:691
  99.8 1.6 copy-start.1
  99.8 1.9 copy-start.2
  99.8 1.9 copy-start.23
  99.8 48.9 %collective-permute-start.2 = (bf16[2,8,256,128]{3,2,1,0:T(8,128)(2,1)}, bf16[2,8,256,128]{3,2,1,0:T(8,128)(2,1)}, u32[]{:S(2)}, u32[]{:S(2)}) collective-permute-start(bf16[2,8,256,128]{3,2,1,0:T(8,128)(2,1)} %gate.3), channel_id=1, source_target_pairs={{0,16},{16,0},{1,17},{17,1},{2,18},{18,2},{3,19},{19,3},{4,20},{20... | collective-permute-start | bytes 3145736 | tf_op jit(solution)/shard_map/ppermute | solution.py:697
  101.6 1.2 copy-start.3
  102.8 3.8 %copy-start.5 = (bf16[16,256,128]{2,1,0:T(8,128)(2,1)S(1)}, bf16[16,256,128]{2,1,0:T(8,128)(2,1)}, u32[]{:S(2)}) copy-start(bf16[16,256,128]{2,1,0:T(8,128)(2,1)} %copy-done.4) | copy-start | bytes 3145732
  102.8 3.8 %copy-start.16 = (bf16[1024,1024]{1,0:T(8,128)(2,1)S(1)}, bf16[1024,1024]{1,0:T(8,128)(2,1)}, u32[]{:S(2)}) copy-start(bf16[1024,1024]{1,0:T(8,128)(2,1)} %copy-done.15) | copy-start | bytes 6291460
  105.2 1.4 copy-start.11
  106.6 17.2 %copy-start.21 = (f32[8,128]{1,0:T(8,128)S(1)}, f32[8,128]{1,0:T(8,128)}, u32[]{:S(2)}) copy-start(f32[8,128]{1,0:T(8,128)} %broadcast_multiply_fusion.refs_2_.coupling) | copy-start | bytes 12292
  108.3 2.1 copy-start.13
  110.4 1.3 copy-start.17
  123.9 1.6 copy-start.12
  125.5 2.2 %copy-start.14 = (f32[1024,1024]{1,0:T(8,128)S(1)}, f32[1024,1024]{1,0:T(8,128)}, u32[]{:S(2)}) copy-start(f32[1024,1024]{1,0:T(8,128)} %copy-done.13) | copy-start | bytes 12582916
  127.6 1.6 copy-start.18
  137.9 10.8 %copy-start.7 = (bf16[16,256,128]{2,1,0:T(8,128)(2,1)S(1)}, bf16[16,256,128]{2,1,0:T(8,128)(2,1)}, u32[]{:S(2)}) copy-start(bf16[16,256,128]{2,1,0:T(8,128)(2,1)} %copy-done.6) | copy-start | bytes 3145732
  137.9 10.8 %copy-start.10 = (bf16[16,512,128]{2,1,0:T(8,128)(2,1)S(1)}, bf16[16,512,128]{2,1,0:T(8,128)(2,1)}, u32[]{:S(2)}) copy-start(bf16[16,512,128]{2,1,0:T(8,128)(2,1)} %to_sigma.1.rest_0_.rest_1_) | copy-start | bytes 6291460
  137.9 35.7 %all-to-all-start.4 = ((bf16[16,512,128]{2,1,0:T(8,128)(2,1)}), bf16[16,512,128]{2,1,0:T(8,128)(2,1)}, u32[]{:S(2)}, u32[]{:S(2)}) async-start(bf16[16,512,128]{2,1,0:T(8,128)(2,1)} %to_sigma.1.rest_0_.rest_1_), calls=%async_computation.4 | async-start | bytes 4194304 | tf_op jit(solution)/shard_map/all_to_all | solution.py:691
  142.6 10.1 %copy-start.9 = (bf16[16,256,128]{2,1,0:T(8,128)(2,1)S(1)}, bf16[16,256,128]{2,1,0:T(8,128)(2,1)}, u32[]{:S(2)}) copy-start(bf16[16,256,128]{2,1,0:T(8,128)(2,1)} %copy-done.8) | copy-start | bytes 3145732
  148.7 1.0 copy-start.20
  149.7 3.0 %copy-start.25 = (bf16[8,256,128]{2,1,0:T(8,128)(2,1)S(1)}, bf16[8,256,128]{2,1,0:T(8,128)(2,1)}, u32[]{:S(2)}) copy-start(bf16[8,256,128]{2,1,0:T(8,128)(2,1)} %copy-done.24) | copy-start | bytes 1572868

commit v12 on v11

--- a/solution.py
+++ b/solution.py
@@ -443,43 +443,79 @@
     )
 
 
-def mirror_kernel(part, parts, count, crossed, table, inverse, out, columns, handed, read):
+def mirror_kernel(part, parts, count, crossed, table, out, read):
     read[...] = crossed[...].astype(F32)
     wide = 2 * crossed.shape[1]
-    own = part_columns(table, part, parts)
+    columns = part_columns(table, part, parts)
     for pair in range(count // 2):
-        out[:, pair * wide : (pair + 1) * wide] = mirrored_term(own, read, 2 * pair, count)
-    columns[...] = part_columns(table, parts - 1, parts)
-    handed[...] = inverse[...]
-
-
-def to_mirror(crossed, table, inverse, part, parts, count):
+        out[:, pair * wide : (pair + 1) * wide] = mirrored_term(columns, read, 2 * pair, count)
+
+
+def to_mirror(crossed, table, part, parts, count):
     lines, lanes = crossed.shape
-    size = table.shape[0]
     return pl.pallas_call(
         functools.partial(mirror_kernel, part, parts, count),
-        out_shape=(
-            jax.ShapeDtypeStruct((size, count * lanes), F32),
-            jax.ShapeDtypeStruct((size, size // parts), BF16),
-            jax.ShapeDtypeStruct((size, size), BF16),
-        ),
-        in_specs=whole(3),
-        out_specs=tuple(whole(3)),
+        out_shape=pltpu.HBM((table.shape[0], count * lanes), F32),
+        in_specs=whole(2),
+        out_specs=whole(1)[0],
         scratch_shapes=[pltpu.VMEM((lines, lanes), F32)],
-        compiler_params=vmem_params(24),
+        compiler_params=vmem_params(),
         name="to_mirror",
-    )(crossed, table, inverse)
+    )(crossed, table)
 
 
 def sigma_kernel(
-    norm_factor, mirror, crossed, sites, columns, inverse, coupling, out, read, written
+    norm_factor,
+    coupling,
+    mirror_from,
+    crossed_from,
+    sites_from,
+    table_from,
+    inverse_from,
+    out,
+    mirror,
+    crossed,
+    sites,
+    columns,
+    inverse,
+    staged,
+    read,
+    written,
+    sems,
 ):
     count = coupling.shape[0]
     momenta = inverse.shape[0] // 2
+    width = columns.shape[1] // 2
+
+    def column_load(at):
+        return pltpu.make_async_copy(
+            table_from.at[:, pl.ds((at * PARTS + PARTS - 1) * width, width)],
+            columns.at[:, pl.ds(at * width, width)],
+            sems.at[1 + at],
+        )
+
+    crossed_load = pltpu.make_async_copy(crossed_from, crossed, sems.at[0])
+    column_loads = [column_load(0), column_load(1)]
+    mirror_load = pltpu.make_async_copy(mirror_from, mirror, sems.at[3])
+    sites_load = pltpu.make_async_copy(sites_from, sites, sems.at[4])
+    inverse_load = pltpu.make_async_copy(inverse_from, inverse, sems.at[5])
+    crossed_load.start()
+    for load in column_loads:
+        load.start()
+    crossed_load.wait()
+    mirror_load.start()
+    sites_load.start()
+    inverse_load.start()
     read[...] = crossed[...].astype(F32)
+    for load in column_loads:
+        load.wait()
     for first in range(0, count, 2):
         span = slice(first * LANES, (first + 2) * LANES)
-        other = mirrored_term(columns[...], read, first, count) + mirror[:, span]
+        other = mirrored_term(columns[...], read, first, count)
+        if first == 0:
+            mirror_load.wait()
+            sites_load.wait()
+        other = other + mirror[:, span]
         other = (other * norm_factor).astype(BF16).astype(F32)
         self_real, self_imaginary = second_born(
             sites[:momenta, span].astype(F32),
@@ -488,6 +524,8 @@
             -other[momenta:],
             jnp.concatenate([coupling[t : t + 1] for t in (first, first + 1)], axis=1),
         )
+        if first == 0:
+            inverse_load.wait()
         product = jnp.dot(
             inverse[...],
             jnp.concatenate([self_real, self_imaginary], axis=0).astype(BF16),
@@ -501,25 +539,42 @@
                 ]
     blocks, height, _ = out.shape
     height = height // PARTS
+    stores = []
     for part in range(PARTS):
+        lines = pl.ds(part * height, height)
         for block in range(blocks):
             start = (part * blocks + block) * height
-            out[block, part * height : (part + 1) * height] = written[
-                start : start + height
-            ].astype(BF16)
-
-
-def to_sigma(mirror, crossed, sites, columns, inverse, coupling, norm_factor, blocks):
+            staged[part, block] = written[start : start + height].astype(BF16)
+        store = pltpu.make_async_copy(staged.at[part], out.at[:, lines], sems.at[6 + part])
+        store.start()
+        stores.append(store)
+    for store in stores:
+        store.wait()
+
+
+def to_sigma(mirror, crossed, sites, table, inverse, coupling, norm_factor, blocks):
     lines, lanes = crossed.shape
+    size = table.shape[0]
+    far = pl.BlockSpec(memory_space=pltpu.HBM)
     return pl.pallas_call(
         functools.partial(sigma_kernel, norm_factor),
         out_shape=pltpu.HBM((blocks, PARTS * lines // blocks, lanes), BF16),
-        in_specs=whole(6),
-        out_specs=whole(1)[0],
-        scratch_shapes=[pltpu.VMEM((lines, lanes), F32), pltpu.VMEM((PARTS * lines, lanes), F32)],
-        compiler_params=vmem_params(34),
+        in_specs=whole(1) + [far] * 5,
+        out_specs=far,
+        scratch_shapes=[
+            pltpu.VMEM(mirror.shape, F32),
+            pltpu.VMEM(crossed.shape, BF16),
+            pltpu.VMEM(sites.shape, BF16),
+            pltpu.VMEM((size, size // PARTS), BF16),
+            pltpu.VMEM(inverse.shape, BF16),
+            pltpu.VMEM((PARTS, blocks, lines // blocks, lanes), BF16),
+            pltpu.VMEM((lines, lanes), F32),
+            pltpu.VMEM((PARTS * lines, lanes), F32),
+            pltpu.SemaphoreType.DMA((6 + PARTS,)),
+        ],
+        compiler_params=vmem_params(),
         name="to_sigma",
-    )(mirror, crossed, sites, columns, inverse, coupling)
+    )(coupling, mirror, crossed, sites, table, inverse)
 
 
 def rights_kernel(rows, half_ref, own, near_ref, away_ref, *rest):
@@ -731,8 +786,8 @@
     far_away = swap(gate(kept, marks[-1:] + crossed[:-1]))
     flat = [blocks.reshape(-1, 2 * cols) for blocks in crossed]
     sites = to_sites(tiles, table, norm_factor, marks[-1:])
-    mirror, columns, handed = to_mirror(flat[0], table, inverse, 0, PARTS, rows)
-    sigma_rows = to_sigma(mirror, flat[1], sites, columns, handed, coupling, norm_factor, group)
+    mirror = to_mirror(flat[0], table, 0, PARTS, rows)
+    sigma_rows = to_sigma(mirror, flat[1], sites, table, inverse, coupling, norm_factor, group)
     sigma = exchange(sigma_rows)
     rights = []
     for part in range(PARTS):

time: 212 us -> 214 us (level)
  local copies, waits for them, and re-layouts: 19.5 us -> 12.4 us
  waiting for transfers between devices: 80.6 us -> 85.5 us
  Pallas kernels: 40.4 us -> 43.9 us
    unnamed x58 -> x48, local copies, waits for them, and re-layouts: 17.1 us -> 9.92 us
    all_to_all x5, waiting for transfers between devices: 68.6 us -> 71.3 us  [exchange(): return lax.all_to_all(blocks, ('tcol', 'line'), 0, 0, tiled=True)]
    ppermute x3, waiting for transfers between devices: 12 us -> 14.2 us  [swap(): return lax.ppermute(array, 'half', [(0, 1), (1, 0)])]
  transfers between devices with their start and end apart: 8 -> 8, of which waited for: 7 -> 7; matrix products, arithmetic and copies ran while one was open for 2% -> 2% of each run, Pallas kernels for 14% -> 16%
where the time goes in v12:
time: 214 us; the launch traced here: 213 us
  waiting for transfers between devices  85.5 us (40%)
  Pallas kernels  43.9 us (21%)
  starting transfers between devices  37.6 us (18%)
  blocking collectives  30 us (14%)
  local copies, waits for them, and re-layouts  12.4 us (6%)
    all_to_all x5, waiting for transfers between devices, exchange(): return lax.all_to_all(blocks, ('tcol', 'line'), 0, 0, tiled=True)  71.3 us
    all_to_all x5, starting transfers between devices, exchange(): return lax.all_to_all(blocks, ('tcol', 'line'), 0, 0, tiled=True)  34.4 us
    all_to_all x1, blocking collectives, exchange(): return lax.all_to_all(blocks, ('tcol', 'line'), 0, 0, tiled=True)  30 us
    ppermute x3, waiting for transfers between devices, swap(): return lax.ppermute(array, 'half', [(0, 1), (1, 0)])  14.2 us
    pallas_call x1, Pallas kernels, to_sigma(): pl.pallas_call(functools.partial(sigma_kernel, norm_factor), out_shape=pl...  10.3 us
    unnamed x48, local copies, waits for them, and re-layouts  9.92 us
    pallas_call x2, Pallas kernels, make_rights(): pl.pallas_call(functools.partial(rights_kernel, rows), grid=(steps,), out...  6.01 us
    pallas_call x2, Pallas kernels, spread(): pl.pallas_call(spread_kernel, grid=(count // LANES,), out_shape=pltpu.HBM...  5.3 us
  transfers between devices with their start and end apart: 8, of which 7 were waited for; matrix products, arithmetic and copies ran while one was open for 2% of the time, Pallas kernels for 16%

profile of v12, /device:TPU:0, one launch (start us, length us, event | category | flops | bytes accessed | tf_op | source)
XLA Modules:
  0.0 212.9 jit_solution(7641004305824875567)
XLA Ops:
  0.6 2.6 %spread.2 = bf16[4096,128]{1,0:T(8,128)(2,1)} custom-call(bf16[2,8,64,512]{3,2,1,0:T(8,128)(2,1)} %lesser.5, bf16[2,8,64,512]{3,2,1,0:T(8,128)(2,1)} %greater.5), custom_call_target="tpu_custom_call" | custom-call | tf_op jit(solution)/shard_map/spread/pallas_call | solution.py:260
  3.3 6.3 %all-to-all-start = ((bf16[16,256,128]{2,1,0:T(8,128)(2,1)}), bf16[16,256,128]{2,1,0:T(8,128)(2,1)S(1)}, u32[]{:S(2)}, u32[]{:S(2)}) async-start(bf16[16,256,128]{2,1,0:T(8,128)(2,1)} %bitcast.14), calls=%async_computation | async-start | bytes 2097152 | tf_op jit(solution)/shard_map/all_to_all | solution.py:746
  9.6 0.0 copy-start.23
  9.6 2.7 %spread.3 = bf16[4096,128]{1,0:T(8,128)(2,1)} custom-call(bf16[2,8,64,512]{3,2,1,0:T(8,128)(2,1)} %lesser.5, bf16[2,8,64,512]{3,2,1,0:T(8,128)(2,1)} %greater.5), custom_call_target="tpu_custom_call" | custom-call | tf_op jit(solution)/shard_map/spread/pallas_call | solution.py:260
  12.9 0.1 fusion.4
  12.9 0.1 dynamic_slice.18
  13.0 0.1 dynamic_slice.19
  13.1 0.0 copy-done.23
  13.1 0.1 copy.9.column_ref
  13.3 4.5 %make_tables.1 = (bf16[1024,1024]{1,0:T(8,128)(2,1)S(1)}, bf16[1024,1024]{1,0:T(8,128)(2,1)S(1)}) custom-call(s32[512,1]{1,0:T(8,128)S(1)} %copy.9.column_ref), custom_call_target="tpu_custom_call" | custom-call | tf_op jit(solution)/shard_map/make_tables/pallas_call | solution.py:323
  17.8 0.0 copy-start
  17.8 1.4 copy-done
  19.2 1.3 copy-done.13
  20.5 0.1 pad_maximum_fusion.1
  20.6 0.7 broadcast_multiply_fusion.refs_2_.coupling
  21.3 4.5 %all-to-all-done.own = bf16[16,256,128]{2,1,0:T(8,128)(2,1)S(1)} async-done(((bf16[16,256,128]{2,1,0:T(8,128)(2,1)}), bf16[16,256,128]{2,1,0:T(8,128)(2,1)S(1)}, u32[]{:S(2)}, u32[]{:S(2)}) %all-to-all-start) | async-done | bytes 1048608 | tf_op jit(solution)/shard_map/all_to_all | solution.py:746
  25.8 3.7 %all-to-all-start.1 = ((bf16[16,256,128]{2,1,0:T(8,128)(2,1)}), bf16[16,256,128]{2,1,0:T(8,128)(2,1)S(1)}, u32[]{:S(2)}, u32[]{:S(2)}) async-start(bf16[16,256,128]{2,1,0:T(8,128)(2,1)} %gate.2), calls=%async_computation.1 | async-start | bytes 2097152 | tf_op jit(solution)/shard_map/all_to_all | solution.py:746
  29.4 1.1 dynamic-slice_bitcast_fusion.1
  30.5 2.6 %collective-permute-start = (bf16[8,256,128]{2,1,0:T(8,128)(2,1)}, bf16[8,256,128]{2,1,0:T(8,128)(2,1)S(1)}, u32[]{:S(2)}, u32[]{:S(2)}) collective-permute-start(bf16[8,256,128]{2,1,0:T(8,128)(2,1)} %get-tuple-element.15), channel_id=1, source_target_pairs={{0,16},{16,0},{1,17},{17,1},{2,18},{18,2},{3,19},{19,3},{4,20},{20... | collective-permute-start | bytes 1572872 | tf_op jit(solution)/shard_map/ppermute | solution.py:752
  33.1 23.6 %all-to-all-done.1.rest_0_.own = bf16[16,256,128]{2,1,0:T(8,128)(2,1)S(1)} async-done(((bf16[16,256,128]{2,1,0:T(8,128)(2,1)}), bf16[16,256,128]{2,1,0:T(8,128)(2,1)S(1)}, u32[]{:S(2)}, u32[]{:S(2)}) %all-to-all-start.1) | async-done | bytes 1048608 | tf_op jit(solution)/shard_map/all_to_all | solution.py:746
  56.7 1.2 dynamic-slice_bitcast_fusion
  57.8 0.0 collective-permute-start.1
  57.8 0.0 collective-permute-done.far.near_ref
  57.8 0.0 copy-done.6
  57.8 2.0 to_crossed.2
  59.8 0.0 copy-done.14
  59.8 15.3 %all-to-all-start.2 = ((bf16[16,256,128]{2,1,0:T(8,128)(2,1)}), bf16[16,256,128]{2,1,0:T(8,128)(2,1)S(1)}, u32[]{:S(2)}, u32[]{:S(2)}) async-start(bf16[16,256,128]{2,1,0:T(8,128)(2,1)} %get-tuple-element.9), calls=%async_computation.2 | async-start | bytes 2097152 | tf_op jit(solution)/shard_map/all_to_all | solution.py:746
  75.1 6.0 %collective-permute-done.1.far.near_ref = bf16[8,256,128]{2,1,0:T(8,128)(2,1)S(1)} collective-permute-done((bf16[8,256,128]{2,1,0:T(8,128)(2,1)}, bf16[8,256,128]{2,1,0:T(8,128)(2,1)S(1)}, u32[]{:S(2)}, u32[]{:S(2)}) %collective-permute-start.1) | collective-permute-done | bytes 524320 | tf_op jit(solution)/shard_map/ppermute | solution.py:752
  81.1 0.0 copy-done.8
  81.1 2.0 to_crossed.3
  83.1 0.0 copy-done.19
  83.1 0.6 copy-done.17
  83.7 10.5 %all-to-all-done.2.refs_2_ = bf16[16,256,128]{2,1,0:T(8,128)(2,1)S(1)} async-done(((bf16[16,256,128]{2,1,0:T(8,128)(2,1)}), bf16[16,256,128]{2,1,0:T(8,128)(2,1)S(1)}, u32[]{:S(2)}, u32[]{:S(2)}) %all-to-all-start.2) | async-done | bytes 1048608 | tf_op jit(solution)/shard_map/all_to_all | solution.py:746
  94.2 4.5 %all-to-all-start.3 = ((bf16[16,256,128]{2,1,0:T(8,128)(2,1)}), bf16[16,256,128]{2,1,0:T(8,128)(2,1)}, u32[]{:S(2)}, u32[]{:S(2)}) async-start(bf16[16,256,128]{2,1,0:T(8,128)(2,1)} %get-tuple-element.11), calls=%async_computation.3 | async-start | bytes 2097152 | tf_op jit(solution)/shard_map/all_to_all | solution.py:746
  98.7 0.0 copy-done.4
  98.7 0.0 copy-done.21
  98.7 0.0 copy-done.22
  98.7 1.1 pad_maximum_fusion.refs_0_
  99.8 0.6 collective-permute-start.2
  100.4 1.0 copy-done.1
  101.4 0.3 copy-done.2
  101.7 0.0 copy-done.18
  101.7 1.2 copy-done.3
  102.9 2.4 %to_sites.1.sites_from = bf16[1024,1024]{1,0:T(8,128)(2,1)S(1)} custom-call(bf16[2,8,64,512]{3,2,1,0:T(8,128)(2,1)S(1)} %copy-done.2, bf16[2,8,64,512]{3,2,1,0:T(8,128)(2,1)S(1)} %copy-done.3, bf16[1024,1024]{1,0:T(8,128)(2,1)S(1)} %copy-done.1, f32[8,128]{1,0:T(8,128)S(1)} %copy-done.18), custom_call_target="tpu_custom_call" | custom-call | tf_op jit(solution)/shard_map/to_sites/pallas_call | solution.py:354
  105.3 0.0 copy-start.11
  105.3 1.4 copy-done.11
  106.7 0.0 copy-done.5
  106.7 3.6 %to_mirror.1.mirror_from = f32[1024,1024]{1,0:T(8,128)} custom-call(bf16[4096,128]{1,0:T(8,128)(2,1)S(1)} %bitcast.12, bf16[1024,1024]{1,0:T(8,128)(2,1)S(1)} %copy-done.1), custom_call_target="tpu_custom_call" | custom-call | tf_op jit(solution)/shard_map/to_mirror/pallas_call | solution.py:456
  110.3 13.6 %all-to-all-done.3 = bf16[16,256,128]{2,1,0:T(8,128)(2,1)} async-done(((bf16[16,256,128]{2,1,0:T(8,128)(2,1)}), bf16[16,256,128]{2,1,0:T(8,128)(2,1)}, u32[]{:S(2)}, u32[]{:S(2)}) %all-to-all-start.3) | async-done | bytes 1048608 | tf_op jit(solution)/shard_map/all_to_all | solution.py:746
  123.9 0.0 copy-done.16
  123.9 1.6 copy-done.12
  125.5 10.3 %to_sigma.1.rest_0_.rest_1_ = bf16[16,512,128]{2,1,0:T(8,128)(2,1)} custom-call(f32[8,128]{1,0:T(8,128)S(1)} %copy-done.16, f32[1024,1024]{1,0:T(8,128)} %to_mirror.1.mirror_from, bf16[4096,128]{1,0:T(8,128)(2,1)} %bitcast.6.crossed_from, bf16[1024,1024]{1,0:T(8,128)(2,1)S(1)} %copy-done.12, bf16[1024,1024]{1,0:T(8,128)(2,1)S(1)} %copy-done.1, ...), custom_call_target="tpu_custom_call" | custom-call | tf_op jit(solution)/shard_map/to_sigma/pallas_call | solution.py:559
  135.7 0.0 copy-start.7
  135.7 0.0 copy-start.10
  135.8 4.7 %all-to-all-start.4 = ((bf16[16,512,128]{2,1,0:T(8,128)(2,1)}), bf16[16,512,128]{2,1,0:T(8,128)(2,1)}, u32[]{:S(2)}, u32[]{:S(2)}) async-start(bf16[16,512,128]{2,1,0:T(8,128)(2,1)} %to_sigma.1.rest_0_.rest_1_), calls=%async_computation.4 | async-start | bytes 4194304 | tf_op jit(solution)/shard_map/all_to_all | solution.py:746
  140.5 8.3 %collective-permute-done.2.away_ref = bf16[2,8,256,128]{3,2,1,0:T(8,128)(2,1)} collective-permute-done((bf16[2,8,256,128]{3,2,1,0:T(8,128)(2,1)}, bf16[2,8,256,128]{3,2,1,0:T(8,128)(2,1)}, u32[]{:S(2)}, u32[]{:S(2)}) %collective-permute-start.2) | collective-permute-done | bytes 1048608 | tf_op jit(solution)/shard_map/ppermute | solution.py:752
  148.7 0.0 copy-done.10
  148.7 1.0 copy-done.15
  149.8 3.0 %make_rights.2.rest_0_ = bf16[32,384,256]{2,1,0:T(8,128)(2,1)} custom-call(s32[1]{0:T(128)} %bitcast.half_ref, bf16[16,256,128]{2,1,0:T(8,128)(2,1)S(1)} %copy-done.7, bf16[8,256,128]{2,1,0:T(8,128)(2,1)S(1)} %copy-done.15, bf16[2,8,256,128]{3,2,1,0:T(8,128)(2,1)} %collective-permute-done.2.away_ref, bf16[16,512,128]{2,1,0:T(8,128)(2,1)S(1)} %copy-done.10), custom_call_target="tpu_custom_call" | custom-call | flops 99999997952 | bytes 1048576 | tf_op jit(solution)/shard_map/make_rights/pallas_call | solution.py:632
  152.8 3.0 %make_rights.3.rights = bf16[32,384,256]{2,1,0:T(8,128)(2,1)} custom-call(s32[1]{0:T(128)} %bitcast.half_ref, bf16[16,256,128]{2,1,0:T(8,128)(2,1)S(1)} %copy-done.9, bf16[8,256,128]{2,1,0:T(8,128)(2,1)S(1)} %copy-done.20, bf16[2,8,256,128]{3,2,1,0:T(8,128)(2,1)} %collective-permute-done.2.away_ref, ...), custom_call_target="tpu_custom_call", output_to_operand_aliasing={{}: (4, {})} | custom-call | flops 99999997952 | bytes 1048576 | tf_op jit(solution)/shard_map/make_rights/pallas_call | solution.py:632
  155.8 19.2 %all-to-all-done.4.sigma = bf16[16,512,128]{2,1,0:T(8,128)(2,1)} async-done(((bf16[16,512,128]{2,1,0:T(8,128)(2,1)}), bf16[16,512,128]{2,1,0:T(8,128)(2,1)}, u32[]{:S(2)}, u32[]{:S(2)}) %all-to-all-start.4) | async-done | bytes 2097184 | tf_op jit(solution)/shard_map/all_to_all | solution.py:746
  175.0 5.3 %volterra.1 = bf16[16,512,128]{2,1,0:T(8,128)(2,1)S(1)} custom-call(s32[1]{0:T(128)} %bitcast.half_ref, bf16[16,512,128]{2,1,0:T(8,128)(2,1)} %all-to-all-done.4.sigma, bf16[32,384,256]{2,1,0:T(8,128)(2,1)} %make_rights.3.rights), custom_call_target="tpu_custom_call" | custom-call | tf_op jit(solution)/shard_map/volterra/pallas_call | solution.py:720
  180.2 30.0 %all_to_all.30.blocks_ref = bf16[16,512,128]{2,1,0:T(8,128)(2,1)S(1)} all-to-all(bf16[16,512,128]{2,1,0:T(8,128)(2,1)S(1)} %volterra.1), channel_id=1, replica_groups=mesh['half'=2,'line'=8,'tcol'=2] {'tcol','line'}, dimensions={0} | all-to-all | bytes 4194304 | tf_op jit(solution)/shard_map/all_to_all | solution.py:746
  210.3 2.6 %collect.1 = (bf16[2,8,64,512]{3,2,1,0:T(8,128)(2,1)}, bf16[2,8,64,512]{3,2,1,0:T(8,128)(2,1)}) custom-call(bf16[16,512,128]{2,1,0:T(8,128)(2,1)S(1)} %all_to_all.30.blocks_ref), custom_call_target="tpu_custom_call" | custom-call | tf_op jit(solution)/shard_map/collect/pallas_call | solution.py:290
  (24 shorter events, 0.0 us)
Async XLA Ops:
  3.3 22.5 %all-to-all-start = ((bf16[16,256,128]{2,1,0:T(8,128)(2,1)}), bf16[16,256,128]{2,1,0:T(8,128)(2,1)S(1)}, u32[]{:S(2)}, u32[]{:S(2)}) async-start(bf16[16,256,128]{2,1,0:T(8,128)(2,1)} %bitcast.14), calls=%async_computation | async-start | bytes 2097152 | tf_op jit(solution)/shard_map/all_to_all | solution.py:746
  9.6 3.5 %copy-start.23 = (s32[512]{0:T(512)S(1)}, s32[512]{0:T(512)}, u32[]{:S(2)}) copy-start(s32[512]{0:T(512)} %param.6) | copy-start | bytes 6148
  17.8 1.4 copy-start
  19.2 1.3 copy-start.13
  25.8 32.1 %copy-start.6 = (bf16[16,256,128]{2,1,0:T(8,128)(2,1)}, bf16[16,256,128]{2,1,0:T(8,128)(2,1)S(1)}, u32[]{:S(2)}) copy-start(bf16[16,256,128]{2,1,0:T(8,128)(2,1)S(1)} %all-to-all-done.own) | copy-start | bytes 3145732
  25.8 30.9 %all-to-all-start.1 = ((bf16[16,256,128]{2,1,0:T(8,128)(2,1)}), bf16[16,256,128]{2,1,0:T(8,128)(2,1)S(1)}, u32[]{:S(2)}, u32[]{:S(2)}) async-start(bf16[16,256,128]{2,1,0:T(8,128)(2,1)} %gate.2), calls=%async_computation.1 | async-start | bytes 2097152 | tf_op jit(solution)/shard_map/all_to_all | solution.py:746
  30.5 27.3 %collective-permute-start = (bf16[8,256,128]{2,1,0:T(8,128)(2,1)}, bf16[8,256,128]{2,1,0:T(8,128)(2,1)S(1)}, u32[]{:S(2)}, u32[]{:S(2)}) collective-permute-start(bf16[8,256,128]{2,1,0:T(8,128)(2,1)} %get-tuple-element.15), channel_id=1, source_target_pairs={{0,16},{16,0},{1,17},{17,1},{2,18},{18,2},{3,19},{19,3},{4,20},{20... | collective-permute-start | bytes 1572872 | tf_op jit(solution)/shard_map/ppermute | solution.py:752
  56.7 24.4 %copy-start.8 = (bf16[16,256,128]{2,1,0:T(8,128)(2,1)}, bf16[16,256,128]{2,1,0:T(8,128)(2,1)S(1)}, u32[]{:S(2)}) copy-start(bf16[16,256,128]{2,1,0:T(8,128)(2,1)S(1)} %all-to-all-done.1.rest_0_.own) | copy-start | bytes 3145732
  57.8 23.3 %collective-permute-start.1 = (bf16[8,256,128]{2,1,0:T(8,128)(2,1)}, bf16[8,256,128]{2,1,0:T(8,128)(2,1)S(1)}, u32[]{:S(2)}, u32[]{:S(2)}) collective-permute-start(bf16[8,256,128]{2,1,0:T(8,128)(2,1)} %get-tuple-element.17), channel_id=1, source_target_pairs={{0,16},{16,0},{1,17},{17,1},{2,18},{18,2},{3,19},{19,3},{4,20},{20... | collective-permute-start | bytes 1572872 | tf_op jit(solution)/shard_map/ppermute | solution.py:752
  57.8 2.0 copy-start.14
  59.8 34.3 %all-to-all-start.2 = ((bf16[16,256,128]{2,1,0:T(8,128)(2,1)}), bf16[16,256,128]{2,1,0:T(8,128)(2,1)S(1)}, u32[]{:S(2)}, u32[]{:S(2)}) async-start(bf16[16,256,128]{2,1,0:T(8,128)(2,1)} %get-tuple-element.9), calls=%async_computation.2 | async-start | bytes 2097152 | tf_op jit(solution)/shard_map/all_to_all | solution.py:746
  81.1 2.0 copy-start.19
  83.1 0.6 copy-start.17
  83.7 15.0 %copy-start.21 = (bf16[1,8,256,128]{3,2,1,0:T(8,128)(2,1)S(1)}, bf16[1,8,256,128]{3,2,1,0:T(8,128)(2,1)}, u32[]{:S(2)}) copy-start(bf16[1,8,256,128]{3,2,1,0:T(8,128)(2,1)} %get-tuple-element.14) | copy-start | bytes 1572868
  83.7 15.0 %copy-start.22 = (bf16[1,8,256,128]{3,2,1,0:T(8,128)(2,1)S(1)}, bf16[1,8,256,128]{3,2,1,0:T(8,128)(2,1)}, u32[]{:S(2)}) copy-start(bf16[1,8,256,128]{3,2,1,0:T(8,128)(2,1)} %get-tuple-element.16) | copy-start | bytes 1572868
  94.2 4.5 %copy-start.4 = (bf16[16,256,128]{2,1,0:T(8,128)(2,1)}, bf16[16,256,128]{2,1,0:T(8,128)(2,1)S(1)}, u32[]{:S(2)}) copy-start(bf16[16,256,128]{2,1,0:T(8,128)(2,1)S(1)} %all-to-all-done.2.refs_2_) | copy-start | bytes 3145732
  94.2 29.7 %all-to-all-start.3 = ((bf16[16,256,128]{2,1,0:T(8,128)(2,1)}), bf16[16,256,128]{2,1,0:T(8,128)(2,1)}, u32[]{:S(2)}, u32[]{:S(2)}) async-start(bf16[16,256,128]{2,1,0:T(8,128)(2,1)} %get-tuple-element.11), calls=%async_computation.3 | async-start | bytes 2097152 | tf_op jit(solution)/shard_map/all_to_all | solution.py:746
  99.8 1.6 copy-start.1
  99.8 1.9 copy-start.2
  99.8 1.9 copy-start.18
  99.8 48.9 %collective-permute-start.2 = (bf16[2,8,256,128]{3,2,1,0:T(8,128)(2,1)}, bf16[2,8,256,128]{3,2,1,0:T(8,128)(2,1)}, u32[]{:S(2)}, u32[]{:S(2)}) collective-permute-start(bf16[2,8,256,128]{3,2,1,0:T(8,128)(2,1)} %gate.3), channel_id=1, source_target_pairs={{0,16},{16,0},{1,17},{17,1},{2,18},{18,2},{3,19},{19,3},{4,20},{20... | collective-permute-start | bytes 3145736 | tf_op jit(solution)/shard_map/ppermute | solution.py:752
  101.7 1.2 copy-start.3
  102.9 3.8 %copy-start.5 = (bf16[16,256,128]{2,1,0:T(8,128)(2,1)S(1)}, bf16[16,256,128]{2,1,0:T(8,128)(2,1)}, u32[]{:S(2)}) copy-start(bf16[16,256,128]{2,1,0:T(8,128)(2,1)} %copy-done.4) | copy-start | bytes 3145732
  105.3 1.4 copy-start.11
  106.7 17.2 %copy-start.16 = (f32[8,128]{1,0:T(8,128)S(1)}, f32[8,128]{1,0:T(8,128)}, u32[]{:S(2)}) copy-start(f32[8,128]{1,0:T(8,128)} %broadcast_multiply_fusion.refs_2_.coupling) | copy-start | bytes 12292
  123.9 1.6 copy-start.12
  135.7 13.0 %copy-start.7 = (bf16[16,256,128]{2,1,0:T(8,128)(2,1)S(1)}, bf16[16,256,128]{2,1,0:T(8,128)(2,1)}, u32[]{:S(2)}) copy-start(bf16[16,256,128]{2,1,0:T(8,128)(2,1)} %copy-done.6) | copy-start | bytes 3145732
  135.7 13.0 %copy-start.10 = (bf16[16,512,128]{2,1,0:T(8,128)(2,1)S(1)}, bf16[16,512,128]{2,1,0:T(8,128)(2,1)}, u32[]{:S(2)}) copy-start(bf16[16,512,128]{2,1,0:T(8,128)(2,1)} %to_sigma.1.rest_0_.rest_1_) | copy-start | bytes 6291460
  135.8 39.2 %all-to-all-start.4 = ((bf16[16,512,128]{2,1,0:T(8,128)(2,1)}), bf16[16,512,128]{2,1,0:T(8,128)(2,1)}, u32[]{:S(2)}, u32[]{:S(2)}) async-start(bf16[16,512,128]{2,1,0:T(8,128)(2,1)} %to_sigma.1.rest_0_.rest_1_), calls=%async_computation.4 | async-start | bytes 4194304 | tf_op jit(solution)/shard_map/all_to_all | solution.py:746
  140.5 12.3 %copy-start.9 = (bf16[16,256,128]{2,1,0:T(8,128)(2,1)S(1)}, bf16[16,256,128]{2,1,0:T(8,128)(2,1)}, u32[]{:S(2)}) copy-start(bf16[16,256,128]{2,1,0:T(8,128)(2,1)} %copy-done.8) | copy-start | bytes 3145732
  148.7 1.0 copy-start.15
  149.8 3.0 %copy-start.20 = (bf16[8,256,128]{2,1,0:T(8,128)(2,1)S(1)}, bf16[8,256,128]{2,1,0:T(8,128)(2,1)}, u32[]{:S(2)}) copy-start(bf16[8,256,128]{2,1,0:T(8,128)(2,1)} %copy-done.19) | copy-start | bytes 1572868

commit v13 on v12

--- a/solution.py
+++ b/solution.py
@@ -353,7 +353,7 @@
     _, rows, cols, momenta = tiles[0].shape
     return pl.pallas_call(
         functools.partial(site_kernel, norm_factor),
-        out_shape=jax.ShapeDtypeStruct((2 * momenta, rows * 2 * cols), BF16),
+        out_shape=pltpu.HBM((2 * momenta, rows * 2 * cols), BF16),
         in_specs=whole(3) + unread(after),
         out_specs=whole(1)[0],
         compiler_params=vmem_params(24),
@@ -766,6 +766,9 @@
         own.append(exchange(gate(blocked(rows_array), [table, coupling])))
     far_near = [swap(lax.dynamic_slice_in_dim(blocks, (1 - half) * lines, lines)) for blocks in own]
 
+    kept = jnp.stack(
+        [lax.dynamic_slice_in_dim(blocks, half * lines, lines) for blocks in own]
+    )
     sent = []
     marks = []
     for part in range(PARTS):
@@ -774,15 +777,12 @@
             own[part],
             far_near[part],
             rows,
-            own[-1:] + marks[-1:],
-            weight() if part > 0 else None,
+            own[-1:] + marks[-1:] + ([kept] if part > 0 else []),
+            None,
         )
         sent.append(blocks)
         marks.append(mark)
     crossed = [exchange(blocks) for blocks in sent]
-    kept = jnp.stack(
-        [lax.dynamic_slice_in_dim(blocks, half * lines, lines) for blocks in own]
-    )
     far_away = swap(gate(kept, marks[-1:] + crossed[:-1]))
     flat = [blocks.reshape(-1, 2 * cols) for blocks in crossed]
     sites = to_sites(tiles, table, norm_factor, marks[-1:])

time: 214 us -> 214 us (level)
    ppermute x3, waiting for transfers between devices: 14.2 us -> 25 us  [swap(): return lax.ppermute(array, 'half', [(0, 1), (1, 0)])]
    all_to_all x5, waiting for transfers between devices: 71.3 us -> 61.5 us  [exchange(): return lax.all_to_all(blocks, ('tcol', 'line'), 0, 0, tiled=True)]
    all_to_all x5, starting transfers between devices: 34.4 us -> 26.9 us  [exchange(): return lax.all_to_all(blocks, ('tcol', 'line'), 0, 0, tiled=True)]
    ppermute x3, starting transfers between devices: 3.16 us -> 8.61 us  [swap(): return lax.ppermute(array, 'half', [(0, 1), (1, 0)])]
    unnamed x48 -> x40, local copies, waits for them, and re-layouts: 9.92 us -> 11.7 us
  transfers between devices with their start and end apart: 8 -> 8, of which waited for: 7 -> 6; matrix products, arithmetic and copies ran while one was open for 2% -> 1% of each run, Pallas kernels for 16% -> 15%
where the time goes in v13:
time: 214 us; the launch traced here: 213 us
  waiting for transfers between devices  86.5 us (40%)
  Pallas kernels  45.2 us (21%)
  starting transfers between devices  35.5 us (17%)
  blocking collectives  30.2 us (14%)
  local copies, waits for them, and re-layouts  13 us (6%)
    all_to_all x5, waiting for transfers between devices, exchange(): return lax.all_to_all(blocks, ('tcol', 'line'), 0, 0, tiled=True)  61.5 us
    all_to_all x1, blocking collectives, exchange(): return lax.all_to_all(blocks, ('tcol', 'line'), 0, 0, tiled=True)  30.2 us
    all_to_all x5, starting transfers between devices, exchange(): return lax.all_to_all(blocks, ('tcol', 'line'), 0, 0, tiled=True)  26.9 us
    ppermute x3, waiting for transfers between devices, swap(): return lax.ppermute(array, 'half', [(0, 1), (1, 0)])  25 us
    unnamed x40, local copies, waits for them, and re-layouts  11.7 us
    pallas_call x1, Pallas kernels, to_sigma(): pl.pallas_call(functools.partial(sigma_kernel, norm_factor), out_shape=pl...  10.2 us
    ppermute x3, starting transfers between devices, swap(): return lax.ppermute(array, 'half', [(0, 1), (1, 0)])  8.61 us
    pallas_call x2, Pallas kernels, make_rights(): pl.pallas_call(functools.partial(rights_kernel, rows), grid=(steps,), out...  6.02 us
  transfers between devices with their start and end apart: 8, of which 6 were waited for; matrix products, arithmetic and copies ran while one was open for 1% of the time, Pallas kernels for 15%

profile of v13, /device:TPU:0, one launch (start us, length us, event | category | flops | bytes accessed | tf_op | source)
XLA Modules:
  0.0 212.8 jit_solution(28960825494718566)
XLA Ops:
  0.6 2.6 %spread.2 = bf16[4096,128]{1,0:T(8,128)(2,1)} custom-call(bf16[2,8,64,512]{3,2,1,0:T(8,128)(2,1)} %lesser.5, bf16[2,8,64,512]{3,2,1,0:T(8,128)(2,1)} %greater.5), custom_call_target="tpu_custom_call" | custom-call | tf_op jit(solution)/shard_map/spread/pallas_call | solution.py:260
  3.3 6.3 %all-to-all-start = ((bf16[16,256,128]{2,1,0:T(8,128)(2,1)}), bf16[16,256,128]{2,1,0:T(8,128)(2,1)S(1)}, u32[]{:S(2)}, u32[]{:S(2)}) async-start(bf16[16,256,128]{2,1,0:T(8,128)(2,1)} %bitcast.14), calls=%async_computation | async-start | bytes 2097152 | tf_op jit(solution)/shard_map/all_to_all | solution.py:746
  9.6 0.0 copy-start.19
  9.6 2.7 %spread.3 = bf16[4096,128]{1,0:T(8,128)(2,1)} custom-call(bf16[2,8,64,512]{3,2,1,0:T(8,128)(2,1)} %lesser.5, bf16[2,8,64,512]{3,2,1,0:T(8,128)(2,1)} %greater.5), custom_call_target="tpu_custom_call" | custom-call | tf_op jit(solution)/shard_map/spread/pallas_call | solution.py:260
  12.9 0.1 fusion.4
  12.9 0.1 dynamic_slice.18
  13.0 0.1 dynamic_slice.19
  13.1 0.0 copy-done.19
  13.1 0.1 copy.9.column_ref
  13.3 4.5 %make_tables.1 = (bf16[1024,1024]{1,0:T(8,128)(2,1)S(1)}, bf16[1024,1024]{1,0:T(8,128)(2,1)S(1)}) custom-call(s32[512,1]{1,0:T(8,128)S(1)} %copy.9.column_ref), custom_call_target="tpu_custom_call" | custom-call | tf_op jit(solution)/shard_map/make_tables/pallas_call | solution.py:323
  17.8 0.0 copy-start
  17.8 1.3 copy-done
  19.2 1.4 copy-done.11
  20.5 0.1 pad_maximum_fusion.1
  20.6 0.7 broadcast_multiply_fusion.refs_2_.coupling
  21.3 4.5 %all-to-all-done.own = bf16[16,256,128]{2,1,0:T(8,128)(2,1)S(1)} async-done(((bf16[16,256,128]{2,1,0:T(8,128)(2,1)}), bf16[16,256,128]{2,1,0:T(8,128)(2,1)S(1)}, u32[]{:S(2)}, u32[]{:S(2)}) %all-to-all-start) | async-done | bytes 1048608 | tf_op jit(solution)/shard_map/all_to_all | solution.py:746
  25.8 3.7 %all-to-all-start.1 = ((bf16[16,256,128]{2,1,0:T(8,128)(2,1)}), bf16[16,256,128]{2,1,0:T(8,128)(2,1)S(1)}, u32[]{:S(2)}, u32[]{:S(2)}) async-start(bf16[16,256,128]{2,1,0:T(8,128)(2,1)} %gate.2), calls=%async_computation.1 | async-start | bytes 2097152 | tf_op jit(solution)/shard_map/all_to_all | solution.py:746
  29.4 0.9 dynamic-slice_bitcast_fusion.1
  30.3 2.6 %collective-permute-start = (bf16[8,256,128]{2,1,0:T(8,128)(2,1)}, bf16[8,256,128]{2,1,0:T(8,128)(2,1)S(1)}, u32[]{:S(2)}, u32[]{:S(2)}) collective-permute-start(bf16[8,256,128]{2,1,0:T(8,128)(2,1)} %get-tuple-element.15), channel_id=1, source_target_pairs={{0,16},{16,0},{1,17},{17,1},{2,18},{18,2},{3,19},{19,3},{4,20},{20... | collective-permute-start | bytes 1572872 | tf_op jit(solution)/shard_map/ppermute | solution.py:752
  32.9 23.9 %all-to-all-done.1.rest_0_.own = bf16[16,256,128]{2,1,0:T(8,128)(2,1)S(1)} async-done(((bf16[16,256,128]{2,1,0:T(8,128)(2,1)}), bf16[16,256,128]{2,1,0:T(8,128)(2,1)S(1)}, u32[]{:S(2)}, u32[]{:S(2)}) %all-to-all-start.1) | async-done | bytes 1048608 | tf_op jit(solution)/shard_map/all_to_all | solution.py:746
  56.8 0.0 collective-permute-done.far.near_ref
  56.8 0.0 copy-done.7
  56.8 2.0 to_crossed.2
  58.8 0.0 copy-done.14
  58.8 4.2 %all-to-all-start.2 = ((bf16[16,256,128]{2,1,0:T(8,128)(2,1)}), bf16[16,256,128]{2,1,0:T(8,128)(2,1)S(1)}, u32[]{:S(2)}, u32[]{:S(2)}) async-start(bf16[16,256,128]{2,1,0:T(8,128)(2,1)} %get-tuple-element.9), calls=%async_computation.2 | async-start | bytes 2097152 | tf_op jit(solution)/shard_map/all_to_all | solution.py:746
  63.0 0.1 dynamic-slice_bitcast_fusion
  63.1 3.3 %collective-permute-start.1 = (bf16[8,256,128]{2,1,0:T(8,128)(2,1)S(1)}, bf16[8,256,128]{2,1,0:T(8,128)(2,1)S(1)}, u32[]{:S(2)}, u32[]{:S(2)}) collective-permute-start(bf16[8,256,128]{2,1,0:T(8,128)(2,1)S(1)} %get-tuple-element.17), channel_id=1, source_target_pairs={{0,16},{16,0},{1,17},{17,1},{2,18},{18,2},{3,19},{19,3},{4,20},{20... | collective-permute-start | bytes 1572872 | tf_op jit(solution)/shard_map/ppermute | solution.py:752
  66.5 0.1 pad_maximum_fusion.rest_2_.refs_0_
  66.6 20.5 %collective-permute-done.1.far.near_ref = bf16[8,256,128]{2,1,0:T(8,128)(2,1)S(1)} collective-permute-done((bf16[8,256,128]{2,1,0:T(8,128)(2,1)S(1)}, bf16[8,256,128]{2,1,0:T(8,128)(2,1)S(1)}, u32[]{:S(2)}, u32[]{:S(2)}) %collective-permute-start.1) | collective-permute-done | bytes 524320 | tf_op jit(solution)/shard_map/ppermute | solution.py:752
  87.0 2.0 to_crossed.3
  89.0 1.0 copy-done.6
  90.0 0.8 copy-done.12
  90.8 0.6 copy-done.17
  91.4 0.0 all-to-all-done.2.refs_2_
  91.4 1.0 copy-done.4
  92.3 8.1 %all-to-all-start.3 = ((bf16[16,256,128]{2,1,0:T(8,128)(2,1)}), bf16[16,256,128]{2,1,0:T(8,128)(2,1)}, u32[]{:S(2)}, u32[]{:S(2)}) async-start(bf16[16,256,128]{2,1,0:T(8,128)(2,1)} %get-tuple-element.11), calls=%async_computation.3 | async-start | bytes 2097152 | tf_op jit(solution)/shard_map/all_to_all | solution.py:746
  100.5 0.0 copy-start.1
  100.5 0.0 copy-start.18
  100.5 2.7 %collective-permute-start.2 = (bf16[2,8,256,128]{3,2,1,0:T(8,128)(2,1)}, bf16[2,8,256,128]{3,2,1,0:T(8,128)(2,1)}, u32[]{:S(2)}, u32[]{:S(2)}) collective-permute-start(bf16[2,8,256,128]{3,2,1,0:T(8,128)(2,1)} %gate.3), channel_id=1, source_target_pairs={{0,16},{16,0},{1,17},{17,1},{2,18},{18,2},{3,19},{19,3},{4,20},{20... | collective-permute-start | bytes 3145736 | tf_op jit(solution)/shard_map/ppermute | solution.py:752
  103.2 0.0 copy-done.1
  103.2 0.0 copy-done.18
  103.2 1.2 copy-done.2
  104.4 1.2 copy-done.3
  105.7 3.8 %to_sites.1.sites_from = bf16[1024,1024]{1,0:T(8,128)(2,1)} custom-call(bf16[2,8,64,512]{3,2,1,0:T(8,128)(2,1)S(1)} %copy-done.2, bf16[2,8,64,512]{3,2,1,0:T(8,128)(2,1)S(1)} %copy-done.3, bf16[1024,1024]{1,0:T(8,128)(2,1)S(1)} %copy-done.1, f32[8,128]{1,0:T(8,128)S(1)} %copy-done.18), custom_call_target="tpu_custom_call" | custom-call | tf_op jit(solution)/shard_map/to_sites/pallas_call | solution.py:354
  109.4 0.0 copy-done.5
  109.4 3.5 %to_mirror.1.mirror_from = f32[1024,1024]{1,0:T(8,128)} custom-call(bf16[4096,128]{1,0:T(8,128)(2,1)S(1)} %bitcast.12, bf16[1024,1024]{1,0:T(8,128)(2,1)S(1)} %copy-done.1), custom_call_target="tpu_custom_call" | custom-call | tf_op jit(solution)/shard_map/to_mirror/pallas_call | solution.py:456
  113.0 15.9 %all-to-all-done.3 = bf16[16,256,128]{2,1,0:T(8,128)(2,1)} async-done(((bf16[16,256,128]{2,1,0:T(8,128)(2,1)}), bf16[16,256,128]{2,1,0:T(8,128)(2,1)}, u32[]{:S(2)}, u32[]{:S(2)}) %all-to-all-start.3) | async-done | bytes 1048608 | tf_op jit(solution)/shard_map/all_to_all | solution.py:746
  128.8 0.0 copy-done.16
  128.8 1.6 copy-done.10
  130.4 10.2 %to_sigma.1.rest_0_.rest_1_ = bf16[16,512,128]{2,1,0:T(8,128)(2,1)} custom-call(f32[8,128]{1,0:T(8,128)S(1)} %copy-done.16, f32[1024,1024]{1,0:T(8,128)} %to_mirror.1.mirror_from, bf16[4096,128]{1,0:T(8,128)(2,1)} %bitcast.8.crossed_from, bf16[1024,1024]{1,0:T(8,128)(2,1)S(1)} %copy-done.10, bf16[1024,1024]{1,0:T(8,128)(2,1)S(1)} %copy-done.1, ...), custom_call_target="tpu_custom_call" | custom-call | tf_op jit(solution)/shard_map/to_sigma/pallas_call | solution.py:559
  140.6 0.0 copy-start.8
  140.6 0.0 copy-start.15
  140.7 4.6 %all-to-all-start.4 = ((bf16[16,512,128]{2,1,0:T(8,128)(2,1)}), bf16[16,512,128]{2,1,0:T(8,128)(2,1)}, u32[]{:S(2)}, u32[]{:S(2)}) async-start(bf16[16,512,128]{2,1,0:T(8,128)(2,1)} %to_sigma.1.rest_0_.rest_1_), calls=%async_computation.4 | async-start | bytes 4194304 | tf_op jit(solution)/shard_map/all_to_all | solution.py:746
  145.2 4.6 %collective-permute-done.2.away_ref = bf16[2,8,256,128]{3,2,1,0:T(8,128)(2,1)} collective-permute-done((bf16[2,8,256,128]{3,2,1,0:T(8,128)(2,1)}, bf16[2,8,256,128]{3,2,1,0:T(8,128)(2,1)}, u32[]{:S(2)}, u32[]{:S(2)}) %collective-permute-start.2) | collective-permute-done | bytes 1048608 | tf_op jit(solution)/shard_map/ppermute | solution.py:752
  149.8 0.0 copy-done.8
  149.8 0.0 copy-done.15
  149.8 1.6 copy-done.9
  151.4 3.0 %make_rights.2.rest_0_ = bf16[32,384,256]{2,1,0:T(8,128)(2,1)} custom-call(s32[1]{0:T(128)} %bitcast.half_ref, bf16[16,256,128]{2,1,0:T(8,128)(2,1)S(1)} %copy-done.8, bf16[8,256,128]{2,1,0:T(8,128)(2,1)S(1)} %copy-done.15, bf16[2,8,256,128]{3,2,1,0:T(8,128)(2,1)} %collective-permute-done.2.away_ref, bf16[16,512,128]{2,1,0:T(8,128)(2,1)S(1)} %copy-done.9), custom_call_target="tpu_custom_call" | custom-call | flops 99999997952 | bytes 1048576 | tf_op jit(solution)/shard_map/make_rights/pallas_call | solution.py:632
  154.4 0.0 copy-done.13
  154.4 3.0 %make_rights.3.rights = bf16[32,384,256]{2,1,0:T(8,128)(2,1)} custom-call(s32[1]{0:T(128)} %bitcast.half_ref, bf16[16,256,128]{2,1,0:T(8,128)(2,1)S(1)} %all-to-all-done.1.rest_0_.own, bf16[8,256,128]{2,1,0:T(8,128)(2,1)S(1)} %copy-done.13, bf16[2,8,256,128]{3,2,1,0:T(8,128)(2,1)} %collective-permute-done.2.away_ref, ...), custom_call_target="tpu_custom_call", output_to_operand_aliasing={{}: (4, {})} | custom-call | flops 99999997952 | bytes 1048576 | tf_op jit(solution)/shard_map/make_rights/pallas_call | solution.py:632
  157.5 17.2 %all-to-all-done.4.sigma = bf16[16,512,128]{2,1,0:T(8,128)(2,1)} async-done(((bf16[16,512,128]{2,1,0:T(8,128)(2,1)}), bf16[16,512,128]{2,1,0:T(8,128)(2,1)}, u32[]{:S(2)}, u32[]{:S(2)}) %all-to-all-start.4) | async-done | bytes 2097184 | tf_op jit(solution)/shard_map/all_to_all | solution.py:746
  174.7 5.3 %volterra.1 = bf16[16,512,128]{2,1,0:T(8,128)(2,1)S(1)} custom-call(s32[1]{0:T(128)} %bitcast.half_ref, bf16[16,512,128]{2,1,0:T(8,128)(2,1)} %all-to-all-done.4.sigma, bf16[32,384,256]{2,1,0:T(8,128)(2,1)} %make_rights.3.rights), custom_call_target="tpu_custom_call" | custom-call | tf_op jit(solution)/shard_map/volterra/pallas_call | solution.py:720
  180.0 30.2 %all_to_all.30.blocks_ref = bf16[16,512,128]{2,1,0:T(8,128)(2,1)S(1)} all-to-all(bf16[16,512,128]{2,1,0:T(8,128)(2,1)S(1)} %volterra.1), channel_id=1, replica_groups=mesh['half'=2,'line'=8,'tcol'=2] {'tcol','line'}, dimensions={0} | all-to-all | bytes 4194304 | tf_op jit(solution)/shard_map/all_to_all | solution.py:746
  210.2 2.6 %collect.1 = (bf16[2,8,64,512]{3,2,1,0:T(8,128)(2,1)}, bf16[2,8,64,512]{3,2,1,0:T(8,128)(2,1)}) custom-call(bf16[16,512,128]{2,1,0:T(8,128)(2,1)S(1)} %all_to_all.30.blocks_ref), custom_call_target="tpu_custom_call" | custom-call | tf_op jit(solution)/shard_map/collect/pallas_call | solution.py:290
  (16 shorter events, 0.0 us)
Async XLA Ops:
  3.3 22.5 %all-to-all-start = ((bf16[16,256,128]{2,1,0:T(8,128)(2,1)}), bf16[16,256,128]{2,1,0:T(8,128)(2,1)S(1)}, u32[]{:S(2)}, u32[]{:S(2)}) async-start(bf16[16,256,128]{2,1,0:T(8,128)(2,1)} %bitcast.14), calls=%async_computation | async-start | bytes 2097152 | tf_op jit(solution)/shard_map/all_to_all | solution.py:746
  9.6 3.5 %copy-start.19 = (s32[512]{0:T(512)S(1)}, s32[512]{0:T(512)}, u32[]{:S(2)}) copy-start(s32[512]{0:T(512)} %param.6) | copy-start | bytes 6148
  17.8 1.4 copy-start
  19.2 1.4 copy-start.11
  25.8 31.1 %copy-start.7 = (bf16[16,256,128]{2,1,0:T(8,128)(2,1)}, bf16[16,256,128]{2,1,0:T(8,128)(2,1)S(1)}, u32[]{:S(2)}) copy-start(bf16[16,256,128]{2,1,0:T(8,128)(2,1)S(1)} %all-to-all-done.own) | copy-start | bytes 3145732
  25.8 31.0 %all-to-all-start.1 = ((bf16[16,256,128]{2,1,0:T(8,128)(2,1)}), bf16[16,256,128]{2,1,0:T(8,128)(2,1)S(1)}, u32[]{:S(2)}, u32[]{:S(2)}) async-start(bf16[16,256,128]{2,1,0:T(8,128)(2,1)} %gate.2), calls=%async_computation.1 | async-start | bytes 2097152 | tf_op jit(solution)/shard_map/all_to_all | solution.py:746
  30.3 26.5 %collective-permute-start = (bf16[8,256,128]{2,1,0:T(8,128)(2,1)}, bf16[8,256,128]{2,1,0:T(8,128)(2,1)S(1)}, u32[]{:S(2)}, u32[]{:S(2)}) collective-permute-start(bf16[8,256,128]{2,1,0:T(8,128)(2,1)} %get-tuple-element.15), channel_id=1, source_target_pairs={{0,16},{16,0},{1,17},{17,1},{2,18},{18,2},{3,19},{19,3},{4,20},{20... | collective-permute-start | bytes 1572872 | tf_op jit(solution)/shard_map/ppermute | solution.py:752
  56.8 2.0 copy-start.14
  58.8 32.6 %all-to-all-start.2 = ((bf16[16,256,128]{2,1,0:T(8,128)(2,1)}), bf16[16,256,128]{2,1,0:T(8,128)(2,1)S(1)}, u32[]{:S(2)}, u32[]{:S(2)}) async-start(bf16[16,256,128]{2,1,0:T(8,128)(2,1)} %get-tuple-element.9), calls=%async_computation.2 | async-start | bytes 2097152 | tf_op jit(solution)/shard_map/all_to_all | solution.py:746
  63.1 23.9 %collective-permute-start.1 = (bf16[8,256,128]{2,1,0:T(8,128)(2,1)S(1)}, bf16[8,256,128]{2,1,0:T(8,128)(2,1)S(1)}, u32[]{:S(2)}, u32[]{:S(2)}) collective-permute-start(bf16[8,256,128]{2,1,0:T(8,128)(2,1)S(1)} %get-tuple-element.17), channel_id=1, source_target_pairs={{0,16},{16,0},{1,17},{17,1},{2,18},{18,2},{3,19},{19,3},{4,20},{20... | collective-permute-start | bytes 1572872 | tf_op jit(solution)/shard_map/ppermute | solution.py:752
  89.0 1.0 copy-start.6
  90.0 0.8 copy-start.12
  90.8 0.6 copy-start.17
  91.4 1.0 copy-start.4
  92.3 36.5 %all-to-all-start.3 = ((bf16[16,256,128]{2,1,0:T(8,128)(2,1)}), bf16[16,256,128]{2,1,0:T(8,128)(2,1)}, u32[]{:S(2)}, u32[]{:S(2)}) async-start(bf16[16,256,128]{2,1,0:T(8,128)(2,1)} %get-tuple-element.11), calls=%async_computation.3 | async-start | bytes 2097152 | tf_op jit(solution)/shard_map/all_to_all | solution.py:746
  100.5 2.7 %copy-start.1 = (bf16[1024,1024]{1,0:T(8,128)(2,1)S(1)}, bf16[1024,1024]{1,0:T(8,128)(2,1)}, u32[]{:S(2)}) copy-start(bf16[1024,1024]{1,0:T(8,128)(2,1)} %copy-done) | copy-start | bytes 6291460
  100.5 2.7 %copy-start.18 = (f32[8,128]{1,0:T(8,128)S(1)}, f32[8,128]{1,0:T(8,128)}, u32[]{:S(2)}) copy-start(f32[8,128]{1,0:T(8,128)} %copy-done.17) | copy-start | bytes 12292
  100.5 49.3 %collective-permute-start.2 = (bf16[2,8,256,128]{3,2,1,0:T(8,128)(2,1)}, bf16[2,8,256,128]{3,2,1,0:T(8,128)(2,1)}, u32[]{:S(2)}, u32[]{:S(2)}) collective-permute-start(bf16[2,8,256,128]{3,2,1,0:T(8,128)(2,1)} %gate.3), channel_id=1, source_target_pairs={{0,16},{16,0},{1,17},{17,1},{2,18},{18,2},{3,19},{19,3},{4,20},{20... | collective-permute-start | bytes 3145736 | tf_op jit(solution)/shard_map/ppermute | solution.py:752
  103.2 1.2 copy-start.2
  104.4 1.2 copy-start.3
  105.7 3.8 %copy-start.5 = (bf16[16,256,128]{2,1,0:T(8,128)(2,1)S(1)}, bf16[16,256,128]{2,1,0:T(8,128)(2,1)}, u32[]{:S(2)}) copy-start(bf16[16,256,128]{2,1,0:T(8,128)(2,1)} %copy-done.4) | copy-start | bytes 3145732
  109.4 19.4 %copy-start.16 = (f32[8,128]{1,0:T(8,128)S(1)}, f32[8,128]{1,0:T(8,128)}, u32[]{:S(2)}) copy-start(f32[8,128]{1,0:T(8,128)} %broadcast_multiply_fusion.refs_2_.coupling) | copy-start | bytes 12292
  128.8 1.6 copy-start.10
  140.6 9.2 %copy-start.8 = (bf16[16,256,128]{2,1,0:T(8,128)(2,1)S(1)}, bf16[16,256,128]{2,1,0:T(8,128)(2,1)}, u32[]{:S(2)}) copy-start(bf16[16,256,128]{2,1,0:T(8,128)(2,1)} %copy-done.7) | copy-start | bytes 3145732
  140.6 9.2 %copy-start.15 = (bf16[8,256,128]{2,1,0:T(8,128)(2,1)S(1)}, bf16[8,256,128]{2,1,0:T(8,128)(2,1)}, u32[]{:S(2)}) copy-start(bf16[8,256,128]{2,1,0:T(8,128)(2,1)} %copy-done.14) | copy-start | bytes 1572868
  140.7 34.0 %all-to-all-start.4 = ((bf16[16,512,128]{2,1,0:T(8,128)(2,1)}), bf16[16,512,128]{2,1,0:T(8,128)(2,1)}, u32[]{:S(2)}, u32[]{:S(2)}) async-start(bf16[16,512,128]{2,1,0:T(8,128)(2,1)} %to_sigma.1.rest_0_.rest_1_), calls=%async_computation.4 | async-start | bytes 4194304 | tf_op jit(solution)/shard_map/all_to_all | solution.py:746
  149.8 1.6 copy-start.9
  151.4 3.0 %copy-start.13 = (bf16[8,256,128]{2,1,0:T(8,128)(2,1)S(1)}, bf16[8,256,128]{2,1,0:T(8,128)(2,1)}, u32[]{:S(2)}) copy-start(bf16[8,256,128]{2,1,0:T(8,128)(2,1)} %copy-done.12) | copy-start | bytes 1572868

commit v14 on v13

--- a/solution.py
+++ b/solution.py
@@ -319,7 +319,7 @@
 
 def make_tables(lattice_map):
     momenta = lattice_map.shape[0]
-    shape = jax.ShapeDtypeStruct((2 * momenta, 2 * momenta), BF16)
+    shape = pltpu.HBM((2 * momenta, 2 * momenta), BF16)
     return pl.pallas_call(
         table_kernel,
         out_shape=(shape, shape),
@@ -777,7 +777,7 @@
             own[part],
             far_near[part],
             rows,
-            own[-1:] + marks[-1:] + ([kept] if part > 0 else []),
+            own[-1:] + marks[-1:],
             None,
         )
         sent.append(blocks)

time: 214 us -> 214 us (level)
  local copies, waits for them, and re-layouts: 13 us -> 9.16 us
    unnamed x40 -> x38, local copies, waits for them, and re-layouts: 11.7 us -> 7.06 us
  transfers between devices with their start and end apart: 8 -> 8, of which waited for: 6 -> 7; matrix products, arithmetic and copies ran while one was open for 1% -> 2% of each run, Pallas kernels for 15% -> 16%
where the time goes in v14:
time: 214 us; the launch traced here: 213 us
  waiting for transfers between devices  87.5 us (41%)
  Pallas kernels  47.2 us (22%)
  starting transfers between devices  36.1 us (17%)
  blocking collectives  30 us (14%)
  local copies, waits for them, and re-layouts  9.16 us (4%)
    all_to_all x5, waiting for transfers between devices, exchange(): return lax.all_to_all(blocks, ('tcol', 'line'), 0, 0, tiled=True)  60.4 us
    all_to_all x1, blocking collectives, exchange(): return lax.all_to_all(blocks, ('tcol', 'line'), 0, 0, tiled=True)  30 us
    ppermute x3, waiting for transfers between devices, swap(): return lax.ppermute(array, 'half', [(0, 1), (1, 0)])  27.1 us
    all_to_all x5, starting transfers between devices, exchange(): return lax.all_to_all(blocks, ('tcol', 'line'), 0, 0, tiled=True)  26.8 us
    pallas_call x1, Pallas kernels, to_sigma(): pl.pallas_call(functools.partial(sigma_kernel, norm_factor), out_shape=pl...  10.2 us
    ppermute x3, starting transfers between devices, swap(): return lax.ppermute(array, 'half', [(0, 1), (1, 0)])  9.31 us
    unnamed x38, local copies, waits for them, and re-layouts  7.06 us
    pallas_call x1, Pallas kernels, make_tables(): pl.pallas_call(table_kernel, out_shape=(shape, shape), in_specs=whole(1),...  6.4 us
  transfers between devices with their start and end apart: 8, of which 7 were waited for; matrix products, arithmetic and copies ran while one was open for 2% of the time, Pallas kernels for 16%

profile of v14, /device:TPU:0, one launch (start us, length us, event | category | flops | bytes accessed | tf_op | source)
XLA Modules:
  0.0 213.3 jit_solution(2327682032028582123)
XLA Ops:
  0.6 2.6 %spread.2 = bf16[4096,128]{1,0:T(8,128)(2,1)} custom-call(bf16[2,8,64,512]{3,2,1,0:T(8,128)(2,1)} %lesser.5, bf16[2,8,64,512]{3,2,1,0:T(8,128)(2,1)} %greater.5), custom_call_target="tpu_custom_call" | custom-call | tf_op jit(solution)/shard_map/spread/pallas_call | solution.py:260
  3.3 6.3 %all-to-all-start = ((bf16[16,256,128]{2,1,0:T(8,128)(2,1)}), bf16[16,256,128]{2,1,0:T(8,128)(2,1)S(1)}, u32[]{:S(2)}, u32[]{:S(2)}) async-start(bf16[16,256,128]{2,1,0:T(8,128)(2,1)} %bitcast.14), calls=%async_computation | async-start | bytes 2097152 | tf_op jit(solution)/shard_map/all_to_all | solution.py:746
  9.6 0.0 copy-start.18
  9.6 2.7 %spread.3 = bf16[4096,128]{1,0:T(8,128)(2,1)} custom-call(bf16[2,8,64,512]{3,2,1,0:T(8,128)(2,1)} %lesser.5, bf16[2,8,64,512]{3,2,1,0:T(8,128)(2,1)} %greater.5), custom_call_target="tpu_custom_call" | custom-call | tf_op jit(solution)/shard_map/spread/pallas_call | solution.py:260
  12.9 0.1 fusion.4
  12.9 0.1 dynamic_slice.18
  13.0 0.1 dynamic_slice.19
  13.1 0.0 copy-done.18
  13.1 0.1 copy.9.column_ref
  13.3 6.4 %make_tables.1 = (bf16[1024,1024]{1,0:T(8,128)(2,1)}, bf16[1024,1024]{1,0:T(8,128)(2,1)}) custom-call(s32[512,1]{1,0:T(8,128)S(1)} %copy.9.column_ref), custom_call_target="tpu_custom_call" | custom-call | tf_op jit(solution)/shard_map/make_tables/pallas_call | solution.py:323
  19.7 0.1 pad_maximum_fusion.1
  19.7 0.7 broadcast_multiply_fusion.refs_2_.coupling
  20.4 5.4 %all-to-all-done.own = bf16[16,256,128]{2,1,0:T(8,128)(2,1)S(1)} async-done(((bf16[16,256,128]{2,1,0:T(8,128)(2,1)}), bf16[16,256,128]{2,1,0:T(8,128)(2,1)S(1)}, u32[]{:S(2)}, u32[]{:S(2)}) %all-to-all-start) | async-done | bytes 1048608 | tf_op jit(solution)/shard_map/all_to_all | solution.py:746
  25.8 0.0 copy-start.5
  25.8 3.7 %all-to-all-start.1 = ((bf16[16,256,128]{2,1,0:T(8,128)(2,1)}), bf16[16,256,128]{2,1,0:T(8,128)(2,1)S(1)}, u32[]{:S(2)}, u32[]{:S(2)}) async-start(bf16[16,256,128]{2,1,0:T(8,128)(2,1)} %gate.2), calls=%async_computation.1 | async-start | bytes 2097152 | tf_op jit(solution)/shard_map/all_to_all | solution.py:746
  29.4 0.9 dynamic-slice_bitcast_fusion.1
  30.3 2.6 %collective-permute-start = (bf16[8,256,128]{2,1,0:T(8,128)(2,1)S(1)}, bf16[8,256,128]{2,1,0:T(8,128)(2,1)S(1)}, u32[]{:S(2)}, u32[]{:S(2)}) collective-permute-start(bf16[8,256,128]{2,1,0:T(8,128)(2,1)S(1)} %get-tuple-element.15), channel_id=1, source_target_pairs={{0,16},{16,0},{1,17},{17,1},{2,18},{18,2},{3,19},{19,3},{4,20},{20... | collective-permute-start | bytes 1572872 | tf_op jit(solution)/shard_map/ppermute | solution.py:752
  32.9 23.9 %all-to-all-done.1.rest_0_.own = bf16[16,256,128]{2,1,0:T(8,128)(2,1)S(1)} async-done(((bf16[16,256,128]{2,1,0:T(8,128)(2,1)}), bf16[16,256,128]{2,1,0:T(8,128)(2,1)S(1)}, u32[]{:S(2)}, u32[]{:S(2)}) %all-to-all-start.1) | async-done | bytes 1048608 | tf_op jit(solution)/shard_map/all_to_all | solution.py:746
  56.8 0.0 collective-permute-done.far.near_ref
  56.8 0.0 copy-done.5
  56.8 2.0 to_crossed.2
  58.8 0.0 copy-done.9
  58.8 3.9 %all-to-all-start.2 = ((bf16[16,256,128]{2,1,0:T(8,128)(2,1)}), bf16[16,256,128]{2,1,0:T(8,128)(2,1)S(1)}, u32[]{:S(2)}, u32[]{:S(2)}) async-start(bf16[16,256,128]{2,1,0:T(8,128)(2,1)} %get-tuple-element.9), calls=%async_computation.2 | async-start | bytes 2097152 | tf_op jit(solution)/shard_map/all_to_all | solution.py:746
  62.8 0.9 dynamic-slice_bitcast_fusion
  63.7 3.4 %collective-permute-start.1 = (bf16[8,256,128]{2,1,0:T(8,128)(2,1)S(1)}, bf16[8,256,128]{2,1,0:T(8,128)(2,1)S(1)}, u32[]{:S(2)}, u32[]{:S(2)}) collective-permute-start(bf16[8,256,128]{2,1,0:T(8,128)(2,1)S(1)} %get-tuple-element.17), channel_id=1, source_target_pairs={{0,16},{16,0},{1,17},{17,1},{2,18},{18,2},{3,19},{19,3},{4,20},{20... | collective-permute-start | bytes 1572872 | tf_op jit(solution)/shard_map/ppermute | solution.py:752
  67.0 19.7 %collective-permute-done.1.far.near_ref = bf16[8,256,128]{2,1,0:T(8,128)(2,1)S(1)} collective-permute-done((bf16[8,256,128]{2,1,0:T(8,128)(2,1)S(1)}, bf16[8,256,128]{2,1,0:T(8,128)(2,1)S(1)}, u32[]{:S(2)}, u32[]{:S(2)}) %collective-permute-start.1) | collective-permute-done | bytes 524320 | tf_op jit(solution)/shard_map/ppermute | solution.py:752
  86.8 0.0 copy-start.16
  86.8 2.0 to_crossed.3
  88.7 0.0 copy-start.11
  88.7 0.8 copy-done.11
  89.5 0.0 copy-start.14
  89.5 0.6 copy-done.14
  90.1 0.1 all-to-all-done.2.refs_2_
  90.2 8.3 %all-to-all-start.3 = ((bf16[16,256,128]{2,1,0:T(8,128)(2,1)}), bf16[16,256,128]{2,1,0:T(8,128)(2,1)}, u32[]{:S(2)}, u32[]{:S(2)}) async-start(bf16[16,256,128]{2,1,0:T(8,128)(2,1)} %get-tuple-element.11), calls=%async_computation.3 | async-start | bytes 2097152 | tf_op jit(solution)/shard_map/all_to_all | solution.py:746
  98.5 0.0 copy-done.3
  98.5 0.0 copy-done.16
  98.5 0.0 copy-done.17
  98.5 1.1 pad_maximum_fusion.refs_0_
  99.6 3.4 %collective-permute-start.2 = (bf16[2,8,256,128]{3,2,1,0:T(8,128)(2,1)}, bf16[2,8,256,128]{3,2,1,0:T(8,128)(2,1)}, u32[]{:S(2)}, u32[]{:S(2)}) collective-permute-start(bf16[2,8,256,128]{3,2,1,0:T(8,128)(2,1)} %gate.3), channel_id=1, source_target_pairs={{0,16},{16,0},{1,17},{17,1},{2,18},{18,2},{3,19},{19,3},{4,20},{20... | collective-permute-start | bytes 3145736 | tf_op jit(solution)/shard_map/ppermute | solution.py:752
  103.0 0.0 copy-done
  103.0 0.0 copy-done.15
  103.0 1.2 copy-done.1
  104.2 1.2 copy-done.2
  105.5 3.7 %to_sites.1.sites_from = bf16[1024,1024]{1,0:T(8,128)(2,1)} custom-call(bf16[2,8,64,512]{3,2,1,0:T(8,128)(2,1)S(1)} %copy-done.1, bf16[2,8,64,512]{3,2,1,0:T(8,128)(2,1)S(1)} %copy-done.2, bf16[1024,1024]{1,0:T(8,128)(2,1)S(1)} %copy-done, f32[8,128]{1,0:T(8,128)S(1)} %copy-done.15), custom_call_target="tpu_custom_call" | custom-call | tf_op jit(solution)/shard_map/to_sites/pallas_call | solution.py:354
  109.1 0.0 copy-done.4
  109.1 3.6 %to_mirror.1.mirror_from = f32[1024,1024]{1,0:T(8,128)} custom-call(bf16[4096,128]{1,0:T(8,128)(2,1)S(1)} %bitcast.12, bf16[1024,1024]{1,0:T(8,128)(2,1)S(1)} %copy-done), custom_call_target="tpu_custom_call" | custom-call | tf_op jit(solution)/shard_map/to_mirror/pallas_call | solution.py:456
  112.8 13.0 %all-to-all-done.3 = bf16[16,256,128]{2,1,0:T(8,128)(2,1)} async-done(((bf16[16,256,128]{2,1,0:T(8,128)(2,1)}), bf16[16,256,128]{2,1,0:T(8,128)(2,1)}, u32[]{:S(2)}, u32[]{:S(2)}) %all-to-all-start.3) | async-done | bytes 1048608 | tf_op jit(solution)/shard_map/all_to_all | solution.py:746
  125.8 0.0 copy-done.13
  125.8 1.6 copy-done.8
  127.4 10.2 %to_sigma.1.rest_0_.rest_1_ = bf16[16,512,128]{2,1,0:T(8,128)(2,1)} custom-call(f32[8,128]{1,0:T(8,128)S(1)} %copy-done.13, f32[1024,1024]{1,0:T(8,128)} %to_mirror.1.mirror_from, bf16[4096,128]{1,0:T(8,128)(2,1)} %bitcast.6.crossed_from, bf16[1024,1024]{1,0:T(8,128)(2,1)S(1)} %copy-done.8, bf16[1024,1024]{1,0:T(8,128)(2,1)S(1)} %copy-done, ...), custom_call_target="tpu_custom_call" | custom-call | tf_op jit(solution)/shard_map/to_sigma/pallas_call | solution.py:559
  137.6 0.0 copy-start.6
  137.6 0.0 copy-start.10
  137.6 4.6 %all-to-all-start.4 = ((bf16[16,512,128]{2,1,0:T(8,128)(2,1)}), bf16[16,512,128]{2,1,0:T(8,128)(2,1)}, u32[]{:S(2)}, u32[]{:S(2)}) async-start(bf16[16,512,128]{2,1,0:T(8,128)(2,1)} %to_sigma.1.rest_0_.rest_1_), calls=%async_computation.4 | async-start | bytes 4194304 | tf_op jit(solution)/shard_map/all_to_all | solution.py:746
  142.2 7.4 %collective-permute-done.2.away_ref = bf16[2,8,256,128]{3,2,1,0:T(8,128)(2,1)} collective-permute-done((bf16[2,8,256,128]{3,2,1,0:T(8,128)(2,1)}, bf16[2,8,256,128]{3,2,1,0:T(8,128)(2,1)}, u32[]{:S(2)}, u32[]{:S(2)}) %collective-permute-start.2) | collective-permute-done | bytes 1048608 | tf_op jit(solution)/shard_map/ppermute | solution.py:752
  149.6 0.0 copy-done.6
  149.6 0.0 copy-done.10
  149.6 1.6 copy-done.7
  151.2 3.1 %make_rights.2.rest_0_ = bf16[32,384,256]{2,1,0:T(8,128)(2,1)} custom-call(s32[1]{0:T(128)} %bitcast.half_ref, bf16[16,256,128]{2,1,0:T(8,128)(2,1)S(1)} %copy-done.6, bf16[8,256,128]{2,1,0:T(8,128)(2,1)S(1)} %copy-done.10, bf16[2,8,256,128]{3,2,1,0:T(8,128)(2,1)} %collective-permute-done.2.away_ref, bf16[16,512,128]{2,1,0:T(8,128)(2,1)S(1)} %copy-done.7), custom_call_target="tpu_custom_call" | custom-call | flops 99999997952 | bytes 1048576 | tf_op jit(solution)/shard_map/make_rights/pallas_call | solution.py:632
  154.3 0.0 copy-done.12
  154.3 3.1 %make_rights.3.rights = bf16[32,384,256]{2,1,0:T(8,128)(2,1)} custom-call(s32[1]{0:T(128)} %bitcast.half_ref, bf16[16,256,128]{2,1,0:T(8,128)(2,1)S(1)} %all-to-all-done.1.rest_0_.own, bf16[8,256,128]{2,1,0:T(8,128)(2,1)S(1)} %copy-done.12, bf16[2,8,256,128]{3,2,1,0:T(8,128)(2,1)} %collective-permute-done.2.away_ref, ...), custom_call_target="tpu_custom_call", output_to_operand_aliasing={{}: (4, {})} | custom-call | flops 99999997952 | bytes 1048576 | tf_op jit(solution)/shard_map/make_rights/pallas_call | solution.py:632
  157.4 18.0 %all-to-all-done.4.sigma = bf16[16,512,128]{2,1,0:T(8,128)(2,1)} async-done(((bf16[16,512,128]{2,1,0:T(8,128)(2,1)}), bf16[16,512,128]{2,1,0:T(8,128)(2,1)}, u32[]{:S(2)}, u32[]{:S(2)}) %all-to-all-start.4) | async-done | bytes 2097184 | tf_op jit(solution)/shard_map/all_to_all | solution.py:746
  175.4 5.3 %volterra.1 = bf16[16,512,128]{2,1,0:T(8,128)(2,1)S(1)} custom-call(s32[1]{0:T(128)} %bitcast.half_ref, bf16[16,512,128]{2,1,0:T(8,128)(2,1)} %all-to-all-done.4.sigma, bf16[32,384,256]{2,1,0:T(8,128)(2,1)} %make_rights.3.rights), custom_call_target="tpu_custom_call" | custom-call | tf_op jit(solution)/shard_map/volterra/pallas_call | solution.py:720
  180.7 30.0 %all_to_all.30.blocks_ref = bf16[16,512,128]{2,1,0:T(8,128)(2,1)S(1)} all-to-all(bf16[16,512,128]{2,1,0:T(8,128)(2,1)S(1)} %volterra.1), channel_id=1, replica_groups=mesh['half'=2,'line'=8,'tcol'=2] {'tcol','line'}, dimensions={0} | all-to-all | bytes 4194304 | tf_op jit(solution)/shard_map/all_to_all | solution.py:746
  210.7 2.6 %collect.1 = (bf16[2,8,64,512]{3,2,1,0:T(8,128)(2,1)}, bf16[2,8,64,512]{3,2,1,0:T(8,128)(2,1)}) custom-call(bf16[16,512,128]{2,1,0:T(8,128)(2,1)S(1)} %all_to_all.30.blocks_ref), custom_call_target="tpu_custom_call" | custom-call | tf_op jit(solution)/shard_map/collect/pallas_call | solution.py:290
  (14 shorter events, 0.0 us)
Async XLA Ops:
  3.3 22.5 %all-to-all-start = ((bf16[16,256,128]{2,1,0:T(8,128)(2,1)}), bf16[16,256,128]{2,1,0:T(8,128)(2,1)S(1)}, u32[]{:S(2)}, u32[]{:S(2)}) async-start(bf16[16,256,128]{2,1,0:T(8,128)(2,1)} %bitcast.14), calls=%async_computation | async-start | bytes 2097152 | tf_op jit(solution)/shard_map/all_to_all | solution.py:746
  9.6 3.5 %copy-start.18 = (s32[512]{0:T(512)S(1)}, s32[512]{0:T(512)}, u32[]{:S(2)}) copy-start(s32[512]{0:T(512)} %param.6) | copy-start | bytes 6148
  25.8 31.1 %copy-start.5 = (bf16[16,256,128]{2,1,0:T(8,128)(2,1)}, bf16[16,256,128]{2,1,0:T(8,128)(2,1)S(1)}, u32[]{:S(2)}) copy-start(bf16[16,256,128]{2,1,0:T(8,128)(2,1)S(1)} %all-to-all-done.own) | copy-start | bytes 3145732
  25.8 31.0 %all-to-all-start.1 = ((bf16[16,256,128]{2,1,0:T(8,128)(2,1)}), bf16[16,256,128]{2,1,0:T(8,128)(2,1)S(1)}, u32[]{:S(2)}, u32[]{:S(2)}) async-start(bf16[16,256,128]{2,1,0:T(8,128)(2,1)} %gate.2), calls=%async_computation.1 | async-start | bytes 2097152 | tf_op jit(solution)/shard_map/all_to_all | solution.py:746
  30.3 26.5 %collective-permute-start = (bf16[8,256,128]{2,1,0:T(8,128)(2,1)S(1)}, bf16[8,256,128]{2,1,0:T(8,128)(2,1)S(1)}, u32[]{:S(2)}, u32[]{:S(2)}) collective-permute-start(bf16[8,256,128]{2,1,0:T(8,128)(2,1)S(1)} %get-tuple-element.15), channel_id=1, source_target_pairs={{0,16},{16,0},{1,17},{17,1},{2,18},{18,2},{3,19},{19,3},{4,20},{20... | collective-permute-start | bytes 1572872 | tf_op jit(solution)/shard_map/ppermute | solution.py:752
  56.8 2.0 copy-start.9
  58.8 31.4 %all-to-all-start.2 = ((bf16[16,256,128]{2,1,0:T(8,128)(2,1)}), bf16[16,256,128]{2,1,0:T(8,128)(2,1)S(1)}, u32[]{:S(2)}, u32[]{:S(2)}) async-start(bf16[16,256,128]{2,1,0:T(8,128)(2,1)} %get-tuple-element.9), calls=%async_computation.2 | async-start | bytes 2097152 | tf_op jit(solution)/shard_map/all_to_all | solution.py:746
  63.7 23.1 %collective-permute-start.1 = (bf16[8,256,128]{2,1,0:T(8,128)(2,1)S(1)}, bf16[8,256,128]{2,1,0:T(8,128)(2,1)S(1)}, u32[]{:S(2)}, u32[]{:S(2)}) collective-permute-start(bf16[8,256,128]{2,1,0:T(8,128)(2,1)S(1)} %get-tuple-element.17), channel_id=1, source_target_pairs={{0,16},{16,0},{1,17},{17,1},{2,18},{18,2},{3,19},{19,3},{4,20},{20... | collective-permute-start | bytes 1572872 | tf_op jit(solution)/shard_map/ppermute | solution.py:752
  86.8 11.8 %copy-start.16 = (bf16[1,8,256,128]{3,2,1,0:T(8,128)(2,1)S(1)}, bf16[1,8,256,128]{3,2,1,0:T(8,128)(2,1)}, u32[]{:S(2)}) copy-start(bf16[1,8,256,128]{3,2,1,0:T(8,128)(2,1)} %get-tuple-element.14) | copy-start | bytes 1572868
  88.7 0.8 copy-start.11
  89.5 0.6 copy-start.14
  90.1 8.4 %copy-start.17 = (bf16[1,8,256,128]{3,2,1,0:T(8,128)(2,1)S(1)}, bf16[1,8,256,128]{3,2,1,0:T(8,128)(2,1)}, u32[]{:S(2)}) copy-start(bf16[1,8,256,128]{3,2,1,0:T(8,128)(2,1)} %get-tuple-element.16) | copy-start | bytes 1572868
  90.2 8.3 %copy-start.3 = (bf16[16,256,128]{2,1,0:T(8,128)(2,1)}, bf16[16,256,128]{2,1,0:T(8,128)(2,1)S(1)}, u32[]{:S(2)}) copy-start(bf16[16,256,128]{2,1,0:T(8,128)(2,1)S(1)} %all-to-all-done.2.refs_2_) | copy-start | bytes 3145732
  90.2 35.6 %all-to-all-start.3 = ((bf16[16,256,128]{2,1,0:T(8,128)(2,1)}), bf16[16,256,128]{2,1,0:T(8,128)(2,1)}, u32[]{:S(2)}, u32[]{:S(2)}) async-start(bf16[16,256,128]{2,1,0:T(8,128)(2,1)} %get-tuple-element.11), calls=%async_computation.3 | async-start | bytes 2097152 | tf_op jit(solution)/shard_map/all_to_all | solution.py:746
  99.6 3.4 %copy-start = (bf16[1024,1024]{1,0:T(8,128)(2,1)S(1)}, bf16[1024,1024]{1,0:T(8,128)(2,1)}, u32[]{:S(2)}) copy-start(bf16[1024,1024]{1,0:T(8,128)(2,1)} %get-tuple-element.8.refs_1_.table.table_from) | copy-start | bytes 6291460
  99.6 3.4 %copy-start.15 = (f32[8,128]{1,0:T(8,128)S(1)}, f32[8,128]{1,0:T(8,128)}, u32[]{:S(2)}) copy-start(f32[8,128]{1,0:T(8,128)} %copy-done.14) | copy-start | bytes 12292
  99.6 50.0 %collective-permute-start.2 = (bf16[2,8,256,128]{3,2,1,0:T(8,128)(2,1)}, bf16[2,8,256,128]{3,2,1,0:T(8,128)(2,1)}, u32[]{:S(2)}, u32[]{:S(2)}) collective-permute-start(bf16[2,8,256,128]{3,2,1,0:T(8,128)(2,1)} %gate.3), channel_id=1, source_target_pairs={{0,16},{16,0},{1,17},{17,1},{2,18},{18,2},{3,19},{19,3},{4,20},{20... | collective-permute-start | bytes 3145736 | tf_op jit(solution)/shard_map/ppermute | solution.py:752
  103.0 1.2 copy-start.1
  104.2 1.2 copy-start.2
  105.5 3.7 %copy-start.4 = (bf16[16,256,128]{2,1,0:T(8,128)(2,1)S(1)}, bf16[16,256,128]{2,1,0:T(8,128)(2,1)}, u32[]{:S(2)}) copy-start(bf16[16,256,128]{2,1,0:T(8,128)(2,1)} %copy-done.3) | copy-start | bytes 3145732
  109.1 16.7 %copy-start.13 = (f32[8,128]{1,0:T(8,128)S(1)}, f32[8,128]{1,0:T(8,128)}, u32[]{:S(2)}) copy-start(f32[8,128]{1,0:T(8,128)} %broadcast_multiply_fusion.refs_2_.coupling) | copy-start | bytes 12292
  125.8 1.6 copy-start.8
  137.6 12.0 %copy-start.6 = (bf16[16,256,128]{2,1,0:T(8,128)(2,1)S(1)}, bf16[16,256,128]{2,1,0:T(8,128)(2,1)}, u32[]{:S(2)}) copy-start(bf16[16,256,128]{2,1,0:T(8,128)(2,1)} %copy-done.5) | copy-start | bytes 3145732
  137.6 12.0 %copy-start.10 = (bf16[8,256,128]{2,1,0:T(8,128)(2,1)S(1)}, bf16[8,256,128]{2,1,0:T(8,128)(2,1)}, u32[]{:S(2)}) copy-start(bf16[8,256,128]{2,1,0:T(8,128)(2,1)} %copy-done.9) | copy-start | bytes 1572868
  137.6 37.9 %all-to-all-start.4 = ((bf16[16,512,128]{2,1,0:T(8,128)(2,1)}), bf16[16,512,128]{2,1,0:T(8,128)(2,1)}, u32[]{:S(2)}, u32[]{:S(2)}) async-start(bf16[16,512,128]{2,1,0:T(8,128)(2,1)} %to_sigma.1.rest_0_.rest_1_), calls=%async_computation.4 | async-start | bytes 4194304 | tf_op jit(solution)/shard_map/all_to_all | solution.py:746
  149.6 1.6 copy-start.7
  151.2 3.1 %copy-start.12 = (bf16[8,256,128]{2,1,0:T(8,128)(2,1)S(1)}, bf16[8,256,128]{2,1,0:T(8,128)(2,1)}, u32[]{:S(2)}) copy-start(bf16[8,256,128]{2,1,0:T(8,128)(2,1)} %copy-done.11) | copy-start | bytes 1572868

commit v15 on v11

--- a/solution.py
+++ b/solution.py
@@ -720,7 +720,7 @@
             far_near[part],
             rows,
             own[-1:] + marks[-1:],
-            weight() if part > 0 else None,
+            None,
         )
         sent.append(blocks)
         marks.append(mark)

time: 212 us -> 214 us (level)
  starting transfers between devices: 37.6 us -> 35.4 us
  local copies, waits for them, and re-layouts: 19.5 us -> 21.7 us
    ppermute x3, waiting for transfers between devices: 12 us -> 23.7 us  [swap(): return lax.ppermute(array, 'half', [(0, 1), (1, 0)])]
    all_to_all x5, waiting for transfers between devices: 68.6 us -> 58.7 us  [exchange(): return lax.all_to_all(blocks, ('tcol', 'line'), 0, 0, tiled=True)]
    all_to_all x5, starting transfers between devices: 34.4 us -> 26.8 us  [exchange(): return lax.all_to_all(blocks, ('tcol', 'line'), 0, 0, tiled=True)]
    ppermute x3, starting transfers between devices: 3.17 us -> 8.54 us  [swap(): return lax.ppermute(array, 'half', [(0, 1), (1, 0)])]
    unnamed x58 -> x54, local copies, waits for them, and re-layouts: 17.1 us -> 20.5 us
  transfers between devices with their start and end apart: 8 -> 8, of which waited for: 7 -> 6; matrix products, arithmetic and copies ran while one was open for 2% -> 1% of each run, Pallas kernels for 14% -> 13%
where the time goes in v15:
time: 214 us; the launch traced here: 213 us
  waiting for transfers between devices  82.3 us (38%)
  Pallas kernels  40.4 us (19%)
  starting transfers between devices  35.4 us (17%)
  blocking collectives  30.3 us (14%)
  local copies, waits for them, and re-layouts  21.7 us (10%)
    all_to_all x5, waiting for transfers between devices, exchange(): return lax.all_to_all(blocks, ('tcol', 'line'), 0, 0, tiled=True)  58.7 us
    all_to_all x1, blocking collectives, exchange(): return lax.all_to_all(blocks, ('tcol', 'line'), 0, 0, tiled=True)  30.3 us
    all_to_all x5, starting transfers between devices, exchange(): return lax.all_to_all(blocks, ('tcol', 'line'), 0, 0, tiled=True)  26.8 us
    ppermute x3, waiting for transfers between devices, swap(): return lax.ppermute(array, 'half', [(0, 1), (1, 0)])  23.7 us
    unnamed x54, local copies, waits for them, and re-layouts  20.5 us
    pallas_call x1, Pallas kernels, to_sigma(): pl.pallas_call(functools.partial(sigma_kernel, norm_factor), out_shape=pl...  8.59 us
    ppermute x3, starting transfers between devices, swap(): return lax.ppermute(array, 'half', [(0, 1), (1, 0)])  8.54 us
    pallas_call x2, Pallas kernels, make_rights(): pl.pallas_call(functools.partial(rights_kernel, rows), grid=(steps,), out...  6.03 us
  transfers between devices with their start and end apart: 8, of which 6 were waited for; matrix products, arithmetic and copies ran while one was open for 1% of the time, Pallas kernels for 13%

profile of v15, /device:TPU:0, one launch (start us, length us, event | category | flops | bytes accessed | tf_op | source)
XLA Modules:
  0.0 213.4 jit_solution(9865962799464785846)
XLA Ops:
  0.6 2.6 %spread.2 = bf16[4096,128]{1,0:T(8,128)(2,1)} custom-call(bf16[2,8,64,512]{3,2,1,0:T(8,128)(2,1)} %lesser.5, bf16[2,8,64,512]{3,2,1,0:T(8,128)(2,1)} %greater.5), custom_call_target="tpu_custom_call" | custom-call | tf_op jit(solution)/shard_map/spread/pallas_call | solution.py:260
  3.3 6.3 %all-to-all-start = ((bf16[16,256,128]{2,1,0:T(8,128)(2,1)}), bf16[16,256,128]{2,1,0:T(8,128)(2,1)S(1)}, u32[]{:S(2)}, u32[]{:S(2)}) async-start(bf16[16,256,128]{2,1,0:T(8,128)(2,1)} %bitcast.14), calls=%async_computation | async-start | bytes 2097152 | tf_op jit(solution)/shard_map/all_to_all | solution.py:691
  9.6 0.0 copy-start.26
  9.6 2.7 %spread.3 = bf16[4096,128]{1,0:T(8,128)(2,1)} custom-call(bf16[2,8,64,512]{3,2,1,0:T(8,128)(2,1)} %lesser.5, bf16[2,8,64,512]{3,2,1,0:T(8,128)(2,1)} %greater.5), custom_call_target="tpu_custom_call" | custom-call | tf_op jit(solution)/shard_map/spread/pallas_call | solution.py:260
  12.2 0.0 copy-done.26
  12.2 0.1 copy.9.column_ref
  12.4 4.5 %make_tables.1 = (bf16[1024,1024]{1,0:T(8,128)(2,1)S(1)}, bf16[1024,1024]{1,0:T(8,128)(2,1)S(1)}) custom-call(s32[512,1]{1,0:T(8,128)S(1)} %copy.9.column_ref), custom_call_target="tpu_custom_call" | custom-call | tf_op jit(solution)/shard_map/make_tables/pallas_call | solution.py:323
  16.9 0.0 copy-start
  16.9 1.3 copy-done
  18.3 1.3 copy-done.13
  20.3 0.1 fusion.4
  20.3 0.1 dynamic_slice.20
  20.4 0.1 dynamic_slice.19
  20.5 0.1 pad_maximum_fusion.1
  20.6 0.7 broadcast_multiply_fusion.refs_2_.coupling
  21.2 4.5 %all-to-all-done.own = bf16[16,256,128]{2,1,0:T(8,128)(2,1)S(1)} async-done(((bf16[16,256,128]{2,1,0:T(8,128)(2,1)}), bf16[16,256,128]{2,1,0:T(8,128)(2,1)S(1)}, u32[]{:S(2)}, u32[]{:S(2)}) %all-to-all-start) | async-done | bytes 1048608 | tf_op jit(solution)/shard_map/all_to_all | solution.py:691
  25.8 3.7 %all-to-all-start.1 = ((bf16[16,256,128]{2,1,0:T(8,128)(2,1)}), bf16[16,256,128]{2,1,0:T(8,128)(2,1)S(1)}, u32[]{:S(2)}, u32[]{:S(2)}) async-start(bf16[16,256,128]{2,1,0:T(8,128)(2,1)} %gate.2), calls=%async_computation.1 | async-start | bytes 2097152 | tf_op jit(solution)/shard_map/all_to_all | solution.py:691
  29.4 0.9 dynamic-slice_bitcast_fusion.1
  30.3 2.6 %collective-permute-start = (bf16[8,256,128]{2,1,0:T(8,128)(2,1)}, bf16[8,256,128]{2,1,0:T(8,128)(2,1)S(1)}, u32[]{:S(2)}, u32[]{:S(2)}) collective-permute-start(bf16[8,256,128]{2,1,0:T(8,128)(2,1)} %get-tuple-element.21), channel_id=1, source_target_pairs={{0,16},{16,0},{1,17},{17,1},{2,18},{18,2},{3,19},{19,3},{4,20},{20... | collective-permute-start | bytes 1572872 | tf_op jit(solution)/shard_map/ppermute | solution.py:697
  32.9 23.9 %all-to-all-done.1.rest_0_.own = bf16[16,256,128]{2,1,0:T(8,128)(2,1)S(1)} async-done(((bf16[16,256,128]{2,1,0:T(8,128)(2,1)}), bf16[16,256,128]{2,1,0:T(8,128)(2,1)S(1)}, u32[]{:S(2)}, u32[]{:S(2)}) %all-to-all-start.1) | async-done | bytes 1048608 | tf_op jit(solution)/shard_map/all_to_all | solution.py:691
  56.8 0.0 collective-permute-done.far.near_ref
  56.8 0.0 copy-done.6
  56.8 2.0 to_crossed.2
  58.8 0.0 copy-done.19
  58.8 4.2 %all-to-all-start.2 = ((bf16[16,256,128]{2,1,0:T(8,128)(2,1)}), bf16[16,256,128]{2,1,0:T(8,128)(2,1)S(1)}, u32[]{:S(2)}, u32[]{:S(2)}) async-start(bf16[16,256,128]{2,1,0:T(8,128)(2,1)} %get-tuple-element.12), calls=%async_computation.2 | async-start | bytes 2097152 | tf_op jit(solution)/shard_map/all_to_all | solution.py:691
  63.0 0.1 dynamic-slice_bitcast_fusion
  63.1 3.3 %collective-permute-start.1 = (bf16[8,256,128]{2,1,0:T(8,128)(2,1)S(1)}, bf16[8,256,128]{2,1,0:T(8,128)(2,1)S(1)}, u32[]{:S(2)}, u32[]{:S(2)}) collective-permute-start(bf16[8,256,128]{2,1,0:T(8,128)(2,1)S(1)} %get-tuple-element.23), channel_id=1, source_target_pairs={{0,16},{16,0},{1,17},{17,1},{2,18},{18,2},{3,19},{19,3},{4,20},{20... | collective-permute-start | bytes 1572872 | tf_op jit(solution)/shard_map/ppermute | solution.py:697
  66.5 20.6 %collective-permute-done.1.far.near_ref = bf16[8,256,128]{2,1,0:T(8,128)(2,1)S(1)} collective-permute-done((bf16[8,256,128]{2,1,0:T(8,128)(2,1)S(1)}, bf16[8,256,128]{2,1,0:T(8,128)(2,1)S(1)}, u32[]{:S(2)}, u32[]{:S(2)}) %collective-permute-start.1) | collective-permute-done | bytes 524320 | tf_op jit(solution)/shard_map/ppermute | solution.py:697
  87.0 2.0 to_crossed.3
  89.0 0.8 copy-done.21
  89.8 0.6 copy-done.24
  90.4 0.0 all-to-all-done.2.refs_2_
  90.5 8.1 %all-to-all-start.3 = ((bf16[16,256,128]{2,1,0:T(8,128)(2,1)}), bf16[16,256,128]{2,1,0:T(8,128)(2,1)}, u32[]{:S(2)}, u32[]{:S(2)}) async-start(bf16[16,256,128]{2,1,0:T(8,128)(2,1)} %get-tuple-element.16), calls=%async_computation.3 | async-start | bytes 2097152 | tf_op jit(solution)/shard_map/all_to_all | solution.py:691
  98.6 0.0 copy-done.4
  98.6 1.0 pad_maximum_fusion.refs_0_
  99.6 2.6 %collective-permute-start.2 = (bf16[2,8,256,128]{3,2,1,0:T(8,128)(2,1)}, bf16[2,8,256,128]{3,2,1,0:T(8,128)(2,1)}, u32[]{:S(2)}, u32[]{:S(2)}) collective-permute-start(bf16[2,8,256,128]{3,2,1,0:T(8,128)(2,1)} %gate.3), channel_id=1, source_target_pairs={{0,16},{16,0},{1,17},{17,1},{2,18},{18,2},{3,19},{19,3},{4,20},{20... | collective-permute-start | bytes 3145736 | tf_op jit(solution)/shard_map/ppermute | solution.py:697
  102.3 0.0 copy-done.1
  102.3 1.2 copy-done.2
  103.5 1.2 copy-done.3
  104.7 2.4 %to_sites.1.sites = bf16[1024,1024]{1,0:T(8,128)(2,1)S(1)} custom-call(bf16[2,8,64,512]{3,2,1,0:T(8,128)(2,1)S(1)} %copy-done.2, bf16[2,8,64,512]{3,2,1,0:T(8,128)(2,1)S(1)} %copy-done.3, bf16[1024,1024]{1,0:T(8,128)(2,1)S(1)} %copy-done.1, f32[8,128]{1,0:T(8,128)S(1)} %copy-done.25), custom_call_target="tpu_custom_call" | custom-call | tf_op jit(solution)/shard_map/to_sites/pallas_call | solution.py:354
  107.1 1.4 copy-done.9
  108.5 0.0 copy-done.14
  108.5 1.7 to_mirror.1
  110.2 2.0 copy-done.11
  112.2 1.4 copy-done.15
  113.6 1.0 copy-done.17
  114.5 11.4 %all-to-all-done.3 = bf16[16,256,128]{2,1,0:T(8,128)(2,1)} async-done(((bf16[16,256,128]{2,1,0:T(8,128)(2,1)}), bf16[16,256,128]{2,1,0:T(8,128)(2,1)}, u32[]{:S(2)}, u32[]{:S(2)}) %all-to-all-start.3) | async-done | bytes 1048608 | tf_op jit(solution)/shard_map/all_to_all | solution.py:691
  125.9 0.0 copy-done.23
  125.9 1.6 copy-done.10
  127.5 2.2 %copy-done.12 = f32[1024,1024]{1,0:T(8,128)S(1)} copy-done((f32[1024,1024]{1,0:T(8,128)S(1)}, f32[1024,1024]{1,0:T(8,128)}, u32[]{:S(2)}) %copy-start.12) | copy-done | bytes 4194328
  129.7 1.6 copy-done.16
  131.3 1.2 copy-done.18
  132.5 8.6 %to_sigma.1.rest_0_.rest_1_ = bf16[16,512,128]{2,1,0:T(8,128)(2,1)} custom-call(f32[1024,1024]{1,0:T(8,128)S(1)} %copy-done.12, bf16[4096,128]{1,0:T(8,128)(2,1)} %bitcast.6.crossed, bf16[1024,1024]{1,0:T(8,128)(2,1)S(1)} %copy-done.10, bf16[1024,512]{1,0:T(8,128)(2,1)S(1)} %copy-done.18, bf16[1024,1024]{1,0:T(8,128)(2,1)S(1)} %copy-done.16, ...), custom_call_target="tpu_custom_call" | custom-call | tf_op jit(solution)/shard_map/to_sigma/pallas_call | solution.py:514
  141.1 4.6 %all-to-all-start.4 = ((bf16[16,512,128]{2,1,0:T(8,128)(2,1)}), bf16[16,512,128]{2,1,0:T(8,128)(2,1)}, u32[]{:S(2)}, u32[]{:S(2)}) async-start(bf16[16,512,128]{2,1,0:T(8,128)(2,1)} %to_sigma.1.rest_0_.rest_1_), calls=%async_computation.4 | async-start | bytes 4194304 | tf_op jit(solution)/shard_map/all_to_all | solution.py:691
  145.7 3.1 %collective-permute-done.2.away_ref = bf16[2,8,256,128]{3,2,1,0:T(8,128)(2,1)} collective-permute-done((bf16[2,8,256,128]{3,2,1,0:T(8,128)(2,1)}, bf16[2,8,256,128]{3,2,1,0:T(8,128)(2,1)}, u32[]{:S(2)}, u32[]{:S(2)}) %collective-permute-start.2) | collective-permute-done | bytes 1048608 | tf_op jit(solution)/shard_map/ppermute | solution.py:697
  148.8 0.0 copy-done.7
  148.8 1.6 copy-done.8
  150.4 3.0 %make_rights.2.rest_0_ = bf16[32,384,256]{2,1,0:T(8,128)(2,1)} custom-call(s32[1]{0:T(128)} %bitcast.half_ref, bf16[16,256,128]{2,1,0:T(8,128)(2,1)S(1)} %copy-done.7, bf16[8,256,128]{2,1,0:T(8,128)(2,1)S(1)} %copy-done.20, bf16[2,8,256,128]{3,2,1,0:T(8,128)(2,1)} %collective-permute-done.2.away_ref, bf16[16,512,128]{2,1,0:T(8,128)(2,1)S(1)} %copy-done.8), custom_call_target="tpu_custom_call" | custom-call | flops 99999997952 | bytes 1048576 | tf_op jit(solution)/shard_map/make_rights/pallas_call | solution.py:577
  153.4 0.0 copy-done.22
  153.4 3.0 %make_rights.3.rights = bf16[32,384,256]{2,1,0:T(8,128)(2,1)} custom-call(s32[1]{0:T(128)} %bitcast.half_ref, bf16[16,256,128]{2,1,0:T(8,128)(2,1)S(1)} %all-to-all-done.1.rest_0_.own, bf16[8,256,128]{2,1,0:T(8,128)(2,1)S(1)} %copy-done.22, bf16[2,8,256,128]{3,2,1,0:T(8,128)(2,1)} %collective-permute-done.2.away_ref, ...), custom_call_target="tpu_custom_call", output_to_operand_aliasing={{}: (4, {})} | custom-call | flops 99999997952 | bytes 1048576 | tf_op jit(solution)/shard_map/make_rights/pallas_call | solution.py:577
  156.4 18.8 %all-to-all-done.4.sigma = bf16[16,512,128]{2,1,0:T(8,128)(2,1)} async-done(((bf16[16,512,128]{2,1,0:T(8,128)(2,1)}), bf16[16,512,128]{2,1,0:T(8,128)(2,1)}, u32[]{:S(2)}, u32[]{:S(2)}) %all-to-all-start.4) | async-done | bytes 2097184 | tf_op jit(solution)/shard_map/all_to_all | solution.py:691
  175.2 5.3 %volterra.1 = bf16[16,512,128]{2,1,0:T(8,128)(2,1)S(1)} custom-call(s32[1]{0:T(128)} %bitcast.half_ref, bf16[16,512,128]{2,1,0:T(8,128)(2,1)} %all-to-all-done.4.sigma, bf16[32,384,256]{2,1,0:T(8,128)(2,1)} %make_rights.3.rights), custom_call_target="tpu_custom_call" | custom-call | tf_op jit(solution)/shard_map/volterra/pallas_call | solution.py:665
  180.5 30.3 %all_to_all.30.blocks_ref = bf16[16,512,128]{2,1,0:T(8,128)(2,1)S(1)} all-to-all(bf16[16,512,128]{2,1,0:T(8,128)(2,1)S(1)} %volterra.1), channel_id=1, replica_groups=mesh['half'=2,'line'=8,'tcol'=2] {'tcol','line'}, dimensions={0} | all-to-all | bytes 4194304 | tf_op jit(solution)/shard_map/all_to_all | solution.py:691
  210.8 2.6 %collect.1 = (bf16[2,8,64,512]{3,2,1,0:T(8,128)(2,1)}, bf16[2,8,64,512]{3,2,1,0:T(8,128)(2,1)}) custom-call(bf16[16,512,128]{2,1,0:T(8,128)(2,1)S(1)} %all_to_all.30.blocks_ref), custom_call_target="tpu_custom_call" | custom-call | tf_op jit(solution)/shard_map/collect/pallas_call | solution.py:290
  (30 shorter events, 0.0 us)
Async XLA Ops:
  3.3 22.5 %all-to-all-start = ((bf16[16,256,128]{2,1,0:T(8,128)(2,1)}), bf16[16,256,128]{2,1,0:T(8,128)(2,1)S(1)}, u32[]{:S(2)}, u32[]{:S(2)}) async-start(bf16[16,256,128]{2,1,0:T(8,128)(2,1)} %bitcast.14), calls=%async_computation | async-start | bytes 2097152 | tf_op jit(solution)/shard_map/all_to_all | solution.py:691
  9.6 2.7 %copy-start.26 = (s32[512]{0:T(512)S(1)}, s32[512]{0:T(512)}, u32[]{:S(2)}) copy-start(s32[512]{0:T(512)} %param.6) | copy-start | bytes 6148
  16.9 1.3 copy-start
  18.3 1.4 copy-start.13
  25.8 31.1 %copy-start.6 = (bf16[16,256,128]{2,1,0:T(8,128)(2,1)}, bf16[16,256,128]{2,1,0:T(8,128)(2,1)S(1)}, u32[]{:S(2)}) copy-start(bf16[16,256,128]{2,1,0:T(8,128)(2,1)S(1)} %all-to-all-done.own) | copy-start | bytes 3145732
  25.8 31.0 %all-to-all-start.1 = ((bf16[16,256,128]{2,1,0:T(8,128)(2,1)}), bf16[16,256,128]{2,1,0:T(8,128)(2,1)S(1)}, u32[]{:S(2)}, u32[]{:S(2)}) async-start(bf16[16,256,128]{2,1,0:T(8,128)(2,1)} %gate.2), calls=%async_computation.1 | async-start | bytes 2097152 | tf_op jit(solution)/shard_map/all_to_all | solution.py:691
  30.3 26.5 %collective-permute-start = (bf16[8,256,128]{2,1,0:T(8,128)(2,1)}, bf16[8,256,128]{2,1,0:T(8,128)(2,1)S(1)}, u32[]{:S(2)}, u32[]{:S(2)}) collective-permute-start(bf16[8,256,128]{2,1,0:T(8,128)(2,1)} %get-tuple-element.21), channel_id=1, source_target_pairs={{0,16},{16,0},{1,17},{17,1},{2,18},{18,2},{3,19},{19,3},{4,20},{20... | collective-permute-start | bytes 1572872 | tf_op jit(solution)/shard_map/ppermute | solution.py:697
  56.8 2.0 copy-start.19
  58.8 31.7 %all-to-all-start.2 = ((bf16[16,256,128]{2,1,0:T(8,128)(2,1)}), bf16[16,256,128]{2,1,0:T(8,128)(2,1)S(1)}, u32[]{:S(2)}, u32[]{:S(2)}) async-start(bf16[16,256,128]{2,1,0:T(8,128)(2,1)} %get-tuple-element.12), calls=%async_computation.2 | async-start | bytes 2097152 | tf_op jit(solution)/shard_map/all_to_all | solution.py:691
  63.1 23.9 %collective-permute-start.1 = (bf16[8,256,128]{2,1,0:T(8,128)(2,1)S(1)}, bf16[8,256,128]{2,1,0:T(8,128)(2,1)S(1)}, u32[]{:S(2)}, u32[]{:S(2)}) collective-permute-start(bf16[8,256,128]{2,1,0:T(8,128)(2,1)S(1)} %get-tuple-element.23), channel_id=1, source_target_pairs={{0,16},{16,0},{1,17},{17,1},{2,18},{18,2},{3,19},{19,3},{4,20},{20... | collective-permute-start | bytes 1572872 | tf_op jit(solution)/shard_map/ppermute | solution.py:697
  89.0 0.8 copy-start.21
  89.8 0.6 copy-start.24
  90.5 8.1 %copy-start.4 = (bf16[16,256,128]{2,1,0:T(8,128)(2,1)}, bf16[16,256,128]{2,1,0:T(8,128)(2,1)S(1)}, u32[]{:S(2)}) copy-start(bf16[16,256,128]{2,1,0:T(8,128)(2,1)S(1)} %all-to-all-done.2.refs_2_) | copy-start | bytes 3145732
  90.5 35.5 %all-to-all-start.3 = ((bf16[16,256,128]{2,1,0:T(8,128)(2,1)}), bf16[16,256,128]{2,1,0:T(8,128)(2,1)}, u32[]{:S(2)}, u32[]{:S(2)}) async-start(bf16[16,256,128]{2,1,0:T(8,128)(2,1)} %get-tuple-element.16), calls=%async_computation.3 | async-start | bytes 2097152 | tf_op jit(solution)/shard_map/all_to_all | solution.py:691
  99.6 2.6 %copy-start.1 = (bf16[1024,1024]{1,0:T(8,128)(2,1)S(1)}, bf16[1024,1024]{1,0:T(8,128)(2,1)}, u32[]{:S(2)}) copy-start(bf16[1024,1024]{1,0:T(8,128)(2,1)} %copy-done) | copy-start | bytes 6291460
  99.6 2.6 %copy-start.25 = (f32[8,128]{1,0:T(8,128)S(1)}, f32[8,128]{1,0:T(8,128)}, u32[]{:S(2)}) copy-start(f32[8,128]{1,0:T(8,128)} %copy-done.24) | copy-start | bytes 12292
  99.6 49.1 %collective-permute-start.2 = (bf16[2,8,256,128]{3,2,1,0:T(8,128)(2,1)}, bf16[2,8,256,128]{3,2,1,0:T(8,128)(2,1)}, u32[]{:S(2)}, u32[]{:S(2)}) collective-permute-start(bf16[2,8,256,128]{3,2,1,0:T(8,128)(2,1)} %gate.3), channel_id=1, source_target_pairs={{0,16},{16,0},{1,17},{17,1},{2,18},{18,2},{3,19},{19,3},{4,20},{20... | collective-permute-start | bytes 3145736 | tf_op jit(solution)/shard_map/ppermute | solution.py:697
  102.3 1.2 copy-start.2
  103.5 1.2 copy-start.3
  104.7 3.8 %copy-start.5 = (bf16[16,256,128]{2,1,0:T(8,128)(2,1)S(1)}, bf16[16,256,128]{2,1,0:T(8,128)(2,1)}, u32[]{:S(2)}) copy-start(bf16[16,256,128]{2,1,0:T(8,128)(2,1)} %copy-done.4) | copy-start | bytes 3145732
  104.7 3.8 %copy-start.14 = (bf16[1024,1024]{1,0:T(8,128)(2,1)S(1)}, bf16[1024,1024]{1,0:T(8,128)(2,1)}, u32[]{:S(2)}) copy-start(bf16[1024,1024]{1,0:T(8,128)(2,1)} %copy-done.13) | copy-start | bytes 6291460
  107.1 1.4 copy-start.9
  108.5 17.4 %copy-start.23 = (f32[8,128]{1,0:T(8,128)S(1)}, f32[8,128]{1,0:T(8,128)}, u32[]{:S(2)}) copy-start(f32[8,128]{1,0:T(8,128)} %broadcast_multiply_fusion.refs_2_.coupling) | copy-start | bytes 12292
  110.2 2.0 copy-start.11
  112.2 1.4 copy-start.15
  113.6 1.0 copy-start.17
  125.9 1.6 copy-start.10
  127.5 2.2 %copy-start.12 = (f32[1024,1024]{1,0:T(8,128)S(1)}, f32[1024,1024]{1,0:T(8,128)}, u32[]{:S(2)}) copy-start(f32[1024,1024]{1,0:T(8,128)} %copy-done.11) | copy-start | bytes 12582916
  129.7 1.6 copy-start.16
  131.3 1.2 copy-start.18
  141.1 7.7 %copy-start.7 = (bf16[16,256,128]{2,1,0:T(8,128)(2,1)S(1)}, bf16[16,256,128]{2,1,0:T(8,128)(2,1)}, u32[]{:S(2)}) copy-start(bf16[16,256,128]{2,1,0:T(8,128)(2,1)} %copy-done.6) | copy-start | bytes 3145732
  141.1 7.7 %copy-start.20 = (bf16[8,256,128]{2,1,0:T(8,128)(2,1)S(1)}, bf16[8,256,128]{2,1,0:T(8,128)(2,1)}, u32[]{:S(2)}) copy-start(bf16[8,256,128]{2,1,0:T(8,128)(2,1)} %copy-done.19) | copy-start | bytes 1572868
  141.1 34.1 %all-to-all-start.4 = ((bf16[16,512,128]{2,1,0:T(8,128)(2,1)}), bf16[16,512,128]{2,1,0:T(8,128)(2,1)}, u32[]{:S(2)}, u32[]{:S(2)}) async-start(bf16[16,512,128]{2,1,0:T(8,128)(2,1)} %to_sigma.1.rest_0_.rest_1_), calls=%async_computation.4 | async-start | bytes 4194304 | tf_op jit(solution)/shard_map/all_to_all | solution.py:691
  148.8 1.6 copy-start.8
  150.4 3.0 %copy-start.22 = (bf16[8,256,128]{2,1,0:T(8,128)(2,1)S(1)}, bf16[8,256,128]{2,1,0:T(8,128)(2,1)}, u32[]{:S(2)}) copy-start(bf16[8,256,128]{2,1,0:T(8,128)(2,1)} %copy-done.21) | copy-start | bytes 1572868

commit v16 on v11

--- a/solution.py
+++ b/solution.py
@@ -564,7 +564,7 @@
         out[at, 2 * lanes :] = jnp.where(keep, greens[0] - greens[1], 0.0).astype(BF16)
 
 
-STEPS = 4
+STEPS = 8
 PARTS = 2
 
 

time: 212 us -> 215 us (1.014)
  Pallas kernels: 40.4 us -> 47.4 us
  waiting for transfers between devices: 80.6 us -> 75.7 us
    pallas_call x2, Pallas kernels: 3.97 us -> 6.6 us  [to_crossed(): pl.pallas_call(functools.partial(cross_kernel, rows), grid=(STEPS,), out_...]
    ppermute x3, waiting for transfers between devices: 12 us -> 9.56 us  [swap(): return lax.ppermute(array, 'half', [(0, 1), (1, 0)])]
    all_to_all x5, waiting for transfers between devices: 68.6 us -> 66.2 us  [exchange(): return lax.all_to_all(blocks, ('tcol', 'line'), 0, 0, tiled=True)]
    pallas_call x1, Pallas kernels: 5.26 us -> 7.55 us  [volterra(): pl.pallas_call(functools.partial(volterra_kernel, rows), grid=(STEPS,), o...]
  transfers between devices with their start and end apart: 8 -> 8, of which waited for: 7 -> 7; matrix products, arithmetic and copies ran while one was open for 2% -> 2% of each run, Pallas kernels for 14% -> 16%
where the time goes in v16:
time: 215 us; the launch traced here: 214 us
  waiting for transfers between devices  75.7 us (35%)
  Pallas kernels  47.4 us (22%)
  starting transfers between devices  38.9 us (18%)
  blocking collectives  30.1 us (14%)
  local copies, waits for them, and re-layouts  18.2 us (8%)
    all_to_all x5, waiting for transfers between devices, exchange(): return lax.all_to_all(blocks, ('tcol', 'line'), 0, 0, tiled=True)  66.2 us
    all_to_all x5, starting transfers between devices, exchange(): return lax.all_to_all(blocks, ('tcol', 'line'), 0, 0, tiled=True)  34.4 us
    all_to_all x1, blocking collectives, exchange(): return lax.all_to_all(blocks, ('tcol', 'line'), 0, 0, tiled=True)  30.1 us
    unnamed x58, local copies, waits for them, and re-layouts  15.8 us
    ppermute x3, waiting for transfers between devices, swap(): return lax.ppermute(array, 'half', [(0, 1), (1, 0)])  9.56 us
    pallas_call x1, Pallas kernels, to_sigma(): pl.pallas_call(functools.partial(sigma_kernel, norm_factor), out_shape=pl...  8.65 us
    pallas_call x2, Pallas kernels, make_rights(): pl.pallas_call(functools.partial(rights_kernel, rows), grid=(steps,), out...  8.06 us
    pallas_call x1, Pallas kernels, volterra(): pl.pallas_call(functools.partial(volterra_kernel, rows), grid=(STEPS,), o...  7.55 us
  transfers between devices with their start and end apart: 8, of which 7 were waited for; matrix products, arithmetic and copies ran while one was open for 2% of the time, Pallas kernels for 16%

profile of v16, /device:TPU:0, one launch (start us, length us, event | category | flops | bytes accessed | tf_op | source)
XLA Modules:
  0.0 213.7 jit_solution(7752117498606579332)
XLA Ops:
  0.6 2.6 %spread.2 = bf16[4096,128]{1,0:T(8,128)(2,1)} custom-call(bf16[2,8,64,512]{3,2,1,0:T(8,128)(2,1)} %lesser.5, bf16[2,8,64,512]{3,2,1,0:T(8,128)(2,1)} %greater.5), custom_call_target="tpu_custom_call" | custom-call | tf_op jit(solution)/shard_map/spread/pallas_call | solution.py:260
  3.3 6.3 %all-to-all-start = ((bf16[16,256,128]{2,1,0:T(8,128)(2,1)}), bf16[16,256,128]{2,1,0:T(8,128)(2,1)S(1)}, u32[]{:S(2)}, u32[]{:S(2)}) async-start(bf16[16,256,128]{2,1,0:T(8,128)(2,1)} %bitcast.14), calls=%async_computation | async-start | bytes 2097152 | tf_op jit(solution)/shard_map/all_to_all | solution.py:691
  9.6 0.0 copy-start.28
  9.6 2.7 %spread.3 = bf16[4096,128]{1,0:T(8,128)(2,1)} custom-call(bf16[2,8,64,512]{3,2,1,0:T(8,128)(2,1)} %lesser.5, bf16[2,8,64,512]{3,2,1,0:T(8,128)(2,1)} %greater.5), custom_call_target="tpu_custom_call" | custom-call | tf_op jit(solution)/shard_map/spread/pallas_call | solution.py:260
  12.2 0.0 copy-done.28
  12.2 0.1 copy.9.column_ref
  12.4 4.5 %make_tables.1 = (bf16[1024,1024]{1,0:T(8,128)(2,1)S(1)}, bf16[1024,1024]{1,0:T(8,128)(2,1)S(1)}) custom-call(s32[512,1]{1,0:T(8,128)S(1)} %copy.9.column_ref), custom_call_target="tpu_custom_call" | custom-call | tf_op jit(solution)/shard_map/make_tables/pallas_call | solution.py:323
  16.9 0.0 copy-start
  16.9 1.4 copy-done
  18.3 1.3 copy-done.15
  20.3 0.1 fusion.4
  20.4 0.1 dynamic_slice.20
  20.5 0.1 dynamic_slice.19
  20.5 0.1 pad_maximum_fusion.1
  20.6 0.7 broadcast_multiply_fusion.refs_2_.coupling
  21.3 4.5 %all-to-all-done.own = bf16[16,256,128]{2,1,0:T(8,128)(2,1)S(1)} async-done(((bf16[16,256,128]{2,1,0:T(8,128)(2,1)}), bf16[16,256,128]{2,1,0:T(8,128)(2,1)S(1)}, u32[]{:S(2)}, u32[]{:S(2)}) %all-to-all-start) | async-done | bytes 1048608 | tf_op jit(solution)/shard_map/all_to_all | solution.py:691
  25.8 3.7 %all-to-all-start.1 = ((bf16[16,256,128]{2,1,0:T(8,128)(2,1)}), bf16[16,256,128]{2,1,0:T(8,128)(2,1)S(1)}, u32[]{:S(2)}, u32[]{:S(2)}) async-start(bf16[16,256,128]{2,1,0:T(8,128)(2,1)} %gate.2), calls=%async_computation.1 | async-start | bytes 2097152 | tf_op jit(solution)/shard_map/all_to_all | solution.py:691
  29.4 1.0 dynamic-slice_bitcast_fusion.1
  30.5 2.6 %collective-permute-start = (bf16[8,256,128]{2,1,0:T(8,128)(2,1)}, bf16[8,256,128]{2,1,0:T(8,128)(2,1)S(1)}, u32[]{:S(2)}, u32[]{:S(2)}) collective-permute-start(bf16[8,256,128]{2,1,0:T(8,128)(2,1)} %get-tuple-element.21), channel_id=1, source_target_pairs={{0,16},{16,0},{1,17},{17,1},{2,18},{18,2},{3,19},{19,3},{4,20},{20... | collective-permute-start | bytes 1572872 | tf_op jit(solution)/shard_map/ppermute | solution.py:697
  33.1 23.6 %all-to-all-done.1.rest_0_.own = bf16[16,256,128]{2,1,0:T(8,128)(2,1)S(1)} async-done(((bf16[16,256,128]{2,1,0:T(8,128)(2,1)}), bf16[16,256,128]{2,1,0:T(8,128)(2,1)S(1)}, u32[]{:S(2)}, u32[]{:S(2)}) %all-to-all-start.1) | async-done | bytes 1048608 | tf_op jit(solution)/shard_map/all_to_all | solution.py:691
  56.7 1.1 dynamic-slice_bitcast_fusion
  57.8 0.0 collective-permute-start.1
  57.8 0.0 collective-permute-done.far.near_ref
  57.8 0.0 copy-done.6
  57.8 3.3 %to_crossed.2 = (bf16[16,256,128]{2,1,0:T(8,128)(2,1)}, f32[8,128]{1,0:T(8,128)S(1)}) custom-call(s32[1]{0:T(128)} %bitcast.half_ref, bf16[16,256,128]{2,1,0:T(8,128)(2,1)S(1)} %all-to-all-done.own, bf16[8,256,128]{2,1,0:T(8,128)(2,1)S(1)} %collective-permute-done.far.near_ref, bf16[16,256,128]{2,1,0:T(8,128)(2,1)S(1)} %all-to-all-done.1.rest_0_.own), custom_call_target="tpu_custom_call" | custom-call | tf_op jit(solution)/shard_map/to_crossed/pallas_call | solution.py:394
  61.1 0.0 copy-done.19
  61.1 15.3 %all-to-all-start.2 = ((bf16[16,256,128]{2,1,0:T(8,128)(2,1)}), bf16[16,256,128]{2,1,0:T(8,128)(2,1)S(1)}, u32[]{:S(2)}, u32[]{:S(2)}) async-start(bf16[16,256,128]{2,1,0:T(8,128)(2,1)} %get-tuple-element.12), calls=%async_computation.2 | async-start | bytes 2097152 | tf_op jit(solution)/shard_map/all_to_all | solution.py:691
  76.4 4.6 %collective-permute-done.1.far.near_ref = bf16[8,256,128]{2,1,0:T(8,128)(2,1)S(1)} collective-permute-done((bf16[8,256,128]{2,1,0:T(8,128)(2,1)}, bf16[8,256,128]{2,1,0:T(8,128)(2,1)S(1)}, u32[]{:S(2)}, u32[]{:S(2)}) %collective-permute-start.1) | collective-permute-done | bytes 524320 | tf_op jit(solution)/shard_map/ppermute | solution.py:697
  81.0 0.0 copy-done.8
  81.0 3.3 %to_crossed.3 = (bf16[16,256,128]{2,1,0:T(8,128)(2,1)}, f32[8,128]{1,0:T(8,128)S(1)}) custom-call(s32[1]{0:T(128)} %bitcast.half_ref, bf16[16,256,128]{2,1,0:T(8,128)(2,1)S(1)} %all-to-all-done.1.rest_0_.own, bf16[8,256,128]{2,1,0:T(8,128)(2,1)S(1)} %collective-permute-done.1.far.near_ref, bf16[16,256,128]{2,1,0:T(8,128)(2,1)S(1)} %all-to-all-done.1.rest_0_.own, ...), custom_call_target="tpu_custom_call" | custom-call | flops 99999997952 | bytes 1048576 | tf_op jit(solution)/shard_map/to_crossed/pallas_call | solution.py:394
  84.3 0.0 copy-done.24
  84.3 0.6 copy-done.22
  84.9 9.2 %all-to-all-done.2.refs_2_ = bf16[16,256,128]{2,1,0:T(8,128)(2,1)S(1)} async-done(((bf16[16,256,128]{2,1,0:T(8,128)(2,1)}), bf16[16,256,128]{2,1,0:T(8,128)(2,1)S(1)}, u32[]{:S(2)}, u32[]{:S(2)}) %all-to-all-start.2) | async-done | bytes 1048608 | tf_op jit(solution)/shard_map/all_to_all | solution.py:691
  94.2 4.5 %all-to-all-start.3 = ((bf16[16,256,128]{2,1,0:T(8,128)(2,1)}), bf16[16,256,128]{2,1,0:T(8,128)(2,1)}, u32[]{:S(2)}, u32[]{:S(2)}) async-start(bf16[16,256,128]{2,1,0:T(8,128)(2,1)} %get-tuple-element.16), calls=%async_computation.3 | async-start | bytes 2097152 | tf_op jit(solution)/shard_map/all_to_all | solution.py:691
  98.7 0.0 copy-done.4
  98.7 0.0 copy-done.26
  98.7 0.0 copy-done.27
  98.7 1.1 pad_maximum_fusion.refs_0_
  99.8 1.9 collective-permute-start.2
  101.6 0.0 copy-done.1
  101.6 0.0 copy-done.2
  101.7 1.2 copy-done.3
  102.9 2.4 %to_sites.1.sites = bf16[1024,1024]{1,0:T(8,128)(2,1)S(1)} custom-call(bf16[2,8,64,512]{3,2,1,0:T(8,128)(2,1)S(1)} %copy-done.2, bf16[2,8,64,512]{3,2,1,0:T(8,128)(2,1)S(1)} %copy-done.3, bf16[1024,1024]{1,0:T(8,128)(2,1)S(1)} %copy-done.1, f32[8,128]{1,0:T(8,128)S(1)} %copy-done.23), custom_call_target="tpu_custom_call" | custom-call | tf_op jit(solution)/shard_map/to_sites/pallas_call | solution.py:354
  105.3 1.4 copy-done.11
  106.6 0.0 copy-done.16
  106.6 1.7 to_mirror.1
  108.4 2.1 copy-done.13
  110.4 1.3 copy-done.17
  111.8 13.3 %all-to-all-done.3 = bf16[16,256,128]{2,1,0:T(8,128)(2,1)} async-done(((bf16[16,256,128]{2,1,0:T(8,128)(2,1)}), bf16[16,256,128]{2,1,0:T(8,128)(2,1)}, u32[]{:S(2)}, u32[]{:S(2)}) %all-to-all-start.3) | async-done | bytes 1048608 | tf_op jit(solution)/shard_map/all_to_all | solution.py:691
  125.0 1.6 copy-done.12
  126.6 2.2 %copy-done.14 = f32[1024,1024]{1,0:T(8,128)S(1)} copy-done((f32[1024,1024]{1,0:T(8,128)S(1)}, f32[1024,1024]{1,0:T(8,128)}, u32[]{:S(2)}) %copy-start.14) | copy-done | bytes 4194328
  128.8 1.6 copy-done.18
  130.4 8.6 %to_sigma.1.rest_0_.rest_1_ = bf16[16,512,128]{2,1,0:T(8,128)(2,1)} custom-call(f32[1024,1024]{1,0:T(8,128)S(1)} %copy-done.14, bf16[4096,128]{1,0:T(8,128)(2,1)} %bitcast.6.crossed, bf16[1024,1024]{1,0:T(8,128)(2,1)S(1)} %copy-done.12, bf16[1024,512]{1,0:T(8,128)(2,1)S(1)} %get-tuple-element.18.columns, bf16[1024,1024]{1,0:T(8,128)(2,1)S(1)} %copy-done.18, ...), custom_call_target="tpu_custom_call" | custom-call | tf_op jit(solution)/shard_map/to_sigma/pallas_call | solution.py:514
  139.1 4.7 %all-to-all-start.4 = ((bf16[16,512,128]{2,1,0:T(8,128)(2,1)}), bf16[16,512,128]{2,1,0:T(8,128)(2,1)}, u32[]{:S(2)}, u32[]{:S(2)}) async-start(bf16[16,512,128]{2,1,0:T(8,128)(2,1)} %to_sigma.1.rest_0_.rest_1_), calls=%async_computation.4 | async-start | bytes 4194304 | tf_op jit(solution)/shard_map/all_to_all | solution.py:691
  143.8 4.9 %collective-permute-done.2.away_ref = bf16[2,8,256,128]{3,2,1,0:T(8,128)(2,1)} collective-permute-done((bf16[2,8,256,128]{3,2,1,0:T(8,128)(2,1)}, bf16[2,8,256,128]{3,2,1,0:T(8,128)(2,1)}, u32[]{:S(2)}, u32[]{:S(2)}) %collective-permute-start.2) | collective-permute-done | bytes 1048608 | tf_op jit(solution)/shard_map/ppermute | solution.py:697
  148.7 0.0 copy-done.10
  148.7 1.0 copy-done.20
  149.8 4.0 %make_rights.2.rest_0_ = bf16[32,384,256]{2,1,0:T(8,128)(2,1)} custom-call(s32[1]{0:T(128)} %bitcast.half_ref, bf16[16,256,128]{2,1,0:T(8,128)(2,1)S(1)} %copy-done.7, bf16[8,256,128]{2,1,0:T(8,128)(2,1)S(1)} %copy-done.20, bf16[2,8,256,128]{3,2,1,0:T(8,128)(2,1)} %collective-permute-done.2.away_ref, bf16[16,512,128]{2,1,0:T(8,128)(2,1)S(1)} %copy-done.10), custom_call_target="tpu_custom_call" | custom-call | flops 99999997952 | bytes 1048576 | tf_op jit(solution)/shard_map/make_rights/pallas_call | solution.py:577
  153.8 0.0 copy-done.9
  153.8 4.0 %make_rights.3.rights = bf16[32,384,256]{2,1,0:T(8,128)(2,1)} custom-call(s32[1]{0:T(128)} %bitcast.half_ref, bf16[16,256,128]{2,1,0:T(8,128)(2,1)S(1)} %copy-done.9, bf16[8,256,128]{2,1,0:T(8,128)(2,1)S(1)} %copy-done.25, bf16[2,8,256,128]{3,2,1,0:T(8,128)(2,1)} %collective-permute-done.2.away_ref, ...), custom_call_target="tpu_custom_call", output_to_operand_aliasing={{}: (4, {})} | custom-call | flops 99999997952 | bytes 1048576 | tf_op jit(solution)/shard_map/make_rights/pallas_call | solution.py:577
  157.8 15.6 %all-to-all-done.4.sigma = bf16[16,512,128]{2,1,0:T(8,128)(2,1)} async-done(((bf16[16,512,128]{2,1,0:T(8,128)(2,1)}), bf16[16,512,128]{2,1,0:T(8,128)(2,1)}, u32[]{:S(2)}, u32[]{:S(2)}) %all-to-all-start.4) | async-done | bytes 2097184 | tf_op jit(solution)/shard_map/all_to_all | solution.py:691
  173.4 7.5 %volterra.1 = bf16[16,512,128]{2,1,0:T(8,128)(2,1)S(1)} custom-call(s32[1]{0:T(128)} %bitcast.half_ref, bf16[16,512,128]{2,1,0:T(8,128)(2,1)} %all-to-all-done.4.sigma, bf16[32,384,256]{2,1,0:T(8,128)(2,1)} %make_rights.3.rights), custom_call_target="tpu_custom_call" | custom-call | tf_op jit(solution)/shard_map/volterra/pallas_call | solution.py:665
  181.0 30.1 %all_to_all.30.blocks_ref = bf16[16,512,128]{2,1,0:T(8,128)(2,1)S(1)} all-to-all(bf16[16,512,128]{2,1,0:T(8,128)(2,1)S(1)} %volterra.1), channel_id=1, replica_groups=mesh['half'=2,'line'=8,'tcol'=2] {'tcol','line'}, dimensions={0} | all-to-all | bytes 4194304 | tf_op jit(solution)/shard_map/all_to_all | solution.py:691
  211.1 2.6 %collect.1 = (bf16[2,8,64,512]{3,2,1,0:T(8,128)(2,1)}, bf16[2,8,64,512]{3,2,1,0:T(8,128)(2,1)}) custom-call(bf16[16,512,128]{2,1,0:T(8,128)(2,1)S(1)} %all_to_all.30.blocks_ref), custom_call_target="tpu_custom_call" | custom-call | tf_op jit(solution)/shard_map/collect/pallas_call | solution.py:290
  (34 shorter events, 0.1 us)
Async XLA Ops:
  3.3 22.5 %all-to-all-start = ((bf16[16,256,128]{2,1,0:T(8,128)(2,1)}), bf16[16,256,128]{2,1,0:T(8,128)(2,1)S(1)}, u32[]{:S(2)}, u32[]{:S(2)}) async-start(bf16[16,256,128]{2,1,0:T(8,128)(2,1)} %bitcast.14), calls=%async_computation | async-start | bytes 2097152 | tf_op jit(solution)/shard_map/all_to_all | solution.py:691
  9.6 2.7 %copy-start.28 = (s32[512]{0:T(512)S(1)}, s32[512]{0:T(512)}, u32[]{:S(2)}) copy-start(s32[512]{0:T(512)} %param.6) | copy-start | bytes 6148
  16.9 1.4 copy-start
  18.3 1.3 copy-start.15
  25.8 32.0 %copy-start.6 = (bf16[16,256,128]{2,1,0:T(8,128)(2,1)}, bf16[16,256,128]{2,1,0:T(8,128)(2,1)S(1)}, u32[]{:S(2)}) copy-start(bf16[16,256,128]{2,1,0:T(8,128)(2,1)S(1)} %all-to-all-done.own) | copy-start | bytes 3145732
  25.8 30.9 %all-to-all-start.1 = ((bf16[16,256,128]{2,1,0:T(8,128)(2,1)}), bf16[16,256,128]{2,1,0:T(8,128)(2,1)S(1)}, u32[]{:S(2)}, u32[]{:S(2)}) async-start(bf16[16,256,128]{2,1,0:T(8,128)(2,1)} %gate.2), calls=%async_computation.1 | async-start | bytes 2097152 | tf_op jit(solution)/shard_map/all_to_all | solution.py:691
  30.5 27.3 %collective-permute-start = (bf16[8,256,128]{2,1,0:T(8,128)(2,1)}, bf16[8,256,128]{2,1,0:T(8,128)(2,1)S(1)}, u32[]{:S(2)}, u32[]{:S(2)}) collective-permute-start(bf16[8,256,128]{2,1,0:T(8,128)(2,1)} %get-tuple-element.21), channel_id=1, source_target_pairs={{0,16},{16,0},{1,17},{17,1},{2,18},{18,2},{3,19},{19,3},{4,20},{20... | collective-permute-start | bytes 1572872 | tf_op jit(solution)/shard_map/ppermute | solution.py:697
  56.7 24.3 %copy-start.8 = (bf16[16,256,128]{2,1,0:T(8,128)(2,1)}, bf16[16,256,128]{2,1,0:T(8,128)(2,1)S(1)}, u32[]{:S(2)}) copy-start(bf16[16,256,128]{2,1,0:T(8,128)(2,1)S(1)} %all-to-all-done.1.rest_0_.own) | copy-start | bytes 3145732
  57.8 23.2 %collective-permute-start.1 = (bf16[8,256,128]{2,1,0:T(8,128)(2,1)}, bf16[8,256,128]{2,1,0:T(8,128)(2,1)S(1)}, u32[]{:S(2)}, u32[]{:S(2)}) collective-permute-start(bf16[8,256,128]{2,1,0:T(8,128)(2,1)} %get-tuple-element.23), channel_id=1, source_target_pairs={{0,16},{16,0},{1,17},{17,1},{2,18},{18,2},{3,19},{19,3},{4,20},{20... | collective-permute-start | bytes 1572872 | tf_op jit(solution)/shard_map/ppermute | solution.py:697
  57.8 3.3 %copy-start.19 = (bf16[8,256,128]{2,1,0:T(8,128)(2,1)}, bf16[8,256,128]{2,1,0:T(8,128)(2,1)S(1)}, u32[]{:S(2)}) copy-start(bf16[8,256,128]{2,1,0:T(8,128)(2,1)S(1)} %collective-permute-done.far.near_ref) | copy-start | bytes 1572868
  61.1 33.0 %all-to-all-start.2 = ((bf16[16,256,128]{2,1,0:T(8,128)(2,1)}), bf16[16,256,128]{2,1,0:T(8,128)(2,1)S(1)}, u32[]{:S(2)}, u32[]{:S(2)}) async-start(bf16[16,256,128]{2,1,0:T(8,128)(2,1)} %get-tuple-element.12), calls=%async_computation.2 | async-start | bytes 2097152 | tf_op jit(solution)/shard_map/all_to_all | solution.py:691
  81.0 3.3 %copy-start.24 = (bf16[8,256,128]{2,1,0:T(8,128)(2,1)}, bf16[8,256,128]{2,1,0:T(8,128)(2,1)S(1)}, u32[]{:S(2)}) copy-start(bf16[8,256,128]{2,1,0:T(8,128)(2,1)S(1)} %collective-permute-done.1.far.near_ref) | copy-start | bytes 1572868
  84.3 0.6 copy-start.22
  84.9 13.8 %copy-start.26 = (bf16[1,8,256,128]{3,2,1,0:T(8,128)(2,1)S(1)}, bf16[1,8,256,128]{3,2,1,0:T(8,128)(2,1)}, u32[]{:S(2)}) copy-start(bf16[1,8,256,128]{3,2,1,0:T(8,128)(2,1)} %get-tuple-element.20) | copy-start | bytes 1572868
  84.9 13.8 %copy-start.27 = (bf16[1,8,256,128]{3,2,1,0:T(8,128)(2,1)S(1)}, bf16[1,8,256,128]{3,2,1,0:T(8,128)(2,1)}, u32[]{:S(2)}) copy-start(bf16[1,8,256,128]{3,2,1,0:T(8,128)(2,1)} %get-tuple-element.22) | copy-start | bytes 1572868
  94.2 4.5 %copy-start.4 = (bf16[16,256,128]{2,1,0:T(8,128)(2,1)}, bf16[16,256,128]{2,1,0:T(8,128)(2,1)S(1)}, u32[]{:S(2)}) copy-start(bf16[16,256,128]{2,1,0:T(8,128)(2,1)S(1)} %all-to-all-done.2.refs_2_) | copy-start | bytes 3145732
  94.2 30.9 %all-to-all-start.3 = ((bf16[16,256,128]{2,1,0:T(8,128)(2,1)}), bf16[16,256,128]{2,1,0:T(8,128)(2,1)}, u32[]{:S(2)}, u32[]{:S(2)}) async-start(bf16[16,256,128]{2,1,0:T(8,128)(2,1)} %get-tuple-element.16), calls=%async_computation.3 | async-start | bytes 2097152 | tf_op jit(solution)/shard_map/all_to_all | solution.py:691
  99.8 1.9 copy-start.1
  99.8 1.9 copy-start.2
  99.8 1.9 copy-start.23
  99.8 48.9 %collective-permute-start.2 = (bf16[2,8,256,128]{3,2,1,0:T(8,128)(2,1)}, bf16[2,8,256,128]{3,2,1,0:T(8,128)(2,1)}, u32[]{:S(2)}, u32[]{:S(2)}) collective-permute-start(bf16[2,8,256,128]{3,2,1,0:T(8,128)(2,1)} %gate.3), channel_id=1, source_target_pairs={{0,16},{16,0},{1,17},{17,1},{2,18},{18,2},{3,19},{19,3},{4,20},{20... | collective-permute-start | bytes 3145736 | tf_op jit(solution)/shard_map/ppermute | solution.py:697
  101.6 1.2 copy-start.3
  102.9 3.8 %copy-start.5 = (bf16[16,256,128]{2,1,0:T(8,128)(2,1)S(1)}, bf16[16,256,128]{2,1,0:T(8,128)(2,1)}, u32[]{:S(2)}) copy-start(bf16[16,256,128]{2,1,0:T(8,128)(2,1)} %copy-done.4) | copy-start | bytes 3145732
  102.9 3.8 %copy-start.16 = (bf16[1024,1024]{1,0:T(8,128)(2,1)S(1)}, bf16[1024,1024]{1,0:T(8,128)(2,1)}, u32[]{:S(2)}) copy-start(bf16[1024,1024]{1,0:T(8,128)(2,1)} %copy-done.15) | copy-start | bytes 6291460
  105.2 1.4 copy-start.11
  106.6 18.4 %copy-start.21 = (f32[8,128]{1,0:T(8,128)S(1)}, f32[8,128]{1,0:T(8,128)}, u32[]{:S(2)}) copy-start(f32[8,128]{1,0:T(8,128)} %broadcast_multiply_fusion.refs_2_.coupling) | copy-start | bytes 12292
  108.4 2.1 copy-start.13
  110.4 1.3 copy-start.17
  125.0 1.6 copy-start.12
  126.6 2.2 %copy-start.14 = (f32[1024,1024]{1,0:T(8,128)S(1)}, f32[1024,1024]{1,0:T(8,128)}, u32[]{:S(2)}) copy-start(f32[1024,1024]{1,0:T(8,128)} %copy-done.13) | copy-start | bytes 12582916
  128.8 1.6 copy-start.18
  139.1 9.7 %copy-start.7 = (bf16[16,256,128]{2,1,0:T(8,128)(2,1)S(1)}, bf16[16,256,128]{2,1,0:T(8,128)(2,1)}, u32[]{:S(2)}) copy-start(bf16[16,256,128]{2,1,0:T(8,128)(2,1)} %copy-done.6) | copy-start | bytes 3145732
  139.1 9.7 %copy-start.10 = (bf16[16,512,128]{2,1,0:T(8,128)(2,1)S(1)}, bf16[16,512,128]{2,1,0:T(8,128)(2,1)}, u32[]{:S(2)}) copy-start(bf16[16,512,128]{2,1,0:T(8,128)(2,1)} %to_sigma.1.rest_0_.rest_1_) | copy-start | bytes 6291460
  139.1 34.3 %all-to-all-start.4 = ((bf16[16,512,128]{2,1,0:T(8,128)(2,1)}), bf16[16,512,128]{2,1,0:T(8,128)(2,1)}, u32[]{:S(2)}, u32[]{:S(2)}) async-start(bf16[16,512,128]{2,1,0:T(8,128)(2,1)} %to_sigma.1.rest_0_.rest_1_), calls=%async_computation.4 | async-start | bytes 4194304 | tf_op jit(solution)/shard_map/all_to_all | solution.py:691
  143.8 10.0 %copy-start.9 = (bf16[16,256,128]{2,1,0:T(8,128)(2,1)S(1)}, bf16[16,256,128]{2,1,0:T(8,128)(2,1)}, u32[]{:S(2)}) copy-start(bf16[16,256,128]{2,1,0:T(8,128)(2,1)} %copy-done.8) | copy-start | bytes 3145732
  148.7 1.0 copy-start.20
  149.8 4.0 %copy-start.25 = (bf16[8,256,128]{2,1,0:T(8,128)(2,1)S(1)}, bf16[8,256,128]{2,1,0:T(8,128)(2,1)}, u32[]{:S(2)}) copy-start(bf16[8,256,128]{2,1,0:T(8,128)(2,1)} %copy-done.24) | copy-start | bytes 1572868

commit v17 on v16

--- a/solution.py
+++ b/solution.py
@@ -564,7 +564,7 @@
         out[at, 2 * lanes :] = jnp.where(keep, greens[0] - greens[1], 0.0).astype(BF16)
 
 
-STEPS = 8
+STEPS = 2
 PARTS = 2
 
 

time: 215 us -> 212 us (0.986)
  Pallas kernels: 47.4 us -> 39.3 us
  waiting for transfers between devices: 75.7 us -> 81 us
    pallas_call x2, Pallas kernels: 6.6 us -> 2.79 us  [to_crossed(): pl.pallas_call(functools.partial(cross_kernel, rows), grid=(STEPS,), out_...]
    ppermute x3, waiting for transfers between devices: 9.56 us -> 12.5 us  [swap(): return lax.ppermute(array, 'half', [(0, 1), (1, 0)])]
    pallas_call x1, Pallas kernels: 7.55 us -> 4.7 us  [volterra(): pl.pallas_call(functools.partial(volterra_kernel, rows), grid=(STEPS,), o...]
    all_to_all x5, waiting for transfers between devices: 66.2 us -> 68.5 us  [exchange(): return lax.all_to_all(blocks, ('tcol', 'line'), 0, 0, tiled=True)]
  transfers between devices with their start and end apart: 8 -> 8, of which waited for: 7 -> 7; matrix products, arithmetic and copies ran while one was open for 2% -> 2% of each run, Pallas kernels for 16% -> 14%
where the time goes in v17:
time: 212 us; the launch traced here: 211 us
  waiting for transfers between devices  81 us (38%)
  Pallas kernels  39.3 us (19%)
  starting transfers between devices  37.6 us (18%)
  blocking collectives  30 us (14%)
  local copies, waits for them, and re-layouts  19.5 us (9%)
    all_to_all x5, waiting for transfers between devices, exchange(): return lax.all_to_all(blocks, ('tcol', 'line'), 0, 0, tiled=True)  68.5 us
    all_to_all x5, starting transfers between devices, exchange(): return lax.all_to_all(blocks, ('tcol', 'line'), 0, 0, tiled=True)  34.4 us
    all_to_all x1, blocking collectives, exchange(): return lax.all_to_all(blocks, ('tcol', 'line'), 0, 0, tiled=True)  30 us
    unnamed x58, local copies, waits for them, and re-layouts  17 us
    ppermute x3, waiting for transfers between devices, swap(): return lax.ppermute(array, 'half', [(0, 1), (1, 0)])  12.5 us
    pallas_call x1, Pallas kernels, to_sigma(): pl.pallas_call(functools.partial(sigma_kernel, norm_factor), out_shape=pl...  8.65 us
    pallas_call x2, Pallas kernels, make_rights(): pl.pallas_call(functools.partial(rights_kernel, rows), grid=(steps,), out...  6.66 us
    pallas_call x2, Pallas kernels, spread(): pl.pallas_call(spread_kernel, grid=(count // LANES,), out_shape=pltpu.HBM...  5.3 us
  transfers between devices with their start and end apart: 8, of which 7 were waited for; matrix products, arithmetic and copies ran while one was open for 2% of the time, Pallas kernels for 14%

profile of v17, /device:TPU:0, one launch (start us, length us, event | category | flops | bytes accessed | tf_op | source)
XLA Modules:
  0.0 210.8 jit_solution(12298526511952051901)
XLA Ops:
  0.6 2.6 %spread.2 = bf16[4096,128]{1,0:T(8,128)(2,1)} custom-call(bf16[2,8,64,512]{3,2,1,0:T(8,128)(2,1)} %lesser.5, bf16[2,8,64,512]{3,2,1,0:T(8,128)(2,1)} %greater.5), custom_call_target="tpu_custom_call" | custom-call | tf_op jit(solution)/shard_map/spread/pallas_call | solution.py:260
  3.3 6.3 %all-to-all-start = ((bf16[16,256,128]{2,1,0:T(8,128)(2,1)}), bf16[16,256,128]{2,1,0:T(8,128)(2,1)S(1)}, u32[]{:S(2)}, u32[]{:S(2)}) async-start(bf16[16,256,128]{2,1,0:T(8,128)(2,1)} %bitcast.14), calls=%async_computation | async-start | bytes 2097152 | tf_op jit(solution)/shard_map/all_to_all | solution.py:691
  9.6 0.0 copy-start.28
  9.6 2.7 %spread.3 = bf16[4096,128]{1,0:T(8,128)(2,1)} custom-call(bf16[2,8,64,512]{3,2,1,0:T(8,128)(2,1)} %lesser.5, bf16[2,8,64,512]{3,2,1,0:T(8,128)(2,1)} %greater.5), custom_call_target="tpu_custom_call" | custom-call | tf_op jit(solution)/shard_map/spread/pallas_call | solution.py:260
  12.2 0.0 copy-done.28
  12.2 0.1 copy.9.column_ref
  12.4 4.5 %make_tables.1 = (bf16[1024,1024]{1,0:T(8,128)(2,1)S(1)}, bf16[1024,1024]{1,0:T(8,128)(2,1)S(1)}) custom-call(s32[512,1]{1,0:T(8,128)S(1)} %copy.9.column_ref), custom_call_target="tpu_custom_call" | custom-call | tf_op jit(solution)/shard_map/make_tables/pallas_call | solution.py:323
  16.9 0.0 copy-start
  16.9 1.4 copy-done
  18.3 1.3 copy-done.15
  20.3 0.1 fusion.4
  20.4 0.1 dynamic_slice.20
  20.5 0.1 dynamic_slice.19
  20.5 0.1 pad_maximum_fusion.1
  20.6 0.7 broadcast_multiply_fusion.refs_2_.coupling
  21.3 4.5 %all-to-all-done.own = bf16[16,256,128]{2,1,0:T(8,128)(2,1)S(1)} async-done(((bf16[16,256,128]{2,1,0:T(8,128)(2,1)}), bf16[16,256,128]{2,1,0:T(8,128)(2,1)S(1)}, u32[]{:S(2)}, u32[]{:S(2)}) %all-to-all-start) | async-done | bytes 1048608 | tf_op jit(solution)/shard_map/all_to_all | solution.py:691
  25.8 3.7 %all-to-all-start.1 = ((bf16[16,256,128]{2,1,0:T(8,128)(2,1)}), bf16[16,256,128]{2,1,0:T(8,128)(2,1)S(1)}, u32[]{:S(2)}, u32[]{:S(2)}) async-start(bf16[16,256,128]{2,1,0:T(8,128)(2,1)} %gate.2), calls=%async_computation.1 | async-start | bytes 2097152 | tf_op jit(solution)/shard_map/all_to_all | solution.py:691
  29.4 1.0 dynamic-slice_bitcast_fusion.1
  30.5 2.6 %collective-permute-start = (bf16[8,256,128]{2,1,0:T(8,128)(2,1)}, bf16[8,256,128]{2,1,0:T(8,128)(2,1)S(1)}, u32[]{:S(2)}, u32[]{:S(2)}) collective-permute-start(bf16[8,256,128]{2,1,0:T(8,128)(2,1)} %get-tuple-element.21), channel_id=1, source_target_pairs={{0,16},{16,0},{1,17},{17,1},{2,18},{18,2},{3,19},{19,3},{4,20},{20... | collective-permute-start | bytes 1572872 | tf_op jit(solution)/shard_map/ppermute | solution.py:697
  33.1 23.6 %all-to-all-done.1.rest_0_.own = bf16[16,256,128]{2,1,0:T(8,128)(2,1)S(1)} async-done(((bf16[16,256,128]{2,1,0:T(8,128)(2,1)}), bf16[16,256,128]{2,1,0:T(8,128)(2,1)S(1)}, u32[]{:S(2)}, u32[]{:S(2)}) %all-to-all-start.1) | async-done | bytes 1048608 | tf_op jit(solution)/shard_map/all_to_all | solution.py:691
  56.7 1.1 dynamic-slice_bitcast_fusion
  57.8 0.0 collective-permute-start.1
  57.8 0.0 collective-permute-done.far.near_ref
  57.8 0.0 copy-done.6
  57.8 1.4 to_crossed.2
  59.2 0.0 copy-done.19
  59.2 15.3 %all-to-all-start.2 = ((bf16[16,256,128]{2,1,0:T(8,128)(2,1)}), bf16[16,256,128]{2,1,0:T(8,128)(2,1)S(1)}, u32[]{:S(2)}, u32[]{:S(2)}) async-start(bf16[16,256,128]{2,1,0:T(8,128)(2,1)} %get-tuple-element.12), calls=%async_computation.2 | async-start | bytes 2097152 | tf_op jit(solution)/shard_map/all_to_all | solution.py:691
  74.5 6.5 %collective-permute-done.1.far.near_ref = bf16[8,256,128]{2,1,0:T(8,128)(2,1)S(1)} collective-permute-done((bf16[8,256,128]{2,1,0:T(8,128)(2,1)}, bf16[8,256,128]{2,1,0:T(8,128)(2,1)S(1)}, u32[]{:S(2)}, u32[]{:S(2)}) %collective-permute-start.1) | collective-permute-done | bytes 524320 | tf_op jit(solution)/shard_map/ppermute | solution.py:697
  81.0 0.0 copy-done.8
  81.0 1.4 to_crossed.3
  82.4 0.0 copy-done.24
  82.4 0.6 copy-done.22
  83.0 11.0 %all-to-all-done.2.refs_2_ = bf16[16,256,128]{2,1,0:T(8,128)(2,1)S(1)} async-done(((bf16[16,256,128]{2,1,0:T(8,128)(2,1)}), bf16[16,256,128]{2,1,0:T(8,128)(2,1)S(1)}, u32[]{:S(2)}, u32[]{:S(2)}) %all-to-all-start.2) | async-done | bytes 1048608 | tf_op jit(solution)/shard_map/all_to_all | solution.py:691
  94.0 4.5 %all-to-all-start.3 = ((bf16[16,256,128]{2,1,0:T(8,128)(2,1)}), bf16[16,256,128]{2,1,0:T(8,128)(2,1)}, u32[]{:S(2)}, u32[]{:S(2)}) async-start(bf16[16,256,128]{2,1,0:T(8,128)(2,1)} %get-tuple-element.16), calls=%async_computation.3 | async-start | bytes 2097152 | tf_op jit(solution)/shard_map/all_to_all | solution.py:691
  98.5 0.0 copy-done.4
  98.6 0.0 copy-done.26
  98.6 1.1 pad_maximum_fusion.refs_0_
  99.6 0.6 collective-permute-start.2
  100.3 1.0 copy-done.1
  101.2 0.3 copy-done.2
  101.5 1.2 copy-done.3
  102.7 2.4 %to_sites.1.sites = bf16[1024,1024]{1,0:T(8,128)(2,1)S(1)} custom-call(bf16[2,8,64,512]{3,2,1,0:T(8,128)(2,1)S(1)} %copy-done.2, bf16[2,8,64,512]{3,2,1,0:T(8,128)(2,1)S(1)} %copy-done.3, bf16[1024,1024]{1,0:T(8,128)(2,1)S(1)} %copy-done.1, f32[8,128]{1,0:T(8,128)S(1)} %copy-done.23), custom_call_target="tpu_custom_call" | custom-call | tf_op jit(solution)/shard_map/to_sites/pallas_call | solution.py:354
  105.1 1.4 copy-done.11
  106.5 0.0 copy-done.16
  106.5 1.7 to_mirror.1
  108.2 2.1 copy-done.13
  110.3 1.3 copy-done.17
  111.6 12.3 %all-to-all-done.3 = bf16[16,256,128]{2,1,0:T(8,128)(2,1)} async-done(((bf16[16,256,128]{2,1,0:T(8,128)(2,1)}), bf16[16,256,128]{2,1,0:T(8,128)(2,1)}, u32[]{:S(2)}, u32[]{:S(2)}) %all-to-all-start.3) | async-done | bytes 1048608 | tf_op jit(solution)/shard_map/all_to_all | solution.py:691
  123.9 0.0 copy-done.21
  123.9 1.6 copy-done.12
  125.5 2.2 %copy-done.14 = f32[1024,1024]{1,0:T(8,128)S(1)} copy-done((f32[1024,1024]{1,0:T(8,128)S(1)}, f32[1024,1024]{1,0:T(8,128)}, u32[]{:S(2)}) %copy-start.14) | copy-done | bytes 4194328
  127.7 1.6 copy-done.18
  129.3 8.7 %to_sigma.1.rest_0_.rest_1_ = bf16[16,512,128]{2,1,0:T(8,128)(2,1)} custom-call(f32[1024,1024]{1,0:T(8,128)S(1)} %copy-done.14, bf16[4096,128]{1,0:T(8,128)(2,1)} %bitcast.6.crossed, bf16[1024,1024]{1,0:T(8,128)(2,1)S(1)} %copy-done.12, bf16[1024,512]{1,0:T(8,128)(2,1)S(1)} %get-tuple-element.18.columns, bf16[1024,1024]{1,0:T(8,128)(2,1)S(1)} %copy-done.18, ...), custom_call_target="tpu_custom_call" | custom-call | tf_op jit(solution)/shard_map/to_sigma/pallas_call | solution.py:514
  137.9 4.7 %all-to-all-start.4 = ((bf16[16,512,128]{2,1,0:T(8,128)(2,1)}), bf16[16,512,128]{2,1,0:T(8,128)(2,1)}, u32[]{:S(2)}, u32[]{:S(2)}) async-start(bf16[16,512,128]{2,1,0:T(8,128)(2,1)} %to_sigma.1.rest_0_.rest_1_), calls=%async_computation.4 | async-start | bytes 4194304 | tf_op jit(solution)/shard_map/all_to_all | solution.py:691
  142.6 6.0 %collective-permute-done.2.away_ref = bf16[2,8,256,128]{3,2,1,0:T(8,128)(2,1)} collective-permute-done((bf16[2,8,256,128]{3,2,1,0:T(8,128)(2,1)}, bf16[2,8,256,128]{3,2,1,0:T(8,128)(2,1)}, u32[]{:S(2)}, u32[]{:S(2)}) %collective-permute-start.2) | collective-permute-done | bytes 1048608 | tf_op jit(solution)/shard_map/ppermute | solution.py:697
  148.6 0.0 copy-done.10
  148.6 1.0 copy-done.20
  149.6 3.3 %make_rights.2.rest_0_ = bf16[32,384,256]{2,1,0:T(8,128)(2,1)} custom-call(s32[1]{0:T(128)} %bitcast.half_ref, bf16[16,256,128]{2,1,0:T(8,128)(2,1)S(1)} %copy-done.7, bf16[8,256,128]{2,1,0:T(8,128)(2,1)S(1)} %copy-done.20, bf16[2,8,256,128]{3,2,1,0:T(8,128)(2,1)} %collective-permute-done.2.away_ref, bf16[16,512,128]{2,1,0:T(8,128)(2,1)S(1)} %copy-done.10), custom_call_target="tpu_custom_call" | custom-call | flops 99999997952 | bytes 1048576 | tf_op jit(solution)/shard_map/make_rights/pallas_call | solution.py:577
  153.0 0.0 copy-done.9
  153.0 3.3 %make_rights.3.rights = bf16[32,384,256]{2,1,0:T(8,128)(2,1)} custom-call(s32[1]{0:T(128)} %bitcast.half_ref, bf16[16,256,128]{2,1,0:T(8,128)(2,1)S(1)} %copy-done.9, bf16[8,256,128]{2,1,0:T(8,128)(2,1)S(1)} %copy-done.25, bf16[2,8,256,128]{3,2,1,0:T(8,128)(2,1)} %collective-permute-done.2.away_ref, ...), custom_call_target="tpu_custom_call", output_to_operand_aliasing={{}: (4, {})} | custom-call | flops 99999997952 | bytes 1048576 | tf_op jit(solution)/shard_map/make_rights/pallas_call | solution.py:577
  156.3 17.1 %all-to-all-done.4.sigma = bf16[16,512,128]{2,1,0:T(8,128)(2,1)} async-done(((bf16[16,512,128]{2,1,0:T(8,128)(2,1)}), bf16[16,512,128]{2,1,0:T(8,128)(2,1)}, u32[]{:S(2)}, u32[]{:S(2)}) %all-to-all-start.4) | async-done | bytes 2097184 | tf_op jit(solution)/shard_map/all_to_all | solution.py:691
  173.4 4.7 %volterra.1 = bf16[16,512,128]{2,1,0:T(8,128)(2,1)S(1)} custom-call(s32[1]{0:T(128)} %bitcast.half_ref, bf16[16,512,128]{2,1,0:T(8,128)(2,1)} %all-to-all-done.4.sigma, bf16[32,384,256]{2,1,0:T(8,128)(2,1)} %make_rights.3.rights), custom_call_target="tpu_custom_call" | custom-call | tf_op jit(solution)/shard_map/volterra/pallas_call | solution.py:665
  178.1 30.0 %all_to_all.30.blocks_ref = bf16[16,512,128]{2,1,0:T(8,128)(2,1)S(1)} all-to-all(bf16[16,512,128]{2,1,0:T(8,128)(2,1)S(1)} %volterra.1), channel_id=1, replica_groups=mesh['half'=2,'line'=8,'tcol'=2] {'tcol','line'}, dimensions={0} | all-to-all | bytes 4194304 | tf_op jit(solution)/shard_map/all_to_all | solution.py:691
  208.2 2.6 %collect.1 = (bf16[2,8,64,512]{3,2,1,0:T(8,128)(2,1)}, bf16[2,8,64,512]{3,2,1,0:T(8,128)(2,1)}) custom-call(bf16[16,512,128]{2,1,0:T(8,128)(2,1)S(1)} %all_to_all.30.blocks_ref), custom_call_target="tpu_custom_call" | custom-call | tf_op jit(solution)/shard_map/collect/pallas_call | solution.py:290
  (34 shorter events, 0.1 us)
Async XLA Ops:
  3.3 22.5 %all-to-all-start = ((bf16[16,256,128]{2,1,0:T(8,128)(2,1)}), bf16[16,256,128]{2,1,0:T(8,128)(2,1)S(1)}, u32[]{:S(2)}, u32[]{:S(2)}) async-start(bf16[16,256,128]{2,1,0:T(8,128)(2,1)} %bitcast.14), calls=%async_computation | async-start | bytes 2097152 | tf_op jit(solution)/shard_map/all_to_all | solution.py:691
  9.6 2.7 %copy-start.28 = (s32[512]{0:T(512)S(1)}, s32[512]{0:T(512)}, u32[]{:S(2)}) copy-start(s32[512]{0:T(512)} %param.6) | copy-start | bytes 6148
  16.9 1.4 copy-start
  18.3 1.3 copy-start.15
  25.8 32.0 %copy-start.6 = (bf16[16,256,128]{2,1,0:T(8,128)(2,1)}, bf16[16,256,128]{2,1,0:T(8,128)(2,1)S(1)}, u32[]{:S(2)}) copy-start(bf16[16,256,128]{2,1,0:T(8,128)(2,1)S(1)} %all-to-all-done.own) | copy-start | bytes 3145732
  25.8 30.9 %all-to-all-start.1 = ((bf16[16,256,128]{2,1,0:T(8,128)(2,1)}), bf16[16,256,128]{2,1,0:T(8,128)(2,1)S(1)}, u32[]{:S(2)}, u32[]{:S(2)}) async-start(bf16[16,256,128]{2,1,0:T(8,128)(2,1)} %gate.2), calls=%async_computation.1 | async-start | bytes 2097152 | tf_op jit(solution)/shard_map/all_to_all | solution.py:691
  30.5 27.3 %collective-permute-start = (bf16[8,256,128]{2,1,0:T(8,128)(2,1)}, bf16[8,256,128]{2,1,0:T(8,128)(2,1)S(1)}, u32[]{:S(2)}, u32[]{:S(2)}) collective-permute-start(bf16[8,256,128]{2,1,0:T(8,128)(2,1)} %get-tuple-element.21), channel_id=1, source_target_pairs={{0,16},{16,0},{1,17},{17,1},{2,18},{18,2},{3,19},{19,3},{4,20},{20... | collective-permute-start | bytes 1572872 | tf_op jit(solution)/shard_map/ppermute | solution.py:697
  56.7 24.3 %copy-start.8 = (bf16[16,256,128]{2,1,0:T(8,128)(2,1)}, bf16[16,256,128]{2,1,0:T(8,128)(2,1)S(1)}, u32[]{:S(2)}) copy-start(bf16[16,256,128]{2,1,0:T(8,128)(2,1)S(1)} %all-to-all-done.1.rest_0_.own) | copy-start | bytes 3145732
  57.8 23.2 %collective-permute-start.1 = (bf16[8,256,128]{2,1,0:T(8,128)(2,1)}, bf16[8,256,128]{2,1,0:T(8,128)(2,1)S(1)}, u32[]{:S(2)}, u32[]{:S(2)}) collective-permute-start(bf16[8,256,128]{2,1,0:T(8,128)(2,1)} %get-tuple-element.23), channel_id=1, source_target_pairs={{0,16},{16,0},{1,17},{17,1},{2,18},{18,2},{3,19},{19,3},{4,20},{20... | collective-permute-start | bytes 1572872 | tf_op jit(solution)/shard_map/ppermute | solution.py:697
  57.8 1.4 copy-start.19
  59.2 34.8 %all-to-all-start.2 = ((bf16[16,256,128]{2,1,0:T(8,128)(2,1)}), bf16[16,256,128]{2,1,0:T(8,128)(2,1)S(1)}, u32[]{:S(2)}, u32[]{:S(2)}) async-start(bf16[16,256,128]{2,1,0:T(8,128)(2,1)} %get-tuple-element.12), calls=%async_computation.2 | async-start | bytes 2097152 | tf_op jit(solution)/shard_map/all_to_all | solution.py:691
  81.0 1.4 copy-start.24
  82.4 0.6 copy-start.22
  83.0 15.5 %copy-start.26 = (bf16[1,8,256,128]{3,2,1,0:T(8,128)(2,1)S(1)}, bf16[1,8,256,128]{3,2,1,0:T(8,128)(2,1)}, u32[]{:S(2)}) copy-start(bf16[1,8,256,128]{3,2,1,0:T(8,128)(2,1)} %get-tuple-element.20) | copy-start | bytes 1572868
  83.0 15.6 %copy-start.27 = (bf16[1,8,256,128]{3,2,1,0:T(8,128)(2,1)S(1)}, bf16[1,8,256,128]{3,2,1,0:T(8,128)(2,1)}, u32[]{:S(2)}) copy-start(bf16[1,8,256,128]{3,2,1,0:T(8,128)(2,1)} %get-tuple-element.22) | copy-start | bytes 1572868
  94.0 4.5 %copy-start.4 = (bf16[16,256,128]{2,1,0:T(8,128)(2,1)}, bf16[16,256,128]{2,1,0:T(8,128)(2,1)S(1)}, u32[]{:S(2)}) copy-start(bf16[16,256,128]{2,1,0:T(8,128)(2,1)S(1)} %all-to-all-done.2.refs_2_) | copy-start | bytes 3145732
  94.0 29.9 %all-to-all-start.3 = ((bf16[16,256,128]{2,1,0:T(8,128)(2,1)}), bf16[16,256,128]{2,1,0:T(8,128)(2,1)}, u32[]{:S(2)}, u32[]{:S(2)}) async-start(bf16[16,256,128]{2,1,0:T(8,128)(2,1)} %get-tuple-element.16), calls=%async_computation.3 | async-start | bytes 2097152 | tf_op jit(solution)/shard_map/all_to_all | solution.py:691
  99.6 1.6 copy-start.1
  99.6 1.9 copy-start.2
  99.6 1.9 copy-start.23
  99.6 48.9 %collective-permute-start.2 = (bf16[2,8,256,128]{3,2,1,0:T(8,128)(2,1)}, bf16[2,8,256,128]{3,2,1,0:T(8,128)(2,1)}, u32[]{:S(2)}, u32[]{:S(2)}) collective-permute-start(bf16[2,8,256,128]{3,2,1,0:T(8,128)(2,1)} %gate.3), channel_id=1, source_target_pairs={{0,16},{16,0},{1,17},{17,1},{2,18},{18,2},{3,19},{19,3},{4,20},{20... | collective-permute-start | bytes 3145736 | tf_op jit(solution)/shard_map/ppermute | solution.py:697
  101.5 1.2 copy-start.3
  102.7 3.8 %copy-start.5 = (bf16[16,256,128]{2,1,0:T(8,128)(2,1)S(1)}, bf16[16,256,128]{2,1,0:T(8,128)(2,1)}, u32[]{:S(2)}) copy-start(bf16[16,256,128]{2,1,0:T(8,128)(2,1)} %copy-done.4) | copy-start | bytes 3145732
  102.7 3.8 %copy-start.16 = (bf16[1024,1024]{1,0:T(8,128)(2,1)S(1)}, bf16[1024,1024]{1,0:T(8,128)(2,1)}, u32[]{:S(2)}) copy-start(bf16[1024,1024]{1,0:T(8,128)(2,1)} %copy-done.15) | copy-start | bytes 6291460
  105.1 1.4 copy-start.11
  106.5 17.4 %copy-start.21 = (f32[8,128]{1,0:T(8,128)S(1)}, f32[8,128]{1,0:T(8,128)}, u32[]{:S(2)}) copy-start(f32[8,128]{1,0:T(8,128)} %broadcast_multiply_fusion.refs_2_.coupling) | copy-start | bytes 12292
  108.2 2.1 copy-start.13
  110.3 1.3 copy-start.17
  123.9 1.6 copy-start.12
  125.5 2.2 %copy-start.14 = (f32[1024,1024]{1,0:T(8,128)S(1)}, f32[1024,1024]{1,0:T(8,128)}, u32[]{:S(2)}) copy-start(f32[1024,1024]{1,0:T(8,128)} %copy-done.13) | copy-start | bytes 12582916
  127.7 1.6 copy-start.18
  137.9 10.7 %copy-start.7 = (bf16[16,256,128]{2,1,0:T(8,128)(2,1)S(1)}, bf16[16,256,128]{2,1,0:T(8,128)(2,1)}, u32[]{:S(2)}) copy-start(bf16[16,256,128]{2,1,0:T(8,128)(2,1)} %copy-done.6) | copy-start | bytes 3145732
  137.9 10.7 %copy-start.10 = (bf16[16,512,128]{2,1,0:T(8,128)(2,1)S(1)}, bf16[16,512,128]{2,1,0:T(8,128)(2,1)}, u32[]{:S(2)}) copy-start(bf16[16,512,128]{2,1,0:T(8,128)(2,1)} %to_sigma.1.rest_0_.rest_1_) | copy-start | bytes 6291460
  137.9 35.5 %all-to-all-start.4 = ((bf16[16,512,128]{2,1,0:T(8,128)(2,1)}), bf16[16,512,128]{2,1,0:T(8,128)(2,1)}, u32[]{:S(2)}, u32[]{:S(2)}) async-start(bf16[16,512,128]{2,1,0:T(8,128)(2,1)} %to_sigma.1.rest_0_.rest_1_), calls=%async_computation.4 | async-start | bytes 4194304 | tf_op jit(solution)/shard_map/all_to_all | solution.py:691
  142.6 10.3 %copy-start.9 = (bf16[16,256,128]{2,1,0:T(8,128)(2,1)S(1)}, bf16[16,256,128]{2,1,0:T(8,128)(2,1)}, u32[]{:S(2)}) copy-start(bf16[16,256,128]{2,1,0:T(8,128)(2,1)} %copy-done.8) | copy-start | bytes 3145732
  148.6 1.0 copy-start.20
  149.6 3.3 %copy-start.25 = (bf16[8,256,128]{2,1,0:T(8,128)(2,1)S(1)}, bf16[8,256,128]{2,1,0:T(8,128)(2,1)}, u32[]{:S(2)}) copy-start(bf16[8,256,128]{2,1,0:T(8,128)(2,1)} %copy-done.24) | copy-start | bytes 1572868
